TPU v7x, 32 devices: a whole 2x2x4 slice. The times are simulated.
32 devices in a mesh: seq: 16 (over z, y, x), shard: 2 (over core).
Axes of the slice: x: 2, y: 2, z: 4, core: 2. Of those that a mesh axis runs over, the one named last changes fastest.
Arguments:
- tokens: bfloat16 [2, 2048, 768], P('shard', 'seq'), may hold values from -6 to 6
- cotangent: bfloat16 [2, 2048, 768], P('shard', 'seq'), may hold values from -6 to 6
- lengths: int32 [2], replicated, may hold values from 1921 to 2048
- qkv_weight: bfloat16 [768, 2304], P('shard'), may hold values from -0.21875 to 0.21875
- query_bias: bfloat16 [768], P('shard'), may hold values from -1.75 to 1.75
- value_bias: bfloat16 [768], P('shard'), may hold values from -1.75 to 1.75
- out_weight: bfloat16 [768, 768], P('shard'), may hold values from -6 to 6
- out_bias: bfloat16 [768], P('shard'), may hold values from -1.75 to 1.75
- first_gain: bfloat16 [768], P('shard'), may hold values from 0.5 to 1.5
- first_shift: bfloat16 [768], P('shard'), may hold values from -1.75 to 1.75
- up_weight: bfloat16 [768, 3072], P('shard'), may hold values from -0.21875 to 0.21875
- up_bias: bfloat16 [3072], P('shard'), may hold values from -1.75 to 1.75
- down_weight: bfloat16 [3072, 768], P('shard'), may hold values from -0.109375 to 0.109375
- down_bias: bfloat16 [768], P('shard'), may hold values from -1.75 to 1.75
- second_gain: bfloat16 [768], P('shard'), may hold values from 0.5 to 1.5
- second_shift: bfloat16 [768], P('shard'), may hold values from -1.75 to 1.75
Outputs:
- layer_out: bfloat16 [2, 2048, 768], P('shard', 'seq')
- input_grad: float32 [2, 2048, 768], P('shard', 'seq')
- qkv_weight_grad: float32 [768, 2304], P('shard')
- query_bias_grad: float32 [768], P('shard')
- value_bias_grad: float32 [768], P('shard')
- out_weight_grad: float32 [768, 768], P('shard')
- out_bias_grad: float32 [768], P('shard')
- first_gain_grad: float32 [768], P('shard')
- first_shift_grad: float32 [768], P('shard')
- up_weight_grad: float32 [768, 3072], P('shard')
- up_bias_grad: float32 [3072], P('shard')
- down_weight_grad: float32 [3072, 768], P('shard')
- down_bias_grad: float32 [768], P('shard')
- second_gain_grad: float32 [768], P('shard')
- second_shift_grad: float32 [768], P('shard')
All inputs are finite; a program needn't handle non-finite values.
Results may differ from a plain program's by a relative error of at most 0.035.
Values may be sent and summed in bfloat16 or wider, within the bound.
No kernel may reach another device: no remote copies, remote signals or barrier semaphores. Data moves between devices by JAX's collectives and lax.ppermute only.
A program may use at most 192 MiB of HBM per device.

v0:
```python
import math

import jax
import jax.numpy as jnp
from jax import lax
from jax.sharding import PartitionSpec as P

HEADS = 12
HEAD_DIM = 64


EPSILON = 1e-12


def from_behind(block, axis, distance):
    devices = range(lax.axis_size(axis))
    route = [((i - distance) % len(devices), i) for i in devices]
    return lax.ppermute(block, axis, route)


def layer_norm(hidden, gain, shift):
    center = hidden - jnp.mean(hidden, axis=-1, keepdims=True)
    spread = jnp.mean(center * center, axis=-1, keepdims=True)
    return center * lax.rsqrt(spread + EPSILON) * gain + shift


def gelu_exact(values):
    return jax.nn.gelu(values, approximate=False)


def in_blocks(block_fn, running, pieces, offset):
    row_count = pieces[0].shape[0]
    block_rows = row_count if row_count <= 2048 else math.gcd(row_count, 2048)
    number = row_count // block_rows
    if number == 1:
        return block_fn(running, pieces, offset)

    def advance(block_index, inner_state):
        sliced = tuple(
            (
                lax.dynamic_slice_in_dim(member, block_index * block_rows, block_rows, 0)
                for member in pieces
            )
        )
        return block_fn(inner_state, sliced, offset + block_index * block_rows)

    return lax.fori_loop(0, number, advance, running)


def forward_block(running, pieces, offset, queries, length):
    key_rows, value_rows = pieces
    highest, totals, weighted = running
    scores = (
        jnp.einsum("qhd,khd->hqk", queries, key_rows, preferred_element_type=jnp.float32) * 0.125
    )
    places = offset + jnp.arange(key_rows.shape[0], dtype=jnp.int32)
    usable = (places < length)[None, None, :]
    block_peak = jnp.max(jnp.where(usable, scores, -1e30), axis=2)
    raised = jnp.maximum(highest, block_peak)
    weights = jnp.where(usable, jnp.exp(scores - raised[:, :, None]), 0.0)
    factor = jnp.exp(highest - raised)
    totals = totals * factor + jnp.sum(weights, axis=2)
    block_mix = jnp.einsum(
        "hqk,khd->qhd", weights.astype(jnp.bfloat16), value_rows, preferred_element_type=jnp.float32
    )
    weighted = weighted * jnp.transpose(factor)[:, :, None] + block_mix
    return (raised, totals, weighted)


def grad_block(queries, out_grad, log_total, correction, key_rows, value_rows, offset, length):
    scores = (
        jnp.einsum("qhd,khd->hqk", queries, key_rows, preferred_element_type=jnp.float32) * 0.125
    )
    places = offset + jnp.arange(key_rows.shape[0], dtype=jnp.int32)
    usable = (places < length)[None, None, :]
    probabilities = jnp.where(usable, jnp.exp(scores - log_total[:, :, None]), 0.0)
    prob_grad = jnp.einsum("qhd,khd->hqk", out_grad, value_rows, preferred_element_type=jnp.float32)
    score_grad = (probabilities * (prob_grad - correction[:, :, None])).astype(jnp.bfloat16)
    query_part = jnp.einsum(
        "hqk,khd->qhd", score_grad, key_rows, preferred_element_type=jnp.float32
    )
    key_part = jnp.einsum("hqk,qhd->khd", score_grad, queries, preferred_element_type=jnp.float32)
    value_part = jnp.einsum(
        "hqk,qhd->khd",
        probabilities.astype(jnp.bfloat16),
        out_grad,
        preferred_element_type=jnp.float32,
    )
    return (query_part, key_part, value_part)


def body(
    tokens,
    cotangent,
    lengths,
    qkv_weight,
    query_bias,
    value_bias,
    out_weight,
    out_bias,
    first_gain,
    first_shift,
    up_weight,
    up_bias,
    down_weight,
    down_bias,
    second_gain,
    second_shift,
):
    gathered = (
        lax.all_gather(qkv_weight, "shard", axis=0, tiled=True),
        lax.all_gather(query_bias, "shard", axis=0, tiled=True),
        lax.all_gather(value_bias, "shard", axis=0, tiled=True),
        lax.all_gather(out_weight, "shard", axis=0, tiled=True),
        lax.all_gather(out_bias, "shard", axis=0, tiled=True),
        lax.all_gather(first_gain, "shard", axis=0, tiled=True),
        lax.all_gather(first_shift, "shard", axis=0, tiled=True),
        lax.all_gather(up_weight, "shard", axis=0, tiled=True),
        lax.all_gather(up_bias, "shard", axis=0, tiled=True),
        lax.all_gather(down_weight, "shard", axis=0, tiled=True),
        lax.all_gather(down_bias, "shard", axis=0, tiled=True),
        lax.all_gather(second_gain, "shard", axis=0, tiled=True),
        lax.all_gather(second_shift, "shard", axis=0, tiled=True),
    )
    (
        qkv_matrix,
        query_offset,
        value_offset,
        out_matrix,
        out_offset,
        gain_one,
        shift_one,
        up_matrix,
        up_offset,
        down_matrix,
        down_offset,
        gain_two,
        shift_two,
    ) = gathered
    row_count = tokens.shape[1]
    model_width = tokens.shape[2]
    cycle_rank = lax.axis_index("seq")
    cycle_size = lax.axis_size("seq")
    length = lengths[lax.axis_index("shard")]
    inputs = tokens[0]
    zero_bias = jnp.zeros_like(query_offset)
    joined = jnp.dot(inputs, qkv_matrix, preferred_element_type=jnp.float32) + jnp.concatenate(
        [query_offset, zero_bias, value_offset]
    ).astype(jnp.float32)
    joined_low = joined.astype(jnp.bfloat16).reshape(row_count, 3, HEADS, HEAD_DIM)
    queries = joined_low[:, 0]
    key_rows = joined_low[:, 1]
    value_rows = joined_low[:, 2]
    initial = (
        jnp.full((HEADS, row_count), -1e30, jnp.float32),
        jnp.zeros((HEADS, row_count), jnp.float32),
        jnp.zeros((row_count, HEADS, HEAD_DIM), jnp.float32),
    )

    def block_fn(inner_state, sliced, start_row):
        return forward_block(inner_state, sliced, start_row, queries, length)

    highest, totals, weighted = in_blocks(
        block_fn,
        initial,
        (
            lax.all_gather(key_rows, "seq", axis=0, tiled=True),
            lax.all_gather(value_rows, "seq", axis=0, tiled=True),
        ),
        jnp.int32(0),
    )
    context = weighted / jnp.transpose(totals)[:, :, None]
    log_total = highest + jnp.log(totals)
    context_low = context.reshape(row_count, model_width).astype(jnp.bfloat16)
    branch = jnp.dot(
        context_low, out_matrix, preferred_element_type=jnp.float32
    ) + out_offset.astype(jnp.float32)
    residual_one = inputs.astype(jnp.float32) + branch
    normed_one, norm_pull_one = jax.vjp(
        layer_norm, residual_one, gain_one.astype(jnp.float32), shift_one.astype(jnp.float32)
    )
    normed_low = normed_one.astype(jnp.bfloat16)
    inner_sum = jnp.dot(
        normed_low, up_matrix, preferred_element_type=jnp.float32
    ) + up_offset.astype(jnp.float32)
    active, gelu_pull = jax.vjp(gelu_exact, inner_sum)
    active_low = active.astype(jnp.bfloat16)
    second = jnp.dot(
        active_low, down_matrix, preferred_element_type=jnp.float32
    ) + down_offset.astype(jnp.float32)
    residual_two = normed_low.astype(jnp.float32) + second
    outputs, norm_pull_two = jax.vjp(
        layer_norm, residual_two, gain_two.astype(jnp.float32), shift_two.astype(jnp.float32)
    )
    residual_two_grad, gain_two_grad, shift_two_grad = norm_pull_two(
        cotangent[0].astype(jnp.float32)
    )
    second_low = residual_two_grad.astype(jnp.bfloat16)
    down_bias_grad = jnp.sum(second_low.astype(jnp.float32), axis=0)
    down_weight_grad = jnp.einsum(
        "tf,td->fd", active_low, second_low, preferred_element_type=jnp.float32
    )
    active_grad = jnp.einsum(
        "td,fd->tf", second_low, down_matrix, preferred_element_type=jnp.float32
    )
    inner_low = gelu_pull(active_grad)[0].astype(jnp.bfloat16)
    up_bias_grad = jnp.sum(inner_low.astype(jnp.float32), axis=0)
    up_weight_grad = jnp.einsum(
        "td,tf->df", normed_low, inner_low, preferred_element_type=jnp.float32
    )
    normed_grad = (
        jnp.einsum("tf,df->td", inner_low, up_matrix, preferred_element_type=jnp.float32)
        + residual_two_grad
    )
    residual_one_grad, gain_one_grad, shift_one_grad = norm_pull_one(normed_grad)
    branch_low = residual_one_grad.astype(jnp.bfloat16)
    out_bias_grad = jnp.sum(branch_low.astype(jnp.float32), axis=0)
    out_weight_grad = jnp.einsum(
        "td,te->de", context_low, branch_low, preferred_element_type=jnp.float32
    )
    context_grad = jnp.einsum(
        "te,de->td", branch_low, out_matrix, preferred_element_type=jnp.float32
    ).astype(jnp.bfloat16)
    context_heads = context_grad.reshape(row_count, HEADS, HEAD_DIM)
    correction = jnp.einsum("qhd,qhd->hq", context_heads.astype(jnp.float32), context)
    zero_heads = jnp.zeros((row_count, HEADS, HEAD_DIM), jnp.float32)

    def cycle_turn(turn_number, cycle_state):
        moving_keys, moving_values, key_grad, value_grad, query_grad = cycle_state
        offset = (cycle_rank - turn_number) % cycle_size * row_count
        query_part, key_part, value_part = grad_block(
            queries,
            context_heads,
            log_total,
            correction,
            moving_keys,
            moving_values,
            offset,
            length,
        )
        moving_keys, moving_values = from_behind((moving_keys, moving_values), "seq", 1)
        key_grad, value_grad = (
            from_behind((key_grad + key_part).astype(jnp.bfloat16), "seq", 1).astype(jnp.float32),
            from_behind((value_grad + value_part).astype(jnp.bfloat16), "seq", 1).astype(
                jnp.float32
            ),
        )
        return (moving_keys, moving_values, key_grad, value_grad, query_grad + query_part)

    final_state = lax.fori_loop(
        0, cycle_size, cycle_turn, (key_rows, value_rows, zero_heads, zero_heads, zero_heads)
    )
    key_grad = final_state[2]
    value_grad = final_state[3]
    query_grad = final_state[4]
    joined_grad = (
        jnp.concatenate([query_grad * 0.125, key_grad * 0.125, value_grad], axis=1)
        .reshape(row_count, 3 * model_width)
        .astype(jnp.bfloat16)
    )
    joined_wide = joined_grad.astype(jnp.float32)
    query_bias_grad = jnp.sum(joined_wide[:, :model_width], axis=0)
    value_bias_grad = jnp.sum(joined_wide[:, 2 * model_width :], axis=0)
    qkv_weight_grad = jnp.einsum(
        "td,te->de", inputs, joined_grad, preferred_element_type=jnp.float32
    )
    input_grad = residual_one_grad + jnp.einsum(
        "te,de->td", joined_grad, qkv_matrix, preferred_element_type=jnp.float32
    )
    scattered = (
        lax.psum_scatter(
            qkv_weight_grad.astype(jnp.bfloat16), "shard", scatter_dimension=0, tiled=True
        ).astype(jnp.float32),
        lax.psum_scatter(
            query_bias_grad.astype(jnp.bfloat16), "shard", scatter_dimension=0, tiled=True
        ).astype(jnp.float32),
        lax.psum_scatter(
            value_bias_grad.astype(jnp.bfloat16), "shard", scatter_dimension=0, tiled=True
        ).astype(jnp.float32),
        lax.psum_scatter(
            out_weight_grad.astype(jnp.bfloat16), "shard", scatter_dimension=0, tiled=True
        ).astype(jnp.float32),
        lax.psum_scatter(
            out_bias_grad.astype(jnp.bfloat16), "shard", scatter_dimension=0, tiled=True
        ).astype(jnp.float32),
        lax.psum_scatter(
            gain_one_grad.astype(jnp.bfloat16), "shard", scatter_dimension=0, tiled=True
        ).astype(jnp.float32),
        lax.psum_scatter(
            shift_one_grad.astype(jnp.bfloat16), "shard", scatter_dimension=0, tiled=True
        ).astype(jnp.float32),
        lax.psum_scatter(
            up_weight_grad.astype(jnp.bfloat16), "shard", scatter_dimension=0, tiled=True
        ).astype(jnp.float32),
        lax.psum_scatter(
            up_bias_grad.astype(jnp.bfloat16), "shard", scatter_dimension=0, tiled=True
        ).astype(jnp.float32),
        lax.psum_scatter(
            down_weight_grad.astype(jnp.bfloat16), "shard", scatter_dimension=0, tiled=True
        ).astype(jnp.float32),
        lax.psum_scatter(
            down_bias_grad.astype(jnp.bfloat16), "shard", scatter_dimension=0, tiled=True
        ).astype(jnp.float32),
        lax.psum_scatter(
            gain_two_grad.astype(jnp.bfloat16), "shard", scatter_dimension=0, tiled=True
        ).astype(jnp.float32),
        lax.psum_scatter(
            shift_two_grad.astype(jnp.bfloat16), "shard", scatter_dimension=0, tiled=True
        ).astype(jnp.float32),
    )
    summed = lax.psum(tuple(scattered), "seq")
    layer_out = outputs.astype(jnp.bfloat16).reshape(1, row_count, model_width)
    return (layer_out, input_grad.reshape(1, row_count, model_width)) + tuple(summed)


def solution(mesh):
    in_specs = (
        P("shard", "seq", None),
        P("shard", "seq", None),
        P(),
        P("shard", None),
        P("shard"),
        P("shard"),
        P("shard", None),
        P("shard"),
        P("shard"),
        P("shard"),
        P("shard", None),
        P("shard"),
        P("shard", None),
        P("shard"),
        P("shard"),
        P("shard"),
    )
    out_specs = (
        P("shard", "seq", None),
        P("shard", "seq", None),
        P("shard", None),
        P("shard"),
        P("shard"),
        P("shard", None),
        P("shard"),
        P("shard"),
        P("shard"),
        P("shard", None),
        P("shard"),
        P("shard", None),
        P("shard"),
        P("shard"),
        P("shard"),
    )
    return jax.shard_map(body, mesh=mesh, in_specs=in_specs, out_specs=out_specs, check_vma=False)
```

profile of v0, /device:TPU:0, one launch (start us, length us, event | category | flops | bytes accessed | tf_op | source)
XLA Modules:
  0.0 1218.1 jit_solution(12762407708655422267)
XLA Ops:
  8.0 1.9 all-gather.3
  10.0 1.8 all-gather.2
  11.8 13.2 %all-gather.18.cloned.1.call-done = bf16[768,2304]{1,0:T(8,128)(2,1)} async-done(((bf16[384,2304]{1,0:T(8,128)(2,1)}), bf16[768,2304]{1,0:T(8,128)(2,1)}) %all-gather.18.cloned.1.call-update) | async-done | bytes 3538960 | tf_op jit(solution)/shard_map/all_gather | solution.py:111
  25.0 2.6 fusion.17
  31.7 1.8 all-gather.8
  33.5 1.8 all-gather.7
  45.8 61.1 %all-gather.26.cloned.1.call-done = bf16[2048,1,12,64]{0,3,2,1:T(8,128)(2,1)} async-done(((bf16[128,1,12,64]{0,3,2,1:T(8,128)(2,1)}), bf16[2048,1,12,64]{0,3,2,1:T(8,128)(2,1)}) %all-gather.26.cloned.1.call-update) | async-done | bytes 3145744 | tf_op jit(solution)/shard_map/all_gather | solution.py:167
  106.8 3.9 select_reduce_fusion
  110.7 3.1 fusion.11
  115.9 69.0 %all-gather.28.cloned.1.call-done = bf16[2048,1,12,64]{0,3,2,1:T(8,128)(2,1)} async-done(((bf16[128,1,12,64]{0,3,2,1:T(8,128)(2,1)}), bf16[2048,1,12,64]{0,3,2,1:T(8,128)(2,1)}) %all-gather.28.cloned.1.call-update) | async-done | bytes 3145744 | tf_op jit(solution)/shard_map/all_gather | solution.py:168
  184.9 9.0 fusion.64
  195.9 14.9 %all-gather.22.cloned.1.call-done = bf16[768,3072]{1,0:T(8,128)(2,1)} async-done(((bf16[384,3072]{1,0:T(8,128)(2,1)}), bf16[768,3072]{1,0:T(8,128)(2,1)}) %all-gather.22.cloned.1.call-update) | async-done | bytes 4718608 | tf_op jit(solution)/shard_map/all_gather | solution.py:118
  210.7 8.5 multiply_convert_fusion
  219.2 8.6 all-gather.24.cloned.1.call-done
  227.8 3.6 fusion.66
  234.0 2.5 fusion.59
  236.5 2.4 multiply_reduce_fusion
  241.4 1.9 convolution_convert_fusion.4
  243.5 322.8 %while.24 = (s32[]{:T(128)}, bf16[128,12,64]{0,2,1:T(8,128)(2,1)S(1)}, bf16[128,12,64]{0,2,1:T(8,128)(2,1)S(1)}, f32[128,12,64]{0,2,1:T(8,128)S(1)}, f32[128,12,...) while((s32[]{:T(128)}, ...), condition=%wide.region_11.12_spmd.clone, body=%wide.region_10.11_spmd.clone.sunk | while | flops 128188688 | bytes 12006102 | solution.py:250
  243.8 1.8 collective-permute-start
  254.5 9.1 collective-permute-done.2
  263.6 3.6 collective-permute-done.3
  272.5 3.3 collective-permute-start.3
  276.2 11.1 collective-permute-done.2
  287.3 2.7 collective-permute-done.3
  294.3 2.3 collective-permute-start.3
  297.0 12.7 %collective-permute-done.2 = bf16[128,12,64]{0,2,1:T(8,128)(2,1)S(1)} collective-permute-done((bf16[128,12,64]{0,2,1:T(8,128)(2,1)}, bf16[128,12,64]{0,2,1:T(8,128)(2,1)S(1)}, u32[]{:S(2)}, u32[]{:S(2)}) %collective-permute-start.2) | collective-permute-done | bytes 196640 | tf_op jit(solution)/shard_map/while/body/eval_jaxpr/ppermute | solution.py:18
  309.8 2.1 collective-permute-done.3
  317.0 13.6 %collective-permute-done.2 = bf16[128,12,64]{0,2,1:T(8,128)(2,1)S(1)} collective-permute-done((bf16[128,12,64]{0,2,1:T(8,128)(2,1)}, bf16[128,12,64]{0,2,1:T(8,128)(2,1)S(1)}, u32[]{:S(2)}, u32[]{:S(2)}) %collective-permute-start.2) | collective-permute-done | bytes 196640 | tf_op jit(solution)/shard_map/while/body/eval_jaxpr/ppermute | solution.py:18
  330.7 2.1 collective-permute-done.3
  337.5 13.2 %collective-permute-done.2 = bf16[128,12,64]{0,2,1:T(8,128)(2,1)S(1)} collective-permute-done((bf16[128,12,64]{0,2,1:T(8,128)(2,1)}, bf16[128,12,64]{0,2,1:T(8,128)(2,1)S(1)}, u32[]{:S(2)}, u32[]{:S(2)}) %collective-permute-start.2) | collective-permute-done | bytes 196640 | tf_op jit(solution)/shard_map/while/body/eval_jaxpr/ppermute | solution.py:18
  350.7 2.1 collective-permute-done.3
  357.5 12.3 %collective-permute-done.2 = bf16[128,12,64]{0,2,1:T(8,128)(2,1)S(1)} collective-permute-done((bf16[128,12,64]{0,2,1:T(8,128)(2,1)}, bf16[128,12,64]{0,2,1:T(8,128)(2,1)S(1)}, u32[]{:S(2)}, u32[]{:S(2)}) %collective-permute-start.2) | collective-permute-done | bytes 196640 | tf_op jit(solution)/shard_map/while/body/eval_jaxpr/ppermute | solution.py:18
  369.7 2.1 collective-permute-done.3
  376.5 11.3 collective-permute-done.2
  387.9 2.1 collective-permute-done.3
  394.7 10.4 collective-permute-done.2
  405.1 2.5 collective-permute-done.3
  412.5 9.5 collective-permute-done.2
  422.0 3.4 collective-permute-done.3
  430.1 9.2 collective-permute-done.2
  439.4 4.2 collective-permute-done.3
  448.2 10.3 collective-permute-done.2
  458.6 4.2 collective-permute-done.3
  467.5 11.4 collective-permute-done.2
  478.9 4.2 collective-permute-done.3
  487.8 12.4 %collective-permute-done.2 = bf16[128,12,64]{0,2,1:T(8,128)(2,1)S(1)} collective-permute-done((bf16[128,12,64]{0,2,1:T(8,128)(2,1)}, bf16[128,12,64]{0,2,1:T(8,128)(2,1)S(1)}, u32[]{:S(2)}, u32[]{:S(2)}) %collective-permute-start.2) | collective-permute-done | bytes 196640 | tf_op jit(solution)/shard_map/while/body/eval_jaxpr/ppermute | solution.py:18
  500.2 4.2 collective-permute-done.3
  509.1 13.5 %collective-permute-done.2 = bf16[128,12,64]{0,2,1:T(8,128)(2,1)S(1)} collective-permute-done((bf16[128,12,64]{0,2,1:T(8,128)(2,1)}, bf16[128,12,64]{0,2,1:T(8,128)(2,1)S(1)}, u32[]{:S(2)}, u32[]{:S(2)}) %collective-permute-start.2) | collective-permute-done | bytes 196640 | tf_op jit(solution)/shard_map/while/body/eval_jaxpr/ppermute | solution.py:18
  522.7 4.2 collective-permute-done.3
  531.6 14.7 %collective-permute-done.2 = bf16[128,12,64]{0,2,1:T(8,128)(2,1)S(1)} collective-permute-done((bf16[128,12,64]{0,2,1:T(8,128)(2,1)}, bf16[128,12,64]{0,2,1:T(8,128)(2,1)S(1)}, u32[]{:S(2)}, u32[]{:S(2)}) %collective-permute-start.2) | collective-permute-done | bytes 196640 | tf_op jit(solution)/shard_map/while/body/eval_jaxpr/ppermute | solution.py:18
  546.4 4.2 collective-permute-done.3
  555.2 8.9 collective-permute-done.2
  564.2 2.1 collective-permute-done.3
  567.3 2.9 fusion.16
  570.1 5.8 copy.50
  577.1 3.8 convolution_convert_fusion.1
  582.3 3.6 convolution_convert_fusion
  592.2 4.7 all-reduce.10
  607.1 3.2 fusion.33
  610.4 3.0 copy.51
  613.5 5.8 reduce-scatter.11.cloned.1.call-done
  619.3 586.8 %all-reduce.12 = (f32[384,2304]{0,1:T(8,128)}, f32[384]{0:T(512)}, f32[384]{0:T(512)}, f32[384,768]{1,0:T(8,128)}, f32[384]{0:T(512)}, /*index=5*/f32[384]{0:T(5...) all-reduce(bf16[384,2304]{0,1:T(8,128)(2,1)S(1)} %copy.51, ...), channel_id=1, replica_groups=mesh['seq'=16,'shard'=2] {'seq'}, use_global_device_ids=true, to_apply=%region_13.14 | all-reduce | flops 3543552 | bytes 21270528 | tf_op jit(solution)/shard_map/psum | solution.py:311
  1206.1 5.2 copy.41
  (446 shorter events, 122.9 us)
Async XLA Ops:
  7.2 17.8 %all-gather.18.cloned.1.call-start = ((), (), s32[]{:S(2)}) async-start(), calls=%async_computation.4 | async-start | bytes 5308416 | tf_op jit(solution)/shard_map/all_gather | solution.py:111
  7.9 98.9 %all-gather.26.cloned.1.call-start = ((), (), s32[]{:S(2)}) async-start(), calls=%async_computation.11 | async-start | bytes 3342336 | tf_op jit(solution)/shard_map/all_gather | solution.py:167
  29.0 155.9 %all-gather.28.cloned.1.call-start = ((), (), s32[]{:S(2)}) async-start(), calls=%async_computation.12 | async-start | bytes 3342336 | tf_op jit(solution)/shard_map/all_gather | solution.py:168
  29.7 164.2 %all-gather.20.cloned.1.call-start = ((), (), s32[]{:S(2)}) async-start(), calls=%async_computation.5 | async-start | bytes 1769472 | tf_op jit(solution)/shard_map/all_gather | solution.py:114
  30.3 180.4 %all-gather.22.cloned.1.call-start = ((), (), s32[]{:S(2)}) async-start(), calls=%async_computation.6 | async-start | bytes 7077888 | tf_op jit(solution)/shard_map/all_gather | solution.py:118
  31.0 196.8 %all-gather.24.cloned.1.call-start = ((), (), s32[]{:S(2)}) async-start(), calls=%async_computation.7 | async-start | bytes 7077888 | tf_op jit(solution)/shard_map/all_gather | solution.py:120
  31.6 578.8 %reduce-scatter.7.cloned.1.call-start = ((), (), s32[]{:S(2)}) async-start(), calls=%async_computation.8 | async-start | bytes 1769472 | tf_op jit(solution)/shard_map/reduce_scatter | solution.py:280
  243.4 367.0 %reduce-scatter.13.cloned.1.call-start = ((), (), s32[]{:S(2)}) async-start(), calls=%async_computation.13 | async-start | bytes 5308416
  243.8 23.5 %collective-permute-start = (bf16[128,12,64]{0,2,1:T(8,128)(2,1)S(1)}, bf16[128,12,64]{0,2,1:T(8,128)(2,1)S(1)}, u32[]{:S(2)}, u32[]{:S(2)}) collective-permute-start(bf16[128,12,64]{0,2,1:T(8,128)(2,1)S(1)} %copy.60), channel_id=1, source_target_pairs={{30,0},{0,2},{2,4},{4,6},{6,8},{8,10},{10,12},{12,14},{14,16},{16,... | collective-permute-start | bytes 589832 | tf_op jit(solution)/shard_map/while/body/eval_jaxpr/ppermute | solution.py:18
  245.6 21.7 %collective-permute-start.1 = (bf16[128,12,64]{0,2,1:T(8,128)(2,1)S(1)}, bf16[128,12,64]{0,2,1:T(8,128)(2,1)S(1)}, u32[]{:S(2)}, u32[]{:S(2)}) collective-permute-start(bf16[128,12,64]{0,2,1:T(8,128)(2,1)S(1)} %copy.61), channel_id=1, source_target_pairs={{30,0},{0,2},{2,4},{4,6},{6,8},{8,10},{10,12},{12,14},{14,16},{16,... | collective-permute-start | bytes 589832 | tf_op jit(solution)/shard_map/while/body/eval_jaxpr/ppermute | solution.py:18
  252.6 14.6 %collective-permute-start.3 = (bf16[128,12,64]{0,2,1:T(8,128)(2,1)}, bf16[128,12,64]{0,2,1:T(8,128)(2,1)S(1)}, u32[]{:S(2)}, u32[]{:S(2)}) collective-permute-start(bf16[128,12,64]{0,2,1:T(8,128)(2,1)} %fusion.124), channel_id=1, source_target_pairs={{30,0},{0,2},{2,4},{4,6},{6,8},{8,10},{10,12},{12,14},{14,16},{16,... | collective-permute-start | bytes 589832 | tf_op jit(solution)/shard_map/while/body/eval_jaxpr/ppermute | solution.py:18
  267.3 22.7 %collective-permute-start = (bf16[128,12,64]{0,2,1:T(8,128)(2,1)S(1)}, bf16[128,12,64]{0,2,1:T(8,128)(2,1)S(1)}, u32[]{:S(2)}, u32[]{:S(2)}) collective-permute-start(bf16[128,12,64]{0,2,1:T(8,128)(2,1)S(1)} %copy.60), channel_id=1, source_target_pairs={{30,0},{0,2},{2,4},{4,6},{6,8},{8,10},{10,12},{12,14},{14,16},{16,... | collective-permute-start | bytes 589832 | tf_op jit(solution)/shard_map/while/body/eval_jaxpr/ppermute | solution.py:18
  267.4 22.6 %collective-permute-start.1 = (bf16[128,12,64]{0,2,1:T(8,128)(2,1)S(1)}, bf16[128,12,64]{0,2,1:T(8,128)(2,1)S(1)}, u32[]{:S(2)}, u32[]{:S(2)}) collective-permute-start(bf16[128,12,64]{0,2,1:T(8,128)(2,1)S(1)} %copy.61), channel_id=1, source_target_pairs={{30,0},{0,2},{2,4},{4,6},{6,8},{8,10},{10,12},{12,14},{14,16},{16,... | collective-permute-start | bytes 589832 | tf_op jit(solution)/shard_map/while/body/eval_jaxpr/ppermute | solution.py:18
  271.0 16.2 %collective-permute-start.2 = (bf16[128,12,64]{0,2,1:T(8,128)(2,1)}, bf16[128,12,64]{0,2,1:T(8,128)(2,1)S(1)}, u32[]{:S(2)}, u32[]{:S(2)}) collective-permute-start(bf16[128,12,64]{0,2,1:T(8,128)(2,1)} %fusion.123), channel_id=1, source_target_pairs={{30,0},{0,2},{2,4},{4,6},{6,8},{8,10},{10,12},{12,14},{14,16},{16,... | collective-permute-start | bytes 589832 | tf_op jit(solution)/shard_map/while/body/eval_jaxpr/ppermute | solution.py:18
  272.5 17.5 %collective-permute-start.3 = (bf16[128,12,64]{0,2,1:T(8,128)(2,1)}, bf16[128,12,64]{0,2,1:T(8,128)(2,1)S(1)}, u32[]{:S(2)}, u32[]{:S(2)}) collective-permute-start(bf16[128,12,64]{0,2,1:T(8,128)(2,1)} %fusion.124), channel_id=1, source_target_pairs={{30,0},{0,2},{2,4},{4,6},{6,8},{8,10},{10,12},{12,14},{14,16},{16,... | collective-permute-start | bytes 589832 | tf_op jit(solution)/shard_map/while/body/eval_jaxpr/ppermute | solution.py:18
  290.1 21.8 %collective-permute-start = (bf16[128,12,64]{0,2,1:T(8,128)(2,1)S(1)}, bf16[128,12,64]{0,2,1:T(8,128)(2,1)S(1)}, u32[]{:S(2)}, u32[]{:S(2)}) collective-permute-start(bf16[128,12,64]{0,2,1:T(8,128)(2,1)S(1)} %copy.60), channel_id=1, source_target_pairs={{30,0},{0,2},{2,4},{4,6},{6,8},{8,10},{10,12},{12,14},{14,16},{16,... | collective-permute-start | bytes 589832 | tf_op jit(solution)/shard_map/while/body/eval_jaxpr/ppermute | solution.py:18
  290.2 21.7 %collective-permute-start.1 = (bf16[128,12,64]{0,2,1:T(8,128)(2,1)S(1)}, bf16[128,12,64]{0,2,1:T(8,128)(2,1)S(1)}, u32[]{:S(2)}, u32[]{:S(2)}) collective-permute-start(bf16[128,12,64]{0,2,1:T(8,128)(2,1)S(1)} %copy.61), channel_id=1, source_target_pairs={{30,0},{0,2},{2,4},{4,6},{6,8},{8,10},{10,12},{12,14},{14,16},{16,... | collective-permute-start | bytes 589832 | tf_op jit(solution)/shard_map/while/body/eval_jaxpr/ppermute | solution.py:18
  293.4 16.3 %collective-permute-start.2 = (bf16[128,12,64]{0,2,1:T(8,128)(2,1)}, bf16[128,12,64]{0,2,1:T(8,128)(2,1)S(1)}, u32[]{:S(2)}, u32[]{:S(2)}) collective-permute-start(bf16[128,12,64]{0,2,1:T(8,128)(2,1)} %fusion.123), channel_id=1, source_target_pairs={{30,0},{0,2},{2,4},{4,6},{6,8},{8,10},{10,12},{12,14},{14,16},{16,... | collective-permute-start | bytes 589832 | tf_op jit(solution)/shard_map/while/body/eval_jaxpr/ppermute | solution.py:18
  294.3 17.5 %collective-permute-start.3 = (bf16[128,12,64]{0,2,1:T(8,128)(2,1)}, bf16[128,12,64]{0,2,1:T(8,128)(2,1)S(1)}, u32[]{:S(2)}, u32[]{:S(2)}) collective-permute-start(bf16[128,12,64]{0,2,1:T(8,128)(2,1)} %fusion.124), channel_id=1, source_target_pairs={{30,0},{0,2},{2,4},{4,6},{6,8},{8,10},{10,12},{12,14},{14,16},{16,... | collective-permute-start | bytes 589832 | tf_op jit(solution)/shard_map/while/body/eval_jaxpr/ppermute | solution.py:18
  311.9 20.9 %collective-permute-start = (bf16[128,12,64]{0,2,1:T(8,128)(2,1)S(1)}, bf16[128,12,64]{0,2,1:T(8,128)(2,1)S(1)}, u32[]{:S(2)}, u32[]{:S(2)}) collective-permute-start(bf16[128,12,64]{0,2,1:T(8,128)(2,1)S(1)} %copy.60), channel_id=1, source_target_pairs={{30,0},{0,2},{2,4},{4,6},{6,8},{8,10},{10,12},{12,14},{14,16},{16,... | collective-permute-start | bytes 589832 | tf_op jit(solution)/shard_map/while/body/eval_jaxpr/ppermute | solution.py:18
  312.0 20.8 %collective-permute-start.1 = (bf16[128,12,64]{0,2,1:T(8,128)(2,1)S(1)}, bf16[128,12,64]{0,2,1:T(8,128)(2,1)S(1)}, u32[]{:S(2)}, u32[]{:S(2)}) collective-permute-start(bf16[128,12,64]{0,2,1:T(8,128)(2,1)S(1)} %copy.61), channel_id=1, source_target_pairs={{30,0},{0,2},{2,4},{4,6},{6,8},{8,10},{10,12},{12,14},{14,16},{16,... | collective-permute-start | bytes 589832 | tf_op jit(solution)/shard_map/while/body/eval_jaxpr/ppermute | solution.py:18
  315.2 15.4 %collective-permute-start.2 = (bf16[128,12,64]{0,2,1:T(8,128)(2,1)}, bf16[128,12,64]{0,2,1:T(8,128)(2,1)S(1)}, u32[]{:S(2)}, u32[]{:S(2)}) collective-permute-start(bf16[128,12,64]{0,2,1:T(8,128)(2,1)} %fusion.123), channel_id=1, source_target_pairs={{30,0},{0,2},{2,4},{4,6},{6,8},{8,10},{10,12},{12,14},{14,16},{16,... | collective-permute-start | bytes 589832 | tf_op jit(solution)/shard_map/while/body/eval_jaxpr/ppermute | solution.py:18
  316.2 16.6 %collective-permute-start.3 = (bf16[128,12,64]{0,2,1:T(8,128)(2,1)}, bf16[128,12,64]{0,2,1:T(8,128)(2,1)S(1)}, u32[]{:S(2)}, u32[]{:S(2)}) collective-permute-start(bf16[128,12,64]{0,2,1:T(8,128)(2,1)} %fusion.124), channel_id=1, source_target_pairs={{30,0},{0,2},{2,4},{4,6},{6,8},{8,10},{10,12},{12,14},{14,16},{16,... | collective-permute-start | bytes 589832 | tf_op jit(solution)/shard_map/while/body/eval_jaxpr/ppermute | solution.py:18
  332.8 19.9 %collective-permute-start = (bf16[128,12,64]{0,2,1:T(8,128)(2,1)S(1)}, bf16[128,12,64]{0,2,1:T(8,128)(2,1)S(1)}, u32[]{:S(2)}, u32[]{:S(2)}) collective-permute-start(bf16[128,12,64]{0,2,1:T(8,128)(2,1)S(1)} %copy.60), channel_id=1, source_target_pairs={{30,0},{0,2},{2,4},{4,6},{6,8},{8,10},{10,12},{12,14},{14,16},{16,... | collective-permute-start | bytes 589832 | tf_op jit(solution)/shard_map/while/body/eval_jaxpr/ppermute | solution.py:18
  332.9 19.9 %collective-permute-start.1 = (bf16[128,12,64]{0,2,1:T(8,128)(2,1)S(1)}, bf16[128,12,64]{0,2,1:T(8,128)(2,1)S(1)}, u32[]{:S(2)}, u32[]{:S(2)}) collective-permute-start(bf16[128,12,64]{0,2,1:T(8,128)(2,1)S(1)} %copy.61), channel_id=1, source_target_pairs={{30,0},{0,2},{2,4},{4,6},{6,8},{8,10},{10,12},{12,14},{14,16},{16,... | collective-permute-start | bytes 589832 | tf_op jit(solution)/shard_map/while/body/eval_jaxpr/ppermute | solution.py:18
  336.2 14.5 %collective-permute-start.2 = (bf16[128,12,64]{0,2,1:T(8,128)(2,1)}, bf16[128,12,64]{0,2,1:T(8,128)(2,1)S(1)}, u32[]{:S(2)}, u32[]{:S(2)}) collective-permute-start(bf16[128,12,64]{0,2,1:T(8,128)(2,1)} %fusion.123), channel_id=1, source_target_pairs={{30,0},{0,2},{2,4},{4,6},{6,8},{8,10},{10,12},{12,14},{14,16},{16,... | collective-permute-start | bytes 589832 | tf_op jit(solution)/shard_map/while/body/eval_jaxpr/ppermute | solution.py:18
  337.1 15.7 %collective-permute-start.3 = (bf16[128,12,64]{0,2,1:T(8,128)(2,1)}, bf16[128,12,64]{0,2,1:T(8,128)(2,1)S(1)}, u32[]{:S(2)}, u32[]{:S(2)}) collective-permute-start(bf16[128,12,64]{0,2,1:T(8,128)(2,1)} %fusion.124), channel_id=1, source_target_pairs={{30,0},{0,2},{2,4},{4,6},{6,8},{8,10},{10,12},{12,14},{14,16},{16,... | collective-permute-start | bytes 589832 | tf_op jit(solution)/shard_map/while/body/eval_jaxpr/ppermute | solution.py:18
  352.8 19.0 %collective-permute-start = (bf16[128,12,64]{0,2,1:T(8,128)(2,1)S(1)}, bf16[128,12,64]{0,2,1:T(8,128)(2,1)S(1)}, u32[]{:S(2)}, u32[]{:S(2)}) collective-permute-start(bf16[128,12,64]{0,2,1:T(8,128)(2,1)S(1)} %copy.60), channel_id=1, source_target_pairs={{30,0},{0,2},{2,4},{4,6},{6,8},{8,10},{10,12},{12,14},{14,16},{16,... | collective-permute-start | bytes 589832 | tf_op jit(solution)/shard_map/while/body/eval_jaxpr/ppermute | solution.py:18
  352.9 18.9 %collective-permute-start.1 = (bf16[128,12,64]{0,2,1:T(8,128)(2,1)S(1)}, bf16[128,12,64]{0,2,1:T(8,128)(2,1)S(1)}, u32[]{:S(2)}, u32[]{:S(2)}) collective-permute-start(bf16[128,12,64]{0,2,1:T(8,128)(2,1)S(1)} %copy.61), channel_id=1, source_target_pairs={{30,0},{0,2},{2,4},{4,6},{6,8},{8,10},{10,12},{12,14},{14,16},{16,... | collective-permute-start | bytes 589832 | tf_op jit(solution)/shard_map/while/body/eval_jaxpr/ppermute | solution.py:18
  356.2 13.6 %collective-permute-start.2 = (bf16[128,12,64]{0,2,1:T(8,128)(2,1)}, bf16[128,12,64]{0,2,1:T(8,128)(2,1)S(1)}, u32[]{:S(2)}, u32[]{:S(2)}) collective-permute-start(bf16[128,12,64]{0,2,1:T(8,128)(2,1)} %fusion.123), channel_id=1, source_target_pairs={{30,0},{0,2},{2,4},{4,6},{6,8},{8,10},{10,12},{12,14},{14,16},{16,... | collective-permute-start | bytes 589832 | tf_op jit(solution)/shard_map/while/body/eval_jaxpr/ppermute | solution.py:18
  357.1 14.7 %collective-permute-start.3 = (bf16[128,12,64]{0,2,1:T(8,128)(2,1)}, bf16[128,12,64]{0,2,1:T(8,128)(2,1)S(1)}, u32[]{:S(2)}, u32[]{:S(2)}) collective-permute-start(bf16[128,12,64]{0,2,1:T(8,128)(2,1)} %fusion.124), channel_id=1, source_target_pairs={{30,0},{0,2},{2,4},{4,6},{6,8},{8,10},{10,12},{12,14},{14,16},{16,... | collective-permute-start | bytes 589832 | tf_op jit(solution)/shard_map/while/body/eval_jaxpr/ppermute | solution.py:18
  371.9 18.1 %collective-permute-start = (bf16[128,12,64]{0,2,1:T(8,128)(2,1)S(1)}, bf16[128,12,64]{0,2,1:T(8,128)(2,1)S(1)}, u32[]{:S(2)}, u32[]{:S(2)}) collective-permute-start(bf16[128,12,64]{0,2,1:T(8,128)(2,1)S(1)} %copy.60), channel_id=1, source_target_pairs={{30,0},{0,2},{2,4},{4,6},{6,8},{8,10},{10,12},{12,14},{14,16},{16,... | collective-permute-start | bytes 589832 | tf_op jit(solution)/shard_map/while/body/eval_jaxpr/ppermute | solution.py:18
  372.0 18.0 %collective-permute-start.1 = (bf16[128,12,64]{0,2,1:T(8,128)(2,1)S(1)}, bf16[128,12,64]{0,2,1:T(8,128)(2,1)S(1)}, u32[]{:S(2)}, u32[]{:S(2)}) collective-permute-start(bf16[128,12,64]{0,2,1:T(8,128)(2,1)S(1)} %copy.61), channel_id=1, source_target_pairs={{30,0},{0,2},{2,4},{4,6},{6,8},{8,10},{10,12},{12,14},{14,16},{16,... | collective-permute-start | bytes 589832 | tf_op jit(solution)/shard_map/while/body/eval_jaxpr/ppermute | solution.py:18
  376.1 13.8 %collective-permute-start.3 = (bf16[128,12,64]{0,2,1:T(8,128)(2,1)}, bf16[128,12,64]{0,2,1:T(8,128)(2,1)S(1)}, u32[]{:S(2)}, u32[]{:S(2)}) collective-permute-start(bf16[128,12,64]{0,2,1:T(8,128)(2,1)} %fusion.124), channel_id=1, source_target_pairs={{30,0},{0,2},{2,4},{4,6},{6,8},{8,10},{10,12},{12,14},{14,16},{16,... | collective-permute-start | bytes 589832 | tf_op jit(solution)/shard_map/while/body/eval_jaxpr/ppermute | solution.py:18
  390.1 17.7 %collective-permute-start = (bf16[128,12,64]{0,2,1:T(8,128)(2,1)S(1)}, bf16[128,12,64]{0,2,1:T(8,128)(2,1)S(1)}, u32[]{:S(2)}, u32[]{:S(2)}) collective-permute-start(bf16[128,12,64]{0,2,1:T(8,128)(2,1)S(1)} %copy.60), channel_id=1, source_target_pairs={{30,0},{0,2},{2,4},{4,6},{6,8},{8,10},{10,12},{12,14},{14,16},{16,... | collective-permute-start | bytes 589832 | tf_op jit(solution)/shard_map/while/body/eval_jaxpr/ppermute | solution.py:18
  390.1 17.6 %collective-permute-start.1 = (bf16[128,12,64]{0,2,1:T(8,128)(2,1)S(1)}, bf16[128,12,64]{0,2,1:T(8,128)(2,1)S(1)}, u32[]{:S(2)}, u32[]{:S(2)}) collective-permute-start(bf16[128,12,64]{0,2,1:T(8,128)(2,1)S(1)} %copy.61), channel_id=1, source_target_pairs={{30,0},{0,2},{2,4},{4,6},{6,8},{8,10},{10,12},{12,14},{14,16},{16,... | collective-permute-start | bytes 589832 | tf_op jit(solution)/shard_map/while/body/eval_jaxpr/ppermute | solution.py:18
  407.8 17.7 %collective-permute-start = (bf16[128,12,64]{0,2,1:T(8,128)(2,1)S(1)}, bf16[128,12,64]{0,2,1:T(8,128)(2,1)S(1)}, u32[]{:S(2)}, u32[]{:S(2)}) collective-permute-start(bf16[128,12,64]{0,2,1:T(8,128)(2,1)S(1)} %copy.60), channel_id=1, source_target_pairs={{30,0},{0,2},{2,4},{4,6},{6,8},{8,10},{10,12},{12,14},{14,16},{16,... | collective-permute-start | bytes 589832 | tf_op jit(solution)/shard_map/while/body/eval_jaxpr/ppermute | solution.py:18
  407.9 17.6 %collective-permute-start.1 = (bf16[128,12,64]{0,2,1:T(8,128)(2,1)S(1)}, bf16[128,12,64]{0,2,1:T(8,128)(2,1)S(1)}, u32[]{:S(2)}, u32[]{:S(2)}) collective-permute-start(bf16[128,12,64]{0,2,1:T(8,128)(2,1)S(1)} %copy.61), channel_id=1, source_target_pairs={{30,0},{0,2},{2,4},{4,6},{6,8},{8,10},{10,12},{12,14},{14,16},{16,... | collective-permute-start | bytes 589832 | tf_op jit(solution)/shard_map/while/body/eval_jaxpr/ppermute | solution.py:18
  412.0 13.4 %collective-permute-start.3 = (bf16[128,12,64]{0,2,1:T(8,128)(2,1)}, bf16[128,12,64]{0,2,1:T(8,128)(2,1)S(1)}, u32[]{:S(2)}, u32[]{:S(2)}) collective-permute-start(bf16[128,12,64]{0,2,1:T(8,128)(2,1)} %fusion.124), channel_id=1, source_target_pairs={{30,0},{0,2},{2,4},{4,6},{6,8},{8,10},{10,12},{12,14},{14,16},{16,... | collective-permute-start | bytes 589832 | tf_op jit(solution)/shard_map/while/body/eval_jaxpr/ppermute | solution.py:18
  425.5 18.1 %collective-permute-start = (bf16[128,12,64]{0,2,1:T(8,128)(2,1)S(1)}, bf16[128,12,64]{0,2,1:T(8,128)(2,1)S(1)}, u32[]{:S(2)}, u32[]{:S(2)}) collective-permute-start(bf16[128,12,64]{0,2,1:T(8,128)(2,1)S(1)} %copy.60), channel_id=1, source_target_pairs={{30,0},{0,2},{2,4},{4,6},{6,8},{8,10},{10,12},{12,14},{14,16},{16,... | collective-permute-start | bytes 589832 | tf_op jit(solution)/shard_map/while/body/eval_jaxpr/ppermute | solution.py:18
  425.6 18.0 %collective-permute-start.1 = (bf16[128,12,64]{0,2,1:T(8,128)(2,1)S(1)}, bf16[128,12,64]{0,2,1:T(8,128)(2,1)S(1)}, u32[]{:S(2)}, u32[]{:S(2)}) collective-permute-start(bf16[128,12,64]{0,2,1:T(8,128)(2,1)S(1)} %copy.61), channel_id=1, source_target_pairs={{30,0},{0,2},{2,4},{4,6},{6,8},{8,10},{10,12},{12,14},{14,16},{16,... | collective-permute-start | bytes 589832 | tf_op jit(solution)/shard_map/while/body/eval_jaxpr/ppermute | solution.py:18
  429.7 13.8 %collective-permute-start.3 = (bf16[128,12,64]{0,2,1:T(8,128)(2,1)}, bf16[128,12,64]{0,2,1:T(8,128)(2,1)S(1)}, u32[]{:S(2)}, u32[]{:S(2)}) collective-permute-start(bf16[128,12,64]{0,2,1:T(8,128)(2,1)} %fusion.124), channel_id=1, source_target_pairs={{30,0},{0,2},{2,4},{4,6},{6,8},{8,10},{10,12},{12,14},{14,16},{16,... | collective-permute-start | bytes 589832 | tf_op jit(solution)/shard_map/while/body/eval_jaxpr/ppermute | solution.py:18
  443.6 19.2 %collective-permute-start = (bf16[128,12,64]{0,2,1:T(8,128)(2,1)S(1)}, bf16[128,12,64]{0,2,1:T(8,128)(2,1)S(1)}, u32[]{:S(2)}, u32[]{:S(2)}) collective-permute-start(bf16[128,12,64]{0,2,1:T(8,128)(2,1)S(1)} %copy.60), channel_id=1, source_target_pairs={{30,0},{0,2},{2,4},{4,6},{6,8},{8,10},{10,12},{12,14},{14,16},{16,... | collective-permute-start | bytes 589832 | tf_op jit(solution)/shard_map/while/body/eval_jaxpr/ppermute | solution.py:18
  443.7 19.1 %collective-permute-start.1 = (bf16[128,12,64]{0,2,1:T(8,128)(2,1)S(1)}, bf16[128,12,64]{0,2,1:T(8,128)(2,1)S(1)}, u32[]{:S(2)}, u32[]{:S(2)}) collective-permute-start(bf16[128,12,64]{0,2,1:T(8,128)(2,1)S(1)} %copy.61), channel_id=1, source_target_pairs={{30,0},{0,2},{2,4},{4,6},{6,8},{8,10},{10,12},{12,14},{14,16},{16,... | collective-permute-start | bytes 589832 | tf_op jit(solution)/shard_map/while/body/eval_jaxpr/ppermute | solution.py:18
  447.9 14.9 %collective-permute-start.3 = (bf16[128,12,64]{0,2,1:T(8,128)(2,1)}, bf16[128,12,64]{0,2,1:T(8,128)(2,1)S(1)}, u32[]{:S(2)}, u32[]{:S(2)}) collective-permute-start(bf16[128,12,64]{0,2,1:T(8,128)(2,1)} %fusion.124), channel_id=1, source_target_pairs={{30,0},{0,2},{2,4},{4,6},{6,8},{8,10},{10,12},{12,14},{14,16},{16,... | collective-permute-start | bytes 589832 | tf_op jit(solution)/shard_map/while/body/eval_jaxpr/ppermute | solution.py:18
  462.8 20.3 %collective-permute-start = (bf16[128,12,64]{0,2,1:T(8,128)(2,1)S(1)}, bf16[128,12,64]{0,2,1:T(8,128)(2,1)S(1)}, u32[]{:S(2)}, u32[]{:S(2)}) collective-permute-start(bf16[128,12,64]{0,2,1:T(8,128)(2,1)S(1)} %copy.60), channel_id=1, source_target_pairs={{30,0},{0,2},{2,4},{4,6},{6,8},{8,10},{10,12},{12,14},{14,16},{16,... | collective-permute-start | bytes 589832 | tf_op jit(solution)/shard_map/while/body/eval_jaxpr/ppermute | solution.py:18
  462.9 20.2 %collective-permute-start.1 = (bf16[128,12,64]{0,2,1:T(8,128)(2,1)S(1)}, bf16[128,12,64]{0,2,1:T(8,128)(2,1)S(1)}, u32[]{:S(2)}, u32[]{:S(2)}) collective-permute-start(bf16[128,12,64]{0,2,1:T(8,128)(2,1)S(1)} %copy.61), channel_id=1, source_target_pairs={{30,0},{0,2},{2,4},{4,6},{6,8},{8,10},{10,12},{12,14},{14,16},{16,... | collective-permute-start | bytes 589832 | tf_op jit(solution)/shard_map/while/body/eval_jaxpr/ppermute | solution.py:18
  467.1 16.0 %collective-permute-start.3 = (bf16[128,12,64]{0,2,1:T(8,128)(2,1)}, bf16[128,12,64]{0,2,1:T(8,128)(2,1)S(1)}, u32[]{:S(2)}, u32[]{:S(2)}) collective-permute-start(bf16[128,12,64]{0,2,1:T(8,128)(2,1)} %fusion.124), channel_id=1, source_target_pairs={{30,0},{0,2},{2,4},{4,6},{6,8},{8,10},{10,12},{12,14},{14,16},{16,... | collective-permute-start | bytes 589832 | tf_op jit(solution)/shard_map/while/body/eval_jaxpr/ppermute | solution.py:18
  483.2 21.3 %collective-permute-start = (bf16[128,12,64]{0,2,1:T(8,128)(2,1)S(1)}, bf16[128,12,64]{0,2,1:T(8,128)(2,1)S(1)}, u32[]{:S(2)}, u32[]{:S(2)}) collective-permute-start(bf16[128,12,64]{0,2,1:T(8,128)(2,1)S(1)} %copy.60), channel_id=1, source_target_pairs={{30,0},{0,2},{2,4},{4,6},{6,8},{8,10},{10,12},{12,14},{14,16},{16,... | collective-permute-start | bytes 589832 | tf_op jit(solution)/shard_map/while/body/eval_jaxpr/ppermute | solution.py:18
  483.2 21.2 %collective-permute-start.1 = (bf16[128,12,64]{0,2,1:T(8,128)(2,1)S(1)}, bf16[128,12,64]{0,2,1:T(8,128)(2,1)S(1)}, u32[]{:S(2)}, u32[]{:S(2)}) collective-permute-start(bf16[128,12,64]{0,2,1:T(8,128)(2,1)S(1)} %copy.61), channel_id=1, source_target_pairs={{30,0},{0,2},{2,4},{4,6},{6,8},{8,10},{10,12},{12,14},{14,16},{16,... | collective-permute-start | bytes 589832 | tf_op jit(solution)/shard_map/while/body/eval_jaxpr/ppermute | solution.py:18
  486.5 13.7 %collective-permute-start.2 = (bf16[128,12,64]{0,2,1:T(8,128)(2,1)}, bf16[128,12,64]{0,2,1:T(8,128)(2,1)S(1)}, u32[]{:S(2)}, u32[]{:S(2)}) collective-permute-start(bf16[128,12,64]{0,2,1:T(8,128)(2,1)} %fusion.123), channel_id=1, source_target_pairs={{30,0},{0,2},{2,4},{4,6},{6,8},{8,10},{10,12},{12,14},{14,16},{16,... | collective-permute-start | bytes 589832 | tf_op jit(solution)/shard_map/while/body/eval_jaxpr/ppermute | solution.py:18
  487.4 17.0 %collective-permute-start.3 = (bf16[128,12,64]{0,2,1:T(8,128)(2,1)}, bf16[128,12,64]{0,2,1:T(8,128)(2,1)S(1)}, u32[]{:S(2)}, u32[]{:S(2)}) collective-permute-start(bf16[128,12,64]{0,2,1:T(8,128)(2,1)} %fusion.124), channel_id=1, source_target_pairs={{30,0},{0,2},{2,4},{4,6},{6,8},{8,10},{10,12},{12,14},{14,16},{16,... | collective-permute-start | bytes 589832 | tf_op jit(solution)/shard_map/while/body/eval_jaxpr/ppermute | solution.py:18
  504.5 22.4 %collective-permute-start = (bf16[128,12,64]{0,2,1:T(8,128)(2,1)S(1)}, bf16[128,12,64]{0,2,1:T(8,128)(2,1)S(1)}, u32[]{:S(2)}, u32[]{:S(2)}) collective-permute-start(bf16[128,12,64]{0,2,1:T(8,128)(2,1)S(1)} %copy.60), channel_id=1, source_target_pairs={{30,0},{0,2},{2,4},{4,6},{6,8},{8,10},{10,12},{12,14},{14,16},{16,... | collective-permute-start | bytes 589832 | tf_op jit(solution)/shard_map/while/body/eval_jaxpr/ppermute | solution.py:18
  504.6 22.3 %collective-permute-start.1 = (bf16[128,12,64]{0,2,1:T(8,128)(2,1)S(1)}, bf16[128,12,64]{0,2,1:T(8,128)(2,1)S(1)}, u32[]{:S(2)}, u32[]{:S(2)}) collective-permute-start(bf16[128,12,64]{0,2,1:T(8,128)(2,1)S(1)} %copy.61), channel_id=1, source_target_pairs={{30,0},{0,2},{2,4},{4,6},{6,8},{8,10},{10,12},{12,14},{14,16},{16,... | collective-permute-start | bytes 589832 | tf_op jit(solution)/shard_map/while/body/eval_jaxpr/ppermute | solution.py:18
  507.8 14.8 %collective-permute-start.2 = (bf16[128,12,64]{0,2,1:T(8,128)(2,1)}, bf16[128,12,64]{0,2,1:T(8,128)(2,1)S(1)}, u32[]{:S(2)}, u32[]{:S(2)}) collective-permute-start(bf16[128,12,64]{0,2,1:T(8,128)(2,1)} %fusion.123), channel_id=1, source_target_pairs={{30,0},{0,2},{2,4},{4,6},{6,8},{8,10},{10,12},{12,14},{14,16},{16,... | collective-permute-start | bytes 589832 | tf_op jit(solution)/shard_map/while/body/eval_jaxpr/ppermute | solution.py:18
  508.8 18.1 %collective-permute-start.3 = (bf16[128,12,64]{0,2,1:T(8,128)(2,1)}, bf16[128,12,64]{0,2,1:T(8,128)(2,1)S(1)}, u32[]{:S(2)}, u32[]{:S(2)}) collective-permute-start(bf16[128,12,64]{0,2,1:T(8,128)(2,1)} %fusion.124), channel_id=1, source_target_pairs={{30,0},{0,2},{2,4},{4,6},{6,8},{8,10},{10,12},{12,14},{14,16},{16,... | collective-permute-start | bytes 589832 | tf_op jit(solution)/shard_map/while/body/eval_jaxpr/ppermute | solution.py:18
  527.0 23.6 %collective-permute-start = (bf16[128,12,64]{0,2,1:T(8,128)(2,1)S(1)}, bf16[128,12,64]{0,2,1:T(8,128)(2,1)S(1)}, u32[]{:S(2)}, u32[]{:S(2)}) collective-permute-start(bf16[128,12,64]{0,2,1:T(8,128)(2,1)S(1)} %copy.60), channel_id=1, source_target_pairs={{30,0},{0,2},{2,4},{4,6},{6,8},{8,10},{10,12},{12,14},{14,16},{16,... | collective-permute-start | bytes 589832 | tf_op jit(solution)/shard_map/while/body/eval_jaxpr/ppermute | solution.py:18
  527.1 23.5 %collective-permute-start.1 = (bf16[128,12,64]{0,2,1:T(8,128)(2,1)S(1)}, bf16[128,12,64]{0,2,1:T(8,128)(2,1)S(1)}, u32[]{:S(2)}, u32[]{:S(2)}) collective-permute-start(bf16[128,12,64]{0,2,1:T(8,128)(2,1)S(1)} %copy.61), channel_id=1, source_target_pairs={{30,0},{0,2},{2,4},{4,6},{6,8},{8,10},{10,12},{12,14},{14,16},{16,... | collective-permute-start | bytes 589832 | tf_op jit(solution)/shard_map/while/body/eval_jaxpr/ppermute | solution.py:18
  530.3 16.0 %collective-permute-start.2 = (bf16[128,12,64]{0,2,1:T(8,128)(2,1)}, bf16[128,12,64]{0,2,1:T(8,128)(2,1)S(1)}, u32[]{:S(2)}, u32[]{:S(2)}) collective-permute-start(bf16[128,12,64]{0,2,1:T(8,128)(2,1)} %fusion.123), channel_id=1, source_target_pairs={{30,0},{0,2},{2,4},{4,6},{6,8},{8,10},{10,12},{12,14},{14,16},{16,... | collective-permute-start | bytes 589832 | tf_op jit(solution)/shard_map/while/body/eval_jaxpr/ppermute | solution.py:18
  531.2 19.3 %collective-permute-start.3 = (bf16[128,12,64]{0,2,1:T(8,128)(2,1)}, bf16[128,12,64]{0,2,1:T(8,128)(2,1)S(1)}, u32[]{:S(2)}, u32[]{:S(2)}) collective-permute-start(bf16[128,12,64]{0,2,1:T(8,128)(2,1)} %fusion.124), channel_id=1, source_target_pairs={{30,0},{0,2},{2,4},{4,6},{6,8},{8,10},{10,12},{12,14},{14,16},{16,... | collective-permute-start | bytes 589832 | tf_op jit(solution)/shard_map/while/body/eval_jaxpr/ppermute | solution.py:18
  550.6 15.7 %collective-permute-start = (bf16[128,12,64]{0,2,1:T(8,128)(2,1)S(1)}, bf16[128,12,64]{0,2,1:T(8,128)(2,1)S(1)}, u32[]{:S(2)}, u32[]{:S(2)}) collective-permute-start(bf16[128,12,64]{0,2,1:T(8,128)(2,1)S(1)} %copy.60), channel_id=1, source_target_pairs={{30,0},{0,2},{2,4},{4,6},{6,8},{8,10},{10,12},{12,14},{14,16},{16,... | collective-permute-start | bytes 589832 | tf_op jit(solution)/shard_map/while/body/eval_jaxpr/ppermute | solution.py:18
  550.7 15.6 %collective-permute-start.1 = (bf16[128,12,64]{0,2,1:T(8,128)(2,1)S(1)}, bf16[128,12,64]{0,2,1:T(8,128)(2,1)S(1)}, u32[]{:S(2)}, u32[]{:S(2)}) collective-permute-start(bf16[128,12,64]{0,2,1:T(8,128)(2,1)S(1)} %copy.61), channel_id=1, source_target_pairs={{30,0},{0,2},{2,4},{4,6},{6,8},{8,10},{10,12},{12,14},{14,16},{16,... | collective-permute-start | bytes 589832 | tf_op jit(solution)/shard_map/while/body/eval_jaxpr/ppermute | solution.py:18
  576.0 37.5 %reduce-scatter.9.cloned.1.call-start = ((), (), s32[]{:S(2)}) async-start(), calls=%async_computation.9 | async-start | bytes 7077888 | tf_op jit(solution)/shard_map/reduce_scatter | solution.py:292
  580.8 38.4 %reduce-scatter.11.cloned.1.call-start = ((), (), s32[]{:S(2)}) async-start(), calls=%async_computation.10 | async-start | bytes 7077888 | tf_op jit(solution)/shard_map/reduce_scatter | solution.py:298
  (55 other events, 453.2 us)
Sparse Core Ops, SparseCore 0:
  9.6 15.3 all-gather.17
  29.1 77.6 all-gather.25
  110.1 74.6 all-gather.27
  186.3 7.4 all-gather.19
  195.1 15.5 all-gather.21
  212.1 15.6 all-gather.23
  243.5 9.8 reduce-scatter.6
  576.1 9.8 reduce-scatter.12
  588.8 13.7 reduce-scatter.8
  605.5 13.7 reduce-scatter.10
where the time goes:
time: 1220 us
  blocking collectives  608 us (50%)
  waiting for transfers between devices  409 us (34%)
  matrix products  111 us (9%)
  other arithmetic  33.8 us (3%)
  local copies, waits for them, and re-layouts  22.6 us (2%)
  between operations  16.2 us (1%)
  starting transfers between devices  15.6 us (1%)
    psum x1, blocking collectives, body(): summed = lax.psum(tuple(scattered), 'seq')  587 us
    ppermute x64, waiting for transfers between devices, from_behind(): return lax.ppermute(block, axis, route)  234 us
    all_gather x1, waiting for transfers between devices, body(): lax.all_gather(value_rows, 'seq', axis=0, tiled=True)  69 us
    all_gather x1, waiting for transfers between devices, body(): lax.all_gather(key_rows, 'seq', axis=0, tiled=True)  61.1 us
  transfers between devices with their start and end apart: 74, of which 38 were waited for; matrix products, arithmetic and copies ran while one was open for 11% of the time, Pallas kernels for 0%

commit v1 on v0

v1 whole, which is shorter than its diff:
```python
import functools

import jax
import jax.numpy as jnp
from jax import lax
from jax.experimental import pallas as pl
from jax.experimental.pallas import tpu as pltpu
from jax.sharding import PartitionSpec as P

HEADS = 12
HEAD_DIM = 64
GROUPS = 4
GROUP_HEADS = HEADS // GROUPS
GROUP_WIDTH = GROUP_HEADS * HEAD_DIM
EPSILON = 1e-12
MASKED = -1e30
F32 = jnp.float32
BF16 = jnp.bfloat16


def dot(left, right, dims=((1,), (0,))):
    return lax.dot_general(left, right, (dims, ((), ())), preferred_element_type=F32)


class Places:
    def __init__(self, size):
        self.size = size
        self.plane_size = size // GROUPS
        self.rest = self.plane_size // 4
        index = lambda g, q, m: (g * 4 + q) * self.rest + m
        groups, quarters, members = range(GROUPS), range(4), range(self.rest)
        self.columns = [[index(g, q, m) for g in groups] for q in quarters for m in members]
        self.planes = [[index(g, q, m) for q in quarters for m in members] for g in groups]
        self.fours = [[index(g, q, m) for q in quarters] for g in groups for m in members]
        self.rests = [[index(g, q, m) for m in members] for g in groups for q in quarters]

    def gather(self, block, groups):
        return lax.all_gather(block, "seq", axis=0, axis_index_groups=groups)

    def exchange(self, blocks, groups):
        return lax.all_to_all(blocks, "seq", 0, 0, axis_index_groups=groups, tiled=True)

    def swap(self, block, bits):
        return lax.ppermute(block, "seq", [(i, i ^ bits) for i in range(self.size)])

    def scatter_sum(self, blocks, groups):
        return jnp.sum(self.exchange(blocks, groups).astype(F32), axis=0)


def layer_norm(hidden, gain, shift):
    center = hidden - jnp.mean(hidden, axis=-1, keepdims=True)
    spread = jnp.mean(center * center, axis=-1, keepdims=True)
    return center * lax.rsqrt(spread + EPSILON) * gain + shift


def gelu_exact(values):
    return jax.nn.gelu(values, approximate=False)


ROWS = 128


def attend_kernel(pieces, chunks, *refs):
    q_ref = refs[0]
    key_refs, value_refs, bias_refs = (refs[1 + i * pieces : 1 + (i + 1) * pieces] for i in range(3))
    context_ref, log_ref = refs[1 + 3 * pieces :]
    rows = q_ref.shape[0]
    chunk = key_refs[0].shape[0] // chunks
    for block in range(rows // ROWS):
        at = slice(block * ROWS, (block + 1) * ROWS)
        for head in range(GROUP_HEADS):
            columns = slice(head * HEAD_DIM, (head + 1) * HEAD_DIM)
            query = q_ref[at, columns] * jnp.asarray(0.125, BF16)

            def step(index, state):
                highest, total, mix = state
                start = pl.multiple_of(index * chunk, chunk)
                here = pl.ds(start, chunk)
                scores = [
                    dot(query, k[here, columns], ((1,), (1,))) + b[:, here]
                    for k, b in zip(key_refs, bias_refs)
                ]
                peak = functools.reduce(
                    jnp.maximum, [jnp.max(s, axis=1, keepdims=True) for s in scores]
                )
                raised = jnp.maximum(highest, peak)
                weights = [jnp.exp(s - raised) for s in scores]
                factor = jnp.exp(highest - raised)
                total = total * factor + sum(jnp.sum(w, axis=1, keepdims=True) for w in weights)
                mix = mix * factor + sum(
                    dot(w.astype(BF16), v[here, columns]) for w, v in zip(weights, value_refs)
                )
                return raised, total, mix

            state = (
                jnp.full((ROWS, 1), MASKED, F32),
                jnp.zeros((ROWS, 1), F32),
                jnp.zeros((ROWS, HEAD_DIM), F32),
            )
            if chunks == 1:
                state = step(0, state)
            else:
                state = lax.fori_loop(0, chunks, step, state)
            highest, total, mix = state
            context_ref[at, columns] = mix / total
            log_ref[at, head : head + 1] = highest + jnp.log(total)


def attend(query, keys, values, bias, chunks):
    rows = query.shape[0]
    return pl.pallas_call(
        functools.partial(attend_kernel, len(keys), chunks),
        out_shape=(
            jax.ShapeDtypeStruct((rows, GROUP_WIDTH), F32),
            jax.ShapeDtypeStruct((rows, 128), F32),
        ),
        compiler_params=pltpu.CompilerParams(vmem_limit_bytes=60 * 2**20),
        name="attend",
    )(query, *keys, *values, *bias)


def attend_grad_kernel(pieces, chunks, *refs):
    q_ref, context_ref, grad_ref, log_ref = refs[:4]
    key_refs, value_refs, bias_refs = (refs[4 + i * pieces : 4 + (i + 1) * pieces] for i in range(3))
    query_grad_ref = refs[4 + 3 * pieces]
    key_value_refs = refs[5 + 3 * pieces :]
    rows = q_ref.shape[0]
    chunk = key_refs[0].shape[0] // chunks
    for head in range(GROUP_HEADS):
        columns = slice(head * HEAD_DIM, (head + 1) * HEAD_DIM)
        key_rows = slice(head * HEAD_DIM, (head + 1) * HEAD_DIM)
        value_rows = slice(GROUP_WIDTH + head * HEAD_DIM, GROUP_WIDTH + (head + 1) * HEAD_DIM)
        query = q_ref[:, columns] * jnp.asarray(0.125, BF16)
        grad = grad_ref[:, columns]
        correction = jnp.sum(grad.astype(F32) * context_ref[:, columns], axis=1, keepdims=True)
        log_total = log_ref[:, head : head + 1]
        query_turned = query.T
        grad_turned = grad.T

        def step(index, query_grad):
            start = pl.multiple_of(index * chunk, chunk)
            here = pl.ds(start, chunk)
            for k, v, b, out in zip(key_refs, value_refs, bias_refs, key_value_refs):
                key = k[here, columns]
                probs = jnp.exp(dot(query, key, ((1,), (1,))) + b[:, here] - log_total)
                probs_grad = dot(grad, v[here, columns], ((1,), (1,)))
                score_grad = (probs * (probs_grad - correction)).astype(BF16)
                query_grad = query_grad + dot(score_grad, key)
                out[key_rows, here] = dot(query_turned, score_grad).astype(BF16)
                out[value_rows, here] = dot(grad_turned, probs.astype(BF16)).astype(BF16)
            return query_grad

        total = jnp.zeros((rows, HEAD_DIM), F32)
        total = step(0, total) if chunks == 1 else lax.fori_loop(0, chunks, step, total)
        query_grad_ref[:, columns] = (total * 0.125).astype(BF16)


def attend_grad(query, context, grad, log_total, keys, values, bias, chunks):
    rows = query.shape[0]
    return pl.pallas_call(
        functools.partial(attend_grad_kernel, len(keys), chunks),
        out_shape=(jax.ShapeDtypeStruct((rows, GROUP_WIDTH), BF16),)
        + tuple(jax.ShapeDtypeStruct((2 * GROUP_WIDTH, k.shape[0]), BF16) for k in keys),
        compiler_params=pltpu.CompilerParams(vmem_limit_bytes=60 * 2**20),
        name="attend_grad",
    )(query, context, grad, log_total, *keys, *values, *bias)


def body(
    tokens,
    cotangent,
    lengths,
    qkv_weight,
    query_bias,
    value_bias,
    out_weight,
    out_bias,
    first_gain,
    first_shift,
    up_weight,
    up_bias,
    down_weight,
    down_bias,
    second_gain,
    second_shift,
):
    row_count, model_width = tokens.shape[1], tokens.shape[2]
    hidden_width = up_weight.shape[1]
    places = Places(lax.axis_size("seq"))
    plane_size = places.plane_size
    rank = lax.axis_index("seq")
    core = lax.axis_index("shard")
    group, position = rank // plane_size, rank % plane_size
    length = lengths[core]
    inputs = tokens[0]
    column_rows = GROUPS * row_count
    half = model_width // 2

    def both(block):
        return lax.all_gather(block, "shard", axis=0, tiled=True)

    at = group * GROUP_WIDTH
    own_columns = lambda w: jnp.concatenate(
        [lax.dynamic_slice_in_dim(w, at + i * model_width, GROUP_WIDTH, w.ndim - 1) for i in range(3)],
        axis=-1,
    )
    group_weight = both(own_columns(qkv_weight))
    vectors = [query_bias, value_bias, out_bias, first_gain, first_shift, down_bias, second_gain, second_shift]
    stacked = jnp.concatenate([jnp.stack(vectors), up_bias.reshape(-1, half)])
    stacked = lax.all_gather(stacked, "shard", axis=0).astype(F32)
    whole = jnp.transpose(stacked[:, : len(vectors)], (1, 0, 2)).reshape(len(vectors), model_width)
    (query_offset, value_offset, out_offset, gain_one, shift_one, down_offset, gain_two, shift_two) = whole
    up_offset = stacked[:, len(vectors) :].reshape(hidden_width)
    out_matrix = both(out_weight)
    up_matrix = both(up_weight)
    down_matrix = both(down_weight)

    column_inputs = places.gather(inputs, places.columns).reshape(column_rows, model_width)
    zero_bias = jnp.zeros_like(query_offset)
    offset = own_columns(jnp.concatenate([query_offset, zero_bias, value_offset]))
    joined = (dot(column_inputs, group_weight) + offset).astype(BF16)
    query = joined[:, :GROUP_WIDTH]
    key = joined[:, GROUP_WIDTH : 2 * GROUP_WIDTH]
    value = joined[:, 2 * GROUP_WIDTH :]

    def masks(who):
        starts = (jnp.arange(GROUPS)[:, None] * plane_size + who) * row_count
        tokens_at = starts[:, :, None] + jnp.arange(row_count)
        return jnp.where(tokens_at.transpose(1, 0, 2).reshape(1, -1) < length, 0.0, MASKED).astype(F32)

    if plane_size == 4:
        chunks = 1
        key_one, value_two = places.swap(key, 1), places.swap(value, 2)
        key_two, key_three = places.swap(key, 2), places.swap(key_one, 2)
        value_one, value_three = places.swap(value, 1), places.swap(value_two, 1)
        keys = (key, key_one, key_two, key_three)
        values = (value, value_one, value_two, value_three)
        bias = tuple(masks((position ^ i)[None]) for i in range(4))
    else:
        chunks = plane_size // 4
        keys = (places.gather(key, places.planes).reshape(-1, GROUP_WIDTH),)
        values = (places.gather(value, places.planes).reshape(-1, GROUP_WIDTH),)
        bias = (masks(jnp.arange(plane_size)),)
    context, log_total = attend(query, keys, values, bias, chunks)

    def to_tokens(block):
        blocks = places.exchange(block.reshape(GROUPS, row_count, GROUP_WIDTH), places.columns)
        return jnp.transpose(blocks, (1, 0, 2)).reshape(row_count, model_width)

    def to_heads(block):
        blocks = jnp.transpose(block.reshape(row_count, GROUPS, GROUP_WIDTH), (1, 0, 2))
        return places.exchange(blocks, places.columns).reshape(column_rows, GROUP_WIDTH)

    context_low = to_tokens(context.astype(BF16))
    branch = dot(context_low, out_matrix) + out_offset
    residual_one = inputs.astype(F32) + branch
    normed_one, norm_pull_one = jax.vjp(layer_norm, residual_one, gain_one, shift_one)
    normed_low = normed_one.astype(BF16)
    inner_sum = dot(normed_low, up_matrix) + up_offset
    active, gelu_pull = jax.vjp(gelu_exact, inner_sum)
    active_low = active.astype(BF16)
    second = dot(active_low, down_matrix) + down_offset
    residual_two = normed_low.astype(F32) + second
    outputs, norm_pull_two = jax.vjp(layer_norm, residual_two, gain_two, shift_two)
    residual_two_grad, gain_two_grad, shift_two_grad = norm_pull_two(cotangent[0].astype(F32))
    second_low = residual_two_grad.astype(BF16)
    down_bias_grad = jnp.sum(second_low.astype(F32), axis=0)
    active_grad = dot(second_low, down_matrix, ((1,), (1,)))
    inner_low = gelu_pull(active_grad)[0].astype(BF16)
    up_bias_grad = jnp.sum(inner_low.astype(F32), axis=0)
    normed_grad = dot(inner_low, up_matrix, ((1,), (1,))) + residual_two_grad
    residual_one_grad, gain_one_grad, shift_one_grad = norm_pull_one(normed_grad)
    branch_low = residual_one_grad.astype(BF16)
    out_bias_grad = jnp.sum(branch_low.astype(F32), axis=0)
    context_grad = to_heads(dot(branch_low, out_matrix, ((1,), (1,))).astype(BF16))

    def core_sum(grad):
        rows = grad.shape[0] // 2
        mine = lax.dynamic_slice_in_dim(grad, core * rows, rows, 0)
        other = lax.dynamic_slice_in_dim(grad, (1 - core) * rows, rows, 0)
        received = lax.ppermute(other, "shard", [(0, 1), (1, 0)])
        return (mine.astype(F32) + received.astype(F32)).astype(BF16)

    def four_sum(blocks):
        total = places.scatter_sum(blocks, places.fours)
        if places.rest > 1:
            total = lax.psum(total, "seq", axis_index_groups=places.rests)
        return total.astype(BF16)

    def all_sum(grad):
        rows, columns = grad.shape
        part = four_sum(grad.reshape(4, rows // 4, columns))
        part = jnp.transpose(part.reshape(rows // 4, GROUPS, columns // GROUPS), (1, 0, 2))
        part = places.scatter_sum(part, places.columns).astype(BF16)
        part = jnp.transpose(places.gather(part, places.columns), (1, 0, 2)).reshape(rows // 4, columns)
        return places.gather(part, places.fours).reshape(rows, columns).astype(F32)

    up_grad = all_sum(core_sum(dot(normed_low, inner_low, ((0,), (0,))).astype(BF16)))
    down_grad = all_sum(core_sum(dot(active_low, second_low, ((0,), (0,))).astype(BF16)))
    out_grad = all_sum(core_sum(dot(context_low, branch_low, ((0,), (0,))).astype(BF16)))
    vector_grads = jnp.concatenate(
        [
            jnp.stack([out_bias_grad, gain_one_grad, shift_one_grad, down_bias_grad, gain_two_grad, shift_two_grad]),
            up_bias_grad.reshape(-1, model_width),
        ]
    )
    vector_grads = lax.psum(vector_grads, ("seq", "shard"))
    halves = lax.dynamic_slice_in_dim(vector_grads[:6], core * half, half, 1)
    up_bias_out = lax.dynamic_slice_in_dim(vector_grads[6:].reshape(-1), core * (hidden_width // 2), hidden_width // 2, 0)

    parts = attend_grad(query, context, context_grad, log_total, keys, values, bias, chunks)
    query_grad, key_value_grads = parts[0], parts[1:]
    if plane_size == 4:
        own, one, two, three = key_value_grads
        one_in, two_in, three_in = places.swap(one, 1), places.swap(two, 2), places.swap(three, 3)
        key_value = own.astype(F32) + one_in.astype(F32) + two_in.astype(F32) + three_in.astype(F32)
    else:
        blocks = key_value_grads[0].reshape(2 * GROUP_WIDTH, plane_size, column_rows)
        key_value = places.scatter_sum(jnp.transpose(blocks, (1, 0, 2)), places.planes)
    joined_grad = jnp.concatenate([query_grad, key_value.T.astype(BF16)], axis=1)
    bias_part = jnp.sum(joined_grad.astype(F32), axis=0)
    weight_part = core_sum(dot(column_inputs, joined_grad, ((0,), (0,))).astype(BF16))
    weight_part = four_sum(weight_part.reshape(4, half // 4, -1))
    input_part = dot(joined_grad, group_weight, ((1,), (1,))).astype(BF16)
    input_part = places.scatter_sum(input_part.reshape(GROUPS, row_count, model_width), places.columns)
    input_grad = residual_one_grad + input_part
    weight_whole = places.gather(places.gather(weight_part, places.columns), places.fours)
    weight_whole = weight_whole.reshape(4, GROUPS, half // 4, 3, GROUP_WIDTH)
    qkv_grad = jnp.transpose(weight_whole, (0, 2, 3, 1, 4)).reshape(half, 3 * model_width).astype(F32)
    spread = jnp.zeros((GROUPS, 3 * GROUP_WIDTH), F32)
    spread = lax.dynamic_update_slice_in_dim(spread, bias_part[None], group, 0)
    spread = lax.psum(spread, ("seq", "shard")).reshape(GROUPS, 3, GROUP_WIDTH)
    query_bias_grad = lax.dynamic_slice_in_dim(spread[:, 0].reshape(model_width), core * half, half, 0)
    value_bias_grad = lax.dynamic_slice_in_dim(spread[:, 2].reshape(model_width), core * half, half, 0)

    shape = (1, row_count, model_width)
    return (
        outputs.astype(BF16).reshape(shape),
        input_grad.reshape(shape),
        qkv_grad,
        query_bias_grad,
        value_bias_grad,
        out_grad,
        halves[0],
        halves[1],
        halves[2],
        up_grad,
        up_bias_out,
        down_grad,
        halves[3],
        halves[4],
        halves[5],
    )


def solution(mesh):
    rows, halves, whole = P("shard", "seq", None), P("shard", None), P("shard")
    in_specs = (rows, rows, P(), halves, whole, whole, halves, whole, whole, whole, halves, whole, halves, whole, whole, whole)
    out_specs = (rows, rows, halves, whole, whole, halves, whole, whole, whole, halves, whole, halves, whole, whole, whole)
    return jax.shard_map(body, mesh=mesh, in_specs=in_specs, out_specs=out_specs, check_vma=False)
```

time: 1220 us -> 449 us (0.37)
  blocking collectives: 608 us -> 152 us
  waiting for transfers between devices: 409 us -> 107 us
  matrix products: 111 us -> 28.6 us
  starting transfers between devices: 15.6 us -> 42.7 us
  Pallas kernels: 0 us -> 19.7 us
  local copies, waits for them, and re-layouts: 22.6 us -> 40.8 us
    psum x1, blocking collectives: 587 us -> 41.6 us  [body(): spread = lax.psum(spread, ('seq', 'shard')).reshape(GROUPS, 3, GROUP_WIDTH)]
    ppermute x64 -> x13, waiting for transfers between devices: 234 us -> 31.2 us  [the longest x9 27.4 us: swap(): return lax.ppermute(block, 'seq', [(i, i ^ bits) for i in range(self.size)])]
    all_gather x6, waiting for transfers between devices: 167 us -> 0.03 us  [the longest x3 0.02 us: both(): return lax.all_gather(block, 'shard', axis=0, tiled=True)]
    all_gather x9 -> x8, blocking collectives: 16.2 us -> 99.3 us  [the longest x6 94.8 us: gather(): return lax.all_gather(block, 'seq', axis=0, axis_index_groups=groups)]
    dot_general x94 -> x12, matrix products: 111 us -> 28.6 us  [dot(): lax.dot_general(left, right, (dims, ((), ())), preferred_element_type=F32)]
    all_to_all x0 -> x9, waiting for transfers between devices: none -> 73.5 us  [exchange(): lax.all_to_all(blocks, 'seq', 0, 0, axis_index_groups=groups, tiled=True)]
    all_to_all x0 -> x9, starting transfers between devices: none -> 32.7 us  [exchange(): lax.all_to_all(blocks, 'seq', 0, 0, axis_index_groups=groups, tiled=True)]
    pallas_call x0 -> x2, Pallas kernels: none -> 19.7 us  [the longest x1 10.5 us: attend_grad(): pl.pallas_call(functools.partial(attend_grad_kernel, len(keys), chunks),...]
  transfers between devices with their start and end apart: 74 -> 28, of which waited for: 38 -> 16; matrix products, arithmetic and copies ran while one was open for 11% -> 19% of each run, Pallas kernels for 0% -> 4%
where the time goes in v1:
time: 449 us; the launch traced here: 441 us
  blocking collectives  152 us (34%)
  waiting for transfers between devices  107 us (24%)
  starting transfers between devices  42.7 us (10%)
  local copies, waits for them, and re-layouts  40.8 us (9%)
  other arithmetic  34.3 us (8%)
  matrix products  28.6 us (6%)
  Pallas kernels  19.7 us (4%)
  between operations  15.8 us (4%)
    all_gather x6, blocking collectives, gather(): return lax.all_gather(block, 'seq', axis=0, axis_index_groups=groups)  94.8 us
    all_to_all x9, waiting for transfers between devices, exchange(): lax.all_to_all(blocks, 'seq', 0, 0, axis_index_groups=groups, tiled=True)  73.5 us
    psum x1, blocking collectives, body(): spread = lax.psum(spread, ('seq', 'shard')).reshape(GROUPS, 3, GROUP_WIDTH)  41.6 us
    all_to_all x9, starting transfers between devices, exchange(): lax.all_to_all(blocks, 'seq', 0, 0, axis_index_groups=groups, tiled=True)  32.7 us
    dot_general x12, matrix products, dot(): lax.dot_general(left, right, (dims, ((), ())), preferred_element_type=F32)  28.6 us
    ppermute x9, waiting for transfers between devices, swap(): return lax.ppermute(block, 'seq', [(i, i ^ bits) for i in range(self.size)])  27.4 us
    convert_element_type x2, local copies, waits for them, and re-layouts, body(): jnp.transpose(weight_whole, (0, 2, 3, 1, 4)).reshape(half, 3 * model_width)  12.7 us
    all_to_all x1, blocking collectives, exchange(): lax.all_to_all(blocks, 'seq', 0, 0, axis_index_groups=groups, tiled=True)  11 us
  transfers between devices with their start and end apart: 28, of which 16 were waited for; matrix products, arithmetic and copies ran while one was open for 19% of the time, Pallas kernels for 4%

profile of v1, /device:TPU:0, one launch (start us, length us, event | category | flops | bytes accessed | tf_op | source)
XLA Modules:
  0.0 440.5 jit_solution(7474607560705470754)
XLA Ops:
  9.8 1.9 all-gather.6
  12.1 1.4 constant_dynamic-slice_fusion.6
  13.6 2.5 all_gather.60
  16.2 21.1 %all_gather.61 = bf16[4,128,768]{2,1,0:T(8,128)(2,1)S(1)} all-gather(bf16[1,128,768]{2,1,0:T(8,128)(2,1)S(1)} %copy-done.25), channel_id=1, replica_groups={{0,8,16,24},{2,10,18,26},{4,12,20,28},{6,14,22,30},{1,9,17,25},{3,11,19..., dimensions={0}, use_global_device_ids=true | all-gather | bytes 983040 | tf_op jit(solution)/shard_map/all_gather | solution.py:38
  39.0 1.5 collective-permute-start
  40.5 1.5 collective-permute-start.1
  43.6 1.3 fusion.19
  44.9 3.3 collective-permute-done.refs_2_.refs_5_
  48.2 1.5 collective-permute-start.2
  49.7 5.3 %collective-permute-done.4.refs_7_.refs_10_ = bf16[512,192]{1,0:T(8,128)(2,1)S(1)} collective-permute-done((bf16[512,192]{1,0:T(8,128)(2,1)S(1)}, bf16[512,192]{1,0:T(8,128)(2,1)S(1)}, u32[]{:S(2)}, u32[]{:S(2)}) %collective-permute-start.4) | collective-permute-done | bytes 196640 | tf_op jit(solution)/shard_map/ppermute | solution.py:44
  57.9 3.6 collective-permute-done.5.refs_8_.refs_11_
  62.2 9.2 %attend.1 = (f32[512,192]{1,0:T(8,128)}, f32[512,128]{1,0:T(8,128)}) custom-call(bf16[512,192]{1,0:T(8,128)(2,1)} %get-tuple-element.69.refs_0_, bf16[512,192]{1,0:T(8,128)(2,1)} %copy-done.5, bf16[512,192]{1,0:T(8,128)(2,1)} %copy-done.13, bf16[512,192]{1,0:T(8,128)(2,1)} %copy-done.14, bf16[512,192]{1,0:T(8,128)(2,1)} %copy-done.17, ...), custom_call_target="tpu_custom_call" | custom-call | tf_op jit(solution)/shard_map/attend/pallas_call | solution.py:111
  73.2 3.8 all-to-all-start
  77.1 6.1 %all-to-all-done = bf16[4,128,192]{1,2,0:T(8,128)(2,1)S(1)} async-done(((bf16[4,128,192]{1,2,0:T(8,128)(2,1)}), bf16[4,128,192]{1,2,0:T(8,128)(2,1)S(1)}, u32[]{:S(2)}, u32[]{:S(2)}) %all-to-all-start) | async-done | bytes 196640 | tf_op jit(solution)/shard_map/all_to_all | solution.py:41
  83.2 1.8 fusion.33
  85.3 8.4 %multiply_convert_fusion = (bf16[128,3072]{1,0:T(8,128)(2,1)S(1)}, f32[128,3072]{1,0:T(8,128)}, f32[128,3072]{1,0:T(8,128)}) fusion(f32[3072]{0:T(1024)S(1)} %add.360, bf16[768,3072]{1,0:T(8,128)(2,1)} %all-gather.16.cloned.1.call-done, f32[128,768]{1,0:T(8,128)S(1)} %get-tuple-element.75, f32[768]{0:T(1024)S(1)} %add.357, f32[768]{0:T(1024)S(1)} %mul.238, ...), kind=kOutput, calls=%fused_computation.13 | convolution fusion | flops 630423552 | bytes 9063424 | tf_op jit(solution)/shard_map/dot_general | solution.py:22
  93.7 3.4 fusion.34
  98.8 2.5 convert_reduce_fusion
  101.2 1.5 convolution_convert_fusion.1
  102.8 2.4 multiply_reduce_fusion
  105.4 1.6 constant_dynamic-slice_fusion.2
  108.2 11.0 %all_to_all.50 = bf16[4,128,192]{1,2,0:T(8,128)(2,1)S(1)} all-to-all(bf16[4,128,192]{1,2,0:T(8,128)(2,1)S(1)} %bitcast.121), channel_id=1, replica_groups={{0,8,16,24},{2,10,18,26},{4,12,20,28},{6,14,22,30},{1,9,17,25},{3,11,19..., dimensions={0} | all-to-all | bytes 393216 | tf_op jit(solution)/shard_map/all_to_all | solution.py:41
  120.1 10.5 %attend_grad.1 = (bf16[512,192]{1,0:T(8,128)(2,1)}, bf16[384,512]{1,0:T(8,128)(2,1)}, bf16[384,512]{1,0:T(8,128)(2,1)}, bf16[384,512]{1,0:T(8,128)(2,1)}, bf16[384,512]{1,0:T(8,128)(2,1)}) custom-call(bf16[512,192]{1,0:T(8,128)(2,1)} %get-tuple-element.69.refs_0_, f32[512,192]{1,0:T(8,128)} %get-tuple-element.22.refs_1_, bf16[512,192]{1,0:T(8,128)(2,1)} %bitcast.120, ...), custom_call_target="tpu_custom_call" | custom-call | tf_op jit(solution)/shard_map/attend_grad/pallas_call | solution.py:160
  130.6 1.6 collective-permute-start.8
  132.6 1.5 collective-permute-start.6
  135.2 8.6 %collective-permute-done.8 = bf16[384,512]{1,0:T(8,128)(2,1)S(1)} collective-permute-done((bf16[384,512]{1,0:T(8,128)(2,1)}, bf16[384,512]{1,0:T(8,128)(2,1)S(1)}, u32[]{:S(2)}, u32[]{:S(2)}) %collective-permute-start.8) | collective-permute-done | bytes 393248 | tf_op jit(solution)/shard_map/ppermute | solution.py:44
  143.8 5.5 %collective-permute-done.7 = bf16[384,512]{1,0:T(8,128)(2,1)S(1)} collective-permute-done((bf16[384,512]{1,0:T(8,128)(2,1)}, bf16[384,512]{1,0:T(8,128)(2,1)S(1)}, u32[]{:S(2)}, u32[]{:S(2)}) %collective-permute-start.7) | collective-permute-done | bytes 393248 | tf_op jit(solution)/shard_map/ppermute | solution.py:44
  149.5 1.3 fusion.17
  151.6 1.8 collective-permute-done.9
  154.5 3.5 all-to-all-start.3
  158.0 4.7 %add_convert_fusion.1 = bf16[384,3072]{1,0:T(8,128)(2,1)} fusion(bf16[384,3072]{1,0:T(8,128)(2,1)} %collective-permute-done.11, bf16[768,3072]{1,0:T(8,128)(2,1)} %copy-done, s32[]{:T(128)S(6)} %select_n.84), kind=kLoop, calls=%fused_computation.4 | loop fusion | flops 4718592 | bytes 7077892 | tf_op jit(solution)/shard_map/convert_element_type | solution.py:282
  162.7 3.5 all-to-all-done.3
  167.0 3.6 all-to-all-start.6
  170.7 3.6 convolution_convert_fusion
  175.4 15.7 %all-gather.1 = bf16[384,576]{1,0:T(8,128)(2,1)} all-gather(bf16[96,576]{1,0:T(8,128)(2,1)S(1)} %reduce_sum.278), channel_id=3, replica_groups={{0,8,16,24},{2,10,18,26},{4,12,20,28},{6,14,22,30},{1,9,17,25},{3,11,19..., dimensions={0}, use_global_device_ids=true | all-gather | bytes 552960 | tf_op jit(solution)/shard_map/all_gather | solution.py:38
  191.1 3.2 constant_dynamic-slice_fusion.1
  194.3 3.7 all-to-all-done.6
  199.8 4.3 all-to-all-start.7
  204.1 15.1 %all-to-all-done.7 = bf16[4,96,768]{2,1,0:T(8,128)(2,1)S(1)} async-done(((bf16[4,96,768]{2,1,0:T(8,128)(2,1)}), bf16[4,96,768]{2,1,0:T(8,128)(2,1)S(1)}, u32[]{:S(2)}, u32[]{:S(2)}) %all-to-all-start.7) | async-done | bytes 589856 | tf_op jit(solution)/shard_map/all_to_all | solution.py:41
  219.2 16.3 %all-gather.4 = bf16[384,768]{1,0:T(8,128)(2,1)S(1)} all-gather(bf16[96,768]{1,0:T(8,128)(2,1)S(1)} %reduce_sum.290), channel_id=6, replica_groups={{0,8,16,24},{2,10,18,26},{4,12,20,28},{6,14,22,30},{1,9,17,25},{3,11,19..., dimensions={0}, use_global_device_ids=true | all-gather | bytes 737280 | tf_op jit(solution)/shard_map/all_gather | solution.py:38
  237.2 4.4 add_convert_fusion
  241.6 3.7 all-to-all-start.8
  245.4 1.5 convolution_convert_fusion.2
  246.8 28.8 %all-to-all-done.8 = bf16[4,384,768]{2,1,0:T(8,128)(2,1)S(1)} async-done(((bf16[4,384,768]{2,1,0:T(8,128)(2,1)}), bf16[4,384,768]{2,1,0:T(8,128)(2,1)S(1)}, u32[]{:S(2)}, u32[]{:S(2)}) %all-to-all-start.8) | async-done | bytes 2359328 | tf_op jit(solution)/shard_map/all_to_all | solution.py:41
  275.7 1.3 reduce_sum.291
  277.0 2.1 copy.97
  279.1 3.5 all-to-all-start.9
  282.7 2.0 collective-permute-done.10
  285.7 11.8 %all-to-all-done.9 = bf16[4,384,192]{1,2,0:T(8,128)(2,1)S(1)} async-done(((bf16[4,384,192]{1,2,0:T(8,128)(2,1)}), bf16[4,384,192]{1,2,0:T(8,128)(2,1)S(1)}, u32[]{:S(2)}, u32[]{:S(2)}) %all-to-all-start.9) | async-done | bytes 589856 | tf_op jit(solution)/shard_map/all_to_all | solution.py:41
  297.4 3.5 all-to-all-start.4
  301.1 16.5 %all-gather.5 = bf16[1536,192]{0,1:T(8,128)(2,1)S(1)} all-gather(bf16[384,192]{0,1:T(8,128)(2,1)S(1)} %reduce_sum.292), channel_id=7, replica_groups={{0,8,16,24},{2,10,18,26},{4,12,20,28},{6,14,22,30},{1,9,17,25},{3,11,19..., dimensions={0}, use_global_device_ids=true | all-gather | bytes 737280 | tf_op jit(solution)/shard_map/all_gather | solution.py:38
  319.9 3.4 all-to-all-start.5
  323.3 1.7 convolution_convert_fusion.4
  325.0 4.5 %all-to-all-done.5 = bf16[4,96,192]{2,1,0:T(8,128)(2,1)S(1)} async-done(((bf16[4,96,192]{2,1,0:T(8,128)(2,1)}), bf16[4,96,192]{2,1,0:T(8,128)(2,1)S(1)}, u32[]{:S(2)}, u32[]{:S(2)}) %all-to-all-start.5) | async-done | bytes 147488 | tf_op jit(solution)/shard_map/all_to_all | solution.py:41
  329.5 3.5 all-to-all-start.2
  333.7 41.6 %all-reduce = (f32[4,3,192]{2,1,0:T(4,128)S(1)}, f32[10,768]{1,0:T(8,128)S(1)}) all-reduce(f32[4,3,192]{2,1,0:T(4,128)S(1)} %reshape.416, f32[10,768]{1,0:T(8,128)S(1)} %concatenate.23), channel_id=1, replica_groups=mesh['seq'=16,'shard'=2] {'seq','shard'}, use_global_device_ids=true, to_apply=%region_11.12 | all-reduce | flops 9984 | bytes 79872 | tf_op jit(solution)/shard_map/psum | solution.py:332
  378.3 13.9 %all-gather.3 = bf16[384,192]{1,0:T(8,128)(2,1)S(1)} all-gather(bf16[96,192]{1,0:T(8,128)(2,1)S(1)} %reduce_sum.281), channel_id=5, replica_groups={{0,8,16,24},{2,10,18,26},{4,12,20,28},{6,14,22,30},{1,9,17,25},{3,11,19..., dimensions={0}, use_global_device_ids=true | all-gather | bytes 184320 | tf_op jit(solution)/shard_map/all_gather | solution.py:38
  392.5 11.4 %all_gather.73 = bf16[4,96,768]{2,1,0:T(8,128)(2,1)S(1)} all-gather(bf16[1,96,768]{2,1,0:T(8,128)(2,1)S(1)} %all_gather_reshape.9), channel_id=1, replica_groups={{0,2,4,6},{8,10,12,14},{16,18,20,22},{24,26,28,30},{1,3,5,7},{9,11,13,1..., dimensions={0}, use_global_device_ids=true | all-gather | bytes 737280 | tf_op jit(solution)/shard_map/all_gather | solution.py:38
  406.0 3.0 copy.90
  409.0 2.8 convert_bitcast_fusion
  411.8 6.8 %copy.91 = f32[4,96,3,4,192]{4,3,2,1,0:T(4,128)} copy(f32[4,96,3,4,192]{1,4,2,3,0:T(8,128)} %convert_bitcast_fusion) | data formatting | bytes 7077888 | tf_op jit(solution)/shard_map/convert_element_type | solution.py:329
  418.6 6.0 %reshape.430 = f32[384,2304]{1,0:T(8,128)} reshape(f32[4,96,3,4,192]{4,3,2,1,0:T(4,128)} %copy.91) | data formatting | bytes 7077888 | tf_op jit(solution)/shard_map/convert_element_type | solution.py:329
  424.5 4.4 %bitcast_convert_fusion.1 = f32[384,3072]{1,0:T(8,128)} fusion(bf16[4,96,3072]{2,1,0:T(8,128)(2,1)} %all-gather.20.cloned.1.call-done), kind=kLoop, calls=%fused_computation.8 | loop fusion | flops 1179648 | bytes 7077888 | tf_op jit(solution)/shard_map/convert_element_type | solution.py:296
  429.0 4.2 bitcast_convert_fusion
  (235 shorter events, 34.3 us)
Async XLA Ops:
  7.2 76.1 %all-gather.14.cloned.1.call-start = ((), (), s32[]{:S(2)}) async-start(), calls=%async_computation.10 | async-start | bytes 1769472 | tf_op jit(solution)/shard_map/all_gather | solution.py:200
  7.9 77.4 %all-gather.16.cloned.1.call-start = ((), (), s32[]{:S(2)}) async-start(), calls=%async_computation.11 | async-start | bytes 7077888 | tf_op jit(solution)/shard_map/all_gather | solution.py:200
  8.7 0.9 copy-start.37
  8.7 0.9 copy-start.38
  8.7 0.9 copy-start.28
  8.8 84.9 %all-gather.18.cloned.1.call-start = ((), (), s32[]{:S(2)}) async-start(), calls=%async_computation.12 | async-start | bytes 7077888 | tf_op jit(solution)/shard_map/all_gather | solution.py:200
  13.5 2.7 copy-start.25
  16.2 21.9 %copy-start.19 = (bf16[768,576]{1,0:T(8,128)(2,1)}, bf16[768,576]{1,0:T(8,128)(2,1)S(1)}, u32[]{:S(2)}) copy-start(bf16[768,576]{1,0:T(8,128)(2,1)S(1)} %all_gather.60) | copy-start | bytes 2654212
  38.2 4.9 %copy-start.39 = (s32[2]{0:T(128)S(1)}, s32[2]{0:T(128)}, u32[]{:S(2)}) copy-start(s32[2]{0:T(128)} %param.18) | copy-start | bytes 28
  39.0 22.5 %copy-start.4 = (bf16[512,192]{1,0:T(8,128)(2,1)}, bf16[512,192]{1,0:T(8,128)(2,1)S(1)}, u32[]{:S(2)}) copy-start(bf16[512,192]{1,0:T(8,128)(2,1)S(1)} %get-tuple-element.67.refs_5_.refs_8_) | copy-start | bytes 589828
  39.0 22.5 %copy-start.5 = (bf16[512,192]{1,0:T(8,128)(2,1)}, bf16[512,192]{1,0:T(8,128)(2,1)S(1)}, u32[]{:S(2)}) copy-start(bf16[512,192]{1,0:T(8,128)(2,1)S(1)} %get-tuple-element.68.refs_1_.refs_4_) | copy-start | bytes 589828
  39.0 9.2 %collective-permute-start = (bf16[512,192]{1,0:T(8,128)(2,1)S(1)}, bf16[512,192]{1,0:T(8,128)(2,1)S(1)}, u32[]{:S(2)}, u32[]{:S(2)}) collective-permute-start(bf16[512,192]{1,0:T(8,128)(2,1)S(1)} %get-tuple-element.68.refs_1_.refs_4_), channel_id=1, source_target_pairs={{0,2},{2,0},{4,6},{6,4},{8,10},{10,8},{12,14},{14,12},{16,18},{18,... | collective-permute-start | bytes 589832 | tf_op jit(solution)/shard_map/ppermute | solution.py:44
  40.5 16.5 %collective-permute-start.1 = (bf16[512,192]{1,0:T(8,128)(2,1)S(1)}, bf16[512,192]{1,0:T(8,128)(2,1)S(1)}, u32[]{:S(2)}, u32[]{:S(2)}) collective-permute-start(bf16[512,192]{1,0:T(8,128)(2,1)S(1)} %get-tuple-element.68.refs_1_.refs_4_), channel_id=1, source_target_pairs={{0,4},{2,6},{4,0},{6,2},{8,12},{10,14},{12,8},{14,10},{16,20},{18,... | collective-permute-start | bytes 589832 | tf_op jit(solution)/shard_map/ppermute | solution.py:44
  42.0 14.9 %collective-permute-start.3 = (bf16[512,192]{1,0:T(8,128)(2,1)S(1)}, bf16[512,192]{1,0:T(8,128)(2,1)S(1)}, u32[]{:S(2)}, u32[]{:S(2)}) collective-permute-start(bf16[512,192]{1,0:T(8,128)(2,1)S(1)} %get-tuple-element.67.refs_5_.refs_8_), channel_id=1, source_target_pairs={{0,2},{2,0},{4,6},{6,4},{8,10},{10,8},{12,14},{14,12},{16,18},{18,... | collective-permute-start | bytes 589832 | tf_op jit(solution)/shard_map/ppermute | solution.py:44
  42.5 12.5 %collective-permute-start.4 = (bf16[512,192]{1,0:T(8,128)(2,1)S(1)}, bf16[512,192]{1,0:T(8,128)(2,1)S(1)}, u32[]{:S(2)}, u32[]{:S(2)}) collective-permute-start(bf16[512,192]{1,0:T(8,128)(2,1)S(1)} %get-tuple-element.67.refs_5_.refs_8_), channel_id=1, source_target_pairs={{0,4},{2,6},{4,0},{6,2},{8,12},{10,14},{12,8},{14,10},{16,20},{18,... | collective-permute-start | bytes 589832 | tf_op jit(solution)/shard_map/ppermute | solution.py:44
  48.2 13.3 %copy-start.13 = (bf16[512,192]{1,0:T(8,128)(2,1)}, bf16[512,192]{1,0:T(8,128)(2,1)S(1)}, u32[]{:S(2)}) copy-start(bf16[512,192]{1,0:T(8,128)(2,1)S(1)} %collective-permute-done.refs_2_.refs_5_) | copy-start | bytes 589828
  48.2 9.7 %collective-permute-start.2 = (bf16[512,192]{1,0:T(8,128)(2,1)S(1)}, bf16[512,192]{1,0:T(8,128)(2,1)S(1)}, u32[]{:S(2)}, u32[]{:S(2)}) collective-permute-start(bf16[512,192]{1,0:T(8,128)(2,1)S(1)} %collective-permute-done.refs_2_.refs_5_), channel_id=1, source_target_pairs={{0,4},{2,6},{4,0},{6,2},{8,12},{10,14},{12,8},{14,10},{16,20},{18,... | collective-permute-start | bytes 589832 | tf_op jit(solution)/shard_map/ppermute | solution.py:44
  55.1 6.4 %copy-start.16 = (bf16[512,192]{1,0:T(8,128)(2,1)}, bf16[512,192]{1,0:T(8,128)(2,1)S(1)}, u32[]{:S(2)}) copy-start(bf16[512,192]{1,0:T(8,128)(2,1)S(1)} %collective-permute-done.4.refs_7_.refs_10_) | copy-start | bytes 589828
  55.1 6.4 %collective-permute-start.5 = (bf16[512,192]{1,0:T(8,128)(2,1)S(1)}, bf16[512,192]{1,0:T(8,128)(2,1)S(1)}, u32[]{:S(2)}, u32[]{:S(2)}) collective-permute-start(bf16[512,192]{1,0:T(8,128)(2,1)S(1)} %collective-permute-done.4.refs_7_.refs_10_), channel_id=1, source_target_pairs={{0,2},{2,0},{4,6},{6,4},{8,10},{10,8},{12,14},{14,12},{16,18},{18,... | collective-permute-start | bytes 589832 | tf_op jit(solution)/shard_map/ppermute | solution.py:44
  56.9 4.6 %copy-start.14 = (bf16[512,192]{1,0:T(8,128)(2,1)}, bf16[512,192]{1,0:T(8,128)(2,1)S(1)}, u32[]{:S(2)}) copy-start(bf16[512,192]{1,0:T(8,128)(2,1)S(1)} %collective-permute-done.1.refs_3_.refs_6_) | copy-start | bytes 589828
  56.9 4.6 %copy-start.15 = (bf16[512,192]{1,0:T(8,128)(2,1)}, bf16[512,192]{1,0:T(8,128)(2,1)S(1)}, u32[]{:S(2)}) copy-start(bf16[512,192]{1,0:T(8,128)(2,1)S(1)} %collective-permute-done.3.refs_6_.refs_9_) | copy-start | bytes 589828
  57.9 3.6 copy-start.17
  73.2 10.0 %all-to-all-start = ((bf16[4,128,192]{1,2,0:T(8,128)(2,1)}), bf16[4,128,192]{1,2,0:T(8,128)(2,1)S(1)}, u32[]{:S(2)}, u32[]{:S(2)}) async-start(bf16[4,128,192]{1,2,0:T(8,128)(2,1)} %copy.85), calls=%async_computation | async-start | bytes 393216 | tf_op jit(solution)/shard_map/all_to_all | solution.py:41
  83.2 10.4 %copy-start.7 = (bf16[4,128,192]{1,2,0:T(8,128)(2,1)}, bf16[4,128,192]{1,2,0:T(8,128)(2,1)S(1)}, u32[]{:S(2)}) copy-start(bf16[4,128,192]{1,2,0:T(8,128)(2,1)S(1)} %all-to-all-done) | copy-start | bytes 589828
  93.7 5.0 %slice-start = ((s8[4718592]{0:T(1024)(128)(4,1)}), s8[4194304]{0:T(1024)(128)(4,1)S(1)}, s32[]{:S(2)}) async-start(s8[4718592]{0:T(1024)(128)(4,1)} %bitcast.108), calls=%async_computation.16 | async-start | bytes 8388608
  93.7 3.7 copy-start.8
  93.7 5.0 %slice-start.1 = ((s8[4718592]{0:T(1024)(128)(4,1)}), s8[524288]{0:T(1024)(128)(4,1)S(1)}, s32[]{:S(2)}) async-start(s8[4718592]{0:T(1024)(128)(4,1)} %bitcast.108), calls=%async_computation.17 | async-start | bytes 1048576
  93.7 5.0 %copy-start.41 = (f32[128,3072]{1,0:T(8,128)S(1)}, f32[128,3072]{1,0:T(8,128)}, u32[]{:S(2)}) copy-start(f32[128,3072]{1,0:T(8,128)} %get-tuple-element.76) | copy-start | bytes 4718596
  97.1 1.6 copy-start.40
  97.6 5.1 %slice-start.2 = ((s8[4718592]{0:T(1024)(128)(4,1)}), s8[4194304]{0:T(1024)(128)(4,1)S(1)}, s32[]{:S(2)}) async-start(s8[4718592]{0:T(1024)(128)(4,1)} %bitcast.110), calls=%async_computation.18 | async-start | bytes 8388608
  98.7 4.0 slice-start.3
  102.7 2.6 copy-start
  105.4 1.6 copy-start.2
  105.4 1.6 copy-start.29
  105.4 2.1 copy-start.1
  107.0 51.0 %collective-permute-start.11 = (bf16[384,3072]{1,0:T(8,128)(2,1)}, bf16[384,3072]{1,0:T(8,128)(2,1)}, u32[]{:S(2)}, u32[]{:S(2)}) collective-permute-start(bf16[384,3072]{1,0:T(8,128)(2,1)} %constant_dynamic-slice_fusion.2), channel_id=1, source_target_pairs={{0,1},{1,0},{2,3},{3,2},{4,5},{5,4},{6,7},{7,6},{8,9},{9,8},{10,11... | collective-permute-start | bytes 7077896 | tf_op jit(solution)/shard_map/ppermute | solution.py:281
  107.1 23.4 %copy-start.10 = (bf16[128,768]{1,0:T(8,128)(2,1)}, bf16[128,768]{1,0:T(8,128)(2,1)S(1)}, u32[]{:S(2)}) copy-start(bf16[128,768]{1,0:T(8,128)(2,1)S(1)} %get-tuple-element.57) | copy-start | bytes 589828
  130.6 20.3 %copy-start.24 = (bf16[4,128,768]{2,1,0:T(8,128)(2,1)S(1)}, bf16[4,128,768]{2,1,0:T(8,128)(2,1)}, u32[]{:S(2)}) copy-start(bf16[4,128,768]{2,1,0:T(8,128)(2,1)} %copy-done.23) | copy-start | bytes 2359300
  130.6 13.2 %collective-permute-start.8 = (bf16[384,512]{1,0:T(8,128)(2,1)}, bf16[384,512]{1,0:T(8,128)(2,1)S(1)}, u32[]{:S(2)}, u32[]{:S(2)}) collective-permute-start(bf16[384,512]{1,0:T(8,128)(2,1)} %get-tuple-element.28), channel_id=1, source_target_pairs={{0,6},{2,4},{4,2},{6,0},{8,14},{10,12},{12,10},{14,8},{16,22},{18,... | collective-permute-start | bytes 1179656 | tf_op jit(solution)/shard_map/ppermute | solution.py:44
  132.1 17.2 %collective-permute-start.7 = (bf16[384,512]{1,0:T(8,128)(2,1)}, bf16[384,512]{1,0:T(8,128)(2,1)S(1)}, u32[]{:S(2)}, u32[]{:S(2)}) collective-permute-start(bf16[384,512]{1,0:T(8,128)(2,1)} %get-tuple-element.27), channel_id=1, source_target_pairs={{0,4},{2,6},{4,0},{6,2},{8,12},{10,14},{12,8},{14,10},{16,20},{18,... | collective-permute-start | bytes 1179656 | tf_op jit(solution)/shard_map/ppermute | solution.py:44
  132.6 16.9 %collective-permute-start.6 = (bf16[384,512]{1,0:T(8,128)(2,1)}, bf16[384,512]{1,0:T(8,128)(2,1)}, u32[]{:S(2)}, u32[]{:S(2)}) collective-permute-start(bf16[384,512]{1,0:T(8,128)(2,1)} %get-tuple-element.26), channel_id=1, source_target_pairs={{0,2},{2,0},{4,6},{6,4},{8,10},{10,8},{12,14},{14,12},{16,18},{18,... | collective-permute-start | bytes 1179656 | tf_op jit(solution)/shard_map/ppermute | solution.py:44
  135.2 16.3 %copy-start.21 = (bf16[512,192]{0,1:T(8,128)(2,1)}, bf16[512,192]{0,1:T(8,128)(2,1)S(1)}, u32[]{:S(2)}) copy-start(bf16[512,192]{0,1:T(8,128)(2,1)S(1)} %copy.88) | copy-start | bytes 589828
  151.6 1.8 collective-permute-start.9
  154.5 11.7 %all-to-all-start.3 = ((bf16[4,96,576]{2,1,0:T(8,128)(2,1)}), bf16[4,96,576]{2,1,0:T(8,128)(2,1)S(1)}, u32[]{:S(2)}, u32[]{:S(2)}) async-start(bf16[4,96,576]{2,1,0:T(8,128)(2,1)} %bitcast.23), calls=%async_computation.3 | async-start | bytes 983040 | tf_op jit(solution)/shard_map/all_to_all | solution.py:41
  167.0 31.0 %all-to-all-start.6 = ((bf16[4,96,3072]{2,1,0:T(8,128)(2,1)}), bf16[4,96,3072]{2,1,0:T(8,128)(2,1)S(1)}, u32[]{:S(2)}, u32[]{:S(2)}) async-start(bf16[4,96,3072]{2,1,0:T(8,128)(2,1)} %bitcast.34), calls=%async_computation.6 | async-start | bytes 4718592 | tf_op jit(solution)/shard_map/all_to_all | solution.py:41
  170.6 235.4 %all-gather.24.cloned.1.call-start = ((), (), s32[]{:S(2)}) async-start(), calls=%async_computation.15 | async-start | bytes 2457600 | tf_op jit(solution)/shard_map/all_gather | solution.py:38
  194.3 42.9 %collective-permute-start.12 = (bf16[1536,768]{1,0:T(8,128)(2,1)}, bf16[1536,768]{1,0:T(8,128)(2,1)}, u32[]{:S(2)}, u32[]{:S(2)}) collective-permute-start(bf16[1536,768]{1,0:T(8,128)(2,1)} %constant_dynamic-slice_fusion.1), channel_id=1, source_target_pairs={{0,1},{1,0},{2,3},{3,2},{4,5},{5,4},{6,7},{7,6},{8,9},{9,8},{10,11... | collective-permute-start | bytes 7077896 | tf_op jit(solution)/shard_map/ppermute | solution.py:281
  199.8 19.3 %all-to-all-start.7 = ((bf16[4,96,768]{2,1,0:T(8,128)(2,1)}), bf16[4,96,768]{2,1,0:T(8,128)(2,1)S(1)}, u32[]{:S(2)}, u32[]{:S(2)}) async-start(bf16[4,96,768]{2,1,0:T(8,128)(2,1)} %copy.95), calls=%async_computation.7 | async-start | bytes 1179648 | tf_op jit(solution)/shard_map/all_to_all | solution.py:41
  204.1 220.5 %all-gather.20.cloned.1.call-start = ((), (), s32[]{:S(2)}) async-start(), calls=%async_computation.13 | async-start | bytes 2949120 | tf_op jit(solution)/shard_map/all_gather | solution.py:38
  241.6 34.1 %all-to-all-start.8 = ((bf16[4,384,768]{2,1,0:T(8,128)(2,1)}), bf16[4,384,768]{2,1,0:T(8,128)(2,1)S(1)}, u32[]{:S(2)}, u32[]{:S(2)}) async-start(bf16[4,384,768]{2,1,0:T(8,128)(2,1)} %bitcast.39), calls=%async_computation.8 | async-start | bytes 4718592 | tf_op jit(solution)/shard_map/all_to_all | solution.py:41
  279.1 18.3 %all-to-all-start.9 = ((bf16[4,384,192]{1,2,0:T(8,128)(2,1)}), bf16[4,384,192]{1,2,0:T(8,128)(2,1)S(1)}, u32[]{:S(2)}, u32[]{:S(2)}) async-start(bf16[4,384,192]{1,2,0:T(8,128)(2,1)} %bitcast.41), calls=%async_computation.9 | async-start | bytes 1179648 | tf_op jit(solution)/shard_map/all_to_all | solution.py:41
  282.6 2.1 collective-permute-start.10
  297.4 21.4 %all-to-all-start.4 = ((bf16[4,96,768]{2,1,0:T(8,128)(2,1)}), bf16[4,96,768]{2,1,0:T(8,128)(2,1)S(1)}, u32[]{:S(2)}, u32[]{:S(2)}) async-start(bf16[4,96,768]{2,1,0:T(8,128)(2,1)} %bitcast.28), calls=%async_computation.4 | async-start | bytes 1179648 | tf_op jit(solution)/shard_map/all_to_all | solution.py:41
  300.9 128.0 %all-gather.22.cloned.1.call-start = ((), (), s32[]{:S(2)}) async-start(), calls=%async_computation.14 | async-start | bytes 2949120 | tf_op jit(solution)/shard_map/all_gather | solution.py:38
  317.8 5.5 %copy-start.12 = (bf16[512,384]{0,1:T(8,128)(2,1)S(1)}, bf16[512,384]{0,1:T(8,128)(2,1)}, u32[]{:S(2)}) copy-start(bf16[512,384]{0,1:T(8,128)(2,1)} %copy-done.11) | copy-start | bytes 1179652
  317.8 5.5 %copy-start.20 = (bf16[768,576]{1,0:T(8,128)(2,1)S(1)}, bf16[768,576]{1,0:T(8,128)(2,1)}, u32[]{:S(2)}) copy-start(bf16[768,576]{1,0:T(8,128)(2,1)} %copy-done.19) | copy-start | bytes 2654212
  317.8 5.5 %copy-start.22 = (bf16[512,192]{0,1:T(8,128)(2,1)S(1)}, bf16[512,192]{0,1:T(8,128)(2,1)}, u32[]{:S(2)}) copy-start(bf16[512,192]{0,1:T(8,128)(2,1)} %copy-done.21) | copy-start | bytes 589828
  319.9 9.6 %all-to-all-start.5 = ((bf16[4,96,192]{2,1,0:T(8,128)(2,1)}), bf16[4,96,192]{2,1,0:T(8,128)(2,1)S(1)}, u32[]{:S(2)}, u32[]{:S(2)}) async-start(bf16[4,96,192]{2,1,0:T(8,128)(2,1)} %copy.92), calls=%async_computation.5 | async-start | bytes 393216 | tf_op jit(solution)/shard_map/all_to_all | solution.py:41
  323.3 9.7 %copy-start.9 = (bf16[1,128,768]{2,1,0:T(8,128)(2,1)S(1)}, bf16[1,128,768]{2,1,0:T(8,128)(2,1)}, u32[]{:S(2)}) copy-start(bf16[1,128,768]{2,1,0:T(8,128)(2,1)} %param.17) | copy-start | bytes 589828
  325.0 8.1 %copy-start.26 = (f32[768]{0:T(1024)S(1)}, f32[768]{0:T(1024)}, u32[]{:S(2)}) copy-start(f32[768]{0:T(1024)} %get-tuple-element.29) | copy-start | bytes 9220
  325.0 8.1 %copy-start.27 = (f32[3072]{0:T(1024)S(1)}, f32[3072]{0:T(1024)}, u32[]{:S(2)}) copy-start(f32[3072]{0:T(1024)} %get-tuple-element.52) | copy-start | bytes 36868
  329.5 75.5 %all-to-all-start.2 = ((bf16[4,128,768]{2,1,0:T(8,128)(2,1)}), bf16[4,128,768]{2,1,0:T(8,128)(2,1)S(1)}, u32[]{:S(2)}, u32[]{:S(2)}) async-start(bf16[4,128,768]{2,1,0:T(8,128)(2,1)} %bitcast.19), calls=%async_computation.2 | async-start | bytes 1572864 | tf_op jit(solution)/shard_map/all_to_all | solution.py:41
  403.9 1.3 copy-start.3
  403.9 1.3 copy-start.30
  (10 other events, 8.3 us)
Sparse Core Ops, SparseCore 0:
  9.6 11.9 all-gather.13
  23.1 15.5 all-gather.15
  40.2 15.5 all-gather.17
  191.2 36.5 all-gather.23
  237.4 51.2 all-gather.19
  319.0 36.9 all-gather.21

commit v2 on v1

v2 whole, which is shorter than its diff:
```python
import functools

import jax
import jax.numpy as jnp
from jax import lax
from jax.experimental import pallas as pl
from jax.experimental.pallas import tpu as pltpu
from jax.sharding import PartitionSpec as P

HEADS = 12
HEAD_DIM = 64
GROUPS = 4
GROUP_HEADS = HEADS // GROUPS
WIDTH = GROUP_HEADS * HEAD_DIM
EPSILON = 1e-12
MASKED = -1e30
F32 = jnp.float32
BF16 = jnp.bfloat16
MIB = 2**20
ROWS = 128
TURNED = ((1,), (1,))
FIRST = ((1,), (0,))


def dot(left, right, dims=FIRST):
    return lax.dot_general(left, right, (dims, ((), ())), preferred_element_type=F32)


def kernel_call(kernel, name, outs, args, vmem, micros, smem=0, anywhere=(), scratch=()):
    spaces = [
        pl.BlockSpec(memory_space=pltpu.SMEM if i < smem else pl.ANY if i in anywhere else pltpu.VMEM)
        for i in range(len(args))
    ]
    return pl.pallas_call(
        kernel,
        out_shape=outs,
        in_specs=spaces,
        scratch_shapes=list(scratch),
        compiler_params=pltpu.CompilerParams(vmem_limit_bytes=vmem * MIB),
        cost_estimate=pl.CostEstimate(flops=0, bytes_accessed=int(micros * 3_500_000), transcendentals=0),
        name=name,
    )(*args)


def shaped(shape, dtype=BF16):
    return jax.ShapeDtypeStruct(shape, dtype)


class Places:
    def __init__(self, size):
        self.size = size
        self.plane_size = size // GROUPS
        self.rest = self.plane_size // 4
        index = lambda g, q, m: (g * 4 + q) * self.rest + m
        groups, quarters, members = range(GROUPS), range(4), range(self.rest)
        self.columns = [[index(g, q, m) for g in groups] for q in quarters for m in members]
        self.planes = [[index(g, q, m) for q in quarters for m in members] for g in groups]
        self.fours = [[index(g, q, m) for q in quarters] for g in groups for m in members]
        self.rests = [[index(g, q, m) for m in members] for g in groups for q in quarters]

    def swap(self, block, bits):
        return lax.ppermute(block, "seq", [(i, i ^ bits) for i in range(self.size)])

    def column_swap(self, block, turn):
        return self.swap(block, turn * self.plane_size)

    def four_swap(self, block, turn):
        return self.swap(block, turn * self.rest)

    def exchange(self, blocks, groups):
        return lax.all_to_all(blocks, "seq", 0, 0, axis_index_groups=groups, tiled=True)


def project_kernel(x0, x1, x2, x3, weight, offset, query_ref, key_value_ref):
    for i, x in enumerate((x0, x1, x2, x3)):
        at = slice(i * ROWS, (i + 1) * ROWS)
        joined = (dot(x[...], weight[...]) + offset[...]).astype(BF16)
        query_ref[at, :] = joined[:, :WIDTH] * jnp.asarray(0.125, BF16)
        key_value_ref[at, :] = joined[:, WIDTH:]


def attend_kernel(pieces, chunks, *refs):
    q_ref = refs[0]
    key_value_refs, bias_refs = refs[1 : 1 + pieces], refs[1 + pieces : 1 + 2 * pieces]
    context_ref, log_ref = refs[1 + 2 * pieces : 3 + 2 * pieces]
    low_refs = refs[3 + 2 * pieces :]
    rows = q_ref.shape[0]
    chunk = key_value_refs[0].shape[0] // chunks
    for block in range(rows // ROWS):
        at = slice(block * ROWS, (block + 1) * ROWS)
        for head in range(GROUP_HEADS):
            columns = slice(head * HEAD_DIM, (head + 1) * HEAD_DIM)
            value_columns = slice(WIDTH + head * HEAD_DIM, WIDTH + (head + 1) * HEAD_DIM)
            query = q_ref[at, columns]

            def step(index, state):
                highest, total, mix = state
                here = pl.ds(pl.multiple_of(index * chunk, chunk), chunk)
                scores = [dot(query, k[here, columns], TURNED) + b[:, here] for k, b in zip(key_value_refs, bias_refs)]
                peak = functools.reduce(jnp.maximum, [jnp.max(s, axis=1, keepdims=True) for s in scores])
                raised = jnp.maximum(highest, peak)
                weights = [jnp.exp(s - raised) for s in scores]
                factor = jnp.exp(highest - raised)
                total = total * factor + sum(jnp.sum(w, axis=1, keepdims=True) for w in weights)
                mix = mix * factor + sum(
                    dot(w.astype(BF16), v[here, value_columns]) for w, v in zip(weights, key_value_refs)
                )
                return raised, total, mix

            state = (
                jnp.full((ROWS, 1), MASKED, F32),
                jnp.zeros((ROWS, 1), F32),
                jnp.zeros((ROWS, HEAD_DIM), F32),
            )
            highest, total, mix = step(0, state) if chunks == 1 else lax.fori_loop(0, chunks, step, state)
            context = mix / total
            context_ref[at, columns] = context
            low_refs[block][:, columns] = context.astype(BF16)
            log_ref[at, head : head + 1] = highest + jnp.log(total)


def attend(query, key_values, bias, chunks):
    rows = query.shape[0]
    outs = (shaped((rows, WIDTH), F32), shaped((rows, 128), F32)) + (shaped((ROWS, WIDTH)),) * GROUPS
    kernel = functools.partial(attend_kernel, len(key_values), chunks)
    found = kernel_call(kernel, "attend", outs, (query, *key_values, *bias), 24 if chunks == 1 else 60, 9)
    return found[0], found[1], found[2:]


def attend_grad_kernel(pieces, chunks, *refs):
    q_ref, context_ref, log_ref = refs[:3]
    grad_refs = refs[3:7]
    key_value_refs, bias_refs = refs[7 : 7 + pieces], refs[7 + pieces : 7 + 2 * pieces]
    query_grad_ref = refs[7 + 2 * pieces]
    out_refs = refs[8 + 2 * pieces :]
    rows = q_ref.shape[0]
    chunk = key_value_refs[0].shape[0] // chunks
    for head in range(GROUP_HEADS):
        columns = slice(head * HEAD_DIM, (head + 1) * HEAD_DIM)
        value_columns = slice(WIDTH + head * HEAD_DIM, WIDTH + (head + 1) * HEAD_DIM)
        query = q_ref[:, columns]
        grad = jnp.concatenate([g[:, columns] for g in grad_refs], axis=0)
        correction = jnp.sum(grad.astype(F32) * context_ref[:, columns], axis=1, keepdims=True)
        log_total = log_ref[:, head : head + 1]
        query_turned = query.T
        grad_turned = grad.T

        def step(index, query_grad):
            here = pl.ds(pl.multiple_of(index * chunk, chunk), chunk)
            for both, b, out in zip(key_value_refs, bias_refs, out_refs):
                key = both[here, columns]
                probs = jnp.exp(dot(query, key, TURNED) + b[:, here] - log_total)
                probs_grad = dot(grad, both[here, value_columns], TURNED)
                score_grad = (probs * (probs_grad - correction)).astype(BF16)
                query_grad = query_grad + dot(score_grad, key)
                out[columns, here] = dot(query_turned, score_grad).astype(BF16)
                out[value_columns, here] = dot(grad_turned, probs.astype(BF16)).astype(BF16)
            return query_grad

        total = jnp.zeros((rows, HEAD_DIM), F32)
        total = step(0, total) if chunks == 1 else lax.fori_loop(0, chunks, step, total)
        query_grad_ref[:, columns] = (total * 0.125).astype(BF16)


def attend_grad(query, context, grads, log_total, key_values, bias, chunks):
    rows = query.shape[0]
    outs = (shaped((rows, WIDTH)),) + tuple(shaped((2 * WIDTH, k.shape[0])) for k in key_values)
    kernel = functools.partial(attend_grad_kernel, len(key_values), chunks)
    args = (query, context, log_total, *grads, *key_values, *bias)
    found = kernel_call(kernel, "attend_grad", outs, args, 32 if chunks == 1 else 60, 11)
    return found[0], found[1:]


def normalize(hidden):
    center = hidden - jnp.mean(hidden, axis=1, keepdims=True)
    scale = lax.rsqrt(jnp.mean(center * center, axis=1, keepdims=True) + EPSILON)
    return center * scale, scale


def normalize_grad(grad, normal, scale):
    return scale * (
        grad
        - jnp.mean(grad, axis=1, keepdims=True)
        - normal * jnp.mean(grad * normal, axis=1, keepdims=True)
    )


def column_sum(values):
    return jnp.sum(values, axis=0, keepdims=True)


def dense_kernel(width, spot, c0, c1, c2, c3, x_ref, grad_ref, vectors, up_offset, out_hbm, up_hbm, down_hbm, *rest):
    (layer_ref, one_grad_ref, normed_ref, active_ref, second_ref, inner_ref, branch_ref, sums_ref) = rest[:8]
    context_grads = rest[8:12]
    out_w, up_w, down_w, slope, sems = rest[12:]
    copies = [
        pltpu.make_async_copy(source, target, sems.at[i])
        for i, (source, target) in enumerate(((out_hbm, out_w), (up_hbm, up_w), (down_hbm, down_w)))
    ]
    for copy in copies:
        copy.start()
    hidden = up_w.shape[1]
    half = width // 2
    out_offset, gain_one, shift_one, down_offset, gain_two, shift_two = (vectors[i : i + 1, :] for i in range(2, 8))
    group = spot[0]

    def turned(i):
        return pl.ds(pl.multiple_of((group ^ i) * WIDTH, WIDTH), WIDTH)

    copies[0].wait()
    branch = sum(dot(c[...], out_w[turned(i), :]) for i, c in enumerate((c0, c1, c2, c3))) + out_offset
    normal_one, scale_one = normalize(x_ref[...].astype(F32) + branch)
    normed_low = (normal_one * gain_one + shift_one).astype(BF16)
    normed_ref[...] = normed_low
    copies[1].wait()
    copies[2].wait()
    step = 768
    second = jnp.zeros((ROWS, width), F32) + down_offset
    for start in range(0, hidden, step):
        at = slice(start, start + step)
        inner = dot(normed_low, up_w[:, at]) + up_offset[:, at]
        share = 0.5 + 0.5 * lax.erf(inner * 0.7071067811865476)
        density = 0.3989422804014327 * jnp.exp(-0.5 * inner * inner)
        slope[:, at] = share + inner * density
        active = (inner * share).astype(BF16)
        active_ref[:, at] = active
        second = second + dot(active, down_w[at, :])
    normal_two, scale_two = normalize(normed_low.astype(F32) + second)
    layer_ref[...] = (normal_two * gain_two + shift_two).astype(BF16)
    grad = grad_ref[...].astype(F32)
    gain_two_grad, shift_two_grad = column_sum(grad * normal_two), column_sum(grad)
    two_grad = normalize_grad(grad * gain_two, normal_two, scale_two)
    second_low = two_grad.astype(BF16)
    second_ref[...] = second_low
    down_bias_grad = column_sum(second_low.astype(F32))
    normed_grad = two_grad
    for start in range(0, hidden, step):
        at = slice(start, start + step)
        inner_low = (dot(second_low, down_w[at, :], TURNED) * slope[:, at]).astype(BF16)
        inner_ref[:, at] = inner_low
        up_sum = column_sum(inner_low.astype(F32))
        for piece in range(step // half):
            place = start // half + piece
            per_core = hidden // 2 // half
            sums_ref[place // per_core, 6 + place % per_core : 7 + place % per_core, :] = up_sum[
                :, piece * half : (piece + 1) * half
            ]
        normed_grad = normed_grad + dot(inner_low, up_w[:, at], TURNED)
    gain_one_grad, shift_one_grad = column_sum(normed_grad * normal_one), column_sum(normed_grad)
    one_grad = normalize_grad(normed_grad * gain_one, normal_one, scale_one)
    one_grad_ref[...] = one_grad
    branch_low = one_grad.astype(BF16)
    branch_ref[...] = branch_low
    for i, ref in enumerate(context_grads):
        ref[...] = dot(branch_low, out_w[turned(i), :], TURNED).astype(BF16)
    out_bias_grad = column_sum(branch_low.astype(F32))
    sums = (out_bias_grad, gain_one_grad, shift_one_grad, down_bias_grad, gain_two_grad, shift_two_grad)
    for core in range(2):
        for i, total in enumerate(sums):
            sums_ref[core, i : i + 1, :] = total[:, core * half : (core + 1) * half]
        sums_ref[core, 10:16, :] = jnp.zeros((6, half), F32)


def dense(spot, contexts, inputs, grad, vectors, up_offset, out_matrix, up_matrix, down_matrix):
    width, hidden = up_matrix.shape
    outs = (
        shaped((ROWS, width)),
        shaped((ROWS, width), F32),
        shaped((ROWS, width)),
        shaped((ROWS, hidden)),
        shaped((ROWS, width)),
        shaped((ROWS, hidden)),
        shaped((ROWS, width)),
        shaped((2, 16, width // 2), F32),
    ) + (shaped((ROWS, WIDTH)),) * GROUPS
    scratch = (
        pltpu.VMEM(out_matrix.shape, BF16),
        pltpu.VMEM(up_matrix.shape, BF16),
        pltpu.VMEM(down_matrix.shape, BF16),
        pltpu.VMEM((ROWS, hidden), F32),
        pltpu.SemaphoreType.DMA((3,)),
    )
    args = (spot, *contexts, inputs, grad, vectors, up_offset, out_matrix, up_matrix, down_matrix)
    return kernel_call(
        functools.partial(dense_kernel, width), "dense", outs, args, 40, 18, 1, (9, 10, 11), scratch
    )


def up_grad_kernel(own, spot, normed, inner, *rest):
    received, out_ref, normed_turned = rest if own else (None, *rest)
    normed_turned[...] = normed[...].T
    rows = out_ref.shape[0]
    core = spot[2] if own else 1 - spot[2]
    left = normed_turned[pl.ds(pl.multiple_of(core * rows, rows), rows), :]
    for start in range(0, out_ref.shape[1], 768):
        at = slice(start, start + 768)
        value = dot(left, inner[:, at])
        if own:
            value = value + received[:, at].astype(F32)
        out_ref[:, at] = value.astype(BF16)


def up_grad_part(spot, normed, inner, received=None):
    width, hidden = normed.shape[1], inner.shape[1]
    args = (spot, normed, inner) + (() if received is None else (received,))
    return kernel_call(
        functools.partial(up_grad_kernel, received is not None),
        "up_grad",
        shaped((width // 2, hidden)),
        args,
        16,
        4,
        1,
        (),
        (pltpu.VMEM((width, ROWS), BF16),),
    )


TALL, SHORT, EXTRA = 96, 24, 8


def down_grad_kernel(own, spot, active, second, c0, c1, c2, c3, branch, sums, *rest):
    received, out_ref, active_turned, context_turned = rest if own else (None, *rest)
    active_turned[...] = active[...].T
    group = spot[0]
    for i, c in enumerate((c0, c1, c2, c3)):
        context_turned[pl.ds(pl.multiple_of((group ^ i) * WIDTH, WIDTH), WIDTH), :] = c[...].T
    core = spot[2] if own else 1 - spot[2]
    tall, short = active_turned.shape[0] // 2, context_turned.shape[0] // 2
    context_half = context_turned[pl.ds(pl.multiple_of(core * short, short), short), :]
    totals = sums[core]
    extra = jnp.concatenate([totals[:EXTRA], totals[EXTRA:]], axis=1)
    for quarter in range(4):
        left = active_turned[pl.ds(pl.multiple_of(core * tall + quarter * (tall // 4), 16), tall // 4), :]
        down = dot(left, second[...])
        out = dot(context_half[quarter * (short // 4) : (quarter + 1) * (short // 4), :], branch[...])
        for g in range(GROUPS):
            value = jnp.concatenate(
                [down[g * TALL : (g + 1) * TALL], out[g * SHORT : (g + 1) * SHORT], extra], axis=0
            )
            if own:
                value = value + received[quarter, g].astype(F32)
            out_ref[quarter, g] = value.astype(BF16)


def down_grad_part(spot, active, second, contexts, branch, sums, received=None):
    width, hidden = second.shape[1], active.shape[1]
    args = (spot, active, second, *contexts, branch, sums) + (() if received is None else (received,))
    return kernel_call(
        functools.partial(down_grad_kernel, received is not None),
        "down_grad",
        shaped((4, GROUPS, TALL + SHORT + EXTRA, width)),
        args,
        24,
        5,
        1,
        (),
        (pltpu.VMEM((hidden, ROWS), BF16), pltpu.VMEM((width, ROWS), BF16)),
    )


BIAS_ROWS = 16


def joined_grad_kernel(pieces, spot, query_grad, *rest):
    key_values = rest[:pieces]
    inputs = rest[pieces : pieces + 4]
    weight = rest[pieces + 4]
    other_ref, own_ref = rest[pieces + 5 : pieces + 7]
    input_grads = rest[pieces + 7 : pieces + 11]
    joined, turned = rest[pieces + 11 :]
    total = sum(k[...].astype(F32) for k in key_values)
    joined[:, :WIDTH] = query_grad[...]
    joined[:, WIDTH:] = total.T.astype(BF16)
    for i, ref in enumerate(input_grads):
        ref[...] = dot(joined[i * ROWS : (i + 1) * ROWS, :], weight[...], TURNED).astype(BF16)
    for i, x in enumerate(inputs):
        turned[:, i * ROWS : (i + 1) * ROWS] = x[...].T
    sums = jnp.concatenate(
        [column_sum(joined[...].astype(F32)), jnp.zeros((BIAS_ROWS - 1, 3 * WIDTH), F32)], axis=0
    ).astype(BF16)
    half = turned.shape[0] // 2
    for ref, core in ((other_ref, 1 - spot[2]), (own_ref, spot[2])):
        value = dot(turned[pl.ds(pl.multiple_of(core * half, half), half), :], joined[...]).astype(BF16)
        for quarter in range(4):
            ref[quarter, : half // 4, :] = value[quarter * (half // 4) : (quarter + 1) * (half // 4)]
            ref[quarter, half // 4 :, :] = sums


def joined_grads(spot, query_grad, key_values, inputs, weight):
    width = weight.shape[0]
    part = shaped((4, width // 8 + BIAS_ROWS, 3 * WIDTH))
    outs = (part, part) + (shaped((ROWS, width)),) * GROUPS
    scratch = (pltpu.VMEM((GROUPS * ROWS, 3 * WIDTH), BF16), pltpu.VMEM((width, GROUPS * ROWS), BF16))
    args = (spot, query_grad, *key_values, *inputs, weight)
    kernel = functools.partial(joined_grad_kernel, len(key_values))
    found = kernel_call(kernel, "joined_grad", outs, args, 24, 6, 1, (), scratch)
    return found[0], found[1], found[2:]


def place_down_kernel(spot, p0, p1, p2, p3, down_ref, out_ref):
    group, quarter = spot[0], spot[1]
    for i, piece in enumerate((p0, p1, p2, p3)):
        for g in range(GROUPS):
            block = piece[group ^ g]
            tall = (quarter ^ i) * (GROUPS * TALL) + g * TALL
            down_ref[pl.ds(pl.multiple_of(tall, 8), TALL), :] = block[:TALL].astype(F32)
            short = (quarter ^ i) * (GROUPS * SHORT) + g * SHORT
            out_ref[pl.ds(pl.multiple_of(short, 8), SHORT), :] = block[TALL : TALL + SHORT].astype(F32)


def place_joined_kernel(spot, p0, p1, p2, p3, weight_ref, bias_ref):
    group, quarter, core = spot[0], spot[1], spot[2]
    width = weight_ref.shape[1] // 3
    rows = p0.shape[1] - BIAS_ROWS
    for i, piece in enumerate((p0, p1, p2, p3)):
        blocks = [piece[group ^ g].astype(F32) for g in range(GROUPS)]
        for part in range(3):
            value = jnp.concatenate([b[:, part * WIDTH : (part + 1) * WIDTH] for b in blocks], axis=1)
            at = pl.ds(pl.multiple_of((quarter ^ i) * rows, 16), rows)
            weight_ref[at, part * width : (part + 1) * width] = value[:rows]
            if i == 0:
                line = value[rows : rows + 1]
                bias_ref[part : part + 1, :] = jnp.where(core == 0, line[:, : width // 2], line[:, width // 2 :])


def body(
    tokens,
    cotangent,
    lengths,
    qkv_weight,
    query_bias,
    value_bias,
    out_weight,
    out_bias,
    first_gain,
    first_shift,
    up_weight,
    up_bias,
    down_weight,
    down_bias,
    second_gain,
    second_shift,
):
    row_count, model_width = tokens.shape[1], tokens.shape[2]
    hidden_width = up_weight.shape[1]
    places = Places(lax.axis_size("seq"))
    plane_size, rest = places.plane_size, places.rest
    rank = lax.axis_index("seq")
    core = lax.axis_index("shard")
    group, position = rank // plane_size, rank % plane_size
    quarter = position // rest
    spot = jnp.stack([group, quarter, core]).astype(jnp.int32)
    length = lengths[core]
    inputs = tokens[0]
    column_rows = GROUPS * row_count
    half = model_width // 2
    turns = range(1, GROUPS)

    column_inputs = (inputs, *(places.column_swap(inputs, i) for i in turns))

    def both(block):
        return lax.all_gather(block, "shard", axis=0, tiled=True)

    def own_columns(w):
        at = group * WIDTH
        parts = [lax.dynamic_slice_in_dim(w, at + i * model_width, WIDTH, w.ndim - 1) for i in range(3)]
        return jnp.concatenate(parts, axis=-1)

    group_weight = both(own_columns(qkv_weight))
    vectors = [query_bias, value_bias, out_bias, first_gain, first_shift, down_bias, second_gain, second_shift]
    stacked = jnp.concatenate([jnp.stack(vectors), up_bias.reshape(-1, half)])
    stacked = lax.all_gather(stacked, "shard", axis=0).astype(F32)
    whole = jnp.transpose(stacked[:, : len(vectors)], (1, 0, 2)).reshape(len(vectors), model_width)
    up_offset = stacked[:, len(vectors) :].reshape(1, hidden_width)
    out_matrix = both(out_weight)
    up_matrix = both(up_weight)
    down_matrix = both(down_weight)

    offset = own_columns(jnp.concatenate([whole[0], jnp.zeros_like(whole[0]), whole[1]])).reshape(1, -1)
    query, key_value = kernel_call(
        project_kernel,
        "project",
        (shaped((column_rows, WIDTH)), shaped((column_rows, 2 * WIDTH))),
        (*column_inputs, group_weight, offset),
        16,
        2,
    )

    def masks(who):
        groups = group ^ jnp.arange(GROUPS)
        starts = (groups[None, :] * plane_size + who[:, None]) * row_count
        tokens_at = starts[:, :, None] + jnp.arange(row_count)
        return jnp.where(tokens_at.reshape(1, -1) < length, 0.0, MASKED).astype(F32)

    if plane_size == 4:
        chunks = 1
        key_values = (key_value, *(places.swap(key_value, i) for i in turns))
        bias = tuple(masks((position ^ i)[None]) for i in range(4))
    else:
        chunks = plane_size // 4
        gathered = lax.all_gather(key_value, "seq", axis=0, axis_index_groups=places.planes)
        key_values = (gathered.reshape(-1, 2 * WIDTH),)
        bias = (masks(jnp.arange(plane_size)),)
    context, log_total, context_lows = attend(query, key_values, bias, chunks)
    contexts = (context_lows[0], *(places.column_swap(context_lows[i], i) for i in turns))

    found = dense(spot, contexts, inputs, cotangent[0], whole, up_offset, out_matrix, up_matrix, down_matrix)
    layer_out, one_grad, normed_low, active, second_low, inner_low, branch_low, sums = found[:8]
    context_grads = found[8:]
    context_grads = (context_grads[0], *(places.column_swap(context_grads[i], i) for i in turns))

    def to_other(block):
        return lax.ppermute(block, "shard", [(0, 1), (1, 0)])

    up_part = up_grad_part(spot, normed_low, inner_low, to_other(up_grad_part(spot, normed_low, inner_low)))
    up_grad = lax.psum(up_part, "seq").astype(F32)

    down_args = (spot, active, second_low, contexts, branch_low, sums)
    down_part = down_grad_part(*down_args, to_other(down_grad_part(*down_args)))

    def four_sum(blocks):
        total = jnp.sum(places.exchange(blocks, places.fours).astype(F32), axis=0)
        if rest > 1:
            total = lax.psum(total, "seq", axis_index_groups=places.rests)
        return total.astype(BF16)

    def gather_all(part):
        column = jnp.stack([part, *(places.column_swap(part, i) for i in turns)])
        return (column, *(places.four_swap(column, i) for i in turns))

    down_sum = four_sum(down_part)
    down_sum = jnp.sum(places.exchange(down_sum, places.columns).astype(F32), axis=0)
    down_pieces = gather_all(down_sum.astype(BF16))
    down_grad, out_grad = kernel_call(
        place_down_kernel,
        "place_down",
        (shaped((hidden_width // 2, model_width), F32), shaped((half, model_width), F32)),
        (spot, *down_pieces),
        24,
        5,
        1,
    )
    extra = down_sum[TALL + SHORT :]
    up_bias_grad = jnp.concatenate([extra[6, :half], extra[7, :half], extra[0, half:], extra[1, half:]])

    query_grad, parts = attend_grad(query, context, context_grads, log_total, key_values, bias, chunks)
    if plane_size == 4:
        key_value_grads = (parts[0], *(places.swap(parts[i], i) for i in turns))
    else:
        blocks = parts[0].reshape(2 * WIDTH, plane_size, column_rows)
        blocks = places.exchange(jnp.transpose(blocks, (1, 0, 2)), places.planes)
        key_value_grads = (jnp.sum(blocks.astype(F32), axis=0),)
    other, own, input_parts = joined_grads(spot, query_grad, key_value_grads, column_inputs, group_weight)
    input_parts = (input_parts[0], *(places.column_swap(input_parts[i], i) for i in turns))
    input_grad = one_grad + sum(p.astype(F32) for p in input_parts)
    joined_part = (own.astype(F32) + to_other(other).astype(F32)).astype(BF16)
    joined_pieces = gather_all(four_sum(joined_part))
    qkv_grad, bias_grad = kernel_call(
        place_joined_kernel,
        "place_joined",
        (shaped((half, 3 * model_width), F32), shaped((8, half), F32)),
        (spot, *joined_pieces),
        24,
        5,
        1,
    )

    shape = (1, row_count, model_width)
    return (
        layer_out.reshape(shape),
        input_grad.reshape(shape),
        qkv_grad,
        bias_grad[0],
        bias_grad[2],
        out_grad,
        extra[0, :half],
        extra[1, :half],
        extra[2, :half],
        up_grad,
        up_bias_grad,
        down_grad,
        extra[3, :half],
        extra[4, :half],
        extra[5, :half],
    )


def solution(mesh):
    rows, halves, whole = P("shard", "seq", None), P("shard", None), P("shard")
    in_specs = (rows, rows, P(), halves, whole, whole, halves, whole, whole, whole, halves, whole, halves, whole, whole, whole)
    out_specs = (rows, rows, halves, whole, whole, halves, whole, whole, whole, halves, whole, halves, whole, whole, whole)
    return jax.shard_map(body, mesh=mesh, in_specs=in_specs, out_specs=out_specs, check_vma=False)
```

time: 449 us -> 381 us (0.85); the launches traced: 441 us -> 380 us
  blocking collectives: 152 us -> 4.32 us
  waiting for transfers between devices: 107 us -> 224 us
  matrix products: 28.6 us -> 0 us
  Pallas kernels: 19.7 us -> 47.8 us
  other arithmetic: 34.3 us -> 12.8 us
  local copies, waits for them, and re-layouts: 40.8 us -> 25.7 us
  starting transfers between devices: 42.7 us -> 50.8 us
    all_gather x6 -> x0, blocking collectives: 94.8 us -> none  [gather(): return lax.all_gather(block, 'seq', axis=0, axis_index_groups=groups)]
    ppermute x9 -> x30, waiting for transfers between devices: 27.4 us -> 121 us  [swap(): return lax.ppermute(block, 'seq', [(i, i ^ bits) for i in range(self.size)])]
    psum x0 -> x1, waiting for transfers between devices: none -> 64.5 us  [body(): up_grad = lax.psum(up_part, 'seq').astype(F32)]
    all_to_all x9 -> x3, waiting for transfers between devices: 73.5 us -> 28.9 us  [exchange(): lax.all_to_all(blocks, 'seq', 0, 0, axis_index_groups=groups, tiled=True)]
    psum x1 -> x0, blocking collectives: 41.6 us -> none  [body(): spread = lax.psum(spread, ('seq', 'shard')).reshape(GROUPS, 3, GROUP_WIDTH)]
    dot_general x12 -> x0, matrix products: 28.6 us -> none  [dot(): lax.dot_general(left, right, (dims, ((), ())), preferred_element_type=F32)]
    ppermute x9 -> x30, starting transfers between devices: 9.66 us -> 38.1 us  [swap(): return lax.ppermute(block, 'seq', [(i, i ^ bits) for i in range(self.size)])]
    pallas_call x2 -> x11, Pallas kernels: 19.7 us -> 47.8 us  [kernel_call(): pl.pallas_call(kernel, out_shape=outs, in_specs=spaces, scratch_shapes=li...]
  transfers between devices with their start and end apart: 28 -> 40, of which waited for: 16 -> 18; matrix products, arithmetic and copies ran while one was open for 19% -> 6% of each run, Pallas kernels for 4% -> 8%
where the time goes in v2:
time: 381 us; the launch traced here: 380 us
  waiting for transfers between devices  224 us (59%)
  starting transfers between devices  50.8 us (13%)
  Pallas kernels  47.8 us (13%)
  local copies, waits for them, and re-layouts  25.7 us (7%)
  between operations  14.5 us (4%)
  other arithmetic  12.8 us (3%)
  blocking collectives  4.32 us (1%)
    ppermute x30, waiting for transfers between devices, swap(): return lax.ppermute(block, 'seq', [(i, i ^ bits) for i in range(self.size)])  121 us
    psum x1, waiting for transfers between devices, body(): up_grad = lax.psum(up_part, 'seq').astype(F32)  64.5 us
    pallas_call x11, Pallas kernels, kernel_call(): pl.pallas_call(kernel, out_shape=outs, in_specs=spaces, scratch_shapes=li...  47.8 us
    ppermute x30, starting transfers between devices, swap(): return lax.ppermute(block, 'seq', [(i, i ^ bits) for i in range(self.size)])  38.1 us
    all_to_all x3, waiting for transfers between devices, exchange(): lax.all_to_all(blocks, 'seq', 0, 0, axis_index_groups=groups, tiled=True)  28.9 us
    unnamed x118, local copies, waits for them, and re-layouts  17.5 us
    all_to_all x3, starting transfers between devices, exchange(): lax.all_to_all(blocks, 'seq', 0, 0, axis_index_groups=groups, tiled=True)  12 us
    ppermute x3, waiting for transfers between devices, to_other(): return lax.ppermute(block, 'shard', [(0, 1), (1, 0)])  7.63 us
  transfers between devices with their start and end apart: 40, of which 18 were waited for; matrix products, arithmetic and copies ran while one was open for 6% of the time, Pallas kernels for 8%

profile of v2, /device:TPU:0, one launch (start us, length us, event | category | flops | bytes accessed | tf_op | source)
XLA Modules:
  0.0 379.5 jit_solution(15007157355278052114)
XLA Ops:
  9.5 5.1 %collective-permute-start.2 = (bf16[128,768]{1,0:T(8,128)(2,1)S(1)}, bf16[128,768]{1,0:T(8,128)(2,1)S(1)}, u32[]{:S(2)}, u32[]{:S(2)}) collective-permute-start(bf16[128,768]{1,0:T(8,128)(2,1)S(1)} %bitcast.28), channel_id=1, source_target_pairs={{0,24},{2,26},{4,28},{6,30},{8,16},{10,18},{12,20},{14,22},{16,8},... | collective-permute-start | bytes 589832 | tf_op jit(solution)/shard_map/ppermute | solution.py:62
  15.5 1.8 all-gather.1
  18.0 1.5 constant_dynamic-slice_fusion.2
  19.7 2.5 all_gather.18.weight.rest_8_
  22.2 9.2 %collective-permute-done.1.x2.rest_6_ = bf16[128,768]{1,0:T(8,128)(2,1)S(1)} collective-permute-done((bf16[128,768]{1,0:T(8,128)(2,1)S(1)}, bf16[128,768]{1,0:T(8,128)(2,1)S(1)}, u32[]{:S(2)}, u32[]{:S(2)}) %collective-permute-start.1) | collective-permute-done | bytes 196640 | tf_op jit(solution)/shard_map/ppermute | solution.py:62
  31.3 0.9 project.1
  32.2 2.5 collective-permute-start.5
  37.4 7.9 %collective-permute-done.5.refs_4_.refs_10_ = bf16[512,384]{1,0:T(8,128)(2,1)S(1)} collective-permute-done((bf16[512,384]{1,0:T(8,128)(2,1)S(1)}, bf16[512,384]{1,0:T(8,128)(2,1)S(1)}, u32[]{:S(2)}, u32[]{:S(2)}) %collective-permute-start.5) | collective-permute-done | bytes 393248 | tf_op jit(solution)/shard_map/ppermute | solution.py:62
  45.3 6.5 %collective-permute-done.4.refs_3_.refs_9_ = bf16[512,384]{1,0:T(8,128)(2,1)S(1)} collective-permute-done((bf16[512,384]{1,0:T(8,128)(2,1)S(1)}, bf16[512,384]{1,0:T(8,128)(2,1)S(1)}, u32[]{:S(2)}, u32[]{:S(2)}) %collective-permute-start.4) | collective-permute-done | bytes 393248 | tf_op jit(solution)/shard_map/ppermute | solution.py:62
  51.9 9.0 %attend.1 = (f32[512,192]{1,0:T(8,128)S(1)}, f32[512,128]{1,0:T(8,128)S(1)}, bf16[128,192]{1,0:T(8,128)(2,1)S(1)}, bf16[128,192]{1,0:T(8,128)(2,1)}, bf16[128,192]{1,0:T(8,128)(2,1)}, /*index=5*/bf16[128,192]{1,0:T(8,128)(2,1)}) custom-call(bf16[512,192]{1,0:T(8,128)(2,1)S(1)} %get-tuple-element.50.refs_0_, ...), custom_call_target="tpu_custom_call" | custom-call | bytes 31500000 | tf_op jit(solution)/shard_map/attend/pallas_call | solution.py:34
  63.0 2.9 collective-permute-start.7
  65.8 1.5 collective-permute-start.8
  67.4 1.3 slice.80
  68.7 1.3 slice.77
  72.3 2.3 copy-done
  74.7 2.3 copy-done.1
  77.0 1.3 copy-done.3
  78.3 0.8 copy-done.16
  79.1 0.8 copy-done.18
  80.0 0.8 copy-done.20
  80.8 0.9 copy-done.28
  82.5 8.7 %dense.1 = (bf16[128,768]{1,0:T(8,128)(2,1)}, f32[128,768]{1,0:T(8,128)S(1)}, bf16[128,768]{1,0:T(8,128)(2,1)S(1)}, bf16[128,3072]{1,0:T(8,128)(2,1)S(1)}, bf16[...) custom-call(s32[3]{0:T(128)S(1)} %pad_add_fusion.spot, ...), custom_call_target="tpu_custom_call" | custom-call | bytes 63000000 | tf_op jit(solution)/shard_map/dense/pallas_call | solution.py:34
  93.0 2.1 down_grad.2
  95.2 5.6 %collective-permute-done.25.rest_0_ = bf16[4,4,128,768]{3,2,1,0:T(8,128)(2,1)S(1)} collective-permute-done((bf16[4,4,128,768]{3,2,1,0:T(8,128)(2,1)S(1)}, bf16[4,4,128,768]{3,2,1,0:T(8,128)(2,1)S(1)}, u32[]{:S(2)}, u32[]{:S(2)}) %collective-permute-start.25) | collective-permute-done | bytes 3145760 | tf_op jit(solution)/shard_map/ppermute | solution.py:514
  100.8 3.7 down_grad.3
  104.6 5.0 %all-to-all-start.1 = ((bf16[4,4,128,768]{3,2,1,0:T(8,128)(2,1)}), bf16[4,4,128,768]{3,2,1,0:T(8,128)(2,1)}, u32[]{:S(2)}, u32[]{:S(2)}) async-start(bf16[4,4,128,768]{3,2,1,0:T(8,128)(2,1)} %down_grad.3), calls=%async_computation.1 | async-start | bytes 6291456 | tf_op jit(solution)/shard_map/all_to_all | solution.py:71
  109.6 1.0 copy-done.7
  110.7 2.8 up_grad.2
  113.6 0.9 collective-permute-start.9
  114.5 1.8 collective-permute-start.10
  116.3 1.7 collective-permute-start.11
  118.0 5.0 %collective-permute-done.10.refs_5_ = bf16[128,192]{1,0:T(8,128)(2,1)S(1)} collective-permute-done((bf16[128,192]{1,0:T(8,128)(2,1)S(1)}, bf16[128,192]{1,0:T(8,128)(2,1)S(1)}, u32[]{:S(2)}, u32[]{:S(2)}) %collective-permute-start.10) | collective-permute-done | bytes 49184 | tf_op jit(solution)/shard_map/ppermute | solution.py:62
  123.1 7.9 %attend_grad.1 = (bf16[512,192]{1,0:T(8,128)(2,1)S(1)}, bf16[384,512]{1,0:T(8,128)(2,1)S(1)}, bf16[384,512]{1,0:T(8,128)(2,1)S(1)}, bf16[384,512]{1,0:T(8,128)(2,1)S(1)}, bf16[384,512]{1,0:T(8,128)(2,1)S(1)}) custom-call(bf16[512,192]{1,0:T(8,128)(2,1)S(1)} %copy-done.5, f32[512,192]{1,0:T(8,128)S(1)} %copy-done.22, f32[512,128]{1,0:T(8,128)S(1)} %copy-done.26, ...), custom_call_target="tpu_custom_call" | custom-call | bytes 38500000 | tf_op jit(solution)/shard_map/attend_grad/pallas_call | solution.py:34
  130.9 1.7 collective-permute-start.12
  132.7 1.5 collective-permute-start.13
  134.5 20.8 %collective-permute-done.12.rest_1_ = bf16[384,512]{1,0:T(8,128)(2,1)S(1)} collective-permute-done((bf16[384,512]{1,0:T(8,128)(2,1)S(1)}, bf16[384,512]{1,0:T(8,128)(2,1)S(1)}, u32[]{:S(2)}, u32[]{:S(2)}) %collective-permute-start.12) | collective-permute-done | bytes 393248 | tf_op jit(solution)/shard_map/ppermute | solution.py:62
  155.3 8.5 %collective-permute-done.14.rest_3_ = bf16[384,512]{1,0:T(8,128)(2,1)S(1)} collective-permute-done((bf16[384,512]{1,0:T(8,128)(2,1)S(1)}, bf16[384,512]{1,0:T(8,128)(2,1)S(1)}, u32[]{:S(2)}, u32[]{:S(2)}) %collective-permute-start.14) | collective-permute-done | bytes 393248 | tf_op jit(solution)/shard_map/ppermute | solution.py:62
  163.8 2.7 joined_grad.1
  167.1 2.0 collective-permute-done.18
  169.1 1.0 add_convert_fusion
  170.1 3.5 all-to-all-start
  173.6 3.5 reduce_sum.34
  177.0 5.6 %all-to-all-done = bf16[4,112,576]{2,1,0:T(8,128)(2,1)S(1)} async-done(((bf16[4,112,576]{2,1,0:T(8,128)(2,1)}), bf16[4,112,576]{2,1,0:T(8,128)(2,1)S(1)}, u32[]{:S(2)}, u32[]{:S(2)}) %all-to-all-start) | async-done | bytes 516128 | tf_op jit(solution)/shard_map/all_to_all | solution.py:71
  182.7 3.5 all-to-all-start.2
  186.5 3.9 %up_grad.3 = bf16[384,3072]{1,0:T(8,128)(2,1)} custom-call(s32[3]{0:T(128)S(1)} %pad_add_fusion.spot, bf16[128,768]{1,0:T(8,128)(2,1)S(1)} %copy-done.8, bf16[128,3072]{1,0:T(8,128)(2,1)S(1)} %get-tuple-element.83.inner, bf16[384,3072]{1,0:T(8,128)(2,1)} %collective-permute-done.32.rest_0_), custom_call_target="tpu_custom_call" | custom-call | bytes 14000000 | tf_op jit(solution)/shard_map/up_grad/pallas_call | solution.py:34
  190.4 1.7 collective-permute-start.15
  192.3 2.4 collective-permute-start.21
  194.8 1.9 collective-permute-start.19
  196.7 23.3 %all-to-all-done.2 = bf16[4,128,768]{2,1,0:T(8,128)(2,1)S(1)} async-done(((bf16[4,128,768]{2,1,0:T(8,128)(2,1)}), bf16[4,128,768]{2,1,0:T(8,128)(2,1)S(1)}, u32[]{:S(2)}, u32[]{:S(2)}) %all-to-all-start.2) | async-done | bytes 786464 | tf_op jit(solution)/shard_map/all_to_all | solution.py:71
  220.6 26.2 %collective-permute-done.20 = bf16[112,576]{1,0:T(8,128)(2,1)S(1)} collective-permute-done((bf16[112,576]{1,0:T(8,128)(2,1)S(1)}, bf16[112,576]{1,0:T(8,128)(2,1)S(1)}, u32[]{:S(2)}, u32[]{:S(2)}) %collective-permute-start.20) | collective-permute-done | bytes 129056 | tf_op jit(solution)/shard_map/ppermute | solution.py:62
  246.9 1.6 collective-permute-start.24
  249.3 2.7 collective-permute-start.26
  252.0 1.1 collective-permute-done.27
  253.2 15.8 %collective-permute-done.26 = bf16[128,768]{1,0:T(8,128)(2,1)S(1)} collective-permute-done((bf16[128,768]{1,0:T(8,128)(2,1)S(1)}, bf16[128,768]{1,0:T(8,128)(2,1)S(1)}, u32[]{:S(2)}, u32[]{:S(2)}) %collective-permute-start.26) | collective-permute-done | bytes 196640 | tf_op jit(solution)/shard_map/ppermute | solution.py:62
  268.9 1.5 collective-permute-start.23
  270.6 2.0 collective-permute-start.31
  272.6 1.5 collective-permute-start.30
  274.2 1.9 add_bitcast_fusion
  276.1 18.9 %collective-permute-done.23.p2 = bf16[4,112,576]{2,1,0:T(8,128)(2,1)S(1)} collective-permute-done((bf16[4,112,576]{2,1,0:T(8,128)(2,1)S(1)}, bf16[4,112,576]{2,1,0:T(8,128)(2,1)S(1)}, u32[]{:S(2)}, u32[]{:S(2)}) %collective-permute-start.23) | collective-permute-done | bytes 516128 | tf_op jit(solution)/shard_map/ppermute | solution.py:62
  295.0 2.8 place_joined.1
  298.4 64.5 %all-reduce.2.cloned.1.call-done = bf16[384,3072]{1,0:T(8,128)(2,1)} async-done(((bf16[384,3072]{1,0:T(8,128)(2,1)}), bf16[384,3072]{1,0:T(8,128)(2,1)}) %all-reduce.2.cloned.1.call-update) | async-done | bytes 2359312 | tf_op jit(solution)/shard_map/psum | solution.py:517
  362.8 4.4 %convert_element_type.58 = f32[384,3072]{1,0:T(8,128)} convert(bf16[384,3072]{1,0:T(8,128)(2,1)} %all-reduce.2.cloned.1.call-done) | non-fusion elementwise | flops 1179648 | bytes 7077888 | tf_op jit(solution)/shard_map/convert_element_type | solution.py:517
  367.3 1.6 slice_reduce_fusion.2
  369.5 3.5 place_down.1
  (199 shorter events, 18.1 us)
Async XLA Ops:
  7.2 65.1 %all-gather.6.cloned.1.call-start = ((), (), s32[]{:S(2)}) async-start(), calls=%async_computation.3 | async-start | bytes 1769472 | tf_op jit(solution)/shard_map/all_gather | solution.py:463
  8.0 64.3 %all-gather.8.cloned.1.call-start = ((), (), s32[]{:S(2)}) async-start(), calls=%async_computation.4 | async-start | bytes 7077888 | tf_op jit(solution)/shard_map/all_gather | solution.py:463
  8.8 63.5 %all-gather.10.cloned.1.call-start = ((), (), s32[]{:S(2)}) async-start(), calls=%async_computation.5 | async-start | bytes 7077888 | tf_op jit(solution)/shard_map/all_gather | solution.py:463
  9.5 12.7 %collective-permute-start.2 = (bf16[128,768]{1,0:T(8,128)(2,1)S(1)}, bf16[128,768]{1,0:T(8,128)(2,1)S(1)}, u32[]{:S(2)}, u32[]{:S(2)}) collective-permute-start(bf16[128,768]{1,0:T(8,128)(2,1)S(1)} %bitcast.28), channel_id=1, source_target_pairs={{0,24},{2,26},{4,28},{6,30},{8,16},{10,18},{12,20},{14,22},{16,8},... | collective-permute-start | bytes 589832 | tf_op jit(solution)/shard_map/ppermute | solution.py:62
  14.6 16.7 %collective-permute-start.1 = (bf16[128,768]{1,0:T(8,128)(2,1)S(1)}, bf16[128,768]{1,0:T(8,128)(2,1)S(1)}, u32[]{:S(2)}, u32[]{:S(2)}) collective-permute-start(bf16[128,768]{1,0:T(8,128)(2,1)S(1)} %bitcast.29), channel_id=1, source_target_pairs={{0,16},{2,18},{4,20},{6,22},{8,24},{10,26},{12,28},{14,30},{16,0},... | collective-permute-start | bytes 589832 | tf_op jit(solution)/shard_map/ppermute | solution.py:62
  14.6 16.7 %collective-permute-start = (bf16[128,768]{1,0:T(8,128)(2,1)S(1)}, bf16[128,768]{1,0:T(8,128)(2,1)S(1)}, u32[]{:S(2)}, u32[]{:S(2)}) collective-permute-start(bf16[128,768]{1,0:T(8,128)(2,1)S(1)} %bitcast.30), channel_id=1, source_target_pairs={{0,8},{2,10},{4,12},{6,14},{8,0},{10,2},{12,4},{14,6},{16,24},{18,... | collective-permute-start | bytes 589832 | tf_op jit(solution)/shard_map/ppermute | solution.py:62
  19.5 16.3 %copy-start.58 = (s32[2]{0:T(128)S(1)}, s32[2]{0:T(128)}, u32[]{:S(2)}) copy-start(s32[2]{0:T(128)} %param.18) | copy-start | bytes 28
  22.2 50.1 %copy-start.9 = (bf16[128,768]{1,0:T(8,128)(2,1)}, bf16[128,768]{1,0:T(8,128)(2,1)S(1)}, u32[]{:S(2)}) copy-start(bf16[128,768]{1,0:T(8,128)(2,1)S(1)} %collective-permute-done.2.x3.rest_7_) | copy-start | bytes 589828
  31.3 41.0 %copy-start.11 = (bf16[128,768]{1,0:T(8,128)(2,1)}, bf16[128,768]{1,0:T(8,128)(2,1)S(1)}, u32[]{:S(2)}) copy-start(bf16[128,768]{1,0:T(8,128)(2,1)S(1)} %collective-permute-done.1.x2.rest_6_) | copy-start | bytes 589828
  32.2 40.1 %copy-start.4 = (bf16[512,192]{1,0:T(8,128)(2,1)}, bf16[512,192]{1,0:T(8,128)(2,1)S(1)}, u32[]{:S(2)}) copy-start(bf16[512,192]{1,0:T(8,128)(2,1)S(1)} %get-tuple-element.50.refs_0_) | copy-start | bytes 589828
  32.2 13.1 %collective-permute-start.5 = (bf16[512,384]{1,0:T(8,128)(2,1)S(1)}, bf16[512,384]{1,0:T(8,128)(2,1)S(1)}, u32[]{:S(2)}, u32[]{:S(2)}) collective-permute-start(bf16[512,384]{1,0:T(8,128)(2,1)S(1)} %get-tuple-element.51.refs_1_.refs_7_), channel_id=1, source_target_pairs={{0,6},{2,4},{4,2},{6,0},{8,14},{10,12},{12,10},{14,8},{16,22},{18,... | collective-permute-start | bytes 1179656 | tf_op jit(solution)/shard_map/ppermute | solution.py:62
  34.7 17.0 %collective-permute-start.4 = (bf16[512,384]{1,0:T(8,128)(2,1)S(1)}, bf16[512,384]{1,0:T(8,128)(2,1)S(1)}, u32[]{:S(2)}, u32[]{:S(2)}) collective-permute-start(bf16[512,384]{1,0:T(8,128)(2,1)S(1)} %get-tuple-element.51.refs_1_.refs_7_), channel_id=1, source_target_pairs={{0,4},{2,6},{4,0},{6,2},{8,12},{10,14},{12,8},{14,10},{16,20},{18,... | collective-permute-start | bytes 1179656 | tf_op jit(solution)/shard_map/ppermute | solution.py:62
  35.2 16.6 %collective-permute-start.3 = (bf16[512,384]{1,0:T(8,128)(2,1)S(1)}, bf16[512,384]{1,0:T(8,128)(2,1)S(1)}, u32[]{:S(2)}, u32[]{:S(2)}) collective-permute-start(bf16[512,384]{1,0:T(8,128)(2,1)S(1)} %get-tuple-element.51.refs_1_.refs_7_), channel_id=1, source_target_pairs={{0,2},{2,0},{4,6},{6,4},{8,10},{10,8},{12,14},{14,12},{16,18},{18,... | collective-permute-start | bytes 1179656 | tf_op jit(solution)/shard_map/ppermute | solution.py:62
  37.3 23.5 %copy-start.38 = (f32[1,512]{1,0:T(1,128)}, f32[1,512]{1,0:T(1,128)S(1)}, u32[]{:S(2)}) copy-start(f32[1,512]{1,0:T(1,128)S(1)} %get-tuple-element.108.refs_5_.refs_11_) | copy-start | bytes 6148
  37.3 31.4 %copy-start.32 = (f32[1,512]{1,0:T(1,128)}, f32[1,512]{1,0:T(1,128)S(1)}, u32[]{:S(2)}) copy-start(f32[1,512]{1,0:T(1,128)S(1)} %get-tuple-element.105.refs_8_.refs_14_) | copy-start | bytes 6148
  37.3 31.4 %copy-start.34 = (f32[1,512]{1,0:T(1,128)}, f32[1,512]{1,0:T(1,128)S(1)}, u32[]{:S(2)}) copy-start(f32[1,512]{1,0:T(1,128)S(1)} %get-tuple-element.106.refs_7_.refs_13_) | copy-start | bytes 6148
  37.4 31.4 %copy-start.36 = (f32[1,512]{1,0:T(1,128)}, f32[1,512]{1,0:T(1,128)S(1)}, u32[]{:S(2)}) copy-start(f32[1,512]{1,0:T(1,128)S(1)} %get-tuple-element.107.refs_6_.refs_12_) | copy-start | bytes 6148
  63.0 7.8 %collective-permute-start.6 = (bf16[128,192]{1,0:T(8,128)(2,1)}, bf16[128,192]{1,0:T(8,128)(2,1)S(1)}, u32[]{:S(2)}, u32[]{:S(2)}) collective-permute-start(bf16[128,192]{1,0:T(8,128)(2,1)} %get-tuple-element.53), channel_id=1, source_target_pairs={{0,8},{2,10},{4,12},{6,14},{8,0},{10,2},{12,4},{14,6},{16,24},{18,... | collective-permute-start | bytes 147464 | tf_op jit(solution)/shard_map/ppermute | solution.py:62
  63.0 8.5 %collective-permute-start.7 = (bf16[128,192]{1,0:T(8,128)(2,1)}, bf16[128,192]{1,0:T(8,128)(2,1)S(1)}, u32[]{:S(2)}, u32[]{:S(2)}) collective-permute-start(bf16[128,192]{1,0:T(8,128)(2,1)} %get-tuple-element.54), channel_id=1, source_target_pairs={{0,16},{2,18},{4,20},{6,22},{8,24},{10,26},{12,28},{14,30},{16,0},... | collective-permute-start | bytes 147464 | tf_op jit(solution)/shard_map/ppermute | solution.py:62
  65.8 6.5 %collective-permute-start.8 = (bf16[128,192]{1,0:T(8,128)(2,1)}, bf16[128,192]{1,0:T(8,128)(2,1)}, u32[]{:S(2)}, u32[]{:S(2)}) collective-permute-start(bf16[128,192]{1,0:T(8,128)(2,1)} %get-tuple-element.55), channel_id=1, source_target_pairs={{0,24},{2,26},{4,28},{6,30},{8,16},{10,18},{12,20},{14,22},{16,8},... | collective-permute-start | bytes 147464 | tf_op jit(solution)/shard_map/ppermute | solution.py:62
  93.0 7.8 %copy-start.44 = (bf16[128,192]{1,0:T(8,128)(2,1)}, bf16[128,192]{1,0:T(8,128)(2,1)S(1)}, u32[]{:S(2)}) copy-start(bf16[128,192]{1,0:T(8,128)(2,1)S(1)} %get-tuple-element.61) | copy-start | bytes 147460
  95.1 5.7 %collective-permute-start.25 = (bf16[4,4,128,768]{3,2,1,0:T(8,128)(2,1)S(1)}, bf16[4,4,128,768]{3,2,1,0:T(8,128)(2,1)S(1)}, u32[]{:S(2)}, u32[]{:S(2)}) collective-permute-start(bf16[4,4,128,768]{3,2,1,0:T(8,128)(2,1)S(1)} %down_grad.2), channel_id=1, source_target_pairs={{0,1},{1,0},{2,3},{3,2},{4,5},{5,4},{6,7},{7,6},{8,9},{9,8},{10,11... | collective-permute-start | bytes 9437192 | tf_op jit(solution)/shard_map/ppermute | solution.py:514
  104.6 18.4 %copy-start.33 = (f32[1,512]{1,0:T(1,128)S(1)}, f32[1,512]{1,0:T(1,128)}, u32[]{:S(2)}) copy-start(f32[1,512]{1,0:T(1,128)} %copy-done.32) | copy-start | bytes 6148
  104.6 18.4 %copy-start.35 = (f32[1,512]{1,0:T(1,128)S(1)}, f32[1,512]{1,0:T(1,128)}, u32[]{:S(2)}) copy-start(f32[1,512]{1,0:T(1,128)} %copy-done.34) | copy-start | bytes 6148
  104.6 18.4 %copy-start.37 = (f32[1,512]{1,0:T(1,128)S(1)}, f32[1,512]{1,0:T(1,128)}, u32[]{:S(2)}) copy-start(f32[1,512]{1,0:T(1,128)} %copy-done.36) | copy-start | bytes 6148
  104.6 65.5 %all-to-all-start.1 = ((bf16[4,4,128,768]{3,2,1,0:T(8,128)(2,1)}), bf16[4,4,128,768]{3,2,1,0:T(8,128)(2,1)}, u32[]{:S(2)}, u32[]{:S(2)}) async-start(bf16[4,4,128,768]{3,2,1,0:T(8,128)(2,1)} %down_grad.3), calls=%async_computation.1 | async-start | bytes 6291456 | tf_op jit(solution)/shard_map/all_to_all | solution.py:71
  109.6 13.4 %copy-start.5 = (bf16[512,192]{1,0:T(8,128)(2,1)S(1)}, bf16[512,192]{1,0:T(8,128)(2,1)}, u32[]{:S(2)}) copy-start(bf16[512,192]{1,0:T(8,128)(2,1)} %copy-done.4) | copy-start | bytes 589828
  110.6 12.4 %copy-start.22 = (f32[512,192]{1,0:T(8,128)S(1)}, f32[512,192]{1,0:T(8,128)}, u32[]{:S(2)}) copy-start(f32[512,192]{1,0:T(8,128)} %copy-done.21) | copy-start | bytes 1179652
  110.6 12.4 %copy-start.26 = (f32[512,128]{1,0:T(8,128)S(1)}, f32[512,128]{1,0:T(8,128)}, u32[]{:S(2)}) copy-start(f32[512,128]{1,0:T(8,128)} %copy-done.25) | copy-start | bytes 786436
  110.6 12.4 %copy-start.31 = (bf16[128,192]{1,0:T(8,128)(2,1)S(1)}, bf16[128,192]{1,0:T(8,128)(2,1)}, u32[]{:S(2)}) copy-start(bf16[128,192]{1,0:T(8,128)(2,1)} %copy-done.30) | copy-start | bytes 147460
  110.6 12.4 %copy-start.39 = (f32[1,512]{1,0:T(1,128)S(1)}, f32[1,512]{1,0:T(1,128)}, u32[]{:S(2)}) copy-start(f32[1,512]{1,0:T(1,128)} %copy-done.38) | copy-start | bytes 6148
  110.6 53.2 %copy-start.10 = (bf16[128,768]{1,0:T(8,128)(2,1)S(1)}, bf16[128,768]{1,0:T(8,128)(2,1)}, u32[]{:S(2)}) copy-start(bf16[128,768]{1,0:T(8,128)(2,1)} %copy-done.9) | copy-start | bytes 589828
  110.6 53.1 %copy-start.12 = (bf16[128,768]{1,0:T(8,128)(2,1)S(1)}, bf16[128,768]{1,0:T(8,128)(2,1)}, u32[]{:S(2)}) copy-start(bf16[128,768]{1,0:T(8,128)(2,1)} %copy-done.11) | copy-start | bytes 589828
  110.6 53.1 %copy-start.14 = (bf16[128,768]{1,0:T(8,128)(2,1)S(1)}, bf16[128,768]{1,0:T(8,128)(2,1)}, u32[]{:S(2)}) copy-start(bf16[128,768]{1,0:T(8,128)(2,1)} %copy-done.13) | copy-start | bytes 589828
  113.5 73.0 %collective-permute-start.32 = (bf16[384,3072]{1,0:T(8,128)(2,1)}, bf16[384,3072]{1,0:T(8,128)(2,1)}, u32[]{:S(2)}, u32[]{:S(2)}) collective-permute-start(bf16[384,3072]{1,0:T(8,128)(2,1)} %up_grad.2), channel_id=1, source_target_pairs={{0,1},{1,0},{2,3},{3,2},{4,5},{5,4},{6,7},{7,6},{8,9},{9,8},{10,11... | collective-permute-start | bytes 7077896 | tf_op jit(solution)/shard_map/ppermute | solution.py:514
  113.6 4.4 %collective-permute-start.9 = (bf16[128,192]{1,0:T(8,128)(2,1)S(1)}, bf16[128,192]{1,0:T(8,128)(2,1)S(1)}, u32[]{:S(2)}, u32[]{:S(2)}) collective-permute-start(bf16[128,192]{1,0:T(8,128)(2,1)S(1)} %copy-done.45), channel_id=1, source_target_pairs={{0,8},{2,10},{4,12},{6,14},{8,0},{10,2},{12,4},{14,6},{16,24},{18,... | collective-permute-start | bytes 147464 | tf_op jit(solution)/shard_map/ppermute | solution.py:62
  114.5 8.5 %collective-permute-start.10 = (bf16[128,192]{1,0:T(8,128)(2,1)S(1)}, bf16[128,192]{1,0:T(8,128)(2,1)S(1)}, u32[]{:S(2)}, u32[]{:S(2)}) collective-permute-start(bf16[128,192]{1,0:T(8,128)(2,1)S(1)} %copy-done.43), channel_id=1, source_target_pairs={{0,16},{2,18},{4,20},{6,22},{8,24},{10,26},{12,28},{14,30},{16,0},... | collective-permute-start | bytes 147464 | tf_op jit(solution)/shard_map/ppermute | solution.py:62
  116.3 6.7 %collective-permute-start.11 = (bf16[128,192]{1,0:T(8,128)(2,1)S(1)}, bf16[128,192]{1,0:T(8,128)(2,1)S(1)}, u32[]{:S(2)}, u32[]{:S(2)}) collective-permute-start(bf16[128,192]{1,0:T(8,128)(2,1)S(1)} %copy-done.41), channel_id=1, source_target_pairs={{0,24},{2,26},{4,28},{6,30},{8,16},{10,18},{12,20},{14,22},{16,8},... | collective-permute-start | bytes 147464 | tf_op jit(solution)/shard_map/ppermute | solution.py:62
  130.9 24.3 %collective-permute-start.12 = (bf16[384,512]{1,0:T(8,128)(2,1)S(1)}, bf16[384,512]{1,0:T(8,128)(2,1)S(1)}, u32[]{:S(2)}, u32[]{:S(2)}) collective-permute-start(bf16[384,512]{1,0:T(8,128)(2,1)S(1)} %get-tuple-element.66), channel_id=1, source_target_pairs={{0,2},{2,0},{4,6},{6,4},{8,10},{10,8},{12,14},{14,12},{16,18},{18,... | collective-permute-start | bytes 1179656 | tf_op jit(solution)/shard_map/ppermute | solution.py:62
  132.7 22.6 %collective-permute-start.13 = (bf16[384,512]{1,0:T(8,128)(2,1)S(1)}, bf16[384,512]{1,0:T(8,128)(2,1)S(1)}, u32[]{:S(2)}, u32[]{:S(2)}) collective-permute-start(bf16[384,512]{1,0:T(8,128)(2,1)S(1)} %get-tuple-element.67), channel_id=1, source_target_pairs={{0,4},{2,6},{4,0},{6,2},{8,12},{10,14},{12,8},{14,10},{16,20},{18,... | collective-permute-start | bytes 1179656 | tf_op jit(solution)/shard_map/ppermute | solution.py:62
  134.1 29.6 %collective-permute-start.14 = (bf16[384,512]{1,0:T(8,128)(2,1)S(1)}, bf16[384,512]{1,0:T(8,128)(2,1)S(1)}, u32[]{:S(2)}, u32[]{:S(2)}) collective-permute-start(bf16[384,512]{1,0:T(8,128)(2,1)S(1)} %get-tuple-element.68), channel_id=1, source_target_pairs={{0,6},{2,4},{4,2},{6,0},{8,14},{10,12},{12,10},{14,8},{16,22},{18,... | collective-permute-start | bytes 1179656 | tf_op jit(solution)/shard_map/ppermute | solution.py:62
  167.1 2.0 collective-permute-start.18
  170.1 12.6 %all-to-all-start = ((bf16[4,112,576]{2,1,0:T(8,128)(2,1)}), bf16[4,112,576]{2,1,0:T(8,128)(2,1)S(1)}, u32[]{:S(2)}, u32[]{:S(2)}) async-start(bf16[4,112,576]{2,1,0:T(8,128)(2,1)} %add_convert_fusion), calls=%async_computation | async-start | bytes 1146880 | tf_op jit(solution)/shard_map/all_to_all | solution.py:71
  173.6 12.9 %copy-start.8 = (bf16[128,768]{1,0:T(8,128)(2,1)S(1)}, bf16[128,768]{1,0:T(8,128)(2,1)}, u32[]{:S(2)}) copy-start(bf16[128,768]{1,0:T(8,128)(2,1)} %copy-done.6) | copy-start | bytes 589828
  182.7 37.4 %all-to-all-start.2 = ((bf16[4,128,768]{2,1,0:T(8,128)(2,1)}), bf16[4,128,768]{2,1,0:T(8,128)(2,1)S(1)}, u32[]{:S(2)}, u32[]{:S(2)}) async-start(bf16[4,128,768]{2,1,0:T(8,128)(2,1)} %reduce_sum.34), calls=%async_computation.2 | async-start | bytes 1572864 | tf_op jit(solution)/shard_map/all_to_all | solution.py:71
  186.2 176.7 %all-reduce.2.cloned.1.call-start = ((), (), s32[]{:S(2)}) async-start(), calls=%async_computation.6 | async-start | bytes 4718592 | tf_op jit(solution)/shard_map/psum | solution.py:517
  190.4 58.8 %collective-permute-start.15 = (bf16[128,768]{1,0:T(8,128)(2,1)S(1)}, bf16[128,768]{1,0:T(8,128)(2,1)S(1)}, u32[]{:S(2)}, u32[]{:S(2)}) collective-permute-start(bf16[128,768]{1,0:T(8,128)(2,1)S(1)} %get-tuple-element.70), channel_id=1, source_target_pairs={{0,8},{2,10},{4,12},{6,14},{8,0},{10,2},{12,4},{14,6},{16,24},{18,... | collective-permute-start | bytes 589832 | tf_op jit(solution)/shard_map/ppermute | solution.py:62
  192.3 81.9 %copy-start.24 = (f32[128,768]{1,0:T(8,128)S(1)}, f32[128,768]{1,0:T(8,128)}, u32[]{:S(2)}) copy-start(f32[128,768]{1,0:T(8,128)} %copy-done.23) | copy-start | bytes 1179652
  192.3 28.3 %collective-permute-start.21 = (bf16[112,576]{1,0:T(8,128)(2,1)S(1)}, bf16[112,576]{1,0:T(8,128)(2,1)S(1)}, u32[]{:S(2)}, u32[]{:S(2)}) collective-permute-start(bf16[112,576]{1,0:T(8,128)(2,1)S(1)} %reduce_sum.33), channel_id=1, source_target_pairs={{0,24},{2,26},{4,28},{6,30},{8,16},{10,18},{12,20},{14,22},{16,8},... | collective-permute-start | bytes 387080 | tf_op jit(solution)/shard_map/ppermute | solution.py:62
  194.7 52.1 %collective-permute-start.20 = (bf16[112,576]{1,0:T(8,128)(2,1)S(1)}, bf16[112,576]{1,0:T(8,128)(2,1)S(1)}, u32[]{:S(2)}, u32[]{:S(2)}) collective-permute-start(bf16[112,576]{1,0:T(8,128)(2,1)S(1)} %reduce_sum.33), channel_id=1, source_target_pairs={{0,16},{2,18},{4,20},{6,22},{8,24},{10,26},{12,28},{14,30},{16,0},... | collective-permute-start | bytes 387080 | tf_op jit(solution)/shard_map/ppermute | solution.py:62
  194.8 52.0 %collective-permute-start.19 = (bf16[112,576]{1,0:T(8,128)(2,1)S(1)}, bf16[112,576]{1,0:T(8,128)(2,1)S(1)}, u32[]{:S(2)}, u32[]{:S(2)}) collective-permute-start(bf16[112,576]{1,0:T(8,128)(2,1)S(1)} %reduce_sum.33), channel_id=1, source_target_pairs={{0,8},{2,10},{4,12},{6,14},{8,0},{10,2},{12,4},{14,6},{16,24},{18,... | collective-permute-start | bytes 387080 | tf_op jit(solution)/shard_map/ppermute | solution.py:62
  220.1 54.0 %copy-start.46 = (f32[128,768]{1,0:T(8,128)}, f32[128,768]{1,0:T(8,128)S(1)}, u32[]{:S(2)}) copy-start(f32[128,768]{1,0:T(8,128)S(1)} %convert_reduce_fusion) | copy-start | bytes 1179652
  220.2 32.9 %collective-permute-start.27 = (bf16[128,768]{1,0:T(8,128)(2,1)S(1)}, bf16[128,768]{1,0:T(8,128)(2,1)S(1)}, u32[]{:S(2)}, u32[]{:S(2)}) collective-permute-start(bf16[128,768]{1,0:T(8,128)(2,1)S(1)} %convert_element_type.56), channel_id=1, source_target_pairs={{0,16},{2,18},{4,20},{6,22},{8,24},{10,26},{12,28},{14,30},{16,0},... | collective-permute-start | bytes 589832 | tf_op jit(solution)/shard_map/ppermute | solution.py:62
  246.9 27.2 %collective-permute-start.24 = (bf16[4,112,576]{2,1,0:T(8,128)(2,1)S(1)}, bf16[4,112,576]{2,1,0:T(8,128)(2,1)S(1)}, u32[]{:S(2)}, u32[]{:S(2)}) collective-permute-start(bf16[4,112,576]{2,1,0:T(8,128)(2,1)S(1)} %pad_maximum_fusion.1.p0), channel_id=1, source_target_pairs={{0,6},{2,4},{4,2},{6,0},{8,14},{10,12},{12,10},{14,8},{16,22},{18,... | collective-permute-start | bytes 1548296 | tf_op jit(solution)/shard_map/ppermute | solution.py:62
  248.5 22.1 %collective-permute-start.16 = (bf16[128,768]{1,0:T(8,128)(2,1)S(1)}, bf16[128,768]{1,0:T(8,128)(2,1)S(1)}, u32[]{:S(2)}, u32[]{:S(2)}) collective-permute-start(bf16[128,768]{1,0:T(8,128)(2,1)S(1)} %get-tuple-element.71), channel_id=1, source_target_pairs={{0,16},{2,18},{4,20},{6,22},{8,24},{10,26},{12,28},{14,30},{16,0},... | collective-permute-start | bytes 589832 | tf_op jit(solution)/shard_map/ppermute | solution.py:62
  248.5 24.1 %collective-permute-start.17 = (bf16[128,768]{1,0:T(8,128)(2,1)S(1)}, bf16[128,768]{1,0:T(8,128)(2,1)S(1)}, u32[]{:S(2)}, u32[]{:S(2)}) collective-permute-start(bf16[128,768]{1,0:T(8,128)(2,1)S(1)} %get-tuple-element.72), channel_id=1, source_target_pairs={{0,24},{2,26},{4,28},{6,30},{8,16},{10,18},{12,20},{14,22},{16,8},... | collective-permute-start | bytes 589832 | tf_op jit(solution)/shard_map/ppermute | solution.py:62
  249.3 21.3 %copy-start.48 = (bf16[128,768]{1,0:T(8,128)(2,1)}, bf16[128,768]{1,0:T(8,128)(2,1)S(1)}, u32[]{:S(2)}) copy-start(bf16[128,768]{1,0:T(8,128)(2,1)S(1)} %collective-permute-done.15) | copy-start | bytes 589828
  249.3 19.7 %collective-permute-start.26 = (bf16[128,768]{1,0:T(8,128)(2,1)S(1)}, bf16[128,768]{1,0:T(8,128)(2,1)S(1)}, u32[]{:S(2)}, u32[]{:S(2)}) collective-permute-start(bf16[128,768]{1,0:T(8,128)(2,1)S(1)} %convert_element_type.56), channel_id=1, source_target_pairs={{0,8},{2,10},{4,12},{6,14},{8,0},{10,2},{12,4},{14,6},{16,24},{18,... | collective-permute-start | bytes 589832 | tf_op jit(solution)/shard_map/ppermute | solution.py:62
  253.1 17.4 %collective-permute-start.28 = (bf16[128,768]{1,0:T(8,128)(2,1)S(1)}, bf16[128,768]{1,0:T(8,128)(2,1)S(1)}, u32[]{:S(2)}, u32[]{:S(2)}) collective-permute-start(bf16[128,768]{1,0:T(8,128)(2,1)S(1)} %convert_element_type.56), channel_id=1, source_target_pairs={{0,24},{2,26},{4,28},{6,30},{8,16},{10,18},{12,20},{14,22},{16,8},... | collective-permute-start | bytes 589832 | tf_op jit(solution)/shard_map/ppermute | solution.py:62
  268.9 26.0 %collective-permute-start.23 = (bf16[4,112,576]{2,1,0:T(8,128)(2,1)S(1)}, bf16[4,112,576]{2,1,0:T(8,128)(2,1)S(1)}, u32[]{:S(2)}, u32[]{:S(2)}) collective-permute-start(bf16[4,112,576]{2,1,0:T(8,128)(2,1)S(1)} %pad_maximum_fusion.1.p0), channel_id=1, source_target_pairs={{0,4},{2,6},{4,0},{6,2},{8,12},{10,14},{12,8},{14,10},{16,20},{18,... | collective-permute-start | bytes 1548296 | tf_op jit(solution)/shard_map/ppermute | solution.py:62
  270.5 24.5 %collective-permute-start.22 = (bf16[4,112,576]{2,1,0:T(8,128)(2,1)S(1)}, bf16[4,112,576]{2,1,0:T(8,128)(2,1)S(1)}, u32[]{:S(2)}, u32[]{:S(2)}) collective-permute-start(bf16[4,112,576]{2,1,0:T(8,128)(2,1)S(1)} %pad_maximum_fusion.1.p0), channel_id=1, source_target_pairs={{0,2},{2,0},{4,6},{6,4},{8,10},{10,8},{12,14},{14,12},{16,18},{18,... | collective-permute-start | bytes 1548296 | tf_op jit(solution)/shard_map/ppermute | solution.py:62
  270.6 98.9 %collective-permute-start.31 = (bf16[4,128,768]{2,1,0:T(8,128)(2,1)S(1)}, bf16[4,128,768]{2,1,0:T(8,128)(2,1)S(1)}, u32[]{:S(2)}, u32[]{:S(2)}) collective-permute-start(bf16[4,128,768]{2,1,0:T(8,128)(2,1)S(1)} %pad_maximum_fusion.p0), channel_id=1, source_target_pairs={{0,6},{2,4},{4,2},{6,0},{8,14},{10,12},{12,10},{14,8},{16,22},{18,... | collective-permute-start | bytes 2359304 | tf_op jit(solution)/shard_map/ppermute | solution.py:62
  272.6 96.9 %collective-permute-start.30 = (bf16[4,128,768]{2,1,0:T(8,128)(2,1)S(1)}, bf16[4,128,768]{2,1,0:T(8,128)(2,1)S(1)}, u32[]{:S(2)}, u32[]{:S(2)}) collective-permute-start(bf16[4,128,768]{2,1,0:T(8,128)(2,1)S(1)} %pad_maximum_fusion.p0), channel_id=1, source_target_pairs={{0,4},{2,6},{4,0},{6,2},{8,12},{10,14},{12,8},{14,10},{16,20},{18,... | collective-permute-start | bytes 2359304 | tf_op jit(solution)/shard_map/ppermute | solution.py:62
  274.2 95.3 %collective-permute-start.29 = (bf16[4,128,768]{2,1,0:T(8,128)(2,1)S(1)}, bf16[4,128,768]{2,1,0:T(8,128)(2,1)S(1)}, u32[]{:S(2)}, u32[]{:S(2)}) collective-permute-start(bf16[4,128,768]{2,1,0:T(8,128)(2,1)S(1)} %pad_maximum_fusion.p0), channel_id=1, source_target_pairs={{0,2},{2,0},{4,6},{6,4},{8,10},{10,8},{12,14},{14,12},{16,18},{18,... | collective-permute-start | bytes 2359304 | tf_op jit(solution)/shard_map/ppermute | solution.py:62
  (35 other events, 114.7 us)
Sparse Core Ops, SparseCore 0:
  9.6 11.9 all-gather.5
  23.1 15.6 all-gather.7
  40.3 15.5 all-gather.9
  192.9 169.9 all-reduce.1

commit v3 on v2

--- a/solution.py
+++ b/solution.py
@@ -56,6 +56,7 @@
         self.columns = [[index(g, q, m) for g in groups] for q in quarters for m in members]
         self.planes = [[index(g, q, m) for q in quarters for m in members] for g in groups]
         self.fours = [[index(g, q, m) for q in quarters] for g in groups for m in members]
+        self.sixteens = [[index(g, q, m) for g in groups for q in quarters] for m in members]
         self.rests = [[index(g, q, m) for m in members] for g in groups for q in quarters]
 
     def swap(self, block, bits):
@@ -189,10 +190,13 @@
     return jnp.sum(values, axis=0, keepdims=True)
 
 
+TALL, SHORT, EXTRA = 96, 24, 8
+
+
 def dense_kernel(width, spot, c0, c1, c2, c3, x_ref, grad_ref, vectors, up_offset, out_hbm, up_hbm, down_hbm, *rest):
-    (layer_ref, one_grad_ref, normed_ref, active_ref, second_ref, inner_ref, branch_ref, sums_ref) = rest[:8]
-    context_grads = rest[8:12]
-    out_w, up_w, down_w, slope, sems = rest[12:]
+    layer_ref, one_grad_ref = rest[:2]
+    context_grads, up_parts, down_parts = rest[2:6], rest[6:10], rest[10:14]
+    out_w, up_w, down_w, slope, active_ref, inner_ref, sums_ref, sems = rest[14:]
     copies = [
         pltpu.make_async_copy(source, target, sems.at[i])
         for i, (source, target) in enumerate(((out_hbm, out_w), (up_hbm, up_w), (down_hbm, down_w)))
@@ -202,16 +206,18 @@
     hidden = up_w.shape[1]
     half = width // 2
     out_offset, gain_one, shift_one, down_offset, gain_two, shift_two = (vectors[i : i + 1, :] for i in range(2, 8))
-    group = spot[0]
+    group, quarter = spot[0], spot[1]
+    contexts = (c0, c1, c2, c3)
 
     def turned(i):
         return pl.ds(pl.multiple_of((group ^ i) * WIDTH, WIDTH), WIDTH)
 
     copies[0].wait()
-    branch = sum(dot(c[...], out_w[turned(i), :]) for i, c in enumerate((c0, c1, c2, c3))) + out_offset
+    branch = sum(dot(c[...], out_w[turned(i), :]) for i, c in enumerate(contexts)) + out_offset
     normal_one, scale_one = normalize(x_ref[...].astype(F32) + branch)
     normed_low = (normal_one * gain_one + shift_one).astype(BF16)
-    normed_ref[...] = normed_low
+    for ref in up_parts:
+        ref[:, :width] = normed_low
     copies[1].wait()
     copies[2].wait()
     step = 768
@@ -231,7 +237,6 @@
     gain_two_grad, shift_two_grad = column_sum(grad * normal_two), column_sum(grad)
     two_grad = normalize_grad(grad * gain_two, normal_two, scale_two)
     second_low = two_grad.astype(BF16)
-    second_ref[...] = second_low
     down_bias_grad = column_sum(second_low.astype(F32))
     normed_grad = two_grad
     for start in range(0, hidden, step):
@@ -242,121 +247,144 @@
         for piece in range(step // half):
             place = start // half + piece
             per_core = hidden // 2 // half
-            sums_ref[place // per_core, 6 + place % per_core : 7 + place % per_core, :] = up_sum[
-                :, piece * half : (piece + 1) * half
-            ]
+            row, core = 6 + place % per_core, place // per_core
+            sums_ref[row : row + 1, core * half : (core + 1) * half] = up_sum[:, piece * half : (piece + 1) * half]
         normed_grad = normed_grad + dot(inner_low, up_w[:, at], TURNED)
     gain_one_grad, shift_one_grad = column_sum(normed_grad * normal_one), column_sum(normed_grad)
     one_grad = normalize_grad(normed_grad * gain_one, normal_one, scale_one)
     one_grad_ref[...] = one_grad
     branch_low = one_grad.astype(BF16)
-    branch_ref[...] = branch_low
     for i, ref in enumerate(context_grads):
         ref[...] = dot(branch_low, out_w[turned(i), :], TURNED).astype(BF16)
     out_bias_grad = column_sum(branch_low.astype(F32))
     sums = (out_bias_grad, gain_one_grad, shift_one_grad, down_bias_grad, gain_two_grad, shift_two_grad)
-    for core in range(2):
-        for i, total in enumerate(sums):
-            sums_ref[core, i : i + 1, :] = total[:, core * half : (core + 1) * half]
-        sums_ref[core, 10:16, :] = jnp.zeros((6, half), F32)
+    for i, total in enumerate(sums):
+        sums_ref[i : i + 1, :] = total
+    sums_ref[10:16, :] = jnp.zeros((6, width), F32)
+    share = hidden // 8
+    for i in range(4):
+        for core in range(2):
+            at = pl.ds(pl.multiple_of(core * (hidden // 2) + (quarter ^ i) * share, share), share)
+            to = slice(width + core * share, width + (core + 1) * share)
+            up_parts[i][:, to] = inner_ref[:, at]
+            down_parts[i][:ROWS, to] = active_ref[:, at]
+        down_parts[i][:ROWS, :width] = second_low
+        down_parts[i][:ROWS, 2 * width : 3 * width] = branch_low
+        down_parts[i][ROWS:, :width] = sums_ref[...].astype(BF16)
+    strip = width // 8
+    for i, c in enumerate(contexts):
+        for g in range(GROUPS):
+            @pl.when((group ^ i) == g)
+            def _():
+                for part in range(2):
+                    core, owner = divmod((g * WIDTH + part * strip) // strip, 4)
+                    for turn in range(4):
+                        @pl.when((quarter ^ turn) == owner)
+                        def _():
+                            to = 3 * width + core * strip
+                            down_parts[turn][:ROWS, to : to + strip] = c[:, part * strip : (part + 1) * strip]
 
 
 def dense(spot, contexts, inputs, grad, vectors, up_offset, out_matrix, up_matrix, down_matrix):
     width, hidden = up_matrix.shape
     outs = (
-        shaped((ROWS, width)),
-        shaped((ROWS, width), F32),
-        shaped((ROWS, width)),
-        shaped((ROWS, hidden)),
-        shaped((ROWS, width)),
-        shaped((ROWS, hidden)),
-        shaped((ROWS, width)),
-        shaped((2, 16, width // 2), F32),
-    ) + (shaped((ROWS, WIDTH)),) * GROUPS
+        (shaped((ROWS, width)), shaped((ROWS, width), F32))
+        + (shaped((ROWS, WIDTH)),) * GROUPS
+        + (shaped((ROWS, width + hidden // 4)),) * 4
+        + (shaped((ROWS + 16, 3 * width + 256)),) * 4
+    )
     scratch = (
         pltpu.VMEM(out_matrix.shape, BF16),
         pltpu.VMEM(up_matrix.shape, BF16),
         pltpu.VMEM(down_matrix.shape, BF16),
         pltpu.VMEM((ROWS, hidden), F32),
+        pltpu.VMEM((ROWS, hidden), BF16),
+        pltpu.VMEM((ROWS, hidden), BF16),
+        pltpu.VMEM((16, width), F32),
         pltpu.SemaphoreType.DMA((3,)),
     )
     args = (spot, *contexts, inputs, grad, vectors, up_offset, out_matrix, up_matrix, down_matrix)
-    return kernel_call(
+    found = kernel_call(
         functools.partial(dense_kernel, width), "dense", outs, args, 40, 18, 1, (9, 10, 11), scratch
     )
-
-
-def up_grad_kernel(own, spot, normed, inner, *rest):
-    received, out_ref, normed_turned = rest if own else (None, *rest)
-    normed_turned[...] = normed[...].T
-    rows = out_ref.shape[0]
-    core = spot[2] if own else 1 - spot[2]
-    left = normed_turned[pl.ds(pl.multiple_of(core * rows, rows), rows), :]
-    for start in range(0, out_ref.shape[1], 768):
-        at = slice(start, start + 768)
-        value = dot(left, inner[:, at])
-        if own:
-            value = value + received[:, at].astype(F32)
-        out_ref[:, at] = value.astype(BF16)
-
-
-def up_grad_part(spot, normed, inner, received=None):
-    width, hidden = normed.shape[1], inner.shape[1]
-    args = (spot, normed, inner) + (() if received is None else (received,))
-    return kernel_call(
-        functools.partial(up_grad_kernel, received is not None),
-        "up_grad",
-        shaped((width // 2, hidden)),
-        args,
-        16,
-        4,
-        1,
-        (),
-        (pltpu.VMEM((width, ROWS), BF16),),
-    )
-
-
-TALL, SHORT, EXTRA = 96, 24, 8
-
-
-def down_grad_kernel(own, spot, active, second, c0, c1, c2, c3, branch, sums, *rest):
-    received, out_ref, active_turned, context_turned = rest if own else (None, *rest)
-    active_turned[...] = active[...].T
-    group = spot[0]
-    for i, c in enumerate((c0, c1, c2, c3)):
-        context_turned[pl.ds(pl.multiple_of((group ^ i) * WIDTH, WIDTH), WIDTH), :] = c[...].T
-    core = spot[2] if own else 1 - spot[2]
-    tall, short = active_turned.shape[0] // 2, context_turned.shape[0] // 2
-    context_half = context_turned[pl.ds(pl.multiple_of(core * short, short), short), :]
-    totals = sums[core]
-    extra = jnp.concatenate([totals[:EXTRA], totals[EXTRA:]], axis=1)
-    for quarter in range(4):
-        left = active_turned[pl.ds(pl.multiple_of(core * tall + quarter * (tall // 4), 16), tall // 4), :]
-        down = dot(left, second[...])
-        out = dot(context_half[quarter * (short // 4) : (quarter + 1) * (short // 4), :], branch[...])
+    return found[0], found[1], found[2:6], found[6:10], found[10:14]
+
+
+def up_grad_kernel(spot, p0, p1, p2, p3, other_ref, own_ref, turned, inner):
+    width = turned.shape[0]
+    for i, part in enumerate((p0, p1, p2, p3)):
+        turned[:, i * ROWS : (i + 1) * ROWS] = part[:, :width].T
+        inner[i * ROWS : (i + 1) * ROWS, :] = part[:, width:]
+    half = width // 2
+    for ref, core in ((other_ref, 1 - spot[2]), (own_ref, spot[2])):
+        value = dot(turned[pl.ds(pl.multiple_of(core * half, half), half), :], inner[...]).astype(BF16)
         for g in range(GROUPS):
-            value = jnp.concatenate(
-                [down[g * TALL : (g + 1) * TALL], out[g * SHORT : (g + 1) * SHORT], extra], axis=0
-            )
-            if own:
-                value = value + received[quarter, g].astype(F32)
-            out_ref[quarter, g] = value.astype(BF16)
-
-
-def down_grad_part(spot, active, second, contexts, branch, sums, received=None):
-    width, hidden = second.shape[1], active.shape[1]
-    args = (spot, active, second, *contexts, branch, sums) + (() if received is None else (received,))
-    return kernel_call(
-        functools.partial(down_grad_kernel, received is not None),
-        "down_grad",
-        shaped((4, GROUPS, TALL + SHORT + EXTRA, width)),
-        args,
-        24,
-        5,
-        1,
-        (),
-        (pltpu.VMEM((hidden, ROWS), BF16), pltpu.VMEM((width, ROWS), BF16)),
-    )
+            ref[g] = value[g * TALL : (g + 1) * TALL]
+
+
+def up_grad_parts(spot, parts, width):
+    tokens, columns = 4 * ROWS, parts[0].shape[1] - width
+    out = shaped((GROUPS, TALL, columns))
+    scratch = (pltpu.VMEM((width, tokens), BF16), pltpu.VMEM((tokens, columns), BF16))
+    return kernel_call(up_grad_kernel, "up_grad", (out, out), (spot, *parts), 16, 4, 1, (), scratch)
+
+
+def down_grad_kernel(spot, p0, p1, p2, p3, other_ref, own_ref, turned, second, branch, sums):
+    parts = (p0, p1, p2, p3)
+    width = second.shape[1]
+    tall, strip = GROUPS * TALL, GROUPS * SHORT
+    for i, part in enumerate(parts):
+        rows = slice(i * ROWS, (i + 1) * ROWS)
+        turned[: 2 * tall, rows] = part[:ROWS, width : 2 * width].T
+        turned[2 * tall : 2 * tall + 256, rows] = part[:ROWS, 3 * width :].T
+        second[rows, :] = part[:ROWS, :width]
+        branch[rows, :] = part[:ROWS, 2 * width : 3 * width]
+    total = sum(part[ROWS:, :width].astype(F32) for part in parts)
+    for core in range(2):
+        start = core * (width // 2)
+        sums[core] = jnp.concatenate(
+            [total[:EXTRA, start : start + width // 2], total[EXTRA:, start : start + width // 2]], axis=1
+        )
+    for ref, core in ((other_ref, 1 - spot[2]), (own_ref, spot[2])):
+        down = dot(turned[pl.ds(pl.multiple_of(core * tall, tall), tall), :], second[...])
+        out = dot(turned[pl.ds(pl.multiple_of(2 * tall + core * strip, 32), strip), :], branch[...])
+        for g in range(GROUPS):
+            ref[g] = jnp.concatenate(
+                [down[g * TALL : (g + 1) * TALL], out[g * SHORT : (g + 1) * SHORT], sums[core]], axis=0
+            ).astype(BF16)
+
+
+def down_grad_parts(spot, parts, width):
+    tokens = 4 * ROWS
+    out = shaped((GROUPS, TALL + SHORT + EXTRA, width))
+    scratch = (
+        pltpu.VMEM((2 * GROUPS * TALL + 256, tokens), BF16),
+        pltpu.VMEM((tokens, width), BF16),
+        pltpu.VMEM((tokens, width), BF16),
+        pltpu.VMEM((2, EXTRA, width), F32),
+    )
+    return kernel_call(down_grad_kernel, "down_grad", (out, out), (spot, *parts), 24, 5, 1, (), scratch)
+
+
+def core_sum_kernel(which, spot, own, received, *outs):
+    at = spot[which]
+    for i, out in enumerate(outs):
+        out[...] = (own[at ^ i].astype(F32) + received[at ^ i].astype(F32)).astype(BF16)
+
+
+def core_sums(spot, own, received, which, name):
+    outs = (shaped(own.shape[1:]),) * 4
+    return kernel_call(functools.partial(core_sum_kernel, which), name, outs, (spot, own, received), 16, 2, 1)
+
+
+def place_up_kernel(gathered, up_ref):
+    share = gathered.shape[3] // 2
+    for g in range(GROUPS):
+        for quarter in range(4):
+            block = gathered[g, quarter].astype(F32)
+            for core in range(2):
+                start = core * 4 * share + quarter * share
+                up_ref[g * TALL : (g + 1) * TALL, start : start + share] = block[:, core * share : (core + 1) * share]
 
 
 BIAS_ROWS = 16
@@ -505,43 +533,32 @@
     context, log_total, context_lows = attend(query, key_values, bias, chunks)
     contexts = (context_lows[0], *(places.column_swap(context_lows[i], i) for i in turns))
 
-    found = dense(spot, contexts, inputs, cotangent[0], whole, up_offset, out_matrix, up_matrix, down_matrix)
-    layer_out, one_grad, normed_low, active, second_low, inner_low, branch_low, sums = found[:8]
-    context_grads = found[8:]
+    layer_out, one_grad, context_grads, up_parts, down_parts = dense(
+        spot, contexts, inputs, cotangent[0], whole, up_offset, out_matrix, up_matrix, down_matrix
+    )
     context_grads = (context_grads[0], *(places.column_swap(context_grads[i], i) for i in turns))
+    up_parts = (up_parts[0], *(places.four_swap(up_parts[i], i) for i in turns))
+    down_parts = (down_parts[0], *(places.four_swap(down_parts[i], i) for i in turns))
 
     def to_other(block):
         return lax.ppermute(block, "shard", [(0, 1), (1, 0)])
 
-    up_part = up_grad_part(spot, normed_low, inner_low, to_other(up_grad_part(spot, normed_low, inner_low)))
-    up_grad = lax.psum(up_part, "seq").astype(F32)
-
-    down_args = (spot, active, second_low, contexts, branch_low, sums)
-    down_part = down_grad_part(*down_args, to_other(down_grad_part(*down_args)))
-
-    def four_sum(blocks):
-        total = jnp.sum(places.exchange(blocks, places.fours).astype(F32), axis=0)
-        if rest > 1:
-            total = lax.psum(total, "seq", axis_index_groups=places.rests)
-        return total.astype(BF16)
+    def total_of(pieces, swap):
+        received = [swap(pieces[i], i) for i in turns]
+        total = pieces[0].astype(F32) + sum(r.astype(F32) for r in received)
+        return lax.psum(total, "seq", axis_index_groups=places.rests) if rest > 1 else total
 
     def gather_all(part):
         column = jnp.stack([part, *(places.column_swap(part, i) for i in turns)])
         return (column, *(places.four_swap(column, i) for i in turns))
 
-    down_sum = four_sum(down_part)
-    down_sum = jnp.sum(places.exchange(down_sum, places.columns).astype(F32), axis=0)
-    down_pieces = gather_all(down_sum.astype(BF16))
-    down_grad, out_grad = kernel_call(
-        place_down_kernel,
-        "place_down",
-        (shaped((hidden_width // 2, model_width), F32), shaped((half, model_width), F32)),
-        (spot, *down_pieces),
-        24,
-        5,
-        1,
-    )
-    extra = down_sum[TALL + SHORT :]
+    other, own = up_grad_parts(spot, up_parts, model_width)
+    up_pieces = core_sums(spot, own, to_other(other), 0, "up_sum")
+    up_part = total_of(up_pieces, places.column_swap).astype(BF16)
+    other, own = down_grad_parts(spot, down_parts, model_width)
+    down_pieces = core_sums(spot, own, to_other(other), 0, "down_sum")
+    down_part = total_of(down_pieces, places.column_swap)
+    extra = down_part[TALL + SHORT :]
     up_bias_grad = jnp.concatenate([extra[6, :half], extra[7, :half], extra[0, half:], extra[1, half:]])
 
     query_grad, parts = attend_grad(query, context, context_grads, log_total, key_values, bias, chunks)
@@ -554,16 +571,36 @@
     other, own, input_parts = joined_grads(spot, query_grad, key_value_grads, column_inputs, group_weight)
     input_parts = (input_parts[0], *(places.column_swap(input_parts[i], i) for i in turns))
     input_grad = one_grad + sum(p.astype(F32) for p in input_parts)
-    joined_part = (own.astype(F32) + to_other(other).astype(F32)).astype(BF16)
-    joined_pieces = gather_all(four_sum(joined_part))
+    joined_pieces = core_sums(spot, own, to_other(other), 1, "joined_sum")
+    joined_part = total_of(joined_pieces, places.four_swap).astype(BF16)
+    up_all = lax.all_gather(up_part, "seq", axis=0, axis_index_groups=places.sixteens)
+    down_all = gather_all(down_part.astype(BF16))
+    joined_all = gather_all(joined_part)
+    down_grad, out_grad = kernel_call(
+        place_down_kernel,
+        "place_down",
+        (shaped((hidden_width // 2, model_width), F32), shaped((half, model_width), F32)),
+        (spot, *down_all),
+        24,
+        5,
+        1,
+    )
     qkv_grad, bias_grad = kernel_call(
         place_joined_kernel,
         "place_joined",
         (shaped((half, 3 * model_width), F32), shaped((8, half), F32)),
-        (spot, *joined_pieces),
+        (spot, *joined_all),
         24,
         5,
         1,
+    )
+    up_grad = kernel_call(
+        place_up_kernel,
+        "place_up",
+        shaped((half, hidden_width), F32),
+        (up_all.reshape(GROUPS, 4, TALL, hidden_width // 4),),
+        24,
+        4,
     )
 
     shape = (1, row_count, model_width)

time: 381 us -> 322 us (0.85)
  waiting for transfers between devices: 224 us -> 165 us
  starting transfers between devices: 50.8 us -> 71.2 us
  other arithmetic: 12.8 us -> 3.61 us
  local copies, waits for them, and re-layouts: 25.7 us -> 16.6 us
    psum x1 -> x0, waiting for transfers between devices: 64.5 us -> none  [body(): up_grad = lax.psum(up_part, 'seq').astype(F32)]
    ppermute x30 -> x45, waiting for transfers between devices: 121 us -> 159 us  [swap(): return lax.ppermute(block, 'seq', [(i, i ^ bits) for i in range(self.size)])]
    ppermute x30 -> x45, starting transfers between devices: 38.1 us -> 70.9 us  [swap(): return lax.ppermute(block, 'seq', [(i, i ^ bits) for i in range(self.size)])]
    all_to_all x3 -> x0, waiting for transfers between devices: 28.9 us -> none  [exchange(): lax.all_to_all(blocks, 'seq', 0, 0, axis_index_groups=groups, tiled=True)]
    all_to_all x3 -> x0, starting transfers between devices: 12 us -> none  [exchange(): lax.all_to_all(blocks, 'seq', 0, 0, axis_index_groups=groups, tiled=True)]
    unnamed x118 -> x68, local copies, waits for them, and re-layouts: 17.5 us -> 12.7 us
    convert_element_type x4 -> x3, other arithmetic: 5.41 us -> 0.93 us  [the longest x1 0.73 us: body(): up_part = total_of(up_pieces, places.column_swap).astype(BF16)]
    pallas_call x11 -> x13, Pallas kernels: 47.8 us -> 46.5 us  [kernel_call(): pl.pallas_call(kernel, out_shape=outs, in_specs=spaces, scratch_shapes=li...]
  transfers between devices with their start and end apart: 40 -> 52, of which waited for: 18 -> 24; matrix products, arithmetic and copies ran while one was open for 6% -> 2% of each run, Pallas kernels for 8% -> 9%
where the time goes in v3:
time: 322 us
  waiting for transfers between devices  165 us (51%)
  starting transfers between devices  71.2 us (22%)
  Pallas kernels  46.5 us (14%)
  local copies, waits for them, and re-layouts  16.6 us (5%)
  between operations  14.3 us (4%)
  blocking collectives  4.57 us (1%)
  other arithmetic  3.61 us (1%)
    ppermute x45, waiting for transfers between devices, swap(): return lax.ppermute(block, 'seq', [(i, i ^ bits) for i in range(self.size)])  159 us
    ppermute x45, starting transfers between devices, swap(): return lax.ppermute(block, 'seq', [(i, i ^ bits) for i in range(self.size)])  70.9 us
    pallas_call x13, Pallas kernels, kernel_call(): pl.pallas_call(kernel, out_shape=outs, in_specs=spaces, scratch_shapes=li...  46.5 us
    unnamed x68, local copies, waits for them, and re-layouts  12.7 us
  transfers between devices with their start and end apart: 52, of which 24 were waited for; matrix products, arithmetic and copies ran while one was open for 2% of the time, Pallas kernels for 9%

profile of v3, /device:TPU:0, one launch (start us, length us, event | category | flops | bytes accessed | tf_op | source)
XLA Modules:
  0.0 321.7 jit_solution(10760714955277698674)
XLA Ops:
  9.6 5.1 %collective-permute-start.2 = (bf16[128,768]{1,0:T(8,128)(2,1)S(1)}, bf16[128,768]{1,0:T(8,128)(2,1)S(1)}, u32[]{:S(2)}, u32[]{:S(2)}) collective-permute-start(bf16[128,768]{1,0:T(8,128)(2,1)S(1)} %bitcast.29), channel_id=1, source_target_pairs={{0,24},{2,26},{4,28},{6,30},{8,16},{10,18},{12,20},{14,22},{16,8},... | collective-permute-start | bytes 589832 | tf_op jit(solution)/shard_map/ppermute | solution.py:63
  15.6 1.8 all-gather.2
  17.7 1.5 constant_dynamic-slice_fusion.2
  19.3 2.8 all_gather.24.weight.rest_8_
  22.1 9.3 %collective-permute-done.1.x2.rest_6_ = bf16[128,768]{1,0:T(8,128)(2,1)S(1)} collective-permute-done((bf16[128,768]{1,0:T(8,128)(2,1)S(1)}, bf16[128,768]{1,0:T(8,128)(2,1)S(1)}, u32[]{:S(2)}, u32[]{:S(2)}) %collective-permute-start.1) | collective-permute-done | bytes 196640 | tf_op jit(solution)/shard_map/ppermute | solution.py:63
  32.3 2.5 collective-permute-start.5
  37.4 8.0 %collective-permute-done.5.refs_4_.refs_10_ = bf16[512,384]{1,0:T(8,128)(2,1)S(1)} collective-permute-done((bf16[512,384]{1,0:T(8,128)(2,1)S(1)}, bf16[512,384]{1,0:T(8,128)(2,1)S(1)}, u32[]{:S(2)}, u32[]{:S(2)}) %collective-permute-start.5) | collective-permute-done | bytes 393248 | tf_op jit(solution)/shard_map/ppermute | solution.py:63
  45.3 6.5 %collective-permute-done.4.refs_3_.refs_9_ = bf16[512,384]{1,0:T(8,128)(2,1)S(1)} collective-permute-done((bf16[512,384]{1,0:T(8,128)(2,1)S(1)}, bf16[512,384]{1,0:T(8,128)(2,1)S(1)}, u32[]{:S(2)}, u32[]{:S(2)}) %collective-permute-start.4) | collective-permute-done | bytes 393248 | tf_op jit(solution)/shard_map/ppermute | solution.py:63
  51.9 9.2 %attend.1 = (f32[512,192]{1,0:T(8,128)S(1)}, f32[512,128]{1,0:T(8,128)S(1)}, bf16[128,192]{1,0:T(8,128)(2,1)S(1)}, bf16[128,192]{1,0:T(8,128)(2,1)}, bf16[128,192]{1,0:T(8,128)(2,1)}, /*index=5*/bf16[128,192]{1,0:T(8,128)(2,1)}) custom-call(bf16[512,192]{1,0:T(8,128)(2,1)S(1)} %get-tuple-element.68.refs_0_, ...), custom_call_target="tpu_custom_call" | custom-call | bytes 31500000 | tf_op jit(solution)/shard_map/attend/pallas_call | solution.py:34
  62.6 2.8 collective-permute-start.7
  65.4 1.5 collective-permute-start.8
  67.9 3.0 collective-permute-done.7.c2
  71.9 2.3 copy-done
  74.3 1.3 copy-done.3
  76.5 11.3 %dense.1 = (bf16[128,768]{1,0:T(8,128)(2,1)}, f32[128,768]{1,0:T(8,128)S(1)}, bf16[128,192]{1,0:T(8,128)(2,1)S(1)}, bf16[128,192]{1,0:T(8,128)(2,1)S(1)}, bf16[1...) custom-call(s32[3]{0:T(128)S(1)} %pad_add_fusion.spot, ...), custom_call_target="tpu_custom_call" | custom-call | bytes 63000000 | tf_op jit(solution)/shard_map/dense/pallas_call | solution.py:34
  90.0 1.5 collective-permute-start.41
  92.1 1.4 collective-permute-start.43
  93.5 8.6 %collective-permute-done.41.p1 = bf16[128,1536]{1,0:T(8,128)(2,1)S(1)} collective-permute-done((bf16[128,1536]{1,0:T(8,128)(2,1)S(1)}, bf16[128,1536]{1,0:T(8,128)(2,1)S(1)}, u32[]{:S(2)}, u32[]{:S(2)}) %collective-permute-start.41) | collective-permute-done | bytes 393248 | tf_op jit(solution)/shard_map/ppermute | solution.py:63
  102.1 6.8 %collective-permute-done.42.p2 = bf16[128,1536]{1,0:T(8,128)(2,1)S(1)} collective-permute-done((bf16[128,1536]{1,0:T(8,128)(2,1)S(1)}, bf16[128,1536]{1,0:T(8,128)(2,1)S(1)}, u32[]{:S(2)}, u32[]{:S(2)}) %collective-permute-start.42) | collective-permute-done | bytes 393248 | tf_op jit(solution)/shard_map/ppermute | solution.py:63
  108.9 1.5 up_grad.1
  110.5 2.0 collective-permute-done.44.received
  113.2 1.5 collective-permute-start.45
  115.9 1.8 collective-permute-start.47
  117.7 3.7 %collective-permute-done.45 = bf16[96,768]{1,0:T(8,128)(2,1)S(1)} collective-permute-done((bf16[96,768]{1,0:T(8,128)(2,1)S(1)}, bf16[96,768]{1,0:T(8,128)(2,1)S(1)}, u32[]{:S(2)}, u32[]{:S(2)}) %collective-permute-start.45) | collective-permute-done | bytes 147488 | tf_op jit(solution)/shard_map/ppermute | solution.py:63
  121.4 7.3 %collective-permute-done.46 = bf16[96,768]{1,0:T(8,128)(2,1)S(1)} collective-permute-done((bf16[96,768]{1,0:T(8,128)(2,1)S(1)}, bf16[96,768]{1,0:T(8,128)(2,1)S(1)}, u32[]{:S(2)}, u32[]{:S(2)}) %collective-permute-start.46) | collective-permute-done | bytes 147488 | tf_op jit(solution)/shard_map/ppermute | solution.py:63
  130.1 1.5 collective-permute-start.29
  131.6 1.4 collective-permute-start.30
  133.0 2.6 collective-permute-start.9
  136.0 2.6 collective-permute-done.9.refs_4_
  138.7 1.3 collective-permute-start.11
  140.0 3.3 %collective-permute-done.10.refs_5_ = bf16[128,192]{1,0:T(8,128)(2,1)S(1)} collective-permute-done((bf16[128,192]{1,0:T(8,128)(2,1)S(1)}, bf16[128,192]{1,0:T(8,128)(2,1)S(1)}, u32[]{:S(2)}, u32[]{:S(2)}) %collective-permute-start.10) | collective-permute-done | bytes 49184 | tf_op jit(solution)/shard_map/ppermute | solution.py:63
  143.3 1.7 collective-permute-done.11.refs_6_
  147.9 8.0 %attend_grad.1 = (bf16[512,192]{1,0:T(8,128)(2,1)S(1)}, bf16[384,512]{1,0:T(8,128)(2,1)S(1)}, bf16[384,512]{1,0:T(8,128)(2,1)S(1)}, bf16[384,512]{1,0:T(8,128)(2,1)S(1)}, bf16[384,512]{1,0:T(8,128)(2,1)S(1)}) custom-call(bf16[512,192]{1,0:T(8,128)(2,1)S(1)} %get-tuple-element.68.refs_0_, f32[512,192]{1,0:T(8,128)S(1)} %copy-done.9, ...), custom_call_target="tpu_custom_call" | custom-call | bytes 38500000 | tf_op jit(solution)/shard_map/attend_grad/pallas_call | solution.py:34
  157.0 1.4 collective-permute-start.13
  159.4 10.7 %collective-permute-done.30.p3 = bf16[144,2560]{1,0:T(8,128)(2,1)S(1)} collective-permute-done((bf16[144,2560]{1,0:T(8,128)(2,1)}, bf16[144,2560]{1,0:T(8,128)(2,1)S(1)}, u32[]{:S(2)}, u32[]{:S(2)}) %collective-permute-start.30) | collective-permute-done | bytes 737312 | tf_op jit(solution)/shard_map/ppermute | solution.py:63
  170.1 1.8 down_grad.1
  172.0 6.7 %collective-permute-done.12.rest_1_ = bf16[384,512]{1,0:T(8,128)(2,1)S(1)} collective-permute-done((bf16[384,512]{1,0:T(8,128)(2,1)S(1)}, bf16[384,512]{1,0:T(8,128)(2,1)S(1)}, u32[]{:S(2)}, u32[]{:S(2)}) %collective-permute-start.12) | collective-permute-done | bytes 393248 | tf_op jit(solution)/shard_map/ppermute | solution.py:63
  178.7 9.1 %collective-permute-done.14.rest_3_ = bf16[384,512]{1,0:T(8,128)(2,1)S(1)} collective-permute-done((bf16[384,512]{1,0:T(8,128)(2,1)S(1)}, bf16[384,512]{1,0:T(8,128)(2,1)S(1)}, u32[]{:S(2)}, u32[]{:S(2)}) %collective-permute-start.14) | collective-permute-done | bytes 393248 | tf_op jit(solution)/shard_map/ppermute | solution.py:63
  187.8 3.0 joined_grad.1
  190.9 2.0 collective-permute-done.18.received
  193.5 3.8 %collective-permute-start.19 = (bf16[112,576]{1,0:T(8,128)(2,1)S(1)}, bf16[112,576]{1,0:T(8,128)(2,1)S(1)}, u32[]{:S(2)}, u32[]{:S(2)}) collective-permute-start(bf16[112,576]{1,0:T(8,128)(2,1)S(1)} %get-tuple-element.94), channel_id=1, source_target_pairs={{0,2},{2,0},{4,6},{6,4},{8,10},{10,8},{12,14},{14,12},{16,18},{18,... | collective-permute-start | bytes 387080 | tf_op jit(solution)/shard_map/ppermute | solution.py:63
  197.5 1.3 collective-permute-start.21
  199.6 5.5 %collective-permute-start.32 = (bf16[128,768]{1,0:T(8,128)(2,1)S(1)}, bf16[128,768]{1,0:T(8,128)(2,1)S(1)}, u32[]{:S(2)}, u32[]{:S(2)}) collective-permute-start(bf16[128,768]{1,0:T(8,128)(2,1)S(1)} %get-tuple-element.106), channel_id=1, source_target_pairs={{0,8},{2,10},{4,12},{6,14},{8,0},{10,2},{12,4},{14,6},{16,24},{18,... | collective-permute-start | bytes 589832 | tf_op jit(solution)/shard_map/ppermute | solution.py:63
  205.3 2.1 collective-permute-start.34
  207.6 1.8 collective-permute-start.24
  209.3 3.6 %collective-permute-start.23 = (bf16[112,576]{1,0:T(8,128)(2,1)S(1)}, bf16[112,576]{1,0:T(8,128)(2,1)S(1)}, u32[]{:S(2)}, u32[]{:S(2)}) collective-permute-start(bf16[112,576]{1,0:T(8,128)(2,1)S(1)} %add_convert_fusion.1), channel_id=1, source_target_pairs={{0,16},{2,18},{4,20},{6,22},{8,24},{10,26},{12,28},{14,30},{16,0},... | collective-permute-start | bytes 387080 | tf_op jit(solution)/shard_map/ppermute | solution.py:63
  212.9 16.5 %collective-permute-done.33 = bf16[128,768]{1,0:T(8,128)(2,1)S(1)} collective-permute-done((bf16[128,768]{1,0:T(8,128)(2,1)S(1)}, bf16[128,768]{1,0:T(8,128)(2,1)S(1)}, u32[]{:S(2)}, u32[]{:S(2)}) %collective-permute-start.33) | collective-permute-done | bytes 196640 | tf_op jit(solution)/shard_map/ppermute | solution.py:63
  229.5 1.3 collective-permute-start.37
  230.8 12.1 %collective-permute-done.23 = bf16[112,576]{1,0:T(8,128)(2,1)S(1)} collective-permute-done((bf16[112,576]{1,0:T(8,128)(2,1)S(1)}, bf16[112,576]{1,0:T(8,128)(2,1)S(1)}, u32[]{:S(2)}, u32[]{:S(2)}) %collective-permute-start.23) | collective-permute-done | bytes 129056 | tf_op jit(solution)/shard_map/ppermute | solution.py:63
  243.1 1.7 collective-permute-start.27
  244.8 2.0 collective-permute-start.35
  246.9 3.5 %collective-permute-start.16 = (bf16[128,768]{1,0:T(8,128)(2,1)S(1)}, bf16[128,768]{1,0:T(8,128)(2,1)S(1)}, u32[]{:S(2)}, u32[]{:S(2)}) collective-permute-start(bf16[128,768]{1,0:T(8,128)(2,1)S(1)} %get-tuple-element.89), channel_id=1, source_target_pairs={{0,16},{2,18},{4,20},{6,22},{8,24},{10,26},{12,28},{14,30},{16,0},... | collective-permute-start | bytes 589832 | tf_op jit(solution)/shard_map/ppermute | solution.py:63
  250.4 7.6 %collective-permute-done.36 = bf16[128,768]{1,0:T(8,128)(2,1)S(1)} collective-permute-done((bf16[128,768]{1,0:T(8,128)(2,1)S(1)}, bf16[128,768]{1,0:T(8,128)(2,1)S(1)}, u32[]{:S(2)}, u32[]{:S(2)}) %collective-permute-start.36) | collective-permute-done | bytes 196640 | tf_op jit(solution)/shard_map/ppermute | solution.py:63
  258.0 1.4 collective-permute-start.17
  259.5 1.5 collective-permute-start.40
  260.9 4.2 %collective-permute-start.39 = (bf16[4,128,768]{2,1,0:T(8,128)(2,1)S(1)}, bf16[4,128,768]{2,1,0:T(8,128)(2,1)S(1)}, u32[]{:S(2)}, u32[]{:S(2)}) collective-permute-start(bf16[4,128,768]{2,1,0:T(8,128)(2,1)S(1)} %pad_maximum_fusion.p0), channel_id=1, source_target_pairs={{0,4},{2,6},{4,0},{6,2},{8,12},{10,14},{12,8},{14,10},{16,20},{18,... | collective-permute-start | bytes 2359304 | tf_op jit(solution)/shard_map/ppermute | solution.py:63
  265.2 3.1 collective-permute-done.16
  268.3 1.7 collective-permute-start.38
  270.0 1.7 collective-permute-start.26
  273.8 30.3 %collective-permute-done.26.p2 = bf16[4,112,576]{2,1,0:T(8,128)(2,1)S(1)} collective-permute-done((bf16[4,112,576]{2,1,0:T(8,128)(2,1)S(1)}, bf16[4,112,576]{2,1,0:T(8,128)(2,1)S(1)}, u32[]{:S(2)}, u32[]{:S(2)}) %collective-permute-start.26) | collective-permute-done | bytes 516128 | tf_op jit(solution)/shard_map/ppermute | solution.py:63
  304.1 2.8 place_joined.1
  307.5 3.5 %place_down.1 = (f32[1536,768]{1,0:T(8,128)}, f32[384,768]{1,0:T(8,128)}) custom-call(s32[3]{0:T(128)S(1)} %pad_add_fusion.spot, bf16[4,128,768]{2,1,0:T(8,128)(2,1)S(1)} %pad_maximum_fusion.p0, bf16[4,128,768]{2,1,0:T(8,128)(2,1)S(1)} %collective-permute-done.38.p1, bf16[4,128,768]{2,1,0:T(8,128)(2,1)S(1)} %collective-permute-done.39.p2, ...), custom_call_target="tpu_custom_call" | custom-call | bytes 17500000 | tf_op jit(solution)/shard_map/place_down/pallas_call | solution.py:34
  311.0 1.7 copy-done.1
  312.7 2.5 place_up.1
  (171 shorter events, 28.1 us)
Async XLA Ops:
  7.2 64.8 %all-gather.8.cloned.1.call-start = ((), (), s32[]{:S(2)}) async-start(), calls=%async_computation | async-start | bytes 1769472 | tf_op jit(solution)/shard_map/all_gather | solution.py:491
  8.0 7.5 %copy-start.24 = (bf16[1536]{0:T(1024)(128)(2,1)S(1)}, bf16[1536]{0:T(1024)(128)(2,1)}, u32[]{:S(2)}) copy-start(bf16[1536]{0:T(1024)(128)(2,1)} %param.27) | copy-start | bytes 9220
  8.0 63.9 %all-gather.10.cloned.1.call-start = ((), (), s32[]{:S(2)}) async-start(), calls=%async_computation.1 | async-start | bytes 7077888 | tf_op jit(solution)/shard_map/all_gather | solution.py:491
  8.8 63.2 %all-gather.12.cloned.1.call-start = ((), (), s32[]{:S(2)}) async-start(), calls=%async_computation.2 | async-start | bytes 7077888 | tf_op jit(solution)/shard_map/all_gather | solution.py:491
  9.5 301.5 %all-gather.14.cloned.1.call-start = ((), (), s32[]{:S(2)}) async-start(), calls=%async_computation.3 | async-start | bytes 2506752 | tf_op jit(solution)/shard_map/all_gather | solution.py:576
  9.6 12.5 %collective-permute-start.2 = (bf16[128,768]{1,0:T(8,128)(2,1)S(1)}, bf16[128,768]{1,0:T(8,128)(2,1)S(1)}, u32[]{:S(2)}, u32[]{:S(2)}) collective-permute-start(bf16[128,768]{1,0:T(8,128)(2,1)S(1)} %bitcast.29), channel_id=1, source_target_pairs={{0,24},{2,26},{4,28},{6,30},{8,16},{10,18},{12,20},{14,22},{16,8},... | collective-permute-start | bytes 589832 | tf_op jit(solution)/shard_map/ppermute | solution.py:63
  14.7 16.7 %collective-permute-start.1 = (bf16[128,768]{1,0:T(8,128)(2,1)S(1)}, bf16[128,768]{1,0:T(8,128)(2,1)S(1)}, u32[]{:S(2)}, u32[]{:S(2)}) collective-permute-start(bf16[128,768]{1,0:T(8,128)(2,1)S(1)} %bitcast.30), channel_id=1, source_target_pairs={{0,16},{2,18},{4,20},{6,22},{8,24},{10,26},{12,28},{14,30},{16,0},... | collective-permute-start | bytes 589832 | tf_op jit(solution)/shard_map/ppermute | solution.py:63
  14.7 16.7 %collective-permute-start = (bf16[128,768]{1,0:T(8,128)(2,1)S(1)}, bf16[128,768]{1,0:T(8,128)(2,1)S(1)}, u32[]{:S(2)}, u32[]{:S(2)}) collective-permute-start(bf16[128,768]{1,0:T(8,128)(2,1)S(1)} %bitcast.31), channel_id=1, source_target_pairs={{0,8},{2,10},{4,12},{6,14},{8,0},{10,2},{12,4},{14,6},{16,24},{18,... | collective-permute-start | bytes 589832 | tf_op jit(solution)/shard_map/ppermute | solution.py:63
  19.1 16.7 %copy-start.33 = (s32[2]{0:T(128)S(1)}, s32[2]{0:T(128)}, u32[]{:S(2)}) copy-start(s32[2]{0:T(128)} %param.18) | copy-start | bytes 28
  32.3 13.1 %collective-permute-start.5 = (bf16[512,384]{1,0:T(8,128)(2,1)S(1)}, bf16[512,384]{1,0:T(8,128)(2,1)S(1)}, u32[]{:S(2)}, u32[]{:S(2)}) collective-permute-start(bf16[512,384]{1,0:T(8,128)(2,1)S(1)} %get-tuple-element.69.refs_1_.refs_7_), channel_id=1, source_target_pairs={{0,6},{2,4},{4,2},{6,0},{8,14},{10,12},{12,10},{14,8},{16,22},{18,... | collective-permute-start | bytes 1179656 | tf_op jit(solution)/shard_map/ppermute | solution.py:63
  34.8 17.0 %collective-permute-start.4 = (bf16[512,384]{1,0:T(8,128)(2,1)S(1)}, bf16[512,384]{1,0:T(8,128)(2,1)S(1)}, u32[]{:S(2)}, u32[]{:S(2)}) collective-permute-start(bf16[512,384]{1,0:T(8,128)(2,1)S(1)} %get-tuple-element.69.refs_1_.refs_7_), channel_id=1, source_target_pairs={{0,4},{2,6},{4,0},{6,2},{8,12},{10,14},{12,8},{14,10},{16,20},{18,... | collective-permute-start | bytes 1179656 | tf_op jit(solution)/shard_map/ppermute | solution.py:63
  35.3 16.6 %collective-permute-start.3 = (bf16[512,384]{1,0:T(8,128)(2,1)S(1)}, bf16[512,384]{1,0:T(8,128)(2,1)S(1)}, u32[]{:S(2)}, u32[]{:S(2)}) collective-permute-start(bf16[512,384]{1,0:T(8,128)(2,1)S(1)} %get-tuple-element.69.refs_1_.refs_7_), channel_id=1, source_target_pairs={{0,2},{2,0},{4,6},{6,4},{8,10},{10,8},{12,14},{14,12},{16,18},{18,... | collective-permute-start | bytes 1179656 | tf_op jit(solution)/shard_map/ppermute | solution.py:63
  62.6 5.3 %collective-permute-start.6 = (bf16[128,192]{1,0:T(8,128)(2,1)}, bf16[128,192]{1,0:T(8,128)(2,1)}, u32[]{:S(2)}, u32[]{:S(2)}) collective-permute-start(bf16[128,192]{1,0:T(8,128)(2,1)} %get-tuple-element.71), channel_id=1, source_target_pairs={{0,8},{2,10},{4,12},{6,14},{8,0},{10,2},{12,4},{14,6},{16,24},{18,... | collective-permute-start | bytes 147464 | tf_op jit(solution)/shard_map/ppermute | solution.py:63
  62.6 8.2 %collective-permute-start.7 = (bf16[128,192]{1,0:T(8,128)(2,1)}, bf16[128,192]{1,0:T(8,128)(2,1)}, u32[]{:S(2)}, u32[]{:S(2)}) collective-permute-start(bf16[128,192]{1,0:T(8,128)(2,1)} %get-tuple-element.72), channel_id=1, source_target_pairs={{0,16},{2,18},{4,20},{6,22},{8,24},{10,26},{12,28},{14,30},{16,0},... | collective-permute-start | bytes 147464 | tf_op jit(solution)/shard_map/ppermute | solution.py:63
  65.4 6.5 %collective-permute-start.8 = (bf16[128,192]{1,0:T(8,128)(2,1)}, bf16[128,192]{1,0:T(8,128)(2,1)}, u32[]{:S(2)}, u32[]{:S(2)}) collective-permute-start(bf16[128,192]{1,0:T(8,128)(2,1)} %get-tuple-element.73), channel_id=1, source_target_pairs={{0,24},{2,26},{4,28},{6,30},{8,16},{10,18},{12,20},{14,22},{16,8},... | collective-permute-start | bytes 147464 | tf_op jit(solution)/shard_map/ppermute | solution.py:63
  89.9 23.3 %copy-start.10 = (f32[128,768]{1,0:T(8,128)}, f32[128,768]{1,0:T(8,128)S(1)}, u32[]{:S(2)}) copy-start(f32[128,768]{1,0:T(8,128)S(1)} %get-tuple-element.75) | copy-start | bytes 1179652
  89.9 23.3 %copy-start.15 = (bf16[128,192]{1,0:T(8,128)(2,1)}, bf16[128,192]{1,0:T(8,128)(2,1)S(1)}, u32[]{:S(2)}) copy-start(bf16[128,192]{1,0:T(8,128)(2,1)S(1)} %get-tuple-element.78.refs_3_) | copy-start | bytes 147460
  89.9 24.8 %copy-start.17 = (bf16[144,2560]{1,0:T(8,128)(2,1)}, bf16[144,2560]{1,0:T(8,128)(2,1)S(1)}, u32[]{:S(2)}) copy-start(bf16[144,2560]{1,0:T(8,128)(2,1)S(1)} %get-tuple-element.102) | copy-start | bytes 2211844
  89.9 24.8 %copy-start.18 = (bf16[144,2560]{1,0:T(8,128)(2,1)}, bf16[144,2560]{1,0:T(8,128)(2,1)S(1)}, u32[]{:S(2)}) copy-start(bf16[144,2560]{1,0:T(8,128)(2,1)S(1)} %get-tuple-element.101) | copy-start | bytes 2211844
  89.9 26.0 %copy-start.19 = (bf16[144,2560]{1,0:T(8,128)(2,1)}, bf16[144,2560]{1,0:T(8,128)(2,1)S(1)}, u32[]{:S(2)}) copy-start(bf16[144,2560]{1,0:T(8,128)(2,1)S(1)} %get-tuple-element.100) | copy-start | bytes 2211844
  89.9 38.8 %copy-start.20 = (bf16[128,192]{1,0:T(8,128)(2,1)}, bf16[128,192]{1,0:T(8,128)(2,1)S(1)}, u32[]{:S(2)}) copy-start(bf16[128,192]{1,0:T(8,128)(2,1)S(1)} %get-tuple-element.81) | copy-start | bytes 147460
  90.0 45.7 %copy-start.22 = (bf16[128,192]{1,0:T(8,128)(2,1)S(1)}, bf16[128,192]{1,0:T(8,128)(2,1)}, u32[]{:S(2)}) copy-start(bf16[128,192]{1,0:T(8,128)(2,1)} %copy-done.21) | copy-start | bytes 147460
  90.0 12.1 %collective-permute-start.41 = (bf16[128,1536]{1,0:T(8,128)(2,1)S(1)}, bf16[128,1536]{1,0:T(8,128)(2,1)S(1)}, u32[]{:S(2)}, u32[]{:S(2)}) collective-permute-start(bf16[128,1536]{1,0:T(8,128)(2,1)S(1)} %get-tuple-element.111), channel_id=1, source_target_pairs={{0,2},{2,0},{4,6},{6,4},{8,10},{10,8},{12,14},{14,12},{16,18},{18,... | collective-permute-start | bytes 1179656 | tf_op jit(solution)/shard_map/ppermute | solution.py:63
  91.5 17.4 %collective-permute-start.42 = (bf16[128,1536]{1,0:T(8,128)(2,1)S(1)}, bf16[128,1536]{1,0:T(8,128)(2,1)S(1)}, u32[]{:S(2)}, u32[]{:S(2)}) collective-permute-start(bf16[128,1536]{1,0:T(8,128)(2,1)S(1)} %get-tuple-element.112), channel_id=1, source_target_pairs={{0,4},{2,6},{4,0},{6,2},{8,12},{10,14},{12,8},{14,10},{16,20},{18,... | collective-permute-start | bytes 1179656 | tf_op jit(solution)/shard_map/ppermute | solution.py:63
  92.1 16.8 %collective-permute-start.43 = (bf16[128,1536]{1,0:T(8,128)(2,1)S(1)}, bf16[128,1536]{1,0:T(8,128)(2,1)S(1)}, u32[]{:S(2)}, u32[]{:S(2)}) collective-permute-start(bf16[128,1536]{1,0:T(8,128)(2,1)S(1)} %get-tuple-element.113), channel_id=1, source_target_pairs={{0,6},{2,4},{4,2},{6,0},{8,14},{10,12},{12,10},{14,8},{16,22},{18,... | collective-permute-start | bytes 1179656 | tf_op jit(solution)/shard_map/ppermute | solution.py:63
  110.4 2.1 collective-permute-start.44
  113.2 8.2 %collective-permute-start.45 = (bf16[96,768]{1,0:T(8,128)(2,1)S(1)}, bf16[96,768]{1,0:T(8,128)(2,1)S(1)}, u32[]{:S(2)}, u32[]{:S(2)}) collective-permute-start(bf16[96,768]{1,0:T(8,128)(2,1)S(1)} %get-tuple-element.117), channel_id=1, source_target_pairs={{0,8},{2,10},{4,12},{6,14},{8,0},{10,2},{12,4},{14,6},{16,24},{18,... | collective-permute-start | bytes 442376 | tf_op jit(solution)/shard_map/ppermute | solution.py:63
  114.8 13.9 %collective-permute-start.46 = (bf16[96,768]{1,0:T(8,128)(2,1)S(1)}, bf16[96,768]{1,0:T(8,128)(2,1)S(1)}, u32[]{:S(2)}, u32[]{:S(2)}) collective-permute-start(bf16[96,768]{1,0:T(8,128)(2,1)S(1)} %get-tuple-element.118), channel_id=1, source_target_pairs={{0,16},{2,18},{4,20},{6,22},{8,24},{10,26},{12,28},{14,30},{16,0},... | collective-permute-start | bytes 442376 | tf_op jit(solution)/shard_map/ppermute | solution.py:63
  115.9 12.8 %collective-permute-start.47 = (bf16[96,768]{1,0:T(8,128)(2,1)S(1)}, bf16[96,768]{1,0:T(8,128)(2,1)S(1)}, u32[]{:S(2)}, u32[]{:S(2)}) collective-permute-start(bf16[96,768]{1,0:T(8,128)(2,1)S(1)} %get-tuple-element.119), channel_id=1, source_target_pairs={{0,24},{2,26},{4,28},{6,30},{8,16},{10,18},{12,20},{14,22},{16,8},... | collective-permute-start | bytes 442376 | tf_op jit(solution)/shard_map/ppermute | solution.py:63
  129.5 40.7 %copy-start.7 = (bf16[144,2560]{1,0:T(8,128)(2,1)S(1)}, bf16[144,2560]{1,0:T(8,128)(2,1)}, u32[]{:S(2)}) copy-start(bf16[144,2560]{1,0:T(8,128)(2,1)} %copy-done.6) | copy-start | bytes 2211844
  129.5 28.9 %collective-permute-start.28 = (bf16[144,2560]{1,0:T(8,128)(2,1)}, bf16[144,2560]{1,0:T(8,128)(2,1)S(1)}, u32[]{:S(2)}, u32[]{:S(2)}) collective-permute-start(bf16[144,2560]{1,0:T(8,128)(2,1)} %copy-done.19), channel_id=1, source_target_pairs={{0,2},{2,0},{4,6},{6,4},{8,10},{10,8},{12,14},{14,12},{16,18},{18,... | collective-permute-start | bytes 2211848 | tf_op jit(solution)/shard_map/ppermute | solution.py:63
  130.1 29.3 %collective-permute-start.29 = (bf16[144,2560]{1,0:T(8,128)(2,1)}, bf16[144,2560]{1,0:T(8,128)(2,1)S(1)}, u32[]{:S(2)}, u32[]{:S(2)}) collective-permute-start(bf16[144,2560]{1,0:T(8,128)(2,1)} %copy-done.18), channel_id=1, source_target_pairs={{0,4},{2,6},{4,0},{6,2},{8,12},{10,14},{12,8},{14,10},{16,20},{18,... | collective-permute-start | bytes 2211848 | tf_op jit(solution)/shard_map/ppermute | solution.py:63
  131.6 38.5 %collective-permute-start.30 = (bf16[144,2560]{1,0:T(8,128)(2,1)}, bf16[144,2560]{1,0:T(8,128)(2,1)S(1)}, u32[]{:S(2)}, u32[]{:S(2)}) collective-permute-start(bf16[144,2560]{1,0:T(8,128)(2,1)} %copy-done.17), channel_id=1, source_target_pairs={{0,6},{2,4},{4,2},{6,0},{8,14},{10,12},{12,10},{14,8},{16,22},{18,... | collective-permute-start | bytes 2211848 | tf_op jit(solution)/shard_map/ppermute | solution.py:63
  133.0 5.6 %collective-permute-start.9 = (bf16[128,192]{1,0:T(8,128)(2,1)}, bf16[128,192]{1,0:T(8,128)(2,1)S(1)}, u32[]{:S(2)}, u32[]{:S(2)}) collective-permute-start(bf16[128,192]{1,0:T(8,128)(2,1)} %copy-done.23), channel_id=1, source_target_pairs={{0,8},{2,10},{4,12},{6,14},{8,0},{10,2},{12,4},{14,6},{16,24},{18,... | collective-permute-start | bytes 147464 | tf_op jit(solution)/shard_map/ppermute | solution.py:63
  135.7 7.7 %collective-permute-start.10 = (bf16[128,192]{1,0:T(8,128)(2,1)S(1)}, bf16[128,192]{1,0:T(8,128)(2,1)S(1)}, u32[]{:S(2)}, u32[]{:S(2)}) collective-permute-start(bf16[128,192]{1,0:T(8,128)(2,1)S(1)} %copy-done.22), channel_id=1, source_target_pairs={{0,16},{2,18},{4,20},{6,22},{8,24},{10,26},{12,28},{14,30},{16,0},... | collective-permute-start | bytes 147464 | tf_op jit(solution)/shard_map/ppermute | solution.py:63
  138.7 6.4 %collective-permute-start.11 = (bf16[128,192]{1,0:T(8,128)(2,1)}, bf16[128,192]{1,0:T(8,128)(2,1)S(1)}, u32[]{:S(2)}, u32[]{:S(2)}) collective-permute-start(bf16[128,192]{1,0:T(8,128)(2,1)} %copy-done.20), channel_id=1, source_target_pairs={{0,24},{2,26},{4,28},{6,30},{8,16},{10,18},{12,20},{14,22},{16,8},... | collective-permute-start | bytes 147464 | tf_op jit(solution)/shard_map/ppermute | solution.py:63
  147.9 39.9 %copy-start.5 = (bf16[128,768]{1,0:T(8,128)(2,1)S(1)}, bf16[128,768]{1,0:T(8,128)(2,1)}, u32[]{:S(2)}) copy-start(bf16[128,768]{1,0:T(8,128)(2,1)} %copy-done.4) | copy-start | bytes 589828
  155.8 22.9 %collective-permute-start.12 = (bf16[384,512]{1,0:T(8,128)(2,1)S(1)}, bf16[384,512]{1,0:T(8,128)(2,1)S(1)}, u32[]{:S(2)}, u32[]{:S(2)}) collective-permute-start(bf16[384,512]{1,0:T(8,128)(2,1)S(1)} %get-tuple-element.84), channel_id=1, source_target_pairs={{0,2},{2,0},{4,6},{6,4},{8,10},{10,8},{12,14},{14,12},{16,18},{18,... | collective-permute-start | bytes 1179656 | tf_op jit(solution)/shard_map/ppermute | solution.py:63
  157.0 21.7 %collective-permute-start.13 = (bf16[384,512]{1,0:T(8,128)(2,1)S(1)}, bf16[384,512]{1,0:T(8,128)(2,1)S(1)}, u32[]{:S(2)}, u32[]{:S(2)}) collective-permute-start(bf16[384,512]{1,0:T(8,128)(2,1)S(1)} %get-tuple-element.85), channel_id=1, source_target_pairs={{0,4},{2,6},{4,0},{6,2},{8,12},{10,14},{12,8},{14,10},{16,20},{18,... | collective-permute-start | bytes 1179656 | tf_op jit(solution)/shard_map/ppermute | solution.py:63
  158.4 29.4 %collective-permute-start.14 = (bf16[384,512]{1,0:T(8,128)(2,1)S(1)}, bf16[384,512]{1,0:T(8,128)(2,1)S(1)}, u32[]{:S(2)}, u32[]{:S(2)}) collective-permute-start(bf16[384,512]{1,0:T(8,128)(2,1)S(1)} %get-tuple-element.86), channel_id=1, source_target_pairs={{0,6},{2,4},{4,2},{6,0},{8,14},{10,12},{12,10},{14,8},{16,22},{18,... | collective-permute-start | bytes 1179656 | tf_op jit(solution)/shard_map/ppermute | solution.py:63
  172.0 26.9 %collective-permute-start.31 = (bf16[4,128,768]{2,1,0:T(8,128)(2,1)S(1)}, bf16[4,128,768]{2,1,0:T(8,128)(2,1)S(1)}, u32[]{:S(2)}, u32[]{:S(2)}) collective-permute-start(bf16[4,128,768]{2,1,0:T(8,128)(2,1)S(1)} %get-tuple-element.104), channel_id=1, source_target_pairs={{0,1},{1,0},{2,3},{3,2},{4,5},{5,4},{6,7},{7,6},{8,9},{9,8},{10,11... | collective-permute-start | bytes 2359304 | tf_op jit(solution)/shard_map/ppermute | solution.py:544
  190.8 2.0 collective-permute-start.18
  193.5 11.8 %collective-permute-start.19 = (bf16[112,576]{1,0:T(8,128)(2,1)S(1)}, bf16[112,576]{1,0:T(8,128)(2,1)S(1)}, u32[]{:S(2)}, u32[]{:S(2)}) collective-permute-start(bf16[112,576]{1,0:T(8,128)(2,1)S(1)} %get-tuple-element.94), channel_id=1, source_target_pairs={{0,2},{2,0},{4,6},{6,4},{8,10},{10,8},{12,14},{14,12},{16,18},{18,... | collective-permute-start | bytes 387080 | tf_op jit(solution)/shard_map/ppermute | solution.py:63
  197.3 10.2 %collective-permute-start.20 = (bf16[112,576]{1,0:T(8,128)(2,1)S(1)}, bf16[112,576]{1,0:T(8,128)(2,1)S(1)}, u32[]{:S(2)}, u32[]{:S(2)}) collective-permute-start(bf16[112,576]{1,0:T(8,128)(2,1)S(1)} %get-tuple-element.95), channel_id=1, source_target_pairs={{0,4},{2,6},{4,0},{6,2},{8,12},{10,14},{12,8},{14,10},{16,20},{18,... | collective-permute-start | bytes 387080 | tf_op jit(solution)/shard_map/ppermute | solution.py:63
  197.5 10.0 %collective-permute-start.21 = (bf16[112,576]{1,0:T(8,128)(2,1)S(1)}, bf16[112,576]{1,0:T(8,128)(2,1)S(1)}, u32[]{:S(2)}, u32[]{:S(2)}) collective-permute-start(bf16[112,576]{1,0:T(8,128)(2,1)S(1)} %get-tuple-element.96), channel_id=1, source_target_pairs={{0,6},{2,4},{4,2},{6,0},{8,14},{10,12},{12,10},{14,8},{16,22},{18,... | collective-permute-start | bytes 387080 | tf_op jit(solution)/shard_map/ppermute | solution.py:63
  199.6 13.4 %collective-permute-start.32 = (bf16[128,768]{1,0:T(8,128)(2,1)S(1)}, bf16[128,768]{1,0:T(8,128)(2,1)S(1)}, u32[]{:S(2)}, u32[]{:S(2)}) collective-permute-start(bf16[128,768]{1,0:T(8,128)(2,1)S(1)} %get-tuple-element.106), channel_id=1, source_target_pairs={{0,8},{2,10},{4,12},{6,14},{8,0},{10,2},{12,4},{14,6},{16,24},{18,... | collective-permute-start | bytes 589832 | tf_op jit(solution)/shard_map/ppermute | solution.py:63
  205.0 24.4 %collective-permute-start.33 = (bf16[128,768]{1,0:T(8,128)(2,1)S(1)}, bf16[128,768]{1,0:T(8,128)(2,1)S(1)}, u32[]{:S(2)}, u32[]{:S(2)}) collective-permute-start(bf16[128,768]{1,0:T(8,128)(2,1)S(1)} %get-tuple-element.107), channel_id=1, source_target_pairs={{0,16},{2,18},{4,20},{6,22},{8,24},{10,26},{12,28},{14,30},{16,0},... | collective-permute-start | bytes 589832 | tf_op jit(solution)/shard_map/ppermute | solution.py:63
  205.3 24.1 %collective-permute-start.34 = (bf16[128,768]{1,0:T(8,128)(2,1)S(1)}, bf16[128,768]{1,0:T(8,128)(2,1)S(1)}, u32[]{:S(2)}, u32[]{:S(2)}) collective-permute-start(bf16[128,768]{1,0:T(8,128)(2,1)S(1)} %get-tuple-element.108), channel_id=1, source_target_pairs={{0,24},{2,26},{4,28},{6,30},{8,16},{10,18},{12,20},{14,22},{16,8},... | collective-permute-start | bytes 589832 | tf_op jit(solution)/shard_map/ppermute | solution.py:63
  207.5 64.2 %copy-start.11 = (f32[128,768]{1,0:T(8,128)S(1)}, f32[128,768]{1,0:T(8,128)}, u32[]{:S(2)}) copy-start(f32[128,768]{1,0:T(8,128)} %copy-done.10) | copy-start | bytes 1179652
  207.6 23.3 %collective-permute-start.24 = (bf16[112,576]{1,0:T(8,128)(2,1)S(1)}, bf16[112,576]{1,0:T(8,128)(2,1)S(1)}, u32[]{:S(2)}, u32[]{:S(2)}) collective-permute-start(bf16[112,576]{1,0:T(8,128)(2,1)S(1)} %add_convert_fusion.1), channel_id=1, source_target_pairs={{0,24},{2,26},{4,28},{6,30},{8,16},{10,18},{12,20},{14,22},{16,8},... | collective-permute-start | bytes 387080 | tf_op jit(solution)/shard_map/ppermute | solution.py:63
  209.3 33.6 %collective-permute-start.23 = (bf16[112,576]{1,0:T(8,128)(2,1)S(1)}, bf16[112,576]{1,0:T(8,128)(2,1)S(1)}, u32[]{:S(2)}, u32[]{:S(2)}) collective-permute-start(bf16[112,576]{1,0:T(8,128)(2,1)S(1)} %add_convert_fusion.1), channel_id=1, source_target_pairs={{0,16},{2,18},{4,20},{6,22},{8,24},{10,26},{12,28},{14,30},{16,0},... | collective-permute-start | bytes 387080 | tf_op jit(solution)/shard_map/ppermute | solution.py:63
  212.9 30.1 %collective-permute-start.22 = (bf16[112,576]{1,0:T(8,128)(2,1)S(1)}, bf16[112,576]{1,0:T(8,128)(2,1)S(1)}, u32[]{:S(2)}, u32[]{:S(2)}) collective-permute-start(bf16[112,576]{1,0:T(8,128)(2,1)S(1)} %add_convert_fusion.1), channel_id=1, source_target_pairs={{0,8},{2,10},{4,12},{6,14},{8,0},{10,2},{12,4},{14,6},{16,24},{18,... | collective-permute-start | bytes 387080 | tf_op jit(solution)/shard_map/ppermute | solution.py:63
  229.5 17.4 %collective-permute-start.37 = (bf16[128,768]{1,0:T(8,128)(2,1)S(1)}, bf16[128,768]{1,0:T(8,128)(2,1)S(1)}, u32[]{:S(2)}, u32[]{:S(2)}) collective-permute-start(bf16[128,768]{1,0:T(8,128)(2,1)S(1)} %get-tuple-element.135), channel_id=1, source_target_pairs={{0,24},{2,26},{4,28},{6,30},{8,16},{10,18},{12,20},{14,22},{16,8},... | collective-permute-start | bytes 589832 | tf_op jit(solution)/shard_map/ppermute | solution.py:63
  243.1 28.6 %collective-permute-start.27 = (bf16[4,112,576]{2,1,0:T(8,128)(2,1)S(1)}, bf16[4,112,576]{2,1,0:T(8,128)(2,1)S(1)}, u32[]{:S(2)}, u32[]{:S(2)}) collective-permute-start(bf16[4,112,576]{2,1,0:T(8,128)(2,1)S(1)} %pad_maximum_fusion.1.p0), channel_id=1, source_target_pairs={{0,6},{2,4},{4,2},{6,0},{8,14},{10,12},{12,10},{14,8},{16,22},{18,... | collective-permute-start | bytes 1548296 | tf_op jit(solution)/shard_map/ppermute | solution.py:63
  244.8 13.2 %collective-permute-start.36 = (bf16[128,768]{1,0:T(8,128)(2,1)S(1)}, bf16[128,768]{1,0:T(8,128)(2,1)S(1)}, u32[]{:S(2)}, u32[]{:S(2)}) collective-permute-start(bf16[128,768]{1,0:T(8,128)(2,1)S(1)} %get-tuple-element.135), channel_id=1, source_target_pairs={{0,16},{2,18},{4,20},{6,22},{8,24},{10,26},{12,28},{14,30},{16,0},... | collective-permute-start | bytes 589832 | tf_op jit(solution)/shard_map/ppermute | solution.py:63
  244.8 14.6 %collective-permute-start.35 = (bf16[128,768]{1,0:T(8,128)(2,1)S(1)}, bf16[128,768]{1,0:T(8,128)(2,1)S(1)}, u32[]{:S(2)}, u32[]{:S(2)}) collective-permute-start(bf16[128,768]{1,0:T(8,128)(2,1)S(1)} %get-tuple-element.135), channel_id=1, source_target_pairs={{0,8},{2,10},{4,12},{6,14},{8,0},{10,2},{12,4},{14,6},{16,24},{18,... | collective-permute-start | bytes 589832 | tf_op jit(solution)/shard_map/ppermute | solution.py:63
  246.8 14.1 %collective-permute-start.15 = (bf16[128,768]{1,0:T(8,128)(2,1)S(1)}, bf16[128,768]{1,0:T(8,128)(2,1)S(1)}, u32[]{:S(2)}, u32[]{:S(2)}) collective-permute-start(bf16[128,768]{1,0:T(8,128)(2,1)S(1)} %get-tuple-element.88), channel_id=1, source_target_pairs={{0,8},{2,10},{4,12},{6,14},{8,0},{10,2},{12,4},{14,6},{16,24},{18,... | collective-permute-start | bytes 589832 | tf_op jit(solution)/shard_map/ppermute | solution.py:63
  246.9 21.4 %collective-permute-start.16 = (bf16[128,768]{1,0:T(8,128)(2,1)S(1)}, bf16[128,768]{1,0:T(8,128)(2,1)S(1)}, u32[]{:S(2)}, u32[]{:S(2)}) collective-permute-start(bf16[128,768]{1,0:T(8,128)(2,1)S(1)} %get-tuple-element.89), channel_id=1, source_target_pairs={{0,16},{2,18},{4,20},{6,22},{8,24},{10,26},{12,28},{14,30},{16,0},... | collective-permute-start | bytes 589832 | tf_op jit(solution)/shard_map/ppermute | solution.py:63
  258.0 12.0 %collective-permute-start.17 = (bf16[128,768]{1,0:T(8,128)(2,1)S(1)}, bf16[128,768]{1,0:T(8,128)(2,1)S(1)}, u32[]{:S(2)}, u32[]{:S(2)}) collective-permute-start(bf16[128,768]{1,0:T(8,128)(2,1)S(1)} %get-tuple-element.90), channel_id=1, source_target_pairs={{0,24},{2,26},{4,28},{6,30},{8,16},{10,18},{12,20},{14,22},{16,8},... | collective-permute-start | bytes 589832 | tf_op jit(solution)/shard_map/ppermute | solution.py:63
  259.5 48.1 %collective-permute-start.40 = (bf16[4,128,768]{2,1,0:T(8,128)(2,1)S(1)}, bf16[4,128,768]{2,1,0:T(8,128)(2,1)S(1)}, u32[]{:S(2)}, u32[]{:S(2)}) collective-permute-start(bf16[4,128,768]{2,1,0:T(8,128)(2,1)S(1)} %pad_maximum_fusion.p0), channel_id=1, source_target_pairs={{0,6},{2,4},{4,2},{6,0},{8,14},{10,12},{12,10},{14,8},{16,22},{18,... | collective-permute-start | bytes 2359304 | tf_op jit(solution)/shard_map/ppermute | solution.py:63
  260.9 46.6 %collective-permute-start.39 = (bf16[4,128,768]{2,1,0:T(8,128)(2,1)S(1)}, bf16[4,128,768]{2,1,0:T(8,128)(2,1)S(1)}, u32[]{:S(2)}, u32[]{:S(2)}) collective-permute-start(bf16[4,128,768]{2,1,0:T(8,128)(2,1)S(1)} %pad_maximum_fusion.p0), channel_id=1, source_target_pairs={{0,4},{2,6},{4,0},{6,2},{8,12},{10,14},{12,8},{14,10},{16,20},{18,... | collective-permute-start | bytes 2359304 | tf_op jit(solution)/shard_map/ppermute | solution.py:63
  268.3 39.3 %collective-permute-start.38 = (bf16[4,128,768]{2,1,0:T(8,128)(2,1)S(1)}, bf16[4,128,768]{2,1,0:T(8,128)(2,1)S(1)}, u32[]{:S(2)}, u32[]{:S(2)}) collective-permute-start(bf16[4,128,768]{2,1,0:T(8,128)(2,1)S(1)} %pad_maximum_fusion.p0), channel_id=1, source_target_pairs={{0,2},{2,0},{4,6},{6,4},{8,10},{10,8},{12,14},{14,12},{16,18},{18,... | collective-permute-start | bytes 2359304 | tf_op jit(solution)/shard_map/ppermute | solution.py:63
  270.0 34.2 %collective-permute-start.26 = (bf16[4,112,576]{2,1,0:T(8,128)(2,1)S(1)}, bf16[4,112,576]{2,1,0:T(8,128)(2,1)S(1)}, u32[]{:S(2)}, u32[]{:S(2)}) collective-permute-start(bf16[4,112,576]{2,1,0:T(8,128)(2,1)S(1)} %pad_maximum_fusion.1.p0), channel_id=1, source_target_pairs={{0,4},{2,6},{4,0},{6,2},{8,12},{10,14},{12,8},{14,10},{16,20},{18,... | collective-permute-start | bytes 1548296 | tf_op jit(solution)/shard_map/ppermute | solution.py:63
  271.7 32.5 %collective-permute-start.25 = (bf16[4,112,576]{2,1,0:T(8,128)(2,1)S(1)}, bf16[4,112,576]{2,1,0:T(8,128)(2,1)S(1)}, u32[]{:S(2)}, u32[]{:S(2)}) collective-permute-start(bf16[4,112,576]{2,1,0:T(8,128)(2,1)S(1)} %pad_maximum_fusion.1.p0), channel_id=1, source_target_pairs={{0,2},{2,0},{4,6},{6,4},{8,10},{10,8},{12,14},{14,12},{16,18},{18,... | collective-permute-start | bytes 1548296 | tf_op jit(solution)/shard_map/ppermute | solution.py:63
  (22 other events, 74.5 us)
Sparse Core Ops, SparseCore 0:
  9.6 12.1 all-gather.7
  23.3 15.4 all-gather.9
  40.4 15.5 all-gather.11
  129.6 72.8 all-gather.13

commit v4 on v3

--- a/solution.py
+++ b/solution.py
@@ -26,20 +26,25 @@
     return lax.dot_general(left, right, (dims, ((), ())), preferred_element_type=F32)
 
 
-def kernel_call(kernel, name, outs, args, vmem, micros, smem=0, anywhere=(), scratch=()):
+def kernel_call(kernel, name, outs, args, vmem, micros, smem=0, left=(), scratch=(), after=()):
     spaces = [
-        pl.BlockSpec(memory_space=pltpu.SMEM if i < smem else pl.ANY if i in anywhere else pltpu.VMEM)
+        pl.BlockSpec(memory_space=pltpu.SMEM if i < smem else pltpu.HBM if i in left else pltpu.VMEM)
         for i in range(len(args))
     ]
+    count = len(args)
+
+    def run(*refs):
+        kernel(*refs[:count], *refs[count + len(after) :])
+
     return pl.pallas_call(
-        kernel,
+        run if after else kernel,
         out_shape=outs,
-        in_specs=spaces,
+        in_specs=spaces + [pl.BlockSpec(memory_space=pl.ANY)] * len(after),
         scratch_shapes=list(scratch),
         compiler_params=pltpu.CompilerParams(vmem_limit_bytes=vmem * MIB),
         cost_estimate=pl.CostEstimate(flops=0, bytes_accessed=int(micros * 3_500_000), transcendentals=0),
         name=name,
-    )(*args)
+    )(*args, *after)
 
 
 def shaped(shape, dtype=BF16):
@@ -305,7 +310,7 @@
     )
     args = (spot, *contexts, inputs, grad, vectors, up_offset, out_matrix, up_matrix, down_matrix)
     found = kernel_call(
-        functools.partial(dense_kernel, width), "dense", outs, args, 40, 18, 1, (9, 10, 11), scratch
+        functools.partial(dense_kernel, width), "dense", outs, args, 22, 10, 1, (9, 10, 11), scratch
     )
     return found[0], found[1], found[2:6], found[6:10], found[10:14]
 
@@ -322,11 +327,11 @@
             ref[g] = value[g * TALL : (g + 1) * TALL]
 
 
-def up_grad_parts(spot, parts, width):
+def up_grad_parts(spot, parts, width, after):
     tokens, columns = 4 * ROWS, parts[0].shape[1] - width
     out = shaped((GROUPS, TALL, columns))
     scratch = (pltpu.VMEM((width, tokens), BF16), pltpu.VMEM((tokens, columns), BF16))
-    return kernel_call(up_grad_kernel, "up_grad", (out, out), (spot, *parts), 16, 4, 1, (), scratch)
+    return kernel_call(up_grad_kernel, "up_grad", (out, out), (spot, *parts), 16, 4, 1, (), scratch, after)
 
 
 def down_grad_kernel(spot, p0, p1, p2, p3, other_ref, own_ref, turned, second, branch, sums):
@@ -354,7 +359,7 @@
             ).astype(BF16)
 
 
-def down_grad_parts(spot, parts, width):
+def down_grad_parts(spot, parts, width, after):
     tokens = 4 * ROWS
     out = shaped((GROUPS, TALL + SHORT + EXTRA, width))
     scratch = (
@@ -363,7 +368,7 @@
         pltpu.VMEM((tokens, width), BF16),
         pltpu.VMEM((2, EXTRA, width), F32),
     )
-    return kernel_call(down_grad_kernel, "down_grad", (out, out), (spot, *parts), 24, 5, 1, (), scratch)
+    return kernel_call(down_grad_kernel, "down_grad", (out, out), (spot, *parts), 16, 5, 1, (), scratch, after)
 
 
 def core_sum_kernel(which, spot, own, received, *outs):
@@ -377,14 +382,16 @@
     return kernel_call(functools.partial(core_sum_kernel, which), name, outs, (spot, own, received), 16, 2, 1)
 
 
-def place_up_kernel(gathered, up_ref):
-    share = gathered.shape[3] // 2
-    for g in range(GROUPS):
-        for quarter in range(4):
-            block = gathered[g, quarter].astype(F32)
+def place_up_kernel(spot, p0, p1, p2, p3, up_ref):
+    group, quarter = spot[0], spot[1]
+    share = p0.shape[2] // 2
+    for i, piece in enumerate((p0, p1, p2, p3)):
+        for g in range(GROUPS):
+            block = piece[group ^ g].astype(F32)
             for core in range(2):
-                start = core * 4 * share + quarter * share
-                up_ref[g * TALL : (g + 1) * TALL, start : start + share] = block[:, core * share : (core + 1) * share]
+                start = core * 4 * share + (quarter ^ i) * share
+                at = pl.ds(pl.multiple_of(start, 128), share)
+                up_ref[g * TALL : (g + 1) * TALL, at] = block[:, core * share : (core + 1) * share]
 
 
 BIAS_ROWS = 16
@@ -415,14 +422,14 @@
             ref[quarter, half // 4 :, :] = sums
 
 
-def joined_grads(spot, query_grad, key_values, inputs, weight):
+def joined_grads(spot, query_grad, key_values, inputs, weight, after):
     width = weight.shape[0]
     part = shaped((4, width // 8 + BIAS_ROWS, 3 * WIDTH))
     outs = (part, part) + (shaped((ROWS, width)),) * GROUPS
     scratch = (pltpu.VMEM((GROUPS * ROWS, 3 * WIDTH), BF16), pltpu.VMEM((width, GROUPS * ROWS), BF16))
     args = (spot, query_grad, *key_values, *inputs, weight)
     kernel = functools.partial(joined_grad_kernel, len(key_values))
-    found = kernel_call(kernel, "joined_grad", outs, args, 24, 6, 1, (), scratch)
+    found = kernel_call(kernel, "joined_grad", outs, args, 16, 6, 1, (), scratch, after)
     return found[0], found[1], found[2:]
 
 
@@ -430,11 +437,10 @@
     group, quarter = spot[0], spot[1]
     for i, piece in enumerate((p0, p1, p2, p3)):
         for g in range(GROUPS):
-            block = piece[group ^ g]
-            tall = (quarter ^ i) * (GROUPS * TALL) + g * TALL
-            down_ref[pl.ds(pl.multiple_of(tall, 8), TALL), :] = block[:TALL].astype(F32)
-            short = (quarter ^ i) * (GROUPS * SHORT) + g * SHORT
-            out_ref[pl.ds(pl.multiple_of(short, 8), SHORT), :] = block[TALL : TALL + SHORT].astype(F32)
+            block = piece[group ^ g].astype(F32)
+            place = (quarter ^ i) * GROUPS + g
+            down_ref[pl.ds(pl.multiple_of(place * TALL, 8), TALL), :] = block[:TALL]
+            out_ref[pl.ds(pl.multiple_of(place * SHORT, 8), SHORT), :] = block[TALL:]
 
 
 def place_joined_kernel(spot, p0, p1, p2, p3, weight_ref, bias_ref):
@@ -552,36 +558,38 @@
         column = jnp.stack([part, *(places.column_swap(part, i) for i in turns)])
         return (column, *(places.four_swap(column, i) for i in turns))
 
-    other, own = up_grad_parts(spot, up_parts, model_width)
-    up_pieces = core_sums(spot, own, to_other(other), 0, "up_sum")
-    up_part = total_of(up_pieces, places.column_swap).astype(BF16)
-    other, own = down_grad_parts(spot, down_parts, model_width)
+    query_grad, parts = attend_grad(query, context, context_grads, log_total, key_values, bias, chunks)
+    other, own = down_grad_parts(spot, down_parts, model_width, (query_grad,))
     down_pieces = core_sums(spot, own, to_other(other), 0, "down_sum")
     down_part = total_of(down_pieces, places.column_swap)
     extra = down_part[TALL + SHORT :]
     up_bias_grad = jnp.concatenate([extra[6, :half], extra[7, :half], extra[0, half:], extra[1, half:]])
-
-    query_grad, parts = attend_grad(query, context, context_grads, log_total, key_values, bias, chunks)
     if plane_size == 4:
         key_value_grads = (parts[0], *(places.swap(parts[i], i) for i in turns))
     else:
         blocks = parts[0].reshape(2 * WIDTH, plane_size, column_rows)
         blocks = places.exchange(jnp.transpose(blocks, (1, 0, 2)), places.planes)
         key_value_grads = (jnp.sum(blocks.astype(F32), axis=0),)
-    other, own, input_parts = joined_grads(spot, query_grad, key_value_grads, column_inputs, group_weight)
+    other, own, input_parts = joined_grads(
+        spot, query_grad, key_value_grads, column_inputs, group_weight, (down_pieces[0],)
+    )
+    up_other, up_own = up_grad_parts(spot, up_parts, model_width, (input_parts[0],))
+    up_pieces = core_sums(spot, up_own, to_other(up_other), 0, "up_sum")
+    up_part = total_of(up_pieces, places.column_swap).astype(BF16)
     input_parts = (input_parts[0], *(places.column_swap(input_parts[i], i) for i in turns))
     input_grad = one_grad + sum(p.astype(F32) for p in input_parts)
     joined_pieces = core_sums(spot, own, to_other(other), 1, "joined_sum")
     joined_part = total_of(joined_pieces, places.four_swap).astype(BF16)
-    up_all = lax.all_gather(up_part, "seq", axis=0, axis_index_groups=places.sixteens)
-    down_all = gather_all(down_part.astype(BF16))
+    low = down_part[: TALL + SHORT].astype(BF16)
+    down_all = gather_all(low)
+    up_all = gather_all(up_part)
     joined_all = gather_all(joined_part)
     down_grad, out_grad = kernel_call(
         place_down_kernel,
         "place_down",
         (shaped((hidden_width // 2, model_width), F32), shaped((half, model_width), F32)),
         (spot, *down_all),
-        24,
+        16,
         5,
         1,
     )
@@ -598,9 +606,10 @@
         place_up_kernel,
         "place_up",
         shaped((half, hidden_width), F32),
-        (up_all.reshape(GROUPS, 4, TALL, hidden_width // 4),),
-        24,
+        (spot, *up_all),
+        16,
         4,
+        1,
     )
 
     shape = (1, row_count, model_width)

time: 322 us -> 318 us (0.988)
  local copies, waits for them, and re-layouts: 16.6 us -> 12.3 us
  starting transfers between devices: 71.2 us -> 75.3 us
    unnamed x68 -> x42, local copies, waits for them, and re-layouts: 12.7 us -> 8.43 us
    ppermute x3, waiting for transfers between devices: 3.96 us -> 0.01 us  [to_other(): return lax.ppermute(block, 'shard', [(0, 1), (1, 0)])]
    ppermute x45 -> x51, starting transfers between devices: 70.9 us -> 74.5 us  [swap(): return lax.ppermute(block, 'seq', [(i, i ^ bits) for i in range(self.size)])]
    ppermute x45 -> x51, waiting for transfers between devices: 159 us -> 161 us  [swap(): return lax.ppermute(block, 'seq', [(i, i ^ bits) for i in range(self.size)])]
  transfers between devices with their start and end apart: 52 -> 57, of which waited for: 24 -> 26; matrix products, arithmetic and copies ran while one was open for 2% -> 2% of each run, Pallas kernels for 9% -> 9%
where the time goes in v4:
time: 318 us
  waiting for transfers between devices  163 us (51%)
  starting transfers between devices  75.3 us (24%)
  Pallas kernels  45.7 us (14%)
  between operations  14.3 us (4%)
  local copies, waits for them, and re-layouts  12.3 us (4%)
  blocking collectives  4.62 us (1%)
    ppermute x51, waiting for transfers between devices, swap(): return lax.ppermute(block, 'seq', [(i, i ^ bits) for i in range(self.size)])  161 us
    ppermute x51, starting transfers between devices, swap(): return lax.ppermute(block, 'seq', [(i, i ^ bits) for i in range(self.size)])  74.5 us
    pallas_call x13, Pallas kernels, kernel_call(): pl.pallas_call(run if after else kernel, out_shape=outs, in_specs=spaces...  45.7 us
    unnamed x42, local copies, waits for them, and re-layouts  8.43 us
  transfers between devices with their start and end apart: 57, of which 26 were waited for; matrix products, arithmetic and copies ran while one was open for 2% of the time, Pallas kernels for 9%

profile of v4, /device:TPU:0, one launch (start us, length us, event | category | flops | bytes accessed | tf_op | source)
XLA Modules:
  0.0 318.1 jit_solution(17269371495602803977)
XLA Ops:
  9.5 5.1 %collective-permute-start.2 = (bf16[128,768]{1,0:T(8,128)(2,1)S(1)}, bf16[128,768]{1,0:T(8,128)(2,1)S(1)}, u32[]{:S(2)}, u32[]{:S(2)}) collective-permute-start(bf16[128,768]{1,0:T(8,128)(2,1)S(1)} %bitcast.32), channel_id=1, source_target_pairs={{0,24},{2,26},{4,28},{6,30},{8,16},{10,18},{12,20},{14,22},{16,8},... | collective-permute-start | bytes 589832 | tf_op jit(solution)/shard_map/ppermute | solution.py:68
  15.5 1.8 all-gather.1
  17.6 1.5 constant_dynamic-slice_fusion.2
  19.3 2.8 all_gather.18.weight.refs_10_
  22.1 9.2 %collective-permute-done.1.x2.refs_8_ = bf16[128,768]{1,0:T(8,128)(2,1)S(1)} collective-permute-done((bf16[128,768]{1,0:T(8,128)(2,1)S(1)}, bf16[128,768]{1,0:T(8,128)(2,1)S(1)}, u32[]{:S(2)}, u32[]{:S(2)}) %collective-permute-start.1) | collective-permute-done | bytes 196640 | tf_op jit(solution)/shard_map/ppermute | solution.py:68
  32.2 2.5 collective-permute-start.5
  37.3 8.0 %collective-permute-done.5.refs_4_.refs_10_ = bf16[512,384]{1,0:T(8,128)(2,1)S(1)} collective-permute-done((bf16[512,384]{1,0:T(8,128)(2,1)S(1)}, bf16[512,384]{1,0:T(8,128)(2,1)S(1)}, u32[]{:S(2)}, u32[]{:S(2)}) %collective-permute-start.5) | collective-permute-done | bytes 393248 | tf_op jit(solution)/shard_map/ppermute | solution.py:68
  45.3 6.5 %collective-permute-done.4.refs_3_.refs_9_ = bf16[512,384]{1,0:T(8,128)(2,1)S(1)} collective-permute-done((bf16[512,384]{1,0:T(8,128)(2,1)S(1)}, bf16[512,384]{1,0:T(8,128)(2,1)S(1)}, u32[]{:S(2)}, u32[]{:S(2)}) %collective-permute-start.4) | collective-permute-done | bytes 393248 | tf_op jit(solution)/shard_map/ppermute | solution.py:68
  51.9 9.2 %attend.1 = (f32[512,192]{1,0:T(8,128)S(1)}, f32[512,128]{1,0:T(8,128)S(1)}, bf16[128,192]{1,0:T(8,128)(2,1)S(1)}, bf16[128,192]{1,0:T(8,128)(2,1)}, bf16[128,192]{1,0:T(8,128)(2,1)}, /*index=5*/bf16[128,192]{1,0:T(8,128)(2,1)}) custom-call(bf16[512,192]{1,0:T(8,128)(2,1)S(1)} %get-tuple-element.68.refs_0_, ...), custom_call_target="tpu_custom_call" | custom-call | bytes 31500000 | tf_op jit(solution)/shard_map/attend/pallas_call | solution.py:39
  62.5 2.8 collective-permute-start.7
  65.4 1.5 collective-permute-start.8
  67.8 2.9 collective-permute-done.7.c2
  71.9 2.3 copy-done
  74.2 2.3 copy-done.1
  76.6 1.3 copy-done.3
  78.8 10.1 %dense.1 = (bf16[128,768]{1,0:T(8,128)(2,1)}, f32[128,768]{1,0:T(8,128)S(1)}, bf16[128,192]{1,0:T(8,128)(2,1)S(1)}, bf16[128,192]{1,0:T(8,128)(2,1)S(1)}, bf16[1...) custom-call(s32[3]{0:T(128)S(1)} %pad_add_fusion.spot.refs_0_, ...), custom_call_target="tpu_custom_call" | custom-call | bytes 35000000 | tf_op jit(solution)/shard_map/dense/pallas_call | solution.py:39
  88.9 1.6 collective-permute-start.15
  91.1 1.4 collective-permute-start.17
  93.4 1.3 collective-permute-start.10
  94.6 2.1 collective-permute-done.9.refs_4_
  96.7 1.6 collective-permute-start.11
  98.3 1.4 collective-permute-done.10.refs_5_
  99.8 3.0 collective-permute-done.11.refs_6_
  102.8 8.0 %attend_grad.1 = (bf16[512,192]{1,0:T(8,128)(2,1)S(1)}, bf16[384,512]{1,0:T(8,128)(2,1)S(1)}, bf16[384,512]{1,0:T(8,128)(2,1)S(1)}, bf16[384,512]{1,0:T(8,128)(2,1)S(1)}, bf16[384,512]{1,0:T(8,128)(2,1)S(1)}) custom-call(bf16[512,192]{1,0:T(8,128)(2,1)S(1)} %get-tuple-element.68.refs_0_, f32[512,192]{1,0:T(8,128)S(1)} %copy-done.7, ...), custom_call_target="tpu_custom_call" | custom-call | bytes 38500000 | tf_op jit(solution)/shard_map/attend_grad/pallas_call | solution.py:39
  110.8 11.8 %collective-permute-done.16.refs_3_ = bf16[144,2560]{1,0:T(8,128)(2,1)S(1)} collective-permute-done((bf16[144,2560]{1,0:T(8,128)(2,1)S(1)}, bf16[144,2560]{1,0:T(8,128)(2,1)S(1)}, u32[]{:S(2)}, u32[]{:S(2)}) %collective-permute-start.16) | collective-permute-done | bytes 737312 | tf_op jit(solution)/shard_map/ppermute | solution.py:68
  122.6 1.8 down_grad.1
  125.1 1.5 collective-permute-start.41
  127.3 1.3 collective-permute-start.14
  128.6 7.9 %collective-permute-done.12.refs_3_ = bf16[384,512]{1,0:T(8,128)(2,1)S(1)} collective-permute-done((bf16[384,512]{1,0:T(8,128)(2,1)S(1)}, bf16[384,512]{1,0:T(8,128)(2,1)S(1)}, u32[]{:S(2)}, u32[]{:S(2)}) %collective-permute-start.12) | collective-permute-done | bytes 393248 | tf_op jit(solution)/shard_map/ppermute | solution.py:68
  137.2 1.3 collective-permute-start.43
  139.2 14.3 %collective-permute-done.14.refs_5_ = bf16[384,512]{1,0:T(8,128)(2,1)S(1)} collective-permute-done((bf16[384,512]{1,0:T(8,128)(2,1)S(1)}, bf16[384,512]{1,0:T(8,128)(2,1)S(1)}, u32[]{:S(2)}, u32[]{:S(2)}) %collective-permute-start.14) | collective-permute-done | bytes 393248 | tf_op jit(solution)/shard_map/ppermute | solution.py:68
  153.6 2.7 joined_grad.1
  156.3 7.3 %collective-permute-done.42.refs_3_ = bf16[128,1536]{1,0:T(8,128)(2,1)S(1)} collective-permute-done((bf16[128,1536]{1,0:T(8,128)(2,1)S(1)}, bf16[128,1536]{1,0:T(8,128)(2,1)S(1)}, u32[]{:S(2)}, u32[]{:S(2)}) %collective-permute-start.42) | collective-permute-done | bytes 393248 | tf_op jit(solution)/shard_map/ppermute | solution.py:68
  163.6 1.5 up_grad.1
  165.7 1.5 collective-permute-start.32
  167.1 1.2 collective-permute-start.33
  168.4 1.7 collective-permute-start.34
  170.1 5.3 %collective-permute-done.32 = bf16[128,768]{1,0:T(8,128)(2,1)S(1)} collective-permute-done((bf16[128,768]{1,0:T(8,128)(2,1)S(1)}, bf16[128,768]{1,0:T(8,128)(2,1)S(1)}, u32[]{:S(2)}, u32[]{:S(2)}) %collective-permute-start.32) | collective-permute-done | bytes 196640 | tf_op jit(solution)/shard_map/ppermute | solution.py:68
  175.4 8.9 %collective-permute-done.33 = bf16[128,768]{1,0:T(8,128)(2,1)S(1)} collective-permute-done((bf16[128,768]{1,0:T(8,128)(2,1)S(1)}, bf16[128,768]{1,0:T(8,128)(2,1)S(1)}, u32[]{:S(2)}, u32[]{:S(2)}) %collective-permute-start.33) | collective-permute-done | bytes 196640 | tf_op jit(solution)/shard_map/ppermute | solution.py:68
  184.4 9.0 %collective-permute-start.35 = (bf16[120,768]{1,0:T(8,128)(2,1)S(1)}, bf16[120,768]{1,0:T(8,128)(2,1)S(1)}, u32[]{:S(2)}, u32[]{:S(2)}) collective-permute-start(bf16[120,768]{1,0:T(8,128)(2,1)S(1)} %slice.113), channel_id=1, source_target_pairs={{0,8},{2,10},{4,12},{6,14},{8,0},{10,2},{12,4},{14,6},{16,24},{18,... | collective-permute-start | bytes 552968 | tf_op jit(solution)/shard_map/ppermute | solution.py:68
  194.8 1.5 collective-permute-start.24
  196.3 1.4 collective-permute-start.25
  199.3 1.6 collective-permute-start.37
  200.9 1.1 collective-permute-start.45
  202.0 1.7 collective-permute-start.46
  203.7 1.6 collective-permute-start.47
  205.4 14.9 %collective-permute-done.36 = bf16[120,768]{1,0:T(8,128)(2,1)S(1)} collective-permute-done((bf16[120,768]{1,0:T(8,128)(2,1)S(1)}, bf16[120,768]{1,0:T(8,128)(2,1)S(1)}, u32[]{:S(2)}, u32[]{:S(2)}) %collective-permute-start.36) | collective-permute-done | bytes 184352 | tf_op jit(solution)/shard_map/ppermute | solution.py:68
  220.6 8.3 %collective-permute-start.27 = (bf16[112,576]{1,0:T(8,128)(2,1)S(1)}, bf16[112,576]{1,0:T(8,128)(2,1)S(1)}, u32[]{:S(2)}, u32[]{:S(2)}) collective-permute-start(bf16[112,576]{1,0:T(8,128)(2,1)S(1)} %add_convert_fusion.1), channel_id=1, source_target_pairs={{0,16},{2,18},{4,20},{6,22},{8,24},{10,26},{12,28},{14,30},{16,0},... | collective-permute-start | bytes 387080 | tf_op jit(solution)/shard_map/ppermute | solution.py:68
  229.0 3.6 %collective-permute-start.21 = (bf16[128,768]{1,0:T(8,128)(2,1)S(1)}, bf16[128,768]{1,0:T(8,128)(2,1)S(1)}, u32[]{:S(2)}, u32[]{:S(2)}) collective-permute-start(bf16[128,768]{1,0:T(8,128)(2,1)S(1)} %get-tuple-element.97), channel_id=1, source_target_pairs={{0,24},{2,26},{4,28},{6,30},{8,16},{10,18},{12,20},{14,22},{16,8},... | collective-permute-start | bytes 589832 | tf_op jit(solution)/shard_map/ppermute | solution.py:68
  232.6 3.4 %collective-permute-start.40 = (bf16[4,120,768]{2,1,0:T(8,128)(2,1)S(1)}, bf16[4,120,768]{2,1,0:T(8,128)(2,1)S(1)}, u32[]{:S(2)}, u32[]{:S(2)}) collective-permute-start(bf16[4,120,768]{2,1,0:T(8,128)(2,1)S(1)} %pad_maximum_fusion.p0), channel_id=1, source_target_pairs={{0,6},{2,4},{4,2},{6,0},{8,14},{10,12},{12,10},{14,8},{16,22},{18,... | collective-permute-start | bytes 2211848 | tf_op jit(solution)/shard_map/ppermute | solution.py:68
  236.6 8.5 %collective-permute-done.27 = bf16[112,576]{1,0:T(8,128)(2,1)S(1)} collective-permute-done((bf16[112,576]{1,0:T(8,128)(2,1)S(1)}, bf16[112,576]{1,0:T(8,128)(2,1)S(1)}, u32[]{:S(2)}, u32[]{:S(2)}) %collective-permute-start.27) | collective-permute-done | bytes 129056 | tf_op jit(solution)/shard_map/ppermute | solution.py:68
  245.2 5.0 %collective-permute-done.26 = bf16[112,576]{1,0:T(8,128)(2,1)S(1)} collective-permute-done((bf16[112,576]{1,0:T(8,128)(2,1)S(1)}, bf16[112,576]{1,0:T(8,128)(2,1)S(1)}, u32[]{:S(2)}, u32[]{:S(2)}) %collective-permute-start.26) | collective-permute-done | bytes 129056 | tf_op jit(solution)/shard_map/ppermute | solution.py:68
  251.1 1.6 collective-permute-start.31
  252.7 4.8 %collective-permute-done.50 = bf16[96,768]{1,0:T(8,128)(2,1)S(1)} collective-permute-done((bf16[96,768]{1,0:T(8,128)(2,1)S(1)}, bf16[96,768]{1,0:T(8,128)(2,1)S(1)}, u32[]{:S(2)}, u32[]{:S(2)}) %collective-permute-start.50) | collective-permute-done | bytes 147488 | tf_op jit(solution)/shard_map/ppermute | solution.py:68
  258.1 7.0 %collective-permute-done.49 = bf16[96,768]{1,0:T(8,128)(2,1)S(1)} collective-permute-done((bf16[96,768]{1,0:T(8,128)(2,1)S(1)}, bf16[96,768]{1,0:T(8,128)(2,1)S(1)}, u32[]{:S(2)}, u32[]{:S(2)}) %collective-permute-start.49) | collective-permute-done | bytes 147488 | tf_op jit(solution)/shard_map/ppermute | solution.py:68
  265.6 4.7 %collective-permute-done.48 = bf16[96,768]{1,0:T(8,128)(2,1)S(1)} collective-permute-done((bf16[96,768]{1,0:T(8,128)(2,1)S(1)}, bf16[96,768]{1,0:T(8,128)(2,1)S(1)}, u32[]{:S(2)}, u32[]{:S(2)}) %collective-permute-start.48) | collective-permute-done | bytes 147488 | tf_op jit(solution)/shard_map/ppermute | solution.py:68
  270.3 1.3 collective-permute-start.29
  271.7 2.2 collective-permute-start.53
  273.9 1.3 collective-permute-start.51
  277.4 3.5 %place_down.1 = (f32[1536,768]{1,0:T(8,128)}, f32[384,768]{1,0:T(8,128)}) custom-call(s32[3]{0:T(128)S(1)} %pad_add_fusion.spot.refs_0_, bf16[4,120,768]{2,1,0:T(8,128)(2,1)S(1)} %pad_maximum_fusion.p0, bf16[4,120,768]{2,1,0:T(8,128)(2,1)S(1)} %collective-permute-done.38.p1, bf16[4,120,768]{2,1,0:T(8,128)(2,1)S(1)} %collective-permute-done.39.p2, ...), custom_call_target="tpu_custom_call" | custom-call | bytes 17500000 | tf_op jit(solution)/shard_map/place_down/pallas_call | solution.py:39
  280.9 16.4 %collective-permute-done.30.p2 = bf16[4,112,576]{2,1,0:T(8,128)(2,1)S(1)} collective-permute-done((bf16[4,112,576]{2,1,0:T(8,128)(2,1)S(1)}, bf16[4,112,576]{2,1,0:T(8,128)(2,1)S(1)}, u32[]{:S(2)}, u32[]{:S(2)}) %collective-permute-start.30) | collective-permute-done | bytes 516128 | tf_op jit(solution)/shard_map/ppermute | solution.py:68
  297.3 2.8 place_joined.1
  300.7 7.7 %collective-permute-done.52.p2 = bf16[4,96,768]{2,1,0:T(8,128)(2,1)S(1)} collective-permute-done((bf16[4,96,768]{2,1,0:T(8,128)(2,1)S(1)}, bf16[4,96,768]{2,1,0:T(8,128)(2,1)S(1)}, u32[]{:S(2)}, u32[]{:S(2)}) %collective-permute-start.52) | collective-permute-done | bytes 589856 | tf_op jit(solution)/shard_map/ppermute | solution.py:68
  308.5 3.1 place_up.1
  (157 shorter events, 25.1 us)
Async XLA Ops:
  7.2 64.7 %all-gather.6.cloned.1.call-start = ((), (), s32[]{:S(2)}) async-start(), calls=%async_computation | async-start | bytes 1769472 | tf_op jit(solution)/shard_map/all_gather | solution.py:497
  8.0 7.4 %copy-start.18 = (bf16[384]{0:T(512)(128)(2,1)S(1)}, bf16[384]{0:T(512)(128)(2,1)}, u32[]{:S(2)}) copy-start(bf16[384]{0:T(512)(128)(2,1)} %param.30) | copy-start | bytes 2308
  8.0 7.4 %copy-start.19 = (bf16[384]{0:T(512)(128)(2,1)S(1)}, bf16[384]{0:T(512)(128)(2,1)}, u32[]{:S(2)}) copy-start(bf16[384]{0:T(512)(128)(2,1)} %param.31) | copy-start | bytes 2308
  8.0 7.4 %copy-start.11 = (bf16[1536]{0:T(1024)(128)(2,1)S(1)}, bf16[1536]{0:T(1024)(128)(2,1)}, u32[]{:S(2)}) copy-start(bf16[1536]{0:T(1024)(128)(2,1)} %param.27) | copy-start | bytes 9220
  8.0 63.9 %all-gather.8.cloned.1.call-start = ((), (), s32[]{:S(2)}) async-start(), calls=%async_computation.1 | async-start | bytes 7077888 | tf_op jit(solution)/shard_map/all_gather | solution.py:497
  8.8 63.1 %all-gather.10.cloned.1.call-start = ((), (), s32[]{:S(2)}) async-start(), calls=%async_computation.2 | async-start | bytes 7077888 | tf_op jit(solution)/shard_map/all_gather | solution.py:497
  9.5 12.6 %collective-permute-start.2 = (bf16[128,768]{1,0:T(8,128)(2,1)S(1)}, bf16[128,768]{1,0:T(8,128)(2,1)S(1)}, u32[]{:S(2)}, u32[]{:S(2)}) collective-permute-start(bf16[128,768]{1,0:T(8,128)(2,1)S(1)} %bitcast.32), channel_id=1, source_target_pairs={{0,24},{2,26},{4,28},{6,30},{8,16},{10,18},{12,20},{14,22},{16,8},... | collective-permute-start | bytes 589832 | tf_op jit(solution)/shard_map/ppermute | solution.py:68
  14.6 16.7 %collective-permute-start.1 = (bf16[128,768]{1,0:T(8,128)(2,1)S(1)}, bf16[128,768]{1,0:T(8,128)(2,1)S(1)}, u32[]{:S(2)}, u32[]{:S(2)}) collective-permute-start(bf16[128,768]{1,0:T(8,128)(2,1)S(1)} %bitcast.33), channel_id=1, source_target_pairs={{0,16},{2,18},{4,20},{6,22},{8,24},{10,26},{12,28},{14,30},{16,0},... | collective-permute-start | bytes 589832 | tf_op jit(solution)/shard_map/ppermute | solution.py:68
  14.6 16.7 %collective-permute-start = (bf16[128,768]{1,0:T(8,128)(2,1)S(1)}, bf16[128,768]{1,0:T(8,128)(2,1)S(1)}, u32[]{:S(2)}, u32[]{:S(2)}) collective-permute-start(bf16[128,768]{1,0:T(8,128)(2,1)S(1)} %bitcast.34), channel_id=1, source_target_pairs={{0,8},{2,10},{4,12},{6,14},{8,0},{10,2},{12,4},{14,6},{16,24},{18,... | collective-permute-start | bytes 589832 | tf_op jit(solution)/shard_map/ppermute | solution.py:68
  19.1 16.7 %copy-start.20 = (s32[2]{0:T(128)S(1)}, s32[2]{0:T(128)}, u32[]{:S(2)}) copy-start(s32[2]{0:T(128)} %param.18) | copy-start | bytes 28
  32.2 13.1 %collective-permute-start.5 = (bf16[512,384]{1,0:T(8,128)(2,1)S(1)}, bf16[512,384]{1,0:T(8,128)(2,1)S(1)}, u32[]{:S(2)}, u32[]{:S(2)}) collective-permute-start(bf16[512,384]{1,0:T(8,128)(2,1)S(1)} %get-tuple-element.69.refs_1_.refs_7_), channel_id=1, source_target_pairs={{0,6},{2,4},{4,2},{6,0},{8,14},{10,12},{12,10},{14,8},{16,22},{18,... | collective-permute-start | bytes 1179656 | tf_op jit(solution)/shard_map/ppermute | solution.py:68
  34.7 17.1 %collective-permute-start.4 = (bf16[512,384]{1,0:T(8,128)(2,1)S(1)}, bf16[512,384]{1,0:T(8,128)(2,1)S(1)}, u32[]{:S(2)}, u32[]{:S(2)}) collective-permute-start(bf16[512,384]{1,0:T(8,128)(2,1)S(1)} %get-tuple-element.69.refs_1_.refs_7_), channel_id=1, source_target_pairs={{0,4},{2,6},{4,0},{6,2},{8,12},{10,14},{12,8},{14,10},{16,20},{18,... | collective-permute-start | bytes 1179656 | tf_op jit(solution)/shard_map/ppermute | solution.py:68
  35.2 16.6 %collective-permute-start.3 = (bf16[512,384]{1,0:T(8,128)(2,1)S(1)}, bf16[512,384]{1,0:T(8,128)(2,1)S(1)}, u32[]{:S(2)}, u32[]{:S(2)}) collective-permute-start(bf16[512,384]{1,0:T(8,128)(2,1)S(1)} %get-tuple-element.69.refs_1_.refs_7_), channel_id=1, source_target_pairs={{0,2},{2,0},{4,6},{6,4},{8,10},{10,8},{12,14},{14,12},{16,18},{18,... | collective-permute-start | bytes 1179656 | tf_op jit(solution)/shard_map/ppermute | solution.py:68
  62.5 5.3 %collective-permute-start.6 = (bf16[128,192]{1,0:T(8,128)(2,1)}, bf16[128,192]{1,0:T(8,128)(2,1)}, u32[]{:S(2)}, u32[]{:S(2)}) collective-permute-start(bf16[128,192]{1,0:T(8,128)(2,1)} %get-tuple-element.71), channel_id=1, source_target_pairs={{0,8},{2,10},{4,12},{6,14},{8,0},{10,2},{12,4},{14,6},{16,24},{18,... | collective-permute-start | bytes 147464 | tf_op jit(solution)/shard_map/ppermute | solution.py:68
  62.5 8.2 %collective-permute-start.7 = (bf16[128,192]{1,0:T(8,128)(2,1)}, bf16[128,192]{1,0:T(8,128)(2,1)}, u32[]{:S(2)}, u32[]{:S(2)}) collective-permute-start(bf16[128,192]{1,0:T(8,128)(2,1)} %get-tuple-element.72), channel_id=1, source_target_pairs={{0,16},{2,18},{4,20},{6,22},{8,24},{10,26},{12,28},{14,30},{16,0},... | collective-permute-start | bytes 147464 | tf_op jit(solution)/shard_map/ppermute | solution.py:68
  65.4 6.5 %collective-permute-start.8 = (bf16[128,192]{1,0:T(8,128)(2,1)}, bf16[128,192]{1,0:T(8,128)(2,1)}, u32[]{:S(2)}, u32[]{:S(2)}) collective-permute-start(bf16[128,192]{1,0:T(8,128)(2,1)} %get-tuple-element.73), channel_id=1, source_target_pairs={{0,24},{2,26},{4,28},{6,30},{8,16},{10,18},{12,20},{14,22},{16,8},... | collective-permute-start | bytes 147464 | tf_op jit(solution)/shard_map/ppermute | solution.py:68
  78.8 24.0 %copy-start.7 = (f32[512,192]{1,0:T(8,128)S(1)}, f32[512,192]{1,0:T(8,128)}, u32[]{:S(2)}) copy-start(f32[512,192]{1,0:T(8,128)} %copy-done.6) | copy-start | bytes 1179652
  78.8 24.0 %copy-start.9 = (f32[512,128]{1,0:T(8,128)S(1)}, f32[512,128]{1,0:T(8,128)}, u32[]{:S(2)}) copy-start(f32[512,128]{1,0:T(8,128)} %copy-done.8) | copy-start | bytes 786436
  88.9 21.9 %collective-permute-start.15 = (bf16[144,2560]{1,0:T(8,128)(2,1)S(1)}, bf16[144,2560]{1,0:T(8,128)(2,1)S(1)}, u32[]{:S(2)}, u32[]{:S(2)}) collective-permute-start(bf16[144,2560]{1,0:T(8,128)(2,1)S(1)} %get-tuple-element.88), channel_id=1, source_target_pairs={{0,2},{2,0},{4,6},{6,4},{8,10},{10,8},{12,14},{14,12},{16,18},{18,... | collective-permute-start | bytes 2211848 | tf_op jit(solution)/shard_map/ppermute | solution.py:68
  90.5 32.1 %collective-permute-start.16 = (bf16[144,2560]{1,0:T(8,128)(2,1)S(1)}, bf16[144,2560]{1,0:T(8,128)(2,1)S(1)}, u32[]{:S(2)}, u32[]{:S(2)}) collective-permute-start(bf16[144,2560]{1,0:T(8,128)(2,1)S(1)} %get-tuple-element.89), channel_id=1, source_target_pairs={{0,4},{2,6},{4,0},{6,2},{8,12},{10,14},{12,8},{14,10},{16,20},{18,... | collective-permute-start | bytes 2211848 | tf_op jit(solution)/shard_map/ppermute | solution.py:68
  91.1 31.5 %collective-permute-start.17 = (bf16[144,2560]{1,0:T(8,128)(2,1)S(1)}, bf16[144,2560]{1,0:T(8,128)(2,1)S(1)}, u32[]{:S(2)}, u32[]{:S(2)}) collective-permute-start(bf16[144,2560]{1,0:T(8,128)(2,1)S(1)} %get-tuple-element.90), channel_id=1, source_target_pairs={{0,6},{2,4},{4,2},{6,0},{8,14},{10,12},{12,10},{14,8},{16,22},{18,... | collective-permute-start | bytes 2211848 | tf_op jit(solution)/shard_map/ppermute | solution.py:68
  92.5 4.3 %collective-permute-start.9 = (bf16[128,192]{1,0:T(8,128)(2,1)S(1)}, bf16[128,192]{1,0:T(8,128)(2,1)S(1)}, u32[]{:S(2)}, u32[]{:S(2)}) collective-permute-start(bf16[128,192]{1,0:T(8,128)(2,1)S(1)} %get-tuple-element.79), channel_id=1, source_target_pairs={{0,8},{2,10},{4,12},{6,14},{8,0},{10,2},{12,4},{14,6},{16,24},{18,... | collective-permute-start | bytes 147464 | tf_op jit(solution)/shard_map/ppermute | solution.py:68
  93.4 6.4 %collective-permute-start.10 = (bf16[128,192]{1,0:T(8,128)(2,1)S(1)}, bf16[128,192]{1,0:T(8,128)(2,1)S(1)}, u32[]{:S(2)}, u32[]{:S(2)}) collective-permute-start(bf16[128,192]{1,0:T(8,128)(2,1)S(1)} %get-tuple-element.80), channel_id=1, source_target_pairs={{0,16},{2,18},{4,20},{6,22},{8,24},{10,26},{12,28},{14,30},{16,0},... | collective-permute-start | bytes 147464 | tf_op jit(solution)/shard_map/ppermute | solution.py:68
  96.7 6.1 %collective-permute-start.11 = (bf16[128,192]{1,0:T(8,128)(2,1)S(1)}, bf16[128,192]{1,0:T(8,128)(2,1)S(1)}, u32[]{:S(2)}, u32[]{:S(2)}) collective-permute-start(bf16[128,192]{1,0:T(8,128)(2,1)S(1)} %get-tuple-element.81), channel_id=1, source_target_pairs={{0,24},{2,26},{4,28},{6,30},{8,16},{10,18},{12,20},{14,22},{16,8},... | collective-permute-start | bytes 147464 | tf_op jit(solution)/shard_map/ppermute | solution.py:68
  122.6 31.0 %copy-start.5 = (bf16[128,768]{1,0:T(8,128)(2,1)S(1)}, bf16[128,768]{1,0:T(8,128)(2,1)}, u32[]{:S(2)}) copy-start(bf16[128,768]{1,0:T(8,128)(2,1)} %copy-done.4) | copy-start | bytes 589828
  124.4 12.7 %collective-permute-start.18 = (bf16[4,128,768]{2,1,0:T(8,128)(2,1)S(1)}, bf16[4,128,768]{2,1,0:T(8,128)(2,1)S(1)}, u32[]{:S(2)}, u32[]{:S(2)}) collective-permute-start(bf16[4,128,768]{2,1,0:T(8,128)(2,1)S(1)} %get-tuple-element.92), channel_id=1, source_target_pairs={{0,1},{1,0},{2,3},{3,2},{4,5},{5,4},{6,7},{7,6},{8,9},{9,8},{10,11... | collective-permute-start | bytes 2359304 | tf_op jit(solution)/shard_map/ppermute | solution.py:550
  124.5 12.0 %collective-permute-start.12 = (bf16[384,512]{1,0:T(8,128)(2,1)S(1)}, bf16[384,512]{1,0:T(8,128)(2,1)S(1)}, u32[]{:S(2)}, u32[]{:S(2)}) collective-permute-start(bf16[384,512]{1,0:T(8,128)(2,1)S(1)} %get-tuple-element.84), channel_id=1, source_target_pairs={{0,2},{2,0},{4,6},{6,4},{8,10},{10,8},{12,14},{14,12},{16,18},{18,... | collective-permute-start | bytes 1179656 | tf_op jit(solution)/shard_map/ppermute | solution.py:68
  125.1 31.2 %collective-permute-start.41 = (bf16[128,1536]{1,0:T(8,128)(2,1)S(1)}, bf16[128,1536]{1,0:T(8,128)(2,1)S(1)}, u32[]{:S(2)}, u32[]{:S(2)}) collective-permute-start(bf16[128,1536]{1,0:T(8,128)(2,1)S(1)} %get-tuple-element.111), channel_id=1, source_target_pairs={{0,2},{2,0},{4,6},{6,4},{8,10},{10,8},{12,14},{14,12},{16,18},{18,... | collective-permute-start | bytes 1179656 | tf_op jit(solution)/shard_map/ppermute | solution.py:68
  126.6 12.6 %collective-permute-start.13 = (bf16[384,512]{1,0:T(8,128)(2,1)S(1)}, bf16[384,512]{1,0:T(8,128)(2,1)S(1)}, u32[]{:S(2)}, u32[]{:S(2)}) collective-permute-start(bf16[384,512]{1,0:T(8,128)(2,1)S(1)} %get-tuple-element.85), channel_id=1, source_target_pairs={{0,4},{2,6},{4,0},{6,2},{8,12},{10,14},{12,8},{14,10},{16,20},{18,... | collective-permute-start | bytes 1179656 | tf_op jit(solution)/shard_map/ppermute | solution.py:68
  127.3 26.3 %collective-permute-start.14 = (bf16[384,512]{1,0:T(8,128)(2,1)S(1)}, bf16[384,512]{1,0:T(8,128)(2,1)S(1)}, u32[]{:S(2)}, u32[]{:S(2)}) collective-permute-start(bf16[384,512]{1,0:T(8,128)(2,1)S(1)} %get-tuple-element.86), channel_id=1, source_target_pairs={{0,6},{2,4},{4,2},{6,0},{8,14},{10,12},{12,10},{14,8},{16,22},{18,... | collective-permute-start | bytes 1179656 | tf_op jit(solution)/shard_map/ppermute | solution.py:68
  136.5 27.1 %collective-permute-start.42 = (bf16[128,1536]{1,0:T(8,128)(2,1)S(1)}, bf16[128,1536]{1,0:T(8,128)(2,1)S(1)}, u32[]{:S(2)}, u32[]{:S(2)}) collective-permute-start(bf16[128,1536]{1,0:T(8,128)(2,1)S(1)} %get-tuple-element.112), channel_id=1, source_target_pairs={{0,4},{2,6},{4,0},{6,2},{8,12},{10,14},{12,8},{14,10},{16,20},{18,... | collective-permute-start | bytes 1179656 | tf_op jit(solution)/shard_map/ppermute | solution.py:68
  137.2 26.4 %collective-permute-start.43 = (bf16[128,1536]{1,0:T(8,128)(2,1)S(1)}, bf16[128,1536]{1,0:T(8,128)(2,1)S(1)}, u32[]{:S(2)}, u32[]{:S(2)}) collective-permute-start(bf16[128,1536]{1,0:T(8,128)(2,1)S(1)} %get-tuple-element.113), channel_id=1, source_target_pairs={{0,6},{2,4},{4,2},{6,0},{8,14},{10,12},{12,10},{14,8},{16,22},{18,... | collective-permute-start | bytes 1179656 | tf_op jit(solution)/shard_map/ppermute | solution.py:68
  165.1 31.2 %collective-permute-start.44 = (bf16[4,96,768]{2,1,0:T(8,128)(2,1)S(1)}, bf16[4,96,768]{2,1,0:T(8,128)(2,1)S(1)}, u32[]{:S(2)}, u32[]{:S(2)}) collective-permute-start(bf16[4,96,768]{2,1,0:T(8,128)(2,1)S(1)} %get-tuple-element.115), channel_id=1, source_target_pairs={{0,1},{1,0},{2,3},{3,2},{4,5},{5,4},{6,7},{7,6},{8,9},{9,8},{10,11... | collective-permute-start | bytes 1769480 | tf_op jit(solution)/shard_map/ppermute | solution.py:550
  165.2 28.3 %collective-permute-start.22 = (bf16[4,112,576]{2,1,0:T(8,128)(2,1)S(1)}, bf16[4,112,576]{2,1,0:T(8,128)(2,1)S(1)}, u32[]{:S(2)}, u32[]{:S(2)}) collective-permute-start(bf16[4,112,576]{2,1,0:T(8,128)(2,1)S(1)} %get-tuple-element.99), channel_id=1, source_target_pairs={{0,1},{1,0},{2,3},{3,2},{4,5},{5,4},{6,7},{7,6},{8,9},{9,8},{10,11... | collective-permute-start | bytes 1548296 | tf_op jit(solution)/shard_map/ppermute | solution.py:550
  165.7 9.7 %collective-permute-start.32 = (bf16[128,768]{1,0:T(8,128)(2,1)S(1)}, bf16[128,768]{1,0:T(8,128)(2,1)S(1)}, u32[]{:S(2)}, u32[]{:S(2)}) collective-permute-start(bf16[128,768]{1,0:T(8,128)(2,1)S(1)} %get-tuple-element.106), channel_id=1, source_target_pairs={{0,8},{2,10},{4,12},{6,14},{8,0},{10,2},{12,4},{14,6},{16,24},{18,... | collective-permute-start | bytes 589832 | tf_op jit(solution)/shard_map/ppermute | solution.py:68
  167.1 17.2 %collective-permute-start.33 = (bf16[128,768]{1,0:T(8,128)(2,1)S(1)}, bf16[128,768]{1,0:T(8,128)(2,1)S(1)}, u32[]{:S(2)}, u32[]{:S(2)}) collective-permute-start(bf16[128,768]{1,0:T(8,128)(2,1)S(1)} %get-tuple-element.107), channel_id=1, source_target_pairs={{0,16},{2,18},{4,20},{6,22},{8,24},{10,26},{12,28},{14,30},{16,0},... | collective-permute-start | bytes 589832 | tf_op jit(solution)/shard_map/ppermute | solution.py:68
  168.4 15.9 %collective-permute-start.34 = (bf16[128,768]{1,0:T(8,128)(2,1)S(1)}, bf16[128,768]{1,0:T(8,128)(2,1)S(1)}, u32[]{:S(2)}, u32[]{:S(2)}) collective-permute-start(bf16[128,768]{1,0:T(8,128)(2,1)S(1)} %get-tuple-element.108), channel_id=1, source_target_pairs={{0,24},{2,26},{4,28},{6,30},{8,16},{10,18},{12,20},{14,22},{16,8},... | collective-permute-start | bytes 589832 | tf_op jit(solution)/shard_map/ppermute | solution.py:68
  175.4 19.4 %collective-permute-start.19 = (bf16[128,768]{1,0:T(8,128)(2,1)S(1)}, bf16[128,768]{1,0:T(8,128)(2,1)S(1)}, u32[]{:S(2)}, u32[]{:S(2)}) collective-permute-start(bf16[128,768]{1,0:T(8,128)(2,1)S(1)} %get-tuple-element.95), channel_id=1, source_target_pairs={{0,8},{2,10},{4,12},{6,14},{8,0},{10,2},{12,4},{14,6},{16,24},{18,... | collective-permute-start | bytes 589832 | tf_op jit(solution)/shard_map/ppermute | solution.py:68
  184.3 14.2 %collective-permute-start.20 = (bf16[128,768]{1,0:T(8,128)(2,1)S(1)}, bf16[128,768]{1,0:T(8,128)(2,1)S(1)}, u32[]{:S(2)}, u32[]{:S(2)}) collective-permute-start(bf16[128,768]{1,0:T(8,128)(2,1)S(1)} %get-tuple-element.96), channel_id=1, source_target_pairs={{0,16},{2,18},{4,20},{6,22},{8,24},{10,26},{12,28},{14,30},{16,0},... | collective-permute-start | bytes 589832 | tf_op jit(solution)/shard_map/ppermute | solution.py:68
  184.4 14.9 %collective-permute-start.35 = (bf16[120,768]{1,0:T(8,128)(2,1)S(1)}, bf16[120,768]{1,0:T(8,128)(2,1)S(1)}, u32[]{:S(2)}, u32[]{:S(2)}) collective-permute-start(bf16[120,768]{1,0:T(8,128)(2,1)S(1)} %slice.113), channel_id=1, source_target_pairs={{0,8},{2,10},{4,12},{6,14},{8,0},{10,2},{12,4},{14,6},{16,24},{18,... | collective-permute-start | bytes 552968 | tf_op jit(solution)/shard_map/ppermute | solution.py:68
  194.2 6.7 %collective-permute-start.23 = (bf16[112,576]{1,0:T(8,128)(2,1)S(1)}, bf16[112,576]{1,0:T(8,128)(2,1)S(1)}, u32[]{:S(2)}, u32[]{:S(2)}) collective-permute-start(bf16[112,576]{1,0:T(8,128)(2,1)S(1)} %get-tuple-element.101), channel_id=1, source_target_pairs={{0,2},{2,0},{4,6},{6,4},{8,10},{10,8},{12,14},{14,12},{16,18},{18,... | collective-permute-start | bytes 387080 | tf_op jit(solution)/shard_map/ppermute | solution.py:68
  194.8 7.2 %collective-permute-start.24 = (bf16[112,576]{1,0:T(8,128)(2,1)S(1)}, bf16[112,576]{1,0:T(8,128)(2,1)S(1)}, u32[]{:S(2)}, u32[]{:S(2)}) collective-permute-start(bf16[112,576]{1,0:T(8,128)(2,1)S(1)} %get-tuple-element.102), channel_id=1, source_target_pairs={{0,4},{2,6},{4,0},{6,2},{8,12},{10,14},{12,8},{14,10},{16,20},{18,... | collective-permute-start | bytes 387080 | tf_op jit(solution)/shard_map/ppermute | solution.py:68
  196.3 7.4 %collective-permute-start.25 = (bf16[112,576]{1,0:T(8,128)(2,1)S(1)}, bf16[112,576]{1,0:T(8,128)(2,1)S(1)}, u32[]{:S(2)}, u32[]{:S(2)}) collective-permute-start(bf16[112,576]{1,0:T(8,128)(2,1)S(1)} %get-tuple-element.103), channel_id=1, source_target_pairs={{0,6},{2,4},{4,2},{6,0},{8,14},{10,12},{12,10},{14,8},{16,22},{18,... | collective-permute-start | bytes 387080 | tf_op jit(solution)/shard_map/ppermute | solution.py:68
  198.5 21.9 %collective-permute-start.36 = (bf16[120,768]{1,0:T(8,128)(2,1)S(1)}, bf16[120,768]{1,0:T(8,128)(2,1)S(1)}, u32[]{:S(2)}, u32[]{:S(2)}) collective-permute-start(bf16[120,768]{1,0:T(8,128)(2,1)S(1)} %slice.113), channel_id=1, source_target_pairs={{0,16},{2,18},{4,20},{6,22},{8,24},{10,26},{12,28},{14,30},{16,0},... | collective-permute-start | bytes 552968 | tf_op jit(solution)/shard_map/ppermute | solution.py:68
  199.3 21.3 %collective-permute-start.37 = (bf16[120,768]{1,0:T(8,128)(2,1)S(1)}, bf16[120,768]{1,0:T(8,128)(2,1)S(1)}, u32[]{:S(2)}, u32[]{:S(2)}) collective-permute-start(bf16[120,768]{1,0:T(8,128)(2,1)S(1)} %slice.113), channel_id=1, source_target_pairs={{0,24},{2,26},{4,28},{6,30},{8,16},{10,18},{12,20},{14,22},{16,8},... | collective-permute-start | bytes 552968 | tf_op jit(solution)/shard_map/ppermute | solution.py:68
  200.9 28.1 %collective-permute-start.45 = (bf16[96,768]{1,0:T(8,128)(2,1)S(1)}, bf16[96,768]{1,0:T(8,128)(2,1)S(1)}, u32[]{:S(2)}, u32[]{:S(2)}) collective-permute-start(bf16[96,768]{1,0:T(8,128)(2,1)S(1)} %get-tuple-element.117), channel_id=1, source_target_pairs={{0,8},{2,10},{4,12},{6,14},{8,0},{10,2},{12,4},{14,6},{16,24},{18,... | collective-permute-start | bytes 442376 | tf_op jit(solution)/shard_map/ppermute | solution.py:68
  202.0 30.6 %collective-permute-start.46 = (bf16[96,768]{1,0:T(8,128)(2,1)S(1)}, bf16[96,768]{1,0:T(8,128)(2,1)S(1)}, u32[]{:S(2)}, u32[]{:S(2)}) collective-permute-start(bf16[96,768]{1,0:T(8,128)(2,1)S(1)} %get-tuple-element.118), channel_id=1, source_target_pairs={{0,16},{2,18},{4,20},{6,22},{8,24},{10,26},{12,28},{14,30},{16,0},... | collective-permute-start | bytes 442376 | tf_op jit(solution)/shard_map/ppermute | solution.py:68
  203.7 32.3 %collective-permute-start.47 = (bf16[96,768]{1,0:T(8,128)(2,1)S(1)}, bf16[96,768]{1,0:T(8,128)(2,1)S(1)}, u32[]{:S(2)}, u32[]{:S(2)}) collective-permute-start(bf16[96,768]{1,0:T(8,128)(2,1)S(1)} %get-tuple-element.119), channel_id=1, source_target_pairs={{0,24},{2,26},{4,28},{6,30},{8,16},{10,18},{12,20},{14,22},{16,8},... | collective-permute-start | bytes 442376 | tf_op jit(solution)/shard_map/ppermute | solution.py:68
  220.4 15.7 %collective-permute-start.28 = (bf16[112,576]{1,0:T(8,128)(2,1)S(1)}, bf16[112,576]{1,0:T(8,128)(2,1)S(1)}, u32[]{:S(2)}, u32[]{:S(2)}) collective-permute-start(bf16[112,576]{1,0:T(8,128)(2,1)S(1)} %add_convert_fusion.1), channel_id=1, source_target_pairs={{0,24},{2,26},{4,28},{6,30},{8,16},{10,18},{12,20},{14,22},{16,8},... | collective-permute-start | bytes 387080 | tf_op jit(solution)/shard_map/ppermute | solution.py:68
  220.6 24.5 %collective-permute-start.27 = (bf16[112,576]{1,0:T(8,128)(2,1)S(1)}, bf16[112,576]{1,0:T(8,128)(2,1)S(1)}, u32[]{:S(2)}, u32[]{:S(2)}) collective-permute-start(bf16[112,576]{1,0:T(8,128)(2,1)S(1)} %add_convert_fusion.1), channel_id=1, source_target_pairs={{0,16},{2,18},{4,20},{6,22},{8,24},{10,26},{12,28},{14,30},{16,0},... | collective-permute-start | bytes 387080 | tf_op jit(solution)/shard_map/ppermute | solution.py:68
  229.0 22.1 %collective-permute-start.21 = (bf16[128,768]{1,0:T(8,128)(2,1)S(1)}, bf16[128,768]{1,0:T(8,128)(2,1)S(1)}, u32[]{:S(2)}, u32[]{:S(2)}) collective-permute-start(bf16[128,768]{1,0:T(8,128)(2,1)S(1)} %get-tuple-element.97), channel_id=1, source_target_pairs={{0,24},{2,26},{4,28},{6,30},{8,16},{10,18},{12,20},{14,22},{16,8},... | collective-permute-start | bytes 589832 | tf_op jit(solution)/shard_map/ppermute | solution.py:68
  232.6 37.7 %collective-permute-start.40 = (bf16[4,120,768]{2,1,0:T(8,128)(2,1)S(1)}, bf16[4,120,768]{2,1,0:T(8,128)(2,1)S(1)}, u32[]{:S(2)}, u32[]{:S(2)}) collective-permute-start(bf16[4,120,768]{2,1,0:T(8,128)(2,1)S(1)} %pad_maximum_fusion.p0), channel_id=1, source_target_pairs={{0,6},{2,4},{4,2},{6,0},{8,14},{10,12},{12,10},{14,8},{16,22},{18,... | collective-permute-start | bytes 2211848 | tf_op jit(solution)/shard_map/ppermute | solution.py:68
  236.0 35.7 %collective-permute-start.39 = (bf16[4,120,768]{2,1,0:T(8,128)(2,1)S(1)}, bf16[4,120,768]{2,1,0:T(8,128)(2,1)S(1)}, u32[]{:S(2)}, u32[]{:S(2)}) collective-permute-start(bf16[4,120,768]{2,1,0:T(8,128)(2,1)S(1)} %pad_maximum_fusion.p0), channel_id=1, source_target_pairs={{0,4},{2,6},{4,0},{6,2},{8,12},{10,14},{12,8},{14,10},{16,20},{18,... | collective-permute-start | bytes 2211848 | tf_op jit(solution)/shard_map/ppermute | solution.py:68
  236.0 37.9 %collective-permute-start.38 = (bf16[4,120,768]{2,1,0:T(8,128)(2,1)S(1)}, bf16[4,120,768]{2,1,0:T(8,128)(2,1)S(1)}, u32[]{:S(2)}, u32[]{:S(2)}) collective-permute-start(bf16[4,120,768]{2,1,0:T(8,128)(2,1)S(1)} %pad_maximum_fusion.p0), channel_id=1, source_target_pairs={{0,2},{2,0},{4,6},{6,4},{8,10},{10,8},{12,14},{14,12},{16,18},{18,... | collective-permute-start | bytes 2211848 | tf_op jit(solution)/shard_map/ppermute | solution.py:68
  245.1 5.1 %collective-permute-start.26 = (bf16[112,576]{1,0:T(8,128)(2,1)S(1)}, bf16[112,576]{1,0:T(8,128)(2,1)S(1)}, u32[]{:S(2)}, u32[]{:S(2)}) collective-permute-start(bf16[112,576]{1,0:T(8,128)(2,1)S(1)} %add_convert_fusion.1), channel_id=1, source_target_pairs={{0,8},{2,10},{4,12},{6,14},{8,0},{10,2},{12,4},{14,6},{16,24},{18,... | collective-permute-start | bytes 387080 | tf_op jit(solution)/shard_map/ppermute | solution.py:68
  250.2 7.3 %collective-permute-start.50 = (bf16[96,768]{1,0:T(8,128)(2,1)S(1)}, bf16[96,768]{1,0:T(8,128)(2,1)S(1)}, u32[]{:S(2)}, u32[]{:S(2)}) collective-permute-start(bf16[96,768]{1,0:T(8,128)(2,1)S(1)} %add_convert_fusion), channel_id=1, source_target_pairs={{0,24},{2,26},{4,28},{6,30},{8,16},{10,18},{12,20},{14,22},{16,8},... | collective-permute-start | bytes 442376 | tf_op jit(solution)/shard_map/ppermute | solution.py:68
  251.1 22.9 %collective-permute-start.31 = (bf16[4,112,576]{2,1,0:T(8,128)(2,1)S(1)}, bf16[4,112,576]{2,1,0:T(8,128)(2,1)S(1)}, u32[]{:S(2)}, u32[]{:S(2)}) collective-permute-start(bf16[4,112,576]{2,1,0:T(8,128)(2,1)S(1)} %pad_maximum_fusion.2.p0), channel_id=1, source_target_pairs={{0,6},{2,4},{4,2},{6,0},{8,14},{10,12},{12,10},{14,8},{16,22},{18,... | collective-permute-start | bytes 1548296 | tf_op jit(solution)/shard_map/ppermute | solution.py:68
  257.5 7.6 %collective-permute-start.49 = (bf16[96,768]{1,0:T(8,128)(2,1)S(1)}, bf16[96,768]{1,0:T(8,128)(2,1)S(1)}, u32[]{:S(2)}, u32[]{:S(2)}) collective-permute-start(bf16[96,768]{1,0:T(8,128)(2,1)S(1)} %add_convert_fusion), channel_id=1, source_target_pairs={{0,16},{2,18},{4,20},{6,22},{8,24},{10,26},{12,28},{14,30},{16,0},... | collective-permute-start | bytes 442376 | tf_op jit(solution)/shard_map/ppermute | solution.py:68
  265.1 5.1 %collective-permute-start.48 = (bf16[96,768]{1,0:T(8,128)(2,1)S(1)}, bf16[96,768]{1,0:T(8,128)(2,1)S(1)}, u32[]{:S(2)}, u32[]{:S(2)}) collective-permute-start(bf16[96,768]{1,0:T(8,128)(2,1)S(1)} %add_convert_fusion), channel_id=1, source_target_pairs={{0,8},{2,10},{4,12},{6,14},{8,0},{10,2},{12,4},{14,6},{16,24},{18,... | collective-permute-start | bytes 442376 | tf_op jit(solution)/shard_map/ppermute | solution.py:68
  270.3 27.0 %collective-permute-start.30 = (bf16[4,112,576]{2,1,0:T(8,128)(2,1)S(1)}, bf16[4,112,576]{2,1,0:T(8,128)(2,1)S(1)}, u32[]{:S(2)}, u32[]{:S(2)}) collective-permute-start(bf16[4,112,576]{2,1,0:T(8,128)(2,1)S(1)} %pad_maximum_fusion.2.p0), channel_id=1, source_target_pairs={{0,4},{2,6},{4,0},{6,2},{8,12},{10,14},{12,8},{14,10},{16,20},{18,... | collective-permute-start | bytes 1548296 | tf_op jit(solution)/shard_map/ppermute | solution.py:68
  270.3 27.0 %collective-permute-start.29 = (bf16[4,112,576]{2,1,0:T(8,128)(2,1)S(1)}, bf16[4,112,576]{2,1,0:T(8,128)(2,1)S(1)}, u32[]{:S(2)}, u32[]{:S(2)}) collective-permute-start(bf16[4,112,576]{2,1,0:T(8,128)(2,1)S(1)} %pad_maximum_fusion.2.p0), channel_id=1, source_target_pairs={{0,2},{2,0},{4,6},{6,4},{8,10},{10,8},{12,14},{14,12},{16,18},{18,... | collective-permute-start | bytes 1548296 | tf_op jit(solution)/shard_map/ppermute | solution.py:68
  271.7 29.0 %collective-permute-start.53 = (bf16[4,96,768]{2,1,0:T(8,128)(2,1)S(1)}, bf16[4,96,768]{2,1,0:T(8,128)(2,1)S(1)}, u32[]{:S(2)}, u32[]{:S(2)}) collective-permute-start(bf16[4,96,768]{2,1,0:T(8,128)(2,1)S(1)} %pad_maximum_fusion.1.p0), channel_id=1, source_target_pairs={{0,6},{2,4},{4,2},{6,0},{8,14},{10,12},{12,10},{14,8},{16,22},{18,... | collective-permute-start | bytes 1769480 | tf_op jit(solution)/shard_map/ppermute | solution.py:68
  273.9 34.5 %collective-permute-start.52 = (bf16[4,96,768]{2,1,0:T(8,128)(2,1)S(1)}, bf16[4,96,768]{2,1,0:T(8,128)(2,1)S(1)}, u32[]{:S(2)}, u32[]{:S(2)}) collective-permute-start(bf16[4,96,768]{2,1,0:T(8,128)(2,1)S(1)} %pad_maximum_fusion.1.p0), channel_id=1, source_target_pairs={{0,4},{2,6},{4,0},{6,2},{8,12},{10,14},{12,8},{14,10},{16,20},{18,... | collective-permute-start | bytes 1769480 | tf_op jit(solution)/shard_map/ppermute | solution.py:68
  273.9 34.5 %collective-permute-start.51 = (bf16[4,96,768]{2,1,0:T(8,128)(2,1)S(1)}, bf16[4,96,768]{2,1,0:T(8,128)(2,1)S(1)}, u32[]{:S(2)}, u32[]{:S(2)}) collective-permute-start(bf16[4,96,768]{2,1,0:T(8,128)(2,1)S(1)} %pad_maximum_fusion.1.p0), channel_id=1, source_target_pairs={{0,2},{2,0},{4,6},{6,4},{8,10},{10,8},{12,14},{14,12},{16,18},{18,... | collective-permute-start | bytes 1769480 | tf_op jit(solution)/shard_map/ppermute | solution.py:68
  (14 other events, 55.0 us)
Sparse Core Ops, SparseCore 0:
  9.6 12.2 all-gather.5
  23.4 15.4 all-gather.7
  40.4 15.6 all-gather.9

commit v5 on v4

--- a/solution.py
+++ b/solution.py
@@ -138,7 +138,13 @@
     grad_refs = refs[3:7]
     key_value_refs, bias_refs = refs[7 : 7 + pieces], refs[7 + pieces : 7 + 2 * pieces]
     query_grad_ref = refs[7 + 2 * pieces]
-    out_refs = refs[8 + 2 * pieces :]
+    outs = refs[8 + 2 * pieces :]
+    if pieces == 4:
+        own_key, own_value, turned_key, turned_value, key_x, value_y = outs
+        key_outs = (own_key, key_x.at[0], turned_key, key_x.at[1])
+        value_outs = (own_value, turned_value, value_y.at[0], value_y.at[1])
+    else:
+        key_outs, value_outs = outs[:1], outs[1:]
     rows = q_ref.shape[0]
     chunk = key_value_refs[0].shape[0] // chunks
     for head in range(GROUP_HEADS):
@@ -153,14 +159,14 @@
 
         def step(index, query_grad):
             here = pl.ds(pl.multiple_of(index * chunk, chunk), chunk)
-            for both, b, out in zip(key_value_refs, bias_refs, out_refs):
+            for both, b, key_out, value_out in zip(key_value_refs, bias_refs, key_outs, value_outs):
                 key = both[here, columns]
                 probs = jnp.exp(dot(query, key, TURNED) + b[:, here] - log_total)
                 probs_grad = dot(grad, both[here, value_columns], TURNED)
                 score_grad = (probs * (probs_grad - correction)).astype(BF16)
                 query_grad = query_grad + dot(score_grad, key)
-                out[columns, here] = dot(query_turned, score_grad).astype(BF16)
-                out[value_columns, here] = dot(grad_turned, probs.astype(BF16)).astype(BF16)
+                key_out[columns, here] = dot(query_turned, score_grad).astype(BF16)
+                value_out[columns, here] = dot(grad_turned, probs.astype(BF16)).astype(BF16)
             return query_grad
 
         total = jnp.zeros((rows, HEAD_DIM), F32)
@@ -169,8 +175,9 @@
 
 
 def attend_grad(query, context, grads, log_total, key_values, bias, chunks):
-    rows = query.shape[0]
-    outs = (shaped((rows, WIDTH)),) + tuple(shaped((2 * WIDTH, k.shape[0])) for k in key_values)
+    rows, keys = query.shape[0], key_values[0].shape[0]
+    one, two = shaped((WIDTH, keys)), shaped((2, WIDTH, keys))
+    outs = (shaped((rows, WIDTH)),) + ((one, one, one, one, two, two) if len(key_values) == 4 else (one, one))
     kernel = functools.partial(attend_grad_kernel, len(key_values), chunks)
     args = (query, context, log_total, *grads, *key_values, *bias)
     found = kernel_call(kernel, "attend_grad", outs, args, 32 if chunks == 1 else 60, 11)
@@ -315,23 +322,27 @@
     return found[0], found[1], found[2:6], found[6:10], found[10:14]
 
 
+def halves_of(spot, first, second):
+    return ((first, 1 - spot[2]), (second, spot[2]))
+
+
 def up_grad_kernel(spot, p0, p1, p2, p3, other_ref, own_ref, turned, inner):
     width = turned.shape[0]
     for i, part in enumerate((p0, p1, p2, p3)):
         turned[:, i * ROWS : (i + 1) * ROWS] = part[:, :width].T
         inner[i * ROWS : (i + 1) * ROWS, :] = part[:, width:]
     half = width // 2
-    for ref, core in ((other_ref, 1 - spot[2]), (own_ref, spot[2])):
+    for ref, core in halves_of(spot, other_ref, own_ref):
         value = dot(turned[pl.ds(pl.multiple_of(core * half, half), half), :], inner[...]).astype(BF16)
         for g in range(GROUPS):
             ref[g] = value[g * TALL : (g + 1) * TALL]
 
 
-def up_grad_parts(spot, parts, width, after):
+def up_grad_parts(spot, parts, width):
     tokens, columns = 4 * ROWS, parts[0].shape[1] - width
     out = shaped((GROUPS, TALL, columns))
     scratch = (pltpu.VMEM((width, tokens), BF16), pltpu.VMEM((tokens, columns), BF16))
-    return kernel_call(up_grad_kernel, "up_grad", (out, out), (spot, *parts), 16, 4, 1, (), scratch, after)
+    return kernel_call(up_grad_kernel, "up_grad", (out, out), (spot, *parts), 16, 4, 1, (), scratch)
 
 
 def down_grad_kernel(spot, p0, p1, p2, p3, other_ref, own_ref, turned, second, branch, sums):
@@ -350,7 +361,7 @@
         sums[core] = jnp.concatenate(
             [total[:EXTRA, start : start + width // 2], total[EXTRA:, start : start + width // 2]], axis=1
         )
-    for ref, core in ((other_ref, 1 - spot[2]), (own_ref, spot[2])):
+    for ref, core in halves_of(spot, other_ref, own_ref):
         down = dot(turned[pl.ds(pl.multiple_of(core * tall, tall), tall), :], second[...])
         out = dot(turned[pl.ds(pl.multiple_of(2 * tall + core * strip, 32), strip), :], branch[...])
         for g in range(GROUPS):
@@ -359,7 +370,7 @@
             ).astype(BF16)
 
 
-def down_grad_parts(spot, parts, width, after):
+def down_grad_parts(spot, parts, width):
     tokens = 4 * ROWS
     out = shaped((GROUPS, TALL + SHORT + EXTRA, width))
     scratch = (
@@ -368,7 +379,7 @@
         pltpu.VMEM((tokens, width), BF16),
         pltpu.VMEM((2, EXTRA, width), F32),
     )
-    return kernel_call(down_grad_kernel, "down_grad", (out, out), (spot, *parts), 16, 5, 1, (), scratch, after)
+    return kernel_call(down_grad_kernel, "down_grad", (out, out), (spot, *parts), 16, 5, 1, (), scratch)
 
 
 def core_sum_kernel(which, spot, own, received, *outs):
@@ -382,32 +393,55 @@
     return kernel_call(functools.partial(core_sum_kernel, which), name, outs, (spot, own, received), 16, 2, 1)
 
 
-def place_up_kernel(spot, p0, p1, p2, p3, up_ref):
+def pair_sum_kernel(spot, own, received, kept, sent):
+    for i, out in ((1, sent.at[0]), (2, sent.at[1]), (3, kept.at[1]), (0, kept.at[0])):
+        at = spot[0] ^ i
+        out[...] = (own[at].astype(F32) + received[at].astype(F32)).astype(BF16)
+
+
+def pair_sums(spot, own, received, name):
+    pair = shaped((2, *own.shape[1:]))
+    return kernel_call(pair_sum_kernel, name, (pair, pair), (spot, own, received), 16, 2, 1)
+
+
+def placed(spot, pieces, turned):
     group, quarter = spot[0], spot[1]
-    share = p0.shape[2] // 2
-    for i, piece in enumerate((p0, p1, p2, p3)):
+    for i in range(4):
         for g in range(GROUPS):
-            block = piece[group ^ g].astype(F32)
-            for core in range(2):
-                start = core * 4 * share + (quarter ^ i) * share
-                at = pl.ds(pl.multiple_of(start, 128), share)
-                up_ref[g * TALL : (g + 1) * TALL, at] = block[:, core * share : (core + 1) * share]
+            turn = group ^ g
+            at = ((turn & 1) << 1) ^ ((turn >> 1) * 3) if turned[1] else g
+            if turned[0]:
+                yield quarter ^ i, g, pieces[i][at]
+            else:
+                yield i, g, pieces[0][i, at]
+
+
+def place_up_kernel(turned, spot, *refs):
+    up_ref = refs[-1]
+    for quarter, g, block in placed(spot, refs[:-1], turned):
+        share = block.shape[1] // 2
+        block = block.astype(F32)
+        for core in range(2):
+            at = pl.ds(pl.multiple_of(core * 4 * share + quarter * share, 128), share)
+            up_ref[g * TALL : (g + 1) * TALL, at] = block[:, core * share : (core + 1) * share]
 
 
 BIAS_ROWS = 16
 
 
 def joined_grad_kernel(pieces, spot, query_grad, *rest):
-    key_values = rest[:pieces]
-    inputs = rest[pieces : pieces + 4]
-    weight = rest[pieces + 4]
-    other_ref, own_ref = rest[pieces + 5 : pieces + 7]
-    input_grads = rest[pieces + 7 : pieces + 11]
-    joined, turned = rest[pieces + 11 :]
-    total = sum(k[...].astype(F32) for k in key_values)
+    keys, values = rest[:pieces], rest[pieces : 2 * pieces]
+    inputs = rest[2 * pieces : 2 * pieces + 4]
+    weight, other_ref, own_ref, kept_ref, sent_ref, joined, turned = rest[2 * pieces + 4 :]
+
+    def total(parts):
+        blocks = [p[0] if len(p.shape) == 3 else p[...] for p in parts]
+        return sum(b.astype(F32) for b in blocks).T.astype(BF16)
+
     joined[:, :WIDTH] = query_grad[...]
-    joined[:, WIDTH:] = total.T.astype(BF16)
-    for i, ref in enumerate(input_grads):
+    joined[:, WIDTH : 2 * WIDTH] = total(keys)
+    joined[:, 2 * WIDTH :] = total(values)
+    for i, ref in ((1, sent_ref.at[0]), (2, sent_ref.at[1]), (3, kept_ref.at[1]), (0, kept_ref.at[0])):
         ref[...] = dot(joined[i * ROWS : (i + 1) * ROWS, :], weight[...], TURNED).astype(BF16)
     for i, x in enumerate(inputs):
         turned[:, i * ROWS : (i + 1) * ROWS] = x[...].T
@@ -415,43 +449,43 @@
         [column_sum(joined[...].astype(F32)), jnp.zeros((BIAS_ROWS - 1, 3 * WIDTH), F32)], axis=0
     ).astype(BF16)
     half = turned.shape[0] // 2
-    for ref, core in ((other_ref, 1 - spot[2]), (own_ref, spot[2])):
+    for ref, core in halves_of(spot, other_ref, own_ref):
         value = dot(turned[pl.ds(pl.multiple_of(core * half, half), half), :], joined[...]).astype(BF16)
         for quarter in range(4):
             ref[quarter, : half // 4, :] = value[quarter * (half // 4) : (quarter + 1) * (half // 4)]
             ref[quarter, half // 4 :, :] = sums
 
 
-def joined_grads(spot, query_grad, key_values, inputs, weight, after):
+def joined_grads(spot, query_grad, keys, values, inputs, weight):
     width = weight.shape[0]
-    part = shaped((4, width // 8 + BIAS_ROWS, 3 * WIDTH))
-    outs = (part, part) + (shaped((ROWS, width)),) * GROUPS
+    part, pair = shaped((4, width // 8 + BIAS_ROWS, 3 * WIDTH)), shaped((2, ROWS, width))
     scratch = (pltpu.VMEM((GROUPS * ROWS, 3 * WIDTH), BF16), pltpu.VMEM((width, GROUPS * ROWS), BF16))
-    args = (spot, query_grad, *key_values, *inputs, weight)
-    kernel = functools.partial(joined_grad_kernel, len(key_values))
-    found = kernel_call(kernel, "joined_grad", outs, args, 16, 6, 1, (), scratch, after)
-    return found[0], found[1], found[2:]
-
-
-def place_down_kernel(spot, p0, p1, p2, p3, down_ref, out_ref):
-    group, quarter = spot[0], spot[1]
-    for i, piece in enumerate((p0, p1, p2, p3)):
-        for g in range(GROUPS):
-            block = piece[group ^ g].astype(F32)
-            place = (quarter ^ i) * GROUPS + g
-            down_ref[pl.ds(pl.multiple_of(place * TALL, 8), TALL), :] = block[:TALL]
-            out_ref[pl.ds(pl.multiple_of(place * SHORT, 8), SHORT), :] = block[TALL:]
-
-
-def place_joined_kernel(spot, p0, p1, p2, p3, weight_ref, bias_ref):
-    group, quarter, core = spot[0], spot[1], spot[2]
+    args = (spot, query_grad, *keys, *values, *inputs, weight)
+    kernel = functools.partial(joined_grad_kernel, len(keys))
+    return kernel_call(kernel, "joined_grad", (part, part, pair, pair), args, 16, 6, 1, (), scratch)
+
+
+def place_down_kernel(turned, spot, *refs):
+    down_ref, out_ref = refs[-2:]
+    for quarter, g, block in placed(spot, refs[:-2], turned):
+        block = block.astype(F32)
+        place = quarter * GROUPS + g
+        down_ref[pl.ds(pl.multiple_of(place * TALL, 8), TALL), :] = block[:TALL]
+        out_ref[pl.ds(pl.multiple_of(place * SHORT, 8), SHORT), :] = block[TALL : TALL + SHORT]
+
+
+def place_joined_kernel(turned, spot, *refs):
+    weight_ref, bias_ref = refs[-2:]
+    core = spot[2]
     width = weight_ref.shape[1] // 3
-    rows = p0.shape[1] - BIAS_ROWS
-    for i, piece in enumerate((p0, p1, p2, p3)):
-        blocks = [piece[group ^ g].astype(F32) for g in range(GROUPS)]
+    found = list(placed(spot, refs[:-2], turned))
+    for i in range(4):
+        quarter = found[i * GROUPS][0]
+        blocks = [block.astype(F32) for _, _, block in found[i * GROUPS : (i + 1) * GROUPS]]
+        rows = blocks[0].shape[0] - BIAS_ROWS
+        at = pl.ds(pl.multiple_of(quarter * rows, 16), rows)
         for part in range(3):
             value = jnp.concatenate([b[:, part * WIDTH : (part + 1) * WIDTH] for b in blocks], axis=1)
-            at = pl.ds(pl.multiple_of((quarter ^ i) * rows, 16), rows)
             weight_ref[at, part * width : (part + 1) * width] = value[:rows]
             if i == 0:
                 line = value[rows : rows + 1]
@@ -542,50 +576,65 @@
     layer_out, one_grad, context_grads, up_parts, down_parts = dense(
         spot, contexts, inputs, cotangent[0], whole, up_offset, out_matrix, up_matrix, down_matrix
     )
-    context_grads = (context_grads[0], *(places.column_swap(context_grads[i], i) for i in turns))
-    up_parts = (up_parts[0], *(places.four_swap(up_parts[i], i) for i in turns))
-    down_parts = (down_parts[0], *(places.four_swap(down_parts[i], i) for i in turns))
+    def after(value, *others):
+        return lax.optimization_barrier((value, *others))[0]
 
     def to_other(block):
         return lax.ppermute(block, "shard", [(0, 1), (1, 0)])
 
-    def total_of(pieces, swap):
-        received = [swap(pieces[i], i) for i in turns]
-        total = pieces[0].astype(F32) + sum(r.astype(F32) for r in received)
+    def rest_sum(total):
         return lax.psum(total, "seq", axis_index_groups=places.rests) if rest > 1 else total
 
-    def gather_all(part):
-        column = jnp.stack([part, *(places.column_swap(part, i) for i in turns)])
+    def add(left, right):
+        return (left.astype(F32) + right.astype(F32)).astype(BF16)
+
+    def column_total(kept, sent):
+        near = places.column_swap(sent, 1)
+        far = places.column_swap(add(kept[1], near[1]), 3)
+        return kept[0].astype(F32) + near[0].astype(F32) + far.astype(F32)
+
+    def column_gather(part):
+        pair = jnp.stack([part, places.column_swap(part, 3)])
+        return jnp.concatenate([pair, places.column_swap(pair, 1)])
+
+    def plane_gather(column):
         return (column, *(places.four_swap(column, i) for i in turns))
 
+    context_grads = (context_grads[0], *(places.column_swap(context_grads[i], i) for i in turns))
+    down_parts = (down_parts[0], *(places.four_swap(down_parts[i], i) for i in turns))
     query_grad, parts = attend_grad(query, context, context_grads, log_total, key_values, bias, chunks)
-    other, own = down_grad_parts(spot, down_parts, model_width, (query_grad,))
-    down_pieces = core_sums(spot, own, to_other(other), 0, "down_sum")
-    down_part = total_of(down_pieces, places.column_swap)
+    if plane_size == 4:
+        own_key, own_value, turned_key, turned_value, key_x, value_y = parts
+        key_x, value_y = places.swap(key_x, 1), places.swap(value_y, 2)
+        keys = (own_key, key_x, places.swap(add(turned_key, key_x[1]), 2))
+        values = (own_value, value_y, places.swap(add(turned_value, value_y[1]), 1))
+    else:
+        blocks = jnp.stack(parts).reshape(2 * WIDTH, plane_size, column_rows)
+        blocks = places.exchange(jnp.transpose(blocks, (1, 0, 2)), places.planes)
+        blocks = jnp.sum(blocks.astype(F32), axis=0)
+        keys, values = (blocks[:WIDTH],), (blocks[WIDTH:],)
+    down_parts = after(down_parts, query_grad)
+    other, own = down_grad_parts(spot, down_parts, model_width)
+    down_part = rest_sum(column_total(*pair_sums(spot, own, to_other(other), "down_sum")))
+    keys, values = after((keys, values), down_part)
+    other, own, kept, sent = joined_grads(spot, query_grad, keys, values, column_inputs, group_weight)
+    input_grad = one_grad + column_total(kept, sent)
+    joined_pieces = core_sums(spot, own, to_other(other), 1, "joined_sum")
+    received = [places.four_swap(joined_pieces[i], i) for i in turns]
+    joined_part = rest_sum(joined_pieces[0].astype(F32) + sum(r.astype(F32) for r in received)).astype(BF16)
+    up_parts = after(up_parts, down_parts)
+    up_parts = (up_parts[0], *(places.four_swap(up_parts[i], i) for i in turns))
+    up_parts = after(up_parts, kept)
+    other, own = up_grad_parts(spot, up_parts, model_width)
+    up_part = rest_sum(column_total(*pair_sums(spot, own, to_other(other), "up_sum"))).astype(BF16)
+    down_all = plane_gather(column_gather(down_part[: TALL + SHORT].astype(BF16)))
+    up_all = plane_gather(column_gather(up_part))
+    joined_all = plane_gather(column_gather(joined_part))
     extra = down_part[TALL + SHORT :]
     up_bias_grad = jnp.concatenate([extra[6, :half], extra[7, :half], extra[0, half:], extra[1, half:]])
-    if plane_size == 4:
-        key_value_grads = (parts[0], *(places.swap(parts[i], i) for i in turns))
-    else:
-        blocks = parts[0].reshape(2 * WIDTH, plane_size, column_rows)
-        blocks = places.exchange(jnp.transpose(blocks, (1, 0, 2)), places.planes)
-        key_value_grads = (jnp.sum(blocks.astype(F32), axis=0),)
-    other, own, input_parts = joined_grads(
-        spot, query_grad, key_value_grads, column_inputs, group_weight, (down_pieces[0],)
-    )
-    up_other, up_own = up_grad_parts(spot, up_parts, model_width, (input_parts[0],))
-    up_pieces = core_sums(spot, up_own, to_other(up_other), 0, "up_sum")
-    up_part = total_of(up_pieces, places.column_swap).astype(BF16)
-    input_parts = (input_parts[0], *(places.column_swap(input_parts[i], i) for i in turns))
-    input_grad = one_grad + sum(p.astype(F32) for p in input_parts)
-    joined_pieces = core_sums(spot, own, to_other(other), 1, "joined_sum")
-    joined_part = total_of(joined_pieces, places.four_swap).astype(BF16)
-    low = down_part[: TALL + SHORT].astype(BF16)
-    down_all = gather_all(low)
-    up_all = gather_all(up_part)
-    joined_all = gather_all(joined_part)
+    turned = (True, True)
     down_grad, out_grad = kernel_call(
-        place_down_kernel,
+        functools.partial(place_down_kernel, turned),
         "place_down",
         (shaped((hidden_width // 2, model_width), F32), shaped((half, model_width), F32)),
         (spot, *down_all),
@@ -594,16 +643,16 @@
         1,
     )
     qkv_grad, bias_grad = kernel_call(
-        place_joined_kernel,
+        functools.partial(place_joined_kernel, turned),
         "place_joined",
         (shaped((half, 3 * model_width), F32), shaped((8, half), F32)),
         (spot, *joined_all),
-        24,
+        16,
         5,
         1,
     )
     up_grad = kernel_call(
-        place_up_kernel,
+        functools.partial(place_up_kernel, turned),
         "place_up",
         shaped((half, hidden_width), F32),
         (spot, *up_all),

time: 318 us -> 292 us (0.918)
  waiting for transfers between devices: 163 us -> 146 us
  starting transfers between devices: 75.3 us -> 65.7 us
    ppermute x51 -> x46, waiting for transfers between devices: 161 us -> 142 us  [swap(): return lax.ppermute(block, 'seq', [(i, i ^ bits) for i in range(self.size)])]
    ppermute x51 -> x46, starting transfers between devices: 74.5 us -> 65.3 us  [swap(): return lax.ppermute(block, 'seq', [(i, i ^ bits) for i in range(self.size)])]
  transfers between devices with their start and end apart: 57 -> 52, of which waited for: 26 -> 35; matrix products, arithmetic and copies ran while one was open for 2% -> 2% of each run, Pallas kernels for 9% -> 11%
where the time goes in v5:
time: 292 us
  waiting for transfers between devices  146 us (50%)
  starting transfers between devices  65.7 us (22%)
  Pallas kernels  46 us (16%)
  between operations  14.3 us (5%)
  local copies, waits for them, and re-layouts  12.3 us (4%)
  blocking collectives  4.62 us (2%)
  other arithmetic  3.2 us (1%)
    ppermute x46, waiting for transfers between devices, swap(): return lax.ppermute(block, 'seq', [(i, i ^ bits) for i in range(self.size)])  142 us
    ppermute x46, starting transfers between devices, swap(): return lax.ppermute(block, 'seq', [(i, i ^ bits) for i in range(self.size)])  65.3 us
    pallas_call x13, Pallas kernels, kernel_call(): pl.pallas_call(run if after else kernel, out_shape=outs, in_specs=spaces...  46 us
    unnamed x42, local copies, waits for them, and re-layouts  8.43 us
  transfers between devices with their start and end apart: 52, of which 35 were waited for; matrix products, arithmetic and copies ran while one was open for 2% of the time, Pallas kernels for 11%

profile of v5, /device:TPU:0, one launch (start us, length us, event | category | flops | bytes accessed | tf_op | source)
XLA Modules:
  0.0 291.7 jit_solution(17049551535307867978)
XLA Ops:
  9.5 5.1 %collective-permute-start.2 = (bf16[128,768]{1,0:T(8,128)(2,1)S(1)}, bf16[128,768]{1,0:T(8,128)(2,1)S(1)}, u32[]{:S(2)}, u32[]{:S(2)}) collective-permute-start(bf16[128,768]{1,0:T(8,128)(2,1)S(1)} %bitcast.54), channel_id=1, source_target_pairs={{0,24},{2,26},{4,28},{6,30},{8,16},{10,18},{12,20},{14,22},{16,8},... | collective-permute-start | bytes 589832 | tf_op jit(solution)/shard_map/ppermute | solution.py:68
  15.5 1.8 all-gather.1
  17.6 1.5 constant_dynamic-slice_fusion.2
  19.3 2.8 all_gather.18.weight.rest_10_
  22.1 9.2 %collective-permute-done.1.x2.rest_8_ = bf16[128,768]{1,0:T(8,128)(2,1)S(1)} collective-permute-done((bf16[128,768]{1,0:T(8,128)(2,1)S(1)}, bf16[128,768]{1,0:T(8,128)(2,1)S(1)}, u32[]{:S(2)}, u32[]{:S(2)}) %collective-permute-start.1) | collective-permute-done | bytes 196640 | tf_op jit(solution)/shard_map/ppermute | solution.py:68
  32.2 2.5 collective-permute-start.5
  37.3 8.0 %collective-permute-done.5.refs_4_.refs_10_ = bf16[512,384]{1,0:T(8,128)(2,1)S(1)} collective-permute-done((bf16[512,384]{1,0:T(8,128)(2,1)S(1)}, bf16[512,384]{1,0:T(8,128)(2,1)S(1)}, u32[]{:S(2)}, u32[]{:S(2)}) %collective-permute-start.5) | collective-permute-done | bytes 393248 | tf_op jit(solution)/shard_map/ppermute | solution.py:68
  45.3 6.5 %collective-permute-done.4.refs_3_.refs_9_ = bf16[512,384]{1,0:T(8,128)(2,1)S(1)} collective-permute-done((bf16[512,384]{1,0:T(8,128)(2,1)S(1)}, bf16[512,384]{1,0:T(8,128)(2,1)S(1)}, u32[]{:S(2)}, u32[]{:S(2)}) %collective-permute-start.4) | collective-permute-done | bytes 393248 | tf_op jit(solution)/shard_map/ppermute | solution.py:68
  51.9 9.2 %attend.1 = (f32[512,192]{1,0:T(8,128)S(1)}, f32[512,128]{1,0:T(8,128)S(1)}, bf16[128,192]{1,0:T(8,128)(2,1)S(1)}, bf16[128,192]{1,0:T(8,128)(2,1)}, bf16[128,192]{1,0:T(8,128)(2,1)}, /*index=5*/bf16[128,192]{1,0:T(8,128)(2,1)}) custom-call(bf16[512,192]{1,0:T(8,128)(2,1)S(1)} %get-tuple-element.82.refs_0_, ...), custom_call_target="tpu_custom_call" | custom-call | bytes 31500000 | tf_op jit(solution)/shard_map/attend/pallas_call | solution.py:39
  62.6 2.8 collective-permute-start.7
  65.4 1.6 collective-permute-start.8
  67.8 3.0 %collective-permute-done.7.c2 = bf16[128,192]{1,0:T(8,128)(2,1)} collective-permute-done((bf16[128,192]{1,0:T(8,128)(2,1)}, bf16[128,192]{1,0:T(8,128)(2,1)}, u32[]{:S(2)}, u32[]{:S(2)}) %collective-permute-start.7) | collective-permute-done | bytes 49184 | tf_op jit(solution)/shard_map/ppermute | solution.py:68
  71.9 2.3 copy-done
  74.2 2.3 copy-done.1
  78.8 10.1 %dense.1 = (bf16[128,768]{1,0:T(8,128)(2,1)}, f32[128,768]{1,0:T(8,128)S(1)}, bf16[128,192]{1,0:T(8,128)(2,1)S(1)}, bf16[128,192]{1,0:T(8,128)(2,1)S(1)}, bf16[1...) custom-call(s32[3]{0:T(128)S(1)} %pad_add_fusion.spot, ...), custom_call_target="tpu_custom_call" | custom-call | bytes 35000000 | tf_op jit(solution)/shard_map/dense/pallas_call | solution.py:39
  88.9 1.6 collective-permute-start.16
  94.6 2.1 collective-permute-done.9.refs_4_
  96.7 1.6 collective-permute-start.11
  98.3 1.4 collective-permute-done.10.refs_5_
  99.8 3.0 %collective-permute-done.11.refs_6_ = bf16[128,192]{1,0:T(8,128)(2,1)S(1)} collective-permute-done((bf16[128,192]{1,0:T(8,128)(2,1)S(1)}, bf16[128,192]{1,0:T(8,128)(2,1)S(1)}, u32[]{:S(2)}, u32[]{:S(2)}) %collective-permute-start.11) | collective-permute-done | bytes 49184 | tf_op jit(solution)/shard_map/ppermute | solution.py:68
  102.8 8.0 %attend_grad.1 = (bf16[512,192]{1,0:T(8,128)(2,1)S(1)}, bf16[192,512]{1,0:T(8,128)(2,1)S(1)}, bf16[192,512]{1,0:T(8,128)(2,1)S(1)}, bf16[192,512]{1,0:T(8,128)(2...) custom-call(bf16[512,192]{1,0:T(8,128)(2,1)S(1)} %get-tuple-element.82.ref, ...), custom_call_target="tpu_custom_call" | custom-call | bytes 38500000 | tf_op jit(solution)/shard_map/attend_grad/pallas_call | solution.py:39
  110.7 11.8 %collective-permute-done.17.p2 = bf16[144,2560]{1,0:T(8,128)(2,1)S(1)} collective-permute-done((bf16[144,2560]{1,0:T(8,128)(2,1)S(1)}, bf16[144,2560]{1,0:T(8,128)(2,1)S(1)}, u32[]{:S(2)}, u32[]{:S(2)}) %collective-permute-start.17) | collective-permute-done | bytes 737312 | tf_op jit(solution)/shard_map/ppermute | solution.py:68
  122.6 1.8 down_grad.1
  125.1 1.6 collective-permute-done.19.received
  127.5 1.5 collective-permute-start.20
  129.4 6.6 %collective-permute-done.12.rest_1_ = bf16[2,192,512]{2,1,0:T(8,128)(2,1)S(1)} collective-permute-done((bf16[2,192,512]{2,1,0:T(8,128)(2,1)S(1)}, bf16[2,192,512]{2,1,0:T(8,128)(2,1)S(1)}, u32[]{:S(2)}, u32[]{:S(2)}) %collective-permute-start.12) | collective-permute-done | bytes 393248 | tf_op jit(solution)/shard_map/ppermute | solution.py:68
  136.8 1.9 collective-permute-done.20
  138.8 2.2 collective-permute-start.21
  141.7 1.5 collective-permute-start.38
  143.6 3.3 %collective-permute-done.21 = bf16[128,768]{1,0:T(8,128)(2,1)S(1)} collective-permute-done((bf16[128,768]{1,0:T(8,128)(2,1)S(1)}, bf16[128,768]{1,0:T(8,128)(2,1)S(1)}, u32[]{:S(2)}, u32[]{:S(2)}) %collective-permute-start.21) | collective-permute-done | bytes 196640 | tf_op jit(solution)/shard_map/ppermute | solution.py:68
  146.8 1.4 collective-permute-start.40
  149.0 2.8 joined_grad.1
  151.8 5.6 %collective-permute-done.38.p1 = bf16[128,1536]{1,0:T(8,128)(2,1)S(1)} collective-permute-done((bf16[128,1536]{1,0:T(8,128)(2,1)S(1)}, bf16[128,1536]{1,0:T(8,128)(2,1)S(1)}, u32[]{:S(2)}, u32[]{:S(2)}) %collective-permute-start.38) | collective-permute-done | bytes 393248 | tf_op jit(solution)/shard_map/ppermute | solution.py:68
  157.4 6.3 %collective-permute-done.40.p3 = bf16[128,1536]{1,0:T(8,128)(2,1)S(1)} collective-permute-done((bf16[128,1536]{1,0:T(8,128)(2,1)S(1)}, bf16[128,1536]{1,0:T(8,128)(2,1)S(1)}, u32[]{:S(2)}, u32[]{:S(2)}) %collective-permute-start.40) | collective-permute-done | bytes 393248 | tf_op jit(solution)/shard_map/ppermute | solution.py:68
  163.7 1.8 up_grad.1
  165.6 2.0 collective-permute-start.33
  170.3 1.6 collective-permute-start.27
  172.6 2.3 collective-permute-done.33
  175.0 1.6 collective-permute-start.42
  178.4 2.4 collective-permute-start.28
  180.7 9.5 %collective-permute-done.42 = bf16[2,96,768]{2,1,0:T(8,128)(2,1)S(1)} collective-permute-done((bf16[2,96,768]{2,1,0:T(8,128)(2,1)S(1)}, bf16[2,96,768]{2,1,0:T(8,128)(2,1)S(1)}, u32[]{:S(2)}, u32[]{:S(2)}) %collective-permute-start.42) | collective-permute-done | bytes 294944 | tf_op jit(solution)/shard_map/ppermute | solution.py:68
  190.3 2.0 collective-permute-start.43
  192.3 5.8 %collective-permute-done.34 = bf16[2,120,768]{2,1,0:T(8,128)(2,1)S(1)} collective-permute-done((bf16[2,120,768]{2,1,0:T(8,128)(2,1)S(1)}, bf16[2,120,768]{2,1,0:T(8,128)(2,1)S(1)}, u32[]{:S(2)}, u32[]{:S(2)}) %collective-permute-start.34) | collective-permute-done | bytes 368672 | tf_op jit(solution)/shard_map/ppermute | solution.py:68
  198.2 1.7 collective-permute-start.37
  199.9 1.5 collective-permute-start.36
  201.4 1.5 collective-permute-start.35
  203.6 2.0 collective-permute-start.44
  205.6 7.2 %collective-permute-done.29 = bf16[2,112,576]{2,1,0:T(8,128)(2,1)S(1)} collective-permute-done((bf16[2,112,576]{2,1,0:T(8,128)(2,1)S(1)}, bf16[2,112,576]{2,1,0:T(8,128)(2,1)S(1)}, u32[]{:S(2)}, u32[]{:S(2)}) %collective-permute-start.29) | collective-permute-done | bytes 258080 | tf_op jit(solution)/shard_map/ppermute | solution.py:68
  212.8 1.9 collective-permute-start.23
  216.6 3.8 %collective-permute-done.23 = bf16[128,768]{1,0:T(8,128)(2,1)S(1)} collective-permute-done((bf16[128,768]{1,0:T(8,128)(2,1)S(1)}, bf16[128,768]{1,0:T(8,128)(2,1)S(1)}, u32[]{:S(2)}, u32[]{:S(2)}) %collective-permute-start.23) | collective-permute-done | bytes 196640 | tf_op jit(solution)/shard_map/ppermute | solution.py:68
  220.4 2.8 collective-permute-start.45
  223.2 1.5 collective-permute-start.31
  224.7 5.2 %collective-permute-done.45 = bf16[2,96,768]{2,1,0:T(8,128)(2,1)S(1)} collective-permute-done((bf16[2,96,768]{2,1,0:T(8,128)(2,1)S(1)}, bf16[2,96,768]{2,1,0:T(8,128)(2,1)S(1)}, u32[]{:S(2)}, u32[]{:S(2)}) %collective-permute-start.45) | collective-permute-done | bytes 294944 | tf_op jit(solution)/shard_map/ppermute | solution.py:68
  229.9 4.1 %collective-permute-start.30 = (bf16[4,112,576]{2,1,0:T(8,128)(2,1)S(1)}, bf16[4,112,576]{2,1,0:T(8,128)(2,1)S(1)}, u32[]{:S(2)}, u32[]{:S(2)}) collective-permute-start(bf16[4,112,576]{2,1,0:T(8,128)(2,1)S(1)} %pad_maximum_fusion.2.refs_0_), channel_id=1, source_target_pairs={{0,2},{2,0},{4,6},{6,4},{8,10},{10,8},{12,14},{14,12},{16,18},{18,... | collective-permute-start | bytes 1548296 | tf_op jit(solution)/shard_map/ppermute | solution.py:68
  234.5 1.6 collective-permute-start.48
  236.1 1.5 collective-permute-start.47
  237.6 9.2 %collective-permute-done.32.refs_3_ = bf16[4,112,576]{2,1,0:T(8,128)(2,1)S(1)} collective-permute-done((bf16[4,112,576]{2,1,0:T(8,128)(2,1)S(1)}, bf16[4,112,576]{2,1,0:T(8,128)(2,1)S(1)}, u32[]{:S(2)}, u32[]{:S(2)}) %collective-permute-start.32) | collective-permute-done | bytes 516128 | tf_op jit(solution)/shard_map/ppermute | solution.py:68
  246.8 1.6 collective-permute-start.46
  250.5 3.5 %place_down.1 = (f32[1536,768]{1,0:T(8,128)}, f32[384,768]{1,0:T(8,128)}) custom-call(s32[3]{0:T(128)S(1)} %pad_add_fusion.spot, bf16[4,120,768]{2,1,0:T(8,128)(2,1)S(1)} %pad_maximum_fusion.refs_0_, bf16[4,120,768]{2,1,0:T(8,128)(2,1)S(1)} %collective-permute-done.35.refs_1_, bf16[4,120,768]{2,1,0:T(8,128)(2,1)S(1)} %collective-permute-done.36.refs_2_, ...), custom_call_target="tpu_custom_call" | custom-call | bytes 17500000 | tf_op jit(solution)/shard_map/place_down/pallas_call | solution.py:39
  254.0 5.1 %collective-permute-done.31.refs_2_ = bf16[4,112,576]{2,1,0:T(8,128)(2,1)S(1)} collective-permute-done((bf16[4,112,576]{2,1,0:T(8,128)(2,1)S(1)}, bf16[4,112,576]{2,1,0:T(8,128)(2,1)S(1)}, u32[]{:S(2)}, u32[]{:S(2)}) %collective-permute-start.31) | collective-permute-done | bytes 516128 | tf_op jit(solution)/shard_map/ppermute | solution.py:68
  259.2 2.8 place_joined.1
  262.6 9.2 %collective-permute-done.48.refs_3_ = bf16[4,96,768]{2,1,0:T(8,128)(2,1)S(1)} collective-permute-done((bf16[4,96,768]{2,1,0:T(8,128)(2,1)S(1)}, bf16[4,96,768]{2,1,0:T(8,128)(2,1)S(1)}, u32[]{:S(2)}, u32[]{:S(2)}) %collective-permute-start.48) | collective-permute-done | bytes 589856 | tf_op jit(solution)/shard_map/ppermute | solution.py:68
  271.8 9.8 %collective-permute-done.47.refs_2_ = bf16[4,96,768]{2,1,0:T(8,128)(2,1)S(1)} collective-permute-done((bf16[4,96,768]{2,1,0:T(8,128)(2,1)S(1)}, bf16[4,96,768]{2,1,0:T(8,128)(2,1)S(1)}, u32[]{:S(2)}, u32[]{:S(2)}) %collective-permute-start.47) | collective-permute-done | bytes 589856 | tf_op jit(solution)/shard_map/ppermute | solution.py:68
  282.1 3.1 %place_up.1 = f32[384,3072]{1,0:T(8,128)} custom-call(s32[3]{0:T(128)S(1)} %pad_add_fusion.spot, bf16[4,96,768]{2,1,0:T(8,128)(2,1)S(1)} %pad_maximum_fusion.1.refs_0_, bf16[4,96,768]{2,1,0:T(8,128)(2,1)S(1)} %collective-permute-done.46.refs_1_, bf16[4,96,768]{2,1,0:T(8,128)(2,1)S(1)} %collective-permute-done.47.refs_2_, ...), custom_call_target="tpu_custom_call" | custom-call | bytes 14000000 | tf_op jit(solution)/shard_map/place_up/pallas_call | solution.py:39
  (155 shorter events, 33.3 us)
Async XLA Ops:
  7.2 64.7 %all-gather.6.cloned.1.call-start = ((), (), s32[]{:S(2)}) async-start(), calls=%async_computation | async-start | bytes 1769472 | tf_op jit(solution)/shard_map/all_gather | solution.py:531
  7.9 7.3 %copy-start.12 = (bf16[384]{0:T(512)(128)(2,1)S(1)}, bf16[384]{0:T(512)(128)(2,1)}, u32[]{:S(2)}) copy-start(bf16[384]{0:T(512)(128)(2,1)} %param.20) | copy-start | bytes 2308
  7.9 7.3 %copy-start.14 = (bf16[384]{0:T(512)(128)(2,1)S(1)}, bf16[384]{0:T(512)(128)(2,1)}, u32[]{:S(2)}) copy-start(bf16[384]{0:T(512)(128)(2,1)} %param.23) | copy-start | bytes 2308
  8.0 7.4 %copy-start.15 = (bf16[384]{0:T(512)(128)(2,1)S(1)}, bf16[384]{0:T(512)(128)(2,1)}, u32[]{:S(2)}) copy-start(bf16[384]{0:T(512)(128)(2,1)} %param.24) | copy-start | bytes 2308
  8.0 7.4 %copy-start.16 = (bf16[384]{0:T(512)(128)(2,1)S(1)}, bf16[384]{0:T(512)(128)(2,1)}, u32[]{:S(2)}) copy-start(bf16[384]{0:T(512)(128)(2,1)} %param.25) | copy-start | bytes 2308
  8.0 7.4 %copy-start.17 = (bf16[384]{0:T(512)(128)(2,1)S(1)}, bf16[384]{0:T(512)(128)(2,1)}, u32[]{:S(2)}) copy-start(bf16[384]{0:T(512)(128)(2,1)} %param.29) | copy-start | bytes 2308
  8.0 7.4 %copy-start.18 = (bf16[384]{0:T(512)(128)(2,1)S(1)}, bf16[384]{0:T(512)(128)(2,1)}, u32[]{:S(2)}) copy-start(bf16[384]{0:T(512)(128)(2,1)} %param.30) | copy-start | bytes 2308
  8.0 7.4 %copy-start.19 = (bf16[384]{0:T(512)(128)(2,1)S(1)}, bf16[384]{0:T(512)(128)(2,1)}, u32[]{:S(2)}) copy-start(bf16[384]{0:T(512)(128)(2,1)} %param.31) | copy-start | bytes 2308
  8.0 7.4 %copy-start.11 = (bf16[1536]{0:T(1024)(128)(2,1)S(1)}, bf16[1536]{0:T(1024)(128)(2,1)}, u32[]{:S(2)}) copy-start(bf16[1536]{0:T(1024)(128)(2,1)} %param.27) | copy-start | bytes 9220
  8.0 63.9 %all-gather.8.cloned.1.call-start = ((), (), s32[]{:S(2)}) async-start(), calls=%async_computation.1 | async-start | bytes 7077888 | tf_op jit(solution)/shard_map/all_gather | solution.py:531
  8.8 63.1 %all-gather.10.cloned.1.call-start = ((), (), s32[]{:S(2)}) async-start(), calls=%async_computation.2 | async-start | bytes 7077888 | tf_op jit(solution)/shard_map/all_gather | solution.py:531
  9.5 12.6 %collective-permute-start.2 = (bf16[128,768]{1,0:T(8,128)(2,1)S(1)}, bf16[128,768]{1,0:T(8,128)(2,1)S(1)}, u32[]{:S(2)}, u32[]{:S(2)}) collective-permute-start(bf16[128,768]{1,0:T(8,128)(2,1)S(1)} %bitcast.54), channel_id=1, source_target_pairs={{0,24},{2,26},{4,28},{6,30},{8,16},{10,18},{12,20},{14,22},{16,8},... | collective-permute-start | bytes 589832 | tf_op jit(solution)/shard_map/ppermute | solution.py:68
  14.6 16.7 %collective-permute-start.1 = (bf16[128,768]{1,0:T(8,128)(2,1)S(1)}, bf16[128,768]{1,0:T(8,128)(2,1)S(1)}, u32[]{:S(2)}, u32[]{:S(2)}) collective-permute-start(bf16[128,768]{1,0:T(8,128)(2,1)S(1)} %bitcast.55), channel_id=1, source_target_pairs={{0,16},{2,18},{4,20},{6,22},{8,24},{10,26},{12,28},{14,30},{16,0},... | collective-permute-start | bytes 589832 | tf_op jit(solution)/shard_map/ppermute | solution.py:68
  14.6 16.7 %collective-permute-start = (bf16[128,768]{1,0:T(8,128)(2,1)S(1)}, bf16[128,768]{1,0:T(8,128)(2,1)S(1)}, u32[]{:S(2)}, u32[]{:S(2)}) collective-permute-start(bf16[128,768]{1,0:T(8,128)(2,1)S(1)} %bitcast.56), channel_id=1, source_target_pairs={{0,8},{2,10},{4,12},{6,14},{8,0},{10,2},{12,4},{14,6},{16,24},{18,... | collective-permute-start | bytes 589832 | tf_op jit(solution)/shard_map/ppermute | solution.py:68
  19.1 16.7 %copy-start.20 = (s32[2]{0:T(128)S(1)}, s32[2]{0:T(128)}, u32[]{:S(2)}) copy-start(s32[2]{0:T(128)} %param.18) | copy-start | bytes 28
  32.2 13.1 %collective-permute-start.5 = (bf16[512,384]{1,0:T(8,128)(2,1)S(1)}, bf16[512,384]{1,0:T(8,128)(2,1)S(1)}, u32[]{:S(2)}, u32[]{:S(2)}) collective-permute-start(bf16[512,384]{1,0:T(8,128)(2,1)S(1)} %get-tuple-element.83.refs_1_.refs_7_), channel_id=1, source_target_pairs={{0,6},{2,4},{4,2},{6,0},{8,14},{10,12},{12,10},{14,8},{16,22},{18,... | collective-permute-start | bytes 1179656 | tf_op jit(solution)/shard_map/ppermute | solution.py:68
  34.7 17.1 %collective-permute-start.4 = (bf16[512,384]{1,0:T(8,128)(2,1)S(1)}, bf16[512,384]{1,0:T(8,128)(2,1)S(1)}, u32[]{:S(2)}, u32[]{:S(2)}) collective-permute-start(bf16[512,384]{1,0:T(8,128)(2,1)S(1)} %get-tuple-element.83.refs_1_.refs_7_), channel_id=1, source_target_pairs={{0,4},{2,6},{4,0},{6,2},{8,12},{10,14},{12,8},{14,10},{16,20},{18,... | collective-permute-start | bytes 1179656 | tf_op jit(solution)/shard_map/ppermute | solution.py:68
  35.2 16.6 %collective-permute-start.3 = (bf16[512,384]{1,0:T(8,128)(2,1)S(1)}, bf16[512,384]{1,0:T(8,128)(2,1)S(1)}, u32[]{:S(2)}, u32[]{:S(2)}) collective-permute-start(bf16[512,384]{1,0:T(8,128)(2,1)S(1)} %get-tuple-element.83.refs_1_.refs_7_), channel_id=1, source_target_pairs={{0,2},{2,0},{4,6},{6,4},{8,10},{10,8},{12,14},{14,12},{16,18},{18,... | collective-permute-start | bytes 1179656 | tf_op jit(solution)/shard_map/ppermute | solution.py:68
  62.6 5.3 %collective-permute-start.6 = (bf16[128,192]{1,0:T(8,128)(2,1)}, bf16[128,192]{1,0:T(8,128)(2,1)}, u32[]{:S(2)}, u32[]{:S(2)}) collective-permute-start(bf16[128,192]{1,0:T(8,128)(2,1)} %get-tuple-element.85), channel_id=1, source_target_pairs={{0,8},{2,10},{4,12},{6,14},{8,0},{10,2},{12,4},{14,6},{16,24},{18,... | collective-permute-start | bytes 147464 | tf_op jit(solution)/shard_map/ppermute | solution.py:68
  62.6 8.2 %collective-permute-start.7 = (bf16[128,192]{1,0:T(8,128)(2,1)}, bf16[128,192]{1,0:T(8,128)(2,1)}, u32[]{:S(2)}, u32[]{:S(2)}) collective-permute-start(bf16[128,192]{1,0:T(8,128)(2,1)} %get-tuple-element.86), channel_id=1, source_target_pairs={{0,16},{2,18},{4,20},{6,22},{8,24},{10,26},{12,28},{14,30},{16,0},... | collective-permute-start | bytes 147464 | tf_op jit(solution)/shard_map/ppermute | solution.py:68
  65.4 6.5 %collective-permute-start.8 = (bf16[128,192]{1,0:T(8,128)(2,1)}, bf16[128,192]{1,0:T(8,128)(2,1)}, u32[]{:S(2)}, u32[]{:S(2)}) collective-permute-start(bf16[128,192]{1,0:T(8,128)(2,1)} %get-tuple-element.87), channel_id=1, source_target_pairs={{0,24},{2,26},{4,28},{6,30},{8,16},{10,18},{12,20},{14,22},{16,8},... | collective-permute-start | bytes 147464 | tf_op jit(solution)/shard_map/ppermute | solution.py:68
  78.8 24.0 %copy-start.7 = (f32[512,192]{1,0:T(8,128)S(1)}, f32[512,192]{1,0:T(8,128)}, u32[]{:S(2)}) copy-start(f32[512,192]{1,0:T(8,128)} %copy-done.6) | copy-start | bytes 1179652
  78.8 24.0 %copy-start.9 = (f32[512,128]{1,0:T(8,128)S(1)}, f32[512,128]{1,0:T(8,128)}, u32[]{:S(2)}) copy-start(f32[512,128]{1,0:T(8,128)} %copy-done.8) | copy-start | bytes 786436
  88.9 21.9 %collective-permute-start.16 = (bf16[144,2560]{1,0:T(8,128)(2,1)S(1)}, bf16[144,2560]{1,0:T(8,128)(2,1)S(1)}, u32[]{:S(2)}, u32[]{:S(2)}) collective-permute-start(bf16[144,2560]{1,0:T(8,128)(2,1)S(1)} %get-tuple-element.104), channel_id=1, source_target_pairs={{0,2},{2,0},{4,6},{6,4},{8,10},{10,8},{12,14},{14,12},{16,18},{18,... | collective-permute-start | bytes 2211848 | tf_op jit(solution)/shard_map/ppermute | solution.py:68
  90.5 32.1 %collective-permute-start.17 = (bf16[144,2560]{1,0:T(8,128)(2,1)S(1)}, bf16[144,2560]{1,0:T(8,128)(2,1)S(1)}, u32[]{:S(2)}, u32[]{:S(2)}) collective-permute-start(bf16[144,2560]{1,0:T(8,128)(2,1)S(1)} %get-tuple-element.105), channel_id=1, source_target_pairs={{0,4},{2,6},{4,0},{6,2},{8,12},{10,14},{12,8},{14,10},{16,20},{18,... | collective-permute-start | bytes 2211848 | tf_op jit(solution)/shard_map/ppermute | solution.py:68
  91.1 31.5 %collective-permute-start.18 = (bf16[144,2560]{1,0:T(8,128)(2,1)S(1)}, bf16[144,2560]{1,0:T(8,128)(2,1)S(1)}, u32[]{:S(2)}, u32[]{:S(2)}) collective-permute-start(bf16[144,2560]{1,0:T(8,128)(2,1)S(1)} %get-tuple-element.106), channel_id=1, source_target_pairs={{0,6},{2,4},{4,2},{6,0},{8,14},{10,12},{12,10},{14,8},{16,22},{18,... | collective-permute-start | bytes 2211848 | tf_op jit(solution)/shard_map/ppermute | solution.py:68
  92.4 4.3 %collective-permute-start.9 = (bf16[128,192]{1,0:T(8,128)(2,1)S(1)}, bf16[128,192]{1,0:T(8,128)(2,1)S(1)}, u32[]{:S(2)}, u32[]{:S(2)}) collective-permute-start(bf16[128,192]{1,0:T(8,128)(2,1)S(1)} %get-tuple-element.93), channel_id=1, source_target_pairs={{0,8},{2,10},{4,12},{6,14},{8,0},{10,2},{12,4},{14,6},{16,24},{18,... | collective-permute-start | bytes 147464 | tf_op jit(solution)/shard_map/ppermute | solution.py:68
  93.4 6.4 %collective-permute-start.10 = (bf16[128,192]{1,0:T(8,128)(2,1)S(1)}, bf16[128,192]{1,0:T(8,128)(2,1)S(1)}, u32[]{:S(2)}, u32[]{:S(2)}) collective-permute-start(bf16[128,192]{1,0:T(8,128)(2,1)S(1)} %get-tuple-element.94), channel_id=1, source_target_pairs={{0,16},{2,18},{4,20},{6,22},{8,24},{10,26},{12,28},{14,30},{16,0},... | collective-permute-start | bytes 147464 | tf_op jit(solution)/shard_map/ppermute | solution.py:68
  96.7 6.1 %collective-permute-start.11 = (bf16[128,192]{1,0:T(8,128)(2,1)S(1)}, bf16[128,192]{1,0:T(8,128)(2,1)S(1)}, u32[]{:S(2)}, u32[]{:S(2)}) collective-permute-start(bf16[128,192]{1,0:T(8,128)(2,1)S(1)} %get-tuple-element.95), channel_id=1, source_target_pairs={{0,24},{2,26},{4,28},{6,30},{8,16},{10,18},{12,20},{14,22},{16,8},... | collective-permute-start | bytes 147464 | tf_op jit(solution)/shard_map/ppermute | solution.py:68
  124.4 24.6 %copy-start.5 = (bf16[128,768]{1,0:T(8,128)(2,1)S(1)}, bf16[128,768]{1,0:T(8,128)(2,1)}, u32[]{:S(2)}) copy-start(bf16[128,768]{1,0:T(8,128)(2,1)} %copy-done.4) | copy-start | bytes 589828
  124.4 2.4 collective-permute-start.19
  124.5 11.5 %collective-permute-start.12 = (bf16[2,192,512]{2,1,0:T(8,128)(2,1)S(1)}, bf16[2,192,512]{2,1,0:T(8,128)(2,1)S(1)}, u32[]{:S(2)}, u32[]{:S(2)}) collective-permute-start(bf16[2,192,512]{2,1,0:T(8,128)(2,1)S(1)} %get-tuple-element.98), channel_id=1, source_target_pairs={{0,2},{2,0},{4,6},{6,4},{8,10},{10,8},{12,14},{14,12},{16,18},{18,... | collective-permute-start | bytes 1179656 | tf_op jit(solution)/shard_map/ppermute | solution.py:68
  127.5 11.2 %collective-permute-start.20 = (bf16[2,128,768]{2,1,0:T(8,128)(2,1)S(1)}, bf16[2,128,768]{2,1,0:T(8,128)(2,1)S(1)}, u32[]{:S(2)}, u32[]{:S(2)}) collective-permute-start(bf16[2,128,768]{2,1,0:T(8,128)(2,1)S(1)} %get-tuple-element.114), channel_id=1, source_target_pairs={{0,8},{2,10},{4,12},{6,14},{8,0},{10,2},{12,4},{14,6},{16,24},{18,... | collective-permute-start | bytes 1179656 | tf_op jit(solution)/shard_map/ppermute | solution.py:68
  129.0 12.0 %collective-permute-start.14 = (bf16[2,192,512]{2,1,0:T(8,128)(2,1)S(1)}, bf16[2,192,512]{2,1,0:T(8,128)(2,1)S(1)}, u32[]{:S(2)}, u32[]{:S(2)}) collective-permute-start(bf16[2,192,512]{2,1,0:T(8,128)(2,1)S(1)} %get-tuple-element.101), channel_id=1, source_target_pairs={{0,4},{2,6},{4,0},{6,2},{8,12},{10,14},{12,8},{14,10},{16,20},{18,... | collective-permute-start | bytes 1179656 | tf_op jit(solution)/shard_map/ppermute | solution.py:68
  136.1 12.2 %collective-permute-start.13 = (bf16[192,512]{1,0:T(8,128)(2,1)S(1)}, bf16[192,512]{1,0:T(8,128)(2,1)S(1)}, u32[]{:S(2)}, u32[]{:S(2)}) collective-permute-start(bf16[192,512]{1,0:T(8,128)(2,1)S(1)} %fusion.1), channel_id=1, source_target_pairs={{0,4},{2,6},{4,0},{6,2},{8,12},{10,14},{12,8},{14,10},{16,20},{18,... | collective-permute-start | bytes 589832 | tf_op jit(solution)/shard_map/ppermute | solution.py:68
  138.8 8.1 %collective-permute-start.21 = (bf16[128,768]{1,0:T(8,128)(2,1)S(1)}, bf16[128,768]{1,0:T(8,128)(2,1)S(1)}, u32[]{:S(2)}, u32[]{:S(2)}) collective-permute-start(bf16[128,768]{1,0:T(8,128)(2,1)S(1)} %fusion.5), channel_id=1, source_target_pairs={{0,24},{2,26},{4,28},{6,30},{8,16},{10,18},{12,20},{14,22},{16,8},... | collective-permute-start | bytes 589832 | tf_op jit(solution)/shard_map/ppermute | solution.py:68
  141.1 7.9 %collective-permute-start.15 = (bf16[192,512]{1,0:T(8,128)(2,1)S(1)}, bf16[192,512]{1,0:T(8,128)(2,1)S(1)}, u32[]{:S(2)}, u32[]{:S(2)}) collective-permute-start(bf16[192,512]{1,0:T(8,128)(2,1)S(1)} %fusion), channel_id=1, source_target_pairs={{0,2},{2,0},{4,6},{6,4},{8,10},{10,8},{12,14},{14,12},{16,18},{18,... | collective-permute-start | bytes 589832 | tf_op jit(solution)/shard_map/ppermute | solution.py:68
  141.7 15.7 %collective-permute-start.38 = (bf16[128,1536]{1,0:T(8,128)(2,1)S(1)}, bf16[128,1536]{1,0:T(8,128)(2,1)S(1)}, u32[]{:S(2)}, u32[]{:S(2)}) collective-permute-start(bf16[128,1536]{1,0:T(8,128)(2,1)S(1)} %get-tuple-element.137), channel_id=1, source_target_pairs={{0,2},{2,0},{4,6},{6,4},{8,10},{10,8},{12,14},{14,12},{16,18},{18,... | collective-permute-start | bytes 1179656 | tf_op jit(solution)/shard_map/ppermute | solution.py:68
  143.2 14.2 %collective-permute-start.39 = (bf16[128,1536]{1,0:T(8,128)(2,1)S(1)}, bf16[128,1536]{1,0:T(8,128)(2,1)S(1)}, u32[]{:S(2)}, u32[]{:S(2)}) collective-permute-start(bf16[128,1536]{1,0:T(8,128)(2,1)S(1)} %get-tuple-element.138), channel_id=1, source_target_pairs={{0,4},{2,6},{4,0},{6,2},{8,12},{10,14},{12,8},{14,10},{16,20},{18,... | collective-permute-start | bytes 1179656 | tf_op jit(solution)/shard_map/ppermute | solution.py:68
  146.8 16.8 %collective-permute-start.40 = (bf16[128,1536]{1,0:T(8,128)(2,1)S(1)}, bf16[128,1536]{1,0:T(8,128)(2,1)S(1)}, u32[]{:S(2)}, u32[]{:S(2)}) collective-permute-start(bf16[128,1536]{1,0:T(8,128)(2,1)S(1)} %get-tuple-element.139), channel_id=1, source_target_pairs={{0,6},{2,4},{4,2},{6,0},{8,14},{10,12},{12,10},{14,8},{16,22},{18,... | collective-permute-start | bytes 1179656 | tf_op jit(solution)/shard_map/ppermute | solution.py:68
  151.7 15.8 %collective-permute-start.24 = (bf16[4,112,576]{2,1,0:T(8,128)(2,1)S(1)}, bf16[4,112,576]{2,1,0:T(8,128)(2,1)S(1)}, u32[]{:S(2)}, u32[]{:S(2)}) collective-permute-start(bf16[4,112,576]{2,1,0:T(8,128)(2,1)S(1)} %get-tuple-element.124), channel_id=1, source_target_pairs={{0,1},{1,0},{2,3},{3,2},{4,5},{5,4},{6,7},{7,6},{8,9},{9,8},{10,11... | collective-permute-start | bytes 1548296 | tf_op jit(solution)/shard_map/ppermute | solution.py:583
  165.5 6.3 %collective-permute-start.41 = (bf16[4,96,768]{2,1,0:T(8,128)(2,1)S(1)}, bf16[4,96,768]{2,1,0:T(8,128)(2,1)S(1)}, u32[]{:S(2)}, u32[]{:S(2)}) collective-permute-start(bf16[4,96,768]{2,1,0:T(8,128)(2,1)S(1)} %get-tuple-element.145), channel_id=1, source_target_pairs={{0,1},{1,0},{2,3},{3,2},{4,5},{5,4},{6,7},{7,6},{8,9},{9,8},{10,11... | collective-permute-start | bytes 1769480 | tf_op jit(solution)/shard_map/ppermute | solution.py:583
  165.6 9.3 %collective-permute-start.33 = (bf16[120,768]{1,0:T(8,128)(2,1)S(1)}, bf16[120,768]{1,0:T(8,128)(2,1)S(1)}, u32[]{:S(2)}, u32[]{:S(2)}) collective-permute-start(bf16[120,768]{1,0:T(8,128)(2,1)S(1)} %slice.195), channel_id=1, source_target_pairs={{0,24},{2,26},{4,28},{6,30},{8,16},{10,18},{12,20},{14,22},{16,8},... | collective-permute-start | bytes 552968 | tf_op jit(solution)/shard_map/ppermute | solution.py:68
  168.3 8.4 %collective-permute-start.25 = (bf16[112,576]{1,0:T(8,128)(2,1)S(1)}, bf16[112,576]{1,0:T(8,128)(2,1)S(1)}, u32[]{:S(2)}, u32[]{:S(2)}) collective-permute-start(bf16[112,576]{1,0:T(8,128)(2,1)S(1)} %get-tuple-element.126), channel_id=1, source_target_pairs={{0,2},{2,0},{4,6},{6,4},{8,10},{10,8},{12,14},{14,12},{16,18},{18,... | collective-permute-start | bytes 387080 | tf_op jit(solution)/shard_map/ppermute | solution.py:68
  169.6 8.7 %collective-permute-start.26 = (bf16[112,576]{1,0:T(8,128)(2,1)S(1)}, bf16[112,576]{1,0:T(8,128)(2,1)S(1)}, u32[]{:S(2)}, u32[]{:S(2)}) collective-permute-start(bf16[112,576]{1,0:T(8,128)(2,1)S(1)} %get-tuple-element.127), channel_id=1, source_target_pairs={{0,4},{2,6},{4,0},{6,2},{8,12},{10,14},{12,8},{14,10},{16,20},{18,... | collective-permute-start | bytes 387080 | tf_op jit(solution)/shard_map/ppermute | solution.py:68
  170.3 8.0 %collective-permute-start.27 = (bf16[112,576]{1,0:T(8,128)(2,1)S(1)}, bf16[112,576]{1,0:T(8,128)(2,1)S(1)}, u32[]{:S(2)}, u32[]{:S(2)}) collective-permute-start(bf16[112,576]{1,0:T(8,128)(2,1)S(1)} %get-tuple-element.128), channel_id=1, source_target_pairs={{0,6},{2,4},{4,2},{6,0},{8,14},{10,12},{12,10},{14,8},{16,22},{18,... | collective-permute-start | bytes 387080 | tf_op jit(solution)/shard_map/ppermute | solution.py:68
  171.8 31.7 %collective-permute-start.22 = (bf16[2,128,768]{2,1,0:T(8,128)(2,1)S(1)}, bf16[2,128,768]{2,1,0:T(8,128)(2,1)S(1)}, u32[]{:S(2)}, u32[]{:S(2)}) collective-permute-start(bf16[2,128,768]{2,1,0:T(8,128)(2,1)S(1)} %get-tuple-element.122), channel_id=1, source_target_pairs={{0,8},{2,10},{4,12},{6,14},{8,0},{10,2},{12,4},{14,6},{16,24},{18,... | collective-permute-start | bytes 1179656 | tf_op jit(solution)/shard_map/ppermute | solution.py:68
  175.0 15.3 %collective-permute-start.42 = (bf16[2,96,768]{2,1,0:T(8,128)(2,1)S(1)}, bf16[2,96,768]{2,1,0:T(8,128)(2,1)S(1)}, u32[]{:S(2)}, u32[]{:S(2)}) collective-permute-start(bf16[2,96,768]{2,1,0:T(8,128)(2,1)S(1)} %get-tuple-element.147), channel_id=1, source_target_pairs={{0,8},{2,10},{4,12},{6,14},{8,0},{10,2},{12,4},{14,6},{16,24},{18,... | collective-permute-start | bytes 884744 | tf_op jit(solution)/shard_map/ppermute | solution.py:68
  176.6 21.5 %collective-permute-start.34 = (bf16[2,120,768]{2,1,0:T(8,128)(2,1)S(1)}, bf16[2,120,768]{2,1,0:T(8,128)(2,1)S(1)}, u32[]{:S(2)}, u32[]{:S(2)}) collective-permute-start(bf16[2,120,768]{2,1,0:T(8,128)(2,1)S(1)} %pad_maximum_fusion.4), channel_id=1, source_target_pairs={{0,8},{2,10},{4,12},{6,14},{8,0},{10,2},{12,4},{14,6},{16,24},{18,... | collective-permute-start | bytes 1105928 | tf_op jit(solution)/shard_map/ppermute | solution.py:68
  178.4 23.1 %collective-permute-start.28 = (bf16[112,576]{1,0:T(8,128)(2,1)S(1)}, bf16[112,576]{1,0:T(8,128)(2,1)S(1)}, u32[]{:S(2)}, u32[]{:S(2)}) collective-permute-start(bf16[112,576]{1,0:T(8,128)(2,1)S(1)} %add_convert_fusion.3), channel_id=1, source_target_pairs={{0,24},{2,26},{4,28},{6,30},{8,16},{10,18},{12,20},{14,22},{16,8},... | collective-permute-start | bytes 387080 | tf_op jit(solution)/shard_map/ppermute | solution.py:68
  190.3 13.2 %collective-permute-start.43 = (bf16[96,768]{1,0:T(8,128)(2,1)S(1)}, bf16[96,768]{1,0:T(8,128)(2,1)S(1)}, u32[]{:S(2)}, u32[]{:S(2)}) collective-permute-start(bf16[96,768]{1,0:T(8,128)(2,1)S(1)} %fusion.7), channel_id=1, source_target_pairs={{0,24},{2,26},{4,28},{6,30},{8,16},{10,18},{12,20},{14,22},{16,8},... | collective-permute-start | bytes 442376 | tf_op jit(solution)/shard_map/ppermute | solution.py:68
  198.2 25.0 %collective-permute-start.37 = (bf16[4,120,768]{2,1,0:T(8,128)(2,1)S(1)}, bf16[4,120,768]{2,1,0:T(8,128)(2,1)S(1)}, u32[]{:S(2)}, u32[]{:S(2)}) collective-permute-start(bf16[4,120,768]{2,1,0:T(8,128)(2,1)S(1)} %pad_maximum_fusion.refs_0_), channel_id=1, source_target_pairs={{0,6},{2,4},{4,2},{6,0},{8,14},{10,12},{12,10},{14,8},{16,22},{18,... | collective-permute-start | bytes 2211848 | tf_op jit(solution)/shard_map/ppermute | solution.py:68
  199.9 34.6 %collective-permute-start.36 = (bf16[4,120,768]{2,1,0:T(8,128)(2,1)S(1)}, bf16[4,120,768]{2,1,0:T(8,128)(2,1)S(1)}, u32[]{:S(2)}, u32[]{:S(2)}) collective-permute-start(bf16[4,120,768]{2,1,0:T(8,128)(2,1)S(1)} %pad_maximum_fusion.refs_0_), channel_id=1, source_target_pairs={{0,4},{2,6},{4,0},{6,2},{8,12},{10,14},{12,8},{14,10},{16,20},{18,... | collective-permute-start | bytes 2211848 | tf_op jit(solution)/shard_map/ppermute | solution.py:68
  201.4 34.6 %collective-permute-start.35 = (bf16[4,120,768]{2,1,0:T(8,128)(2,1)S(1)}, bf16[4,120,768]{2,1,0:T(8,128)(2,1)S(1)}, u32[]{:S(2)}, u32[]{:S(2)}) collective-permute-start(bf16[4,120,768]{2,1,0:T(8,128)(2,1)S(1)} %pad_maximum_fusion.refs_0_), channel_id=1, source_target_pairs={{0,2},{2,0},{4,6},{6,4},{8,10},{10,8},{12,14},{14,12},{16,18},{18,... | collective-permute-start | bytes 2211848 | tf_op jit(solution)/shard_map/ppermute | solution.py:68
  203.5 9.3 %collective-permute-start.29 = (bf16[2,112,576]{2,1,0:T(8,128)(2,1)S(1)}, bf16[2,112,576]{2,1,0:T(8,128)(2,1)S(1)}, u32[]{:S(2)}, u32[]{:S(2)}) collective-permute-start(bf16[2,112,576]{2,1,0:T(8,128)(2,1)S(1)} %pad_maximum_fusion.6), channel_id=1, source_target_pairs={{0,8},{2,10},{4,12},{6,14},{8,0},{10,2},{12,4},{14,6},{16,24},{18,... | collective-permute-start | bytes 774152 | tf_op jit(solution)/shard_map/ppermute | solution.py:68
  203.6 11.9 %collective-permute-start.44 = (bf16[96,768]{1,0:T(8,128)(2,1)S(1)}, bf16[96,768]{1,0:T(8,128)(2,1)S(1)}, u32[]{:S(2)}, u32[]{:S(2)}) collective-permute-start(bf16[96,768]{1,0:T(8,128)(2,1)S(1)} %fusion.4), channel_id=1, source_target_pairs={{0,24},{2,26},{4,28},{6,30},{8,16},{10,18},{12,20},{14,22},{16,8},... | collective-permute-start | bytes 442376 | tf_op jit(solution)/shard_map/ppermute | solution.py:68
  212.8 7.6 %collective-permute-start.23 = (bf16[128,768]{1,0:T(8,128)(2,1)S(1)}, bf16[128,768]{1,0:T(8,128)(2,1)S(1)}, u32[]{:S(2)}, u32[]{:S(2)}) collective-permute-start(bf16[128,768]{1,0:T(8,128)(2,1)S(1)} %fusion.6), channel_id=1, source_target_pairs={{0,24},{2,26},{4,28},{6,30},{8,16},{10,18},{12,20},{14,22},{16,8},... | collective-permute-start | bytes 589832 | tf_op jit(solution)/shard_map/ppermute | solution.py:68
  215.4 31.4 %collective-permute-start.32 = (bf16[4,112,576]{2,1,0:T(8,128)(2,1)S(1)}, bf16[4,112,576]{2,1,0:T(8,128)(2,1)S(1)}, u32[]{:S(2)}, u32[]{:S(2)}) collective-permute-start(bf16[4,112,576]{2,1,0:T(8,128)(2,1)S(1)} %pad_maximum_fusion.2.refs_0_), channel_id=1, source_target_pairs={{0,6},{2,4},{4,2},{6,0},{8,14},{10,12},{12,10},{14,8},{16,22},{18,... | collective-permute-start | bytes 1548296 | tf_op jit(solution)/shard_map/ppermute | solution.py:68
  220.4 9.5 %collective-permute-start.45 = (bf16[2,96,768]{2,1,0:T(8,128)(2,1)S(1)}, bf16[2,96,768]{2,1,0:T(8,128)(2,1)S(1)}, u32[]{:S(2)}, u32[]{:S(2)}) collective-permute-start(bf16[2,96,768]{2,1,0:T(8,128)(2,1)S(1)} %pad_maximum_fusion.5), channel_id=1, source_target_pairs={{0,8},{2,10},{4,12},{6,14},{8,0},{10,2},{12,4},{14,6},{16,24},{18,... | collective-permute-start | bytes 884744 | tf_op jit(solution)/shard_map/ppermute | solution.py:68
  223.2 35.9 %collective-permute-start.31 = (bf16[4,112,576]{2,1,0:T(8,128)(2,1)S(1)}, bf16[4,112,576]{2,1,0:T(8,128)(2,1)S(1)}, u32[]{:S(2)}, u32[]{:S(2)}) collective-permute-start(bf16[4,112,576]{2,1,0:T(8,128)(2,1)S(1)} %pad_maximum_fusion.2.refs_0_), channel_id=1, source_target_pairs={{0,4},{2,6},{4,0},{6,2},{8,12},{10,14},{12,8},{14,10},{16,20},{18,... | collective-permute-start | bytes 1548296 | tf_op jit(solution)/shard_map/ppermute | solution.py:68
  229.9 29.3 %collective-permute-start.30 = (bf16[4,112,576]{2,1,0:T(8,128)(2,1)S(1)}, bf16[4,112,576]{2,1,0:T(8,128)(2,1)S(1)}, u32[]{:S(2)}, u32[]{:S(2)}) collective-permute-start(bf16[4,112,576]{2,1,0:T(8,128)(2,1)S(1)} %pad_maximum_fusion.2.refs_0_), channel_id=1, source_target_pairs={{0,2},{2,0},{4,6},{6,4},{8,10},{10,8},{12,14},{14,12},{16,18},{18,... | collective-permute-start | bytes 1548296 | tf_op jit(solution)/shard_map/ppermute | solution.py:68
  234.5 37.2 %collective-permute-start.48 = (bf16[4,96,768]{2,1,0:T(8,128)(2,1)S(1)}, bf16[4,96,768]{2,1,0:T(8,128)(2,1)S(1)}, u32[]{:S(2)}, u32[]{:S(2)}) collective-permute-start(bf16[4,96,768]{2,1,0:T(8,128)(2,1)S(1)} %pad_maximum_fusion.1.refs_0_), channel_id=1, source_target_pairs={{0,6},{2,4},{4,2},{6,0},{8,14},{10,12},{12,10},{14,8},{16,22},{18,... | collective-permute-start | bytes 1769480 | tf_op jit(solution)/shard_map/ppermute | solution.py:68
  236.1 45.5 %collective-permute-start.47 = (bf16[4,96,768]{2,1,0:T(8,128)(2,1)S(1)}, bf16[4,96,768]{2,1,0:T(8,128)(2,1)S(1)}, u32[]{:S(2)}, u32[]{:S(2)}) collective-permute-start(bf16[4,96,768]{2,1,0:T(8,128)(2,1)S(1)} %pad_maximum_fusion.1.refs_0_), channel_id=1, source_target_pairs={{0,4},{2,6},{4,0},{6,2},{8,12},{10,14},{12,8},{14,10},{16,20},{18,... | collective-permute-start | bytes 1769480 | tf_op jit(solution)/shard_map/ppermute | solution.py:68
  246.8 35.3 %collective-permute-start.46 = (bf16[4,96,768]{2,1,0:T(8,128)(2,1)S(1)}, bf16[4,96,768]{2,1,0:T(8,128)(2,1)S(1)}, u32[]{:S(2)}, u32[]{:S(2)}) collective-permute-start(bf16[4,96,768]{2,1,0:T(8,128)(2,1)S(1)} %pad_maximum_fusion.1.refs_0_), channel_id=1, source_target_pairs={{0,2},{2,0},{4,6},{6,4},{8,10},{10,8},{12,14},{14,12},{16,18},{18,... | collective-permute-start | bytes 1769480 | tf_op jit(solution)/shard_map/ppermute | solution.py:68
  (9 other events, 18.2 us)
Sparse Core Ops, SparseCore 0:
  9.6 12.2 all-gather.5
  23.4 15.4 all-gather.7
  40.4 15.6 all-gather.9

commit v6 on v5

--- a/solution.py
+++ b/solution.py
@@ -45,6 +45,10 @@
         cost_estimate=pl.CostEstimate(flops=0, bytes_accessed=int(micros * 3_500_000), transcendentals=0),
         name=name,
     )(*args, *after)
+
+
+def in_hbm(array):
+    return pltpu.with_memory_space_constraint(array, pltpu.HBM)
 
 
 def shaped(shape, dtype=BF16):
@@ -382,43 +386,34 @@
     return kernel_call(down_grad_kernel, "down_grad", (out, out), (spot, *parts), 16, 5, 1, (), scratch)
 
 
-def core_sum_kernel(which, spot, own, received, *outs):
-    at = spot[which]
-    for i, out in enumerate(outs):
-        out[...] = (own[at ^ i].astype(F32) + received[at ^ i].astype(F32)).astype(BF16)
-
-
-def core_sums(spot, own, received, which, name):
-    outs = (shaped(own.shape[1:]),) * 4
-    return kernel_call(functools.partial(core_sum_kernel, which), name, outs, (spot, own, received), 16, 2, 1)
-
-
-def pair_sum_kernel(spot, own, received, kept, sent):
-    for i, out in ((1, sent.at[0]), (2, sent.at[1]), (3, kept.at[1]), (0, kept.at[0])):
-        at = spot[0] ^ i
+def pair_sum_kernel(which, turns, spot, own, received, kept, sent):
+    for i, out in zip(turns, (sent.at[0], sent.at[1], kept.at[1], kept.at[0])):
+        at = spot[which] ^ i
         out[...] = (own[at].astype(F32) + received[at].astype(F32)).astype(BF16)
 
 
-def pair_sums(spot, own, received, name):
+def pair_sums(spot, own, received, name, which=0, turns=(1, 2, 3, 0)):
     pair = shaped((2, *own.shape[1:]))
-    return kernel_call(pair_sum_kernel, name, (pair, pair), (spot, own, received), 16, 2, 1)
-
-
-def placed(spot, pieces, turned):
+    kernel = functools.partial(pair_sum_kernel, which, turns)
+    return kernel_call(kernel, name, (pair, pair), (spot, own, received), 16, 2, 1)
+
+
+def placed(spot, pieces):
     group, quarter = spot[0], spot[1]
     for i in range(4):
         for g in range(GROUPS):
             turn = group ^ g
-            at = ((turn & 1) << 1) ^ ((turn >> 1) * 3) if turned[1] else g
-            if turned[0]:
-                yield quarter ^ i, g, pieces[i][at]
+            at = ((turn & 1) << 1) ^ ((turn >> 1) * 3)
+            if i < 3:
+                block = pieces[i][at]
             else:
-                yield i, g, pieces[0][i, at]
-
-
-def place_up_kernel(turned, spot, *refs):
+                block = jnp.where(at < 2, pieces[3][at & 1], pieces[4][at & 1])
+            yield quarter ^ i, g, block
+
+
+def place_up_kernel(spot, *refs):
     up_ref = refs[-1]
-    for quarter, g, block in placed(spot, refs[:-1], turned):
+    for quarter, g, block in placed(spot, refs[:-1]):
         share = block.shape[1] // 2
         block = block.astype(F32)
         for core in range(2):
@@ -465,20 +460,20 @@
     return kernel_call(kernel, "joined_grad", (part, part, pair, pair), args, 16, 6, 1, (), scratch)
 
 
-def place_down_kernel(turned, spot, *refs):
+def place_down_kernel(spot, *refs):
     down_ref, out_ref = refs[-2:]
-    for quarter, g, block in placed(spot, refs[:-2], turned):
+    for quarter, g, block in placed(spot, refs[:-2]):
         block = block.astype(F32)
         place = quarter * GROUPS + g
         down_ref[pl.ds(pl.multiple_of(place * TALL, 8), TALL), :] = block[:TALL]
         out_ref[pl.ds(pl.multiple_of(place * SHORT, 8), SHORT), :] = block[TALL : TALL + SHORT]
 
 
-def place_joined_kernel(turned, spot, *refs):
+def place_joined_kernel(spot, *refs):
     weight_ref, bias_ref = refs[-2:]
     core = spot[2]
     width = weight_ref.shape[1] // 3
-    found = list(placed(spot, refs[:-2], turned))
+    found = list(placed(spot, refs[:-2]))
     for i in range(4):
         quarter = found[i * GROUPS][0]
         blocks = [block.astype(F32) for _, _, block in found[i * GROUPS : (i + 1) * GROUPS]]
@@ -541,9 +536,9 @@
     stacked = lax.all_gather(stacked, "shard", axis=0).astype(F32)
     whole = jnp.transpose(stacked[:, : len(vectors)], (1, 0, 2)).reshape(len(vectors), model_width)
     up_offset = stacked[:, len(vectors) :].reshape(1, hidden_width)
-    out_matrix = both(out_weight)
-    up_matrix = both(up_weight)
-    down_matrix = both(down_weight)
+    out_matrix = in_hbm(both(out_weight))
+    up_matrix = in_hbm(both(up_weight))
+    down_matrix = in_hbm(both(down_weight))
 
     offset = own_columns(jnp.concatenate([whole[0], jnp.zeros_like(whole[0]), whole[1]])).reshape(1, -1)
     query, key_value = kernel_call(
@@ -593,12 +588,18 @@
         far = places.column_swap(add(kept[1], near[1]), 3)
         return kept[0].astype(F32) + near[0].astype(F32) + far.astype(F32)
 
+    def four_total(kept, sent):
+        near = places.four_swap(sent, 1)
+        far = places.four_swap(add(kept[1], near[1]), 2)
+        return kept[0].astype(F32) + near[0].astype(F32) + far.astype(F32)
+
     def column_gather(part):
         pair = jnp.stack([part, places.column_swap(part, 3)])
         return jnp.concatenate([pair, places.column_swap(pair, 1)])
 
     def plane_gather(column):
-        return (column, *(places.four_swap(column, i) for i in turns))
+        first, second = places.four_swap(column, 1), places.four_swap(column, 2)
+        return column, first, second, places.four_swap(first[:2], 2), places.four_swap(second[2:], 1)
 
     context_grads = (context_grads[0], *(places.column_swap(context_grads[i], i) for i in turns))
     down_parts = (down_parts[0], *(places.four_swap(down_parts[i], i) for i in turns))
@@ -617,24 +618,23 @@
     other, own = down_grad_parts(spot, down_parts, model_width)
     down_part = rest_sum(column_total(*pair_sums(spot, own, to_other(other), "down_sum")))
     keys, values = after((keys, values), down_part)
+    down_column = column_gather(down_part[: TALL + SHORT].astype(BF16))
     other, own, kept, sent = joined_grads(spot, query_grad, keys, values, column_inputs, group_weight)
     input_grad = one_grad + column_total(kept, sent)
-    joined_pieces = core_sums(spot, own, to_other(other), 1, "joined_sum")
-    received = [places.four_swap(joined_pieces[i], i) for i in turns]
-    joined_part = rest_sum(joined_pieces[0].astype(F32) + sum(r.astype(F32) for r in received)).astype(BF16)
+    joined_pieces = pair_sums(spot, own, to_other(other), "joined_sum", 1, (1, 3, 2, 0))
+    joined_part = rest_sum(four_total(*joined_pieces)).astype(BF16)
     up_parts = after(up_parts, down_parts)
     up_parts = (up_parts[0], *(places.four_swap(up_parts[i], i) for i in turns))
-    up_parts = after(up_parts, kept)
+    up_parts = after(up_parts, kept, down_column)
     other, own = up_grad_parts(spot, up_parts, model_width)
     up_part = rest_sum(column_total(*pair_sums(spot, own, to_other(other), "up_sum"))).astype(BF16)
-    down_all = plane_gather(column_gather(down_part[: TALL + SHORT].astype(BF16)))
-    up_all = plane_gather(column_gather(up_part))
-    joined_all = plane_gather(column_gather(joined_part))
+    down_all = plane_gather(down_column)
+    up_all = plane_gather(after(column_gather(up_part), down_all))
+    joined_all = plane_gather(after(column_gather(joined_part), down_all))
     extra = down_part[TALL + SHORT :]
     up_bias_grad = jnp.concatenate([extra[6, :half], extra[7, :half], extra[0, half:], extra[1, half:]])
-    turned = (True, True)
     down_grad, out_grad = kernel_call(
-        functools.partial(place_down_kernel, turned),
+        place_down_kernel,
         "place_down",
         (shaped((hidden_width // 2, model_width), F32), shaped((half, model_width), F32)),
         (spot, *down_all),
@@ -643,7 +643,7 @@
         1,
     )
     qkv_grad, bias_grad = kernel_call(
-        functools.partial(place_joined_kernel, turned),
+        place_joined_kernel,
         "place_joined",
         (shaped((half, 3 * model_width), F32), shaped((8, half), F32)),
         (spot, *joined_all),
@@ -652,7 +652,7 @@
         1,
     )
     up_grad = kernel_call(
-        functools.partial(place_up_kernel, turned),
+        place_up_kernel,
         "place_up",
         shaped((half, hidden_width), F32),
         (spot, *up_all),

time: 292 us -> 262 us (0.90)
  waiting for transfers between devices: 146 us -> 115 us
  local copies, waits for them, and re-layouts: 12.3 us -> 6.53 us
  starting transfers between devices: 65.7 us -> 69.6 us
    ppermute x46 -> x48, waiting for transfers between devices: 142 us -> 109 us  [swap(): return lax.ppermute(block, 'seq', [(i, i ^ bits) for i in range(self.size)])]
    unnamed x42 -> x36, local copies, waits for them, and re-layouts: 8.43 us -> 2.49 us
    ppermute x46 -> x48, starting transfers between devices: 65.3 us -> 68.9 us  [swap(): return lax.ppermute(block, 'seq', [(i, i ^ bits) for i in range(self.size)])]
  transfers between devices with their start and end apart: 52 -> 54, of which waited for: 35 -> 27; matrix products, arithmetic and copies ran while one was open for 2% -> 3% of each run, Pallas kernels for 11% -> 11%
where the time goes in v6:
time: 262 us
  waiting for transfers between devices  115 us (44%)
  starting transfers between devices  69.6 us (27%)
  Pallas kernels  48.3 us (18%)
  between operations  14.4 us (5%)
  local copies, waits for them, and re-layouts  6.53 us (2%)
  blocking collectives  4.62 us (2%)
  other arithmetic  3.22 us (1%)
    ppermute x48, waiting for transfers between devices, swap(): return lax.ppermute(block, 'seq', [(i, i ^ bits) for i in range(self.size)])  109 us
    ppermute x48, starting transfers between devices, swap(): return lax.ppermute(block, 'seq', [(i, i ^ bits) for i in range(self.size)])  68.9 us
    pallas_call x13, Pallas kernels, kernel_call(): pl.pallas_call(run if after else kernel, out_shape=outs, in_specs=spaces...  48.3 us
  transfers between devices with their start and end apart: 54, of which 27 were waited for; matrix products, arithmetic and copies ran while one was open for 3% of the time, Pallas kernels for 11%

profile of v6, /device:TPU:0, one launch (start us, length us, event | category | flops | bytes accessed | tf_op | source)
XLA Modules:
  0.0 261.5 jit_solution(1516351402099895396)
XLA Ops:
  9.5 5.1 %collective-permute-start.2 = (bf16[128,768]{1,0:T(8,128)(2,1)S(1)}, bf16[128,768]{1,0:T(8,128)(2,1)S(1)}, u32[]{:S(2)}, u32[]{:S(2)}) collective-permute-start(bf16[128,768]{1,0:T(8,128)(2,1)S(1)} %bitcast.60), channel_id=1, source_target_pairs={{0,24},{2,26},{4,28},{6,30},{8,16},{10,18},{12,20},{14,22},{16,8},... | collective-permute-start | bytes 589832 | tf_op jit(solution)/shard_map/ppermute | solution.py:72
  15.5 1.8 all-gather.1
  17.6 1.5 constant_dynamic-slice_fusion.2
  19.3 2.8 %all_gather.18.weight.rest_10_ = bf16[768,576]{1,0:T(8,128)(2,1)S(1)} all-gather(bf16[384,576]{1,0:T(8,128)(2,1)S(1)} %pad_maximum_fusion.3), channel_id=1, replica_groups=mesh['seq'=16,'shard'=2] {'shard'}, dimensions={0}, use_global_device_ids=true | all-gather | bytes 1327104 | tf_op jit(solution)/shard_map/all_gather | solution.py:526
  22.1 9.2 %collective-permute-done.1.x2.rest_8_ = bf16[128,768]{1,0:T(8,128)(2,1)S(1)} collective-permute-done((bf16[128,768]{1,0:T(8,128)(2,1)S(1)}, bf16[128,768]{1,0:T(8,128)(2,1)S(1)}, u32[]{:S(2)}, u32[]{:S(2)}) %collective-permute-start.1) | collective-permute-done | bytes 196640 | tf_op jit(solution)/shard_map/ppermute | solution.py:72
  32.2 2.5 collective-permute-start.5
  37.3 8.0 %collective-permute-done.5.refs_4_.refs_10_ = bf16[512,384]{1,0:T(8,128)(2,1)S(1)} collective-permute-done((bf16[512,384]{1,0:T(8,128)(2,1)S(1)}, bf16[512,384]{1,0:T(8,128)(2,1)S(1)}, u32[]{:S(2)}, u32[]{:S(2)}) %collective-permute-start.5) | collective-permute-done | bytes 393248 | tf_op jit(solution)/shard_map/ppermute | solution.py:72
  45.3 6.5 %collective-permute-done.4.refs_3_.refs_9_ = bf16[512,384]{1,0:T(8,128)(2,1)S(1)} collective-permute-done((bf16[512,384]{1,0:T(8,128)(2,1)S(1)}, bf16[512,384]{1,0:T(8,128)(2,1)S(1)}, u32[]{:S(2)}, u32[]{:S(2)}) %collective-permute-start.4) | collective-permute-done | bytes 393248 | tf_op jit(solution)/shard_map/ppermute | solution.py:72
  51.9 9.2 %attend.1 = (f32[512,192]{1,0:T(8,128)S(1)}, f32[512,128]{1,0:T(8,128)S(1)}, bf16[128,192]{1,0:T(8,128)(2,1)S(1)}, bf16[128,192]{1,0:T(8,128)(2,1)}, bf16[128,192]{1,0:T(8,128)(2,1)}, /*index=5*/bf16[128,192]{1,0:T(8,128)(2,1)}) custom-call(bf16[512,192]{1,0:T(8,128)(2,1)S(1)} %get-tuple-element.82.refs_0_, ...), custom_call_target="tpu_custom_call" | custom-call | bytes 31500000 | tf_op jit(solution)/shard_map/attend/pallas_call | solution.py:39
  62.5 2.8 %collective-permute-start.7 = (bf16[128,192]{1,0:T(8,128)(2,1)}, bf16[128,192]{1,0:T(8,128)(2,1)}, u32[]{:S(2)}, u32[]{:S(2)}) collective-permute-start(bf16[128,192]{1,0:T(8,128)(2,1)} %get-tuple-element.86), channel_id=1, source_target_pairs={{0,16},{2,18},{4,20},{6,22},{8,24},{10,26},{12,28},{14,30},{16,0},... | collective-permute-start | bytes 147464 | tf_op jit(solution)/shard_map/ppermute | solution.py:72
  65.4 1.5 collective-permute-start.8
  67.8 2.9 %collective-permute-done.7.c2 = bf16[128,192]{1,0:T(8,128)(2,1)} collective-permute-done((bf16[128,192]{1,0:T(8,128)(2,1)}, bf16[128,192]{1,0:T(8,128)(2,1)}, u32[]{:S(2)}, u32[]{:S(2)}) %collective-permute-start.7) | collective-permute-done | bytes 49184 | tf_op jit(solution)/shard_map/ppermute | solution.py:72
  70.8 1.1 collective-permute-done.8.c3
  72.8 12.4 %dense.1 = (bf16[128,768]{1,0:T(8,128)(2,1)}, f32[128,768]{1,0:T(8,128)S(1)}, bf16[128,192]{1,0:T(8,128)(2,1)S(1)}, bf16[128,192]{1,0:T(8,128)(2,1)S(1)}, bf16[1...) custom-call(s32[3]{0:T(128)S(1)} %pad_add_fusion.spot, ...), custom_call_target="tpu_custom_call" | custom-call | bytes 35000000 | tf_op jit(solution)/shard_map/dense/pallas_call | solution.py:39
  85.2 1.6 collective-permute-start.16
  87.4 1.4 collective-permute-start.18
  89.7 1.3 collective-permute-start.10
  90.9 2.1 collective-permute-done.9.refs_4_
  93.0 1.6 collective-permute-start.11
  94.6 1.4 collective-permute-done.10.refs_5_
  96.0 3.0 %collective-permute-done.11.refs_6_ = bf16[128,192]{1,0:T(8,128)(2,1)S(1)} collective-permute-done((bf16[128,192]{1,0:T(8,128)(2,1)S(1)}, bf16[128,192]{1,0:T(8,128)(2,1)S(1)}, u32[]{:S(2)}, u32[]{:S(2)}) %collective-permute-start.11) | collective-permute-done | bytes 49184 | tf_op jit(solution)/shard_map/ppermute | solution.py:72
  99.1 8.0 %attend_grad.1 = (bf16[512,192]{1,0:T(8,128)(2,1)S(1)}, bf16[192,512]{1,0:T(8,128)(2,1)S(1)}, bf16[192,512]{1,0:T(8,128)(2,1)S(1)}, bf16[192,512]{1,0:T(8,128)(2...) custom-call(bf16[512,192]{1,0:T(8,128)(2,1)S(1)} %get-tuple-element.82.ref, ...), custom_call_target="tpu_custom_call" | custom-call | bytes 38500000 | tf_op jit(solution)/shard_map/attend_grad/pallas_call | solution.py:39
  107.1 11.8 %collective-permute-done.17.p2 = bf16[144,2560]{1,0:T(8,128)(2,1)S(1)} collective-permute-done((bf16[144,2560]{1,0:T(8,128)(2,1)S(1)}, bf16[144,2560]{1,0:T(8,128)(2,1)S(1)}, u32[]{:S(2)}, u32[]{:S(2)}) %collective-permute-start.17) | collective-permute-done | bytes 737312 | tf_op jit(solution)/shard_map/ppermute | solution.py:72
  118.9 1.8 down_grad.1
  120.8 2.3 collective-permute-done.19.received
  123.8 1.5 collective-permute-start.20
  125.9 1.5 collective-permute-start.14
  127.4 7.6 %collective-permute-done.20 = bf16[2,128,768]{2,1,0:T(8,128)(2,1)S(1)} collective-permute-done((bf16[2,128,768]{2,1,0:T(8,128)(2,1)S(1)}, bf16[2,128,768]{2,1,0:T(8,128)(2,1)S(1)}, u32[]{:S(2)}, u32[]{:S(2)}) %collective-permute-start.20) | collective-permute-done | bytes 393248 | tf_op jit(solution)/shard_map/ppermute | solution.py:72
  135.1 2.2 collective-permute-start.21
  137.8 1.7 collective-permute-start.39
  140.0 3.2 %collective-permute-done.21 = bf16[128,768]{1,0:T(8,128)(2,1)S(1)} collective-permute-done((bf16[128,768]{1,0:T(8,128)(2,1)S(1)}, bf16[128,768]{1,0:T(8,128)(2,1)S(1)}, u32[]{:S(2)}, u32[]{:S(2)}) %collective-permute-start.21) | collective-permute-done | bytes 196640 | tf_op jit(solution)/shard_map/ppermute | solution.py:72
  143.3 2.2 collective-permute-start.29
  145.5 5.3 %collective-permute-done.29 = bf16[120,768]{1,0:T(8,128)(2,1)S(1)} collective-permute-done((bf16[120,768]{1,0:T(8,128)(2,1)S(1)}, bf16[120,768]{1,0:T(8,128)(2,1)S(1)}, u32[]{:S(2)}, u32[]{:S(2)}) %collective-permute-start.29) | collective-permute-done | bytes 184352 | tf_op jit(solution)/shard_map/ppermute | solution.py:72
  150.8 1.4 collective-permute-start.41
  152.2 4.3 %collective-permute-start.30 = (bf16[2,120,768]{2,1,0:T(8,128)(2,1)S(1)}, bf16[2,120,768]{2,1,0:T(8,128)(2,1)S(1)}, u32[]{:S(2)}, u32[]{:S(2)}) collective-permute-start(bf16[2,120,768]{2,1,0:T(8,128)(2,1)S(1)} %pad_maximum_fusion.4), channel_id=1, source_target_pairs={{0,8},{2,10},{4,12},{6,14},{8,0},{10,2},{12,4},{14,6},{16,24},{18,... | collective-permute-start | bytes 1105928 | tf_op jit(solution)/shard_map/ppermute | solution.py:72
  156.9 6.3 %collective-permute-done.15.rest_5_ = bf16[192,512]{1,0:T(8,128)(2,1)S(1)} collective-permute-done((bf16[192,512]{1,0:T(8,128)(2,1)S(1)}, bf16[192,512]{1,0:T(8,128)(2,1)S(1)}, u32[]{:S(2)}, u32[]{:S(2)}) %collective-permute-start.15) | collective-permute-done | bytes 196640 | tf_op jit(solution)/shard_map/ppermute | solution.py:72
  163.3 2.8 %joined_grad.1 = (bf16[4,112,576]{2,1,0:T(8,128)(2,1)S(1)}, bf16[4,112,576]{2,1,0:T(8,128)(2,1)S(1)}, bf16[2,128,768]{2,1,0:T(8,128)(2,1)S(1)}, bf16[2,128,768]{2,1,0:T(8,128)(2,1)S(1)}) custom-call(s32[3]{0:T(128)S(1)} %pad_add_fusion.spot, bf16[512,192]{1,0:T(8,128)(2,1)S(1)} %get-tuple-element.96.query_grad, ...), custom_call_target="tpu_custom_call" | custom-call | bytes 21000000 | tf_op jit(solution)/shard_map/joined_grad/pallas_call | solution.py:39
  166.2 1.8 up_grad.1
  168.5 1.5 collective-permute-done.42.received
  170.7 6.0 %collective-permute-start.43 = (bf16[2,96,768]{2,1,0:T(8,128)(2,1)S(1)}, bf16[2,96,768]{2,1,0:T(8,128)(2,1)S(1)}, u32[]{:S(2)}, u32[]{:S(2)}) collective-permute-start(bf16[2,96,768]{2,1,0:T(8,128)(2,1)S(1)} %get-tuple-element.146), channel_id=1, source_target_pairs={{0,8},{2,10},{4,12},{6,14},{8,0},{10,2},{12,4},{14,6},{16,24},{18,... | collective-permute-start | bytes 884744 | tf_op jit(solution)/shard_map/ppermute | solution.py:72
  178.5 1.5 collective-permute-start.31
  180.0 4.0 %collective-permute-done.43 = bf16[2,96,768]{2,1,0:T(8,128)(2,1)S(1)} collective-permute-done((bf16[2,96,768]{2,1,0:T(8,128)(2,1)S(1)}, bf16[2,96,768]{2,1,0:T(8,128)(2,1)S(1)}, u32[]{:S(2)}, u32[]{:S(2)}) %collective-permute-start.43) | collective-permute-done | bytes 294944 | tf_op jit(solution)/shard_map/ppermute | solution.py:72
  184.1 1.9 collective-permute-start.44
  186.0 1.3 collective-permute-done.25
  187.8 3.6 %collective-permute-done.44 = bf16[96,768]{1,0:T(8,128)(2,1)S(1)} collective-permute-done((bf16[96,768]{1,0:T(8,128)(2,1)S(1)}, bf16[96,768]{1,0:T(8,128)(2,1)S(1)}, u32[]{:S(2)}, u32[]{:S(2)}) %collective-permute-start.44) | collective-permute-done | bytes 147488 | tf_op jit(solution)/shard_map/ppermute | solution.py:72
  191.5 1.9 collective-permute-start.45
  193.4 5.8 %collective-permute-done.26 = bf16[112,576]{1,0:T(8,128)(2,1)S(1)} collective-permute-done((bf16[112,576]{1,0:T(8,128)(2,1)S(1)}, bf16[112,576]{1,0:T(8,128)(2,1)S(1)}, u32[]{:S(2)}, u32[]{:S(2)}) %collective-permute-start.26) | collective-permute-done | bytes 129056 | tf_op jit(solution)/shard_map/ppermute | solution.py:72
  199.2 2.8 %collective-permute-start.27 = (bf16[112,576]{1,0:T(8,128)(2,1)S(1)}, bf16[112,576]{1,0:T(8,128)(2,1)S(1)}, u32[]{:S(2)}, u32[]{:S(2)}) collective-permute-start(bf16[112,576]{1,0:T(8,128)(2,1)S(1)} %fusion.5), channel_id=1, source_target_pairs={{0,24},{2,26},{4,28},{6,30},{8,16},{10,18},{12,20},{14,22},{16,8},... | collective-permute-start | bytes 387080 | tf_op jit(solution)/shard_map/ppermute | solution.py:72
  202.8 1.6 collective-permute-start.33
  204.3 3.5 %collective-permute-done.27 = bf16[112,576]{1,0:T(8,128)(2,1)S(1)} collective-permute-done((bf16[112,576]{1,0:T(8,128)(2,1)S(1)}, bf16[112,576]{1,0:T(8,128)(2,1)S(1)}, u32[]{:S(2)}, u32[]{:S(2)}) %collective-permute-start.27) | collective-permute-done | bytes 129056 | tf_op jit(solution)/shard_map/ppermute | solution.py:72
  207.9 2.0 collective-permute-start.22
  209.9 3.2 %collective-permute-done.46 = bf16[2,96,768]{2,1,0:T(8,128)(2,1)S(1)} collective-permute-done((bf16[2,96,768]{2,1,0:T(8,128)(2,1)S(1)}, bf16[2,96,768]{2,1,0:T(8,128)(2,1)S(1)}, u32[]{:S(2)}, u32[]{:S(2)}) %collective-permute-start.46) | collective-permute-done | bytes 294944 | tf_op jit(solution)/shard_map/ppermute | solution.py:72
  213.7 1.5 collective-permute-start.47
  215.2 4.1 %collective-permute-done.28 = bf16[2,112,576]{2,1,0:T(8,128)(2,1)S(1)} collective-permute-done((bf16[2,112,576]{2,1,0:T(8,128)(2,1)S(1)}, bf16[2,112,576]{2,1,0:T(8,128)(2,1)S(1)}, u32[]{:S(2)}, u32[]{:S(2)}) %collective-permute-start.28) | collective-permute-done | bytes 258080 | tf_op jit(solution)/shard_map/ppermute | solution.py:72
  219.9 1.5 collective-permute-start.35
  221.4 5.0 %collective-permute-done.22 = bf16[2,128,768]{2,1,0:T(8,128)(2,1)S(1)} collective-permute-done((bf16[2,128,768]{2,1,0:T(8,128)(2,1)S(1)}, bf16[2,128,768]{2,1,0:T(8,128)(2,1)S(1)}, u32[]{:S(2)}, u32[]{:S(2)}) %collective-permute-start.22) | collective-permute-done | bytes 393248 | tf_op jit(solution)/shard_map/ppermute | solution.py:72
  226.5 1.8 collective-permute-start.23
  229.5 8.8 %collective-permute-done.36.refs_2_ = bf16[4,112,576]{2,1,0:T(8,128)(2,1)S(1)} collective-permute-done((bf16[4,112,576]{2,1,0:T(8,128)(2,1)S(1)}, bf16[4,112,576]{2,1,0:T(8,128)(2,1)S(1)}, u32[]{:S(2)}, u32[]{:S(2)}) %collective-permute-start.36) | collective-permute-done | bytes 516128 | tf_op jit(solution)/shard_map/ppermute | solution.py:72
  238.4 1.5 collective-permute-start.38
  239.9 2.4 collective-permute-start.37
  242.3 1.4 collective-permute-start.50
  244.6 3.5 %place_down.1 = (f32[1536,768]{1,0:T(8,128)}, f32[384,768]{1,0:T(8,128)}) custom-call(s32[3]{0:T(128)S(1)} %pad_add_fusion.spot, bf16[4,120,768]{2,1,0:T(8,128)(2,1)S(1)} %pad_maximum_fusion.refs_0_, bf16[4,120,768]{2,1,0:T(8,128)(2,1)S(1)} %collective-permute-done.31.refs_1_, bf16[4,120,768]{2,1,0:T(8,128)(2,1)S(1)} %collective-permute-done.32.refs_2_, ...), custom_call_target="tpu_custom_call" | custom-call | bytes 17500000 | tf_op jit(solution)/shard_map/place_down/pallas_call | solution.py:39
  248.5 2.8 %place_joined.1 = (f32[384,2304]{1,0:T(8,128)}, f32[8,384]{1,0:T(8,128)S(1)}) custom-call(s32[3]{0:T(128)S(1)} %pad_add_fusion.spot, bf16[4,112,576]{2,1,0:T(8,128)(2,1)S(1)} %pad_maximum_fusion.2.refs_0_, bf16[4,112,576]{2,1,0:T(8,128)(2,1)S(1)} %collective-permute-done.35.refs_1_, bf16[4,112,576]{2,1,0:T(8,128)(2,1)S(1)} %collective-permute-done.36.refs_2_, ...), custom_call_target="tpu_custom_call" | custom-call | bytes 17500000 | tf_op jit(solution)/shard_map/place_joined/pallas_call | solution.py:39
  251.9 3.1 %place_up.1 = f32[384,3072]{1,0:T(8,128)} custom-call(s32[3]{0:T(128)S(1)} %pad_add_fusion.spot, bf16[4,96,768]{2,1,0:T(8,128)(2,1)S(1)} %pad_maximum_fusion.1.refs_0_, bf16[4,96,768]{2,1,0:T(8,128)(2,1)S(1)} %collective-permute-done.47.refs_1_, bf16[4,96,768]{2,1,0:T(8,128)(2,1)S(1)} %collective-permute-done.48.refs_2_, ...), custom_call_target="tpu_custom_call" | custom-call | bytes 14000000 | tf_op jit(solution)/shard_map/place_up/pallas_call | solution.py:39
  (160 shorter events, 23.9 us)
Async XLA Ops:
  7.2 64.7 %all-gather.6.cloned.1.call-start = ((), (), s32[]{:S(2)}) async-start(), calls=%async_computation | async-start | bytes 1769472 | tf_op jit(solution)/shard_map/all_gather | solution.py:526
  8.0 7.4 %copy-start.12 = (bf16[384]{0:T(512)(128)(2,1)S(1)}, bf16[384]{0:T(512)(128)(2,1)}, u32[]{:S(2)}) copy-start(bf16[384]{0:T(512)(128)(2,1)} %param.24) | copy-start | bytes 2308
  8.0 7.4 %copy-start.13 = (bf16[384]{0:T(512)(128)(2,1)S(1)}, bf16[384]{0:T(512)(128)(2,1)}, u32[]{:S(2)}) copy-start(bf16[384]{0:T(512)(128)(2,1)} %param.25) | copy-start | bytes 2308
  8.0 7.4 %copy-start.14 = (bf16[384]{0:T(512)(128)(2,1)S(1)}, bf16[384]{0:T(512)(128)(2,1)}, u32[]{:S(2)}) copy-start(bf16[384]{0:T(512)(128)(2,1)} %param.29) | copy-start | bytes 2308
  8.0 7.4 %copy-start.15 = (bf16[384]{0:T(512)(128)(2,1)S(1)}, bf16[384]{0:T(512)(128)(2,1)}, u32[]{:S(2)}) copy-start(bf16[384]{0:T(512)(128)(2,1)} %param.30) | copy-start | bytes 2308
  8.0 7.4 %copy-start.16 = (bf16[384]{0:T(512)(128)(2,1)S(1)}, bf16[384]{0:T(512)(128)(2,1)}, u32[]{:S(2)}) copy-start(bf16[384]{0:T(512)(128)(2,1)} %param.31) | copy-start | bytes 2308
  8.0 7.4 %copy-start.8 = (bf16[1536]{0:T(1024)(128)(2,1)S(1)}, bf16[1536]{0:T(1024)(128)(2,1)}, u32[]{:S(2)}) copy-start(bf16[1536]{0:T(1024)(128)(2,1)} %param.27) | copy-start | bytes 9220
  8.0 63.9 %all-gather.8.cloned.1.call-start = ((), (), s32[]{:S(2)}) async-start(), calls=%async_computation.1 | async-start | bytes 7077888 | tf_op jit(solution)/shard_map/all_gather | solution.py:526
  8.8 63.1 %all-gather.10.cloned.1.call-start = ((), (), s32[]{:S(2)}) async-start(), calls=%async_computation.2 | async-start | bytes 7077888 | tf_op jit(solution)/shard_map/all_gather | solution.py:526
  9.5 12.6 %collective-permute-start.2 = (bf16[128,768]{1,0:T(8,128)(2,1)S(1)}, bf16[128,768]{1,0:T(8,128)(2,1)S(1)}, u32[]{:S(2)}, u32[]{:S(2)}) collective-permute-start(bf16[128,768]{1,0:T(8,128)(2,1)S(1)} %bitcast.60), channel_id=1, source_target_pairs={{0,24},{2,26},{4,28},{6,30},{8,16},{10,18},{12,20},{14,22},{16,8},... | collective-permute-start | bytes 589832 | tf_op jit(solution)/shard_map/ppermute | solution.py:72
  14.6 16.7 %collective-permute-start.1 = (bf16[128,768]{1,0:T(8,128)(2,1)S(1)}, bf16[128,768]{1,0:T(8,128)(2,1)S(1)}, u32[]{:S(2)}, u32[]{:S(2)}) collective-permute-start(bf16[128,768]{1,0:T(8,128)(2,1)S(1)} %bitcast.61), channel_id=1, source_target_pairs={{0,16},{2,18},{4,20},{6,22},{8,24},{10,26},{12,28},{14,30},{16,0},... | collective-permute-start | bytes 589832 | tf_op jit(solution)/shard_map/ppermute | solution.py:72
  14.6 16.7 %collective-permute-start = (bf16[128,768]{1,0:T(8,128)(2,1)S(1)}, bf16[128,768]{1,0:T(8,128)(2,1)S(1)}, u32[]{:S(2)}, u32[]{:S(2)}) collective-permute-start(bf16[128,768]{1,0:T(8,128)(2,1)S(1)} %bitcast.62), channel_id=1, source_target_pairs={{0,8},{2,10},{4,12},{6,14},{8,0},{10,2},{12,4},{14,6},{16,24},{18,... | collective-permute-start | bytes 589832 | tf_op jit(solution)/shard_map/ppermute | solution.py:72
  19.1 16.7 %copy-start.17 = (s32[2]{0:T(128)S(1)}, s32[2]{0:T(128)}, u32[]{:S(2)}) copy-start(s32[2]{0:T(128)} %param.18) | copy-start | bytes 28
  32.2 13.1 %collective-permute-start.5 = (bf16[512,384]{1,0:T(8,128)(2,1)S(1)}, bf16[512,384]{1,0:T(8,128)(2,1)S(1)}, u32[]{:S(2)}, u32[]{:S(2)}) collective-permute-start(bf16[512,384]{1,0:T(8,128)(2,1)S(1)} %get-tuple-element.83.refs_1_.refs_7_), channel_id=1, source_target_pairs={{0,6},{2,4},{4,2},{6,0},{8,14},{10,12},{12,10},{14,8},{16,22},{18,... | collective-permute-start | bytes 1179656 | tf_op jit(solution)/shard_map/ppermute | solution.py:72
  34.7 17.1 %collective-permute-start.4 = (bf16[512,384]{1,0:T(8,128)(2,1)S(1)}, bf16[512,384]{1,0:T(8,128)(2,1)S(1)}, u32[]{:S(2)}, u32[]{:S(2)}) collective-permute-start(bf16[512,384]{1,0:T(8,128)(2,1)S(1)} %get-tuple-element.83.refs_1_.refs_7_), channel_id=1, source_target_pairs={{0,4},{2,6},{4,0},{6,2},{8,12},{10,14},{12,8},{14,10},{16,20},{18,... | collective-permute-start | bytes 1179656 | tf_op jit(solution)/shard_map/ppermute | solution.py:72
  35.2 16.6 %collective-permute-start.3 = (bf16[512,384]{1,0:T(8,128)(2,1)S(1)}, bf16[512,384]{1,0:T(8,128)(2,1)S(1)}, u32[]{:S(2)}, u32[]{:S(2)}) collective-permute-start(bf16[512,384]{1,0:T(8,128)(2,1)S(1)} %get-tuple-element.83.refs_1_.refs_7_), channel_id=1, source_target_pairs={{0,2},{2,0},{4,6},{6,4},{8,10},{10,8},{12,14},{14,12},{16,18},{18,... | collective-permute-start | bytes 1179656 | tf_op jit(solution)/shard_map/ppermute | solution.py:72
  62.5 5.3 %collective-permute-start.6 = (bf16[128,192]{1,0:T(8,128)(2,1)}, bf16[128,192]{1,0:T(8,128)(2,1)}, u32[]{:S(2)}, u32[]{:S(2)}) collective-permute-start(bf16[128,192]{1,0:T(8,128)(2,1)} %get-tuple-element.85), channel_id=1, source_target_pairs={{0,8},{2,10},{4,12},{6,14},{8,0},{10,2},{12,4},{14,6},{16,24},{18,... | collective-permute-start | bytes 147464 | tf_op jit(solution)/shard_map/ppermute | solution.py:72
  62.5 8.2 %collective-permute-start.7 = (bf16[128,192]{1,0:T(8,128)(2,1)}, bf16[128,192]{1,0:T(8,128)(2,1)}, u32[]{:S(2)}, u32[]{:S(2)}) collective-permute-start(bf16[128,192]{1,0:T(8,128)(2,1)} %get-tuple-element.86), channel_id=1, source_target_pairs={{0,16},{2,18},{4,20},{6,22},{8,24},{10,26},{12,28},{14,30},{16,0},... | collective-permute-start | bytes 147464 | tf_op jit(solution)/shard_map/ppermute | solution.py:72
  65.4 6.5 %collective-permute-start.8 = (bf16[128,192]{1,0:T(8,128)(2,1)}, bf16[128,192]{1,0:T(8,128)(2,1)}, u32[]{:S(2)}, u32[]{:S(2)}) collective-permute-start(bf16[128,192]{1,0:T(8,128)(2,1)} %get-tuple-element.87), channel_id=1, source_target_pairs={{0,24},{2,26},{4,28},{6,30},{8,16},{10,18},{12,20},{14,22},{16,8},... | collective-permute-start | bytes 147464 | tf_op jit(solution)/shard_map/ppermute | solution.py:72
  72.8 26.3 %copy-start.4 = (f32[512,192]{1,0:T(8,128)S(1)}, f32[512,192]{1,0:T(8,128)}, u32[]{:S(2)}) copy-start(f32[512,192]{1,0:T(8,128)} %copy-done.3) | copy-start | bytes 1179652
  72.8 26.3 %copy-start.6 = (f32[512,128]{1,0:T(8,128)S(1)}, f32[512,128]{1,0:T(8,128)}, u32[]{:S(2)}) copy-start(f32[512,128]{1,0:T(8,128)} %copy-done.5) | copy-start | bytes 786436
  85.2 21.9 %collective-permute-start.16 = (bf16[144,2560]{1,0:T(8,128)(2,1)S(1)}, bf16[144,2560]{1,0:T(8,128)(2,1)S(1)}, u32[]{:S(2)}, u32[]{:S(2)}) collective-permute-start(bf16[144,2560]{1,0:T(8,128)(2,1)S(1)} %get-tuple-element.104), channel_id=1, source_target_pairs={{0,2},{2,0},{4,6},{6,4},{8,10},{10,8},{12,14},{14,12},{16,18},{18,... | collective-permute-start | bytes 2211848 | tf_op jit(solution)/shard_map/ppermute | solution.py:72
  86.8 32.1 %collective-permute-start.17 = (bf16[144,2560]{1,0:T(8,128)(2,1)S(1)}, bf16[144,2560]{1,0:T(8,128)(2,1)S(1)}, u32[]{:S(2)}, u32[]{:S(2)}) collective-permute-start(bf16[144,2560]{1,0:T(8,128)(2,1)S(1)} %get-tuple-element.105), channel_id=1, source_target_pairs={{0,4},{2,6},{4,0},{6,2},{8,12},{10,14},{12,8},{14,10},{16,20},{18,... | collective-permute-start | bytes 2211848 | tf_op jit(solution)/shard_map/ppermute | solution.py:72
  87.4 31.5 %collective-permute-start.18 = (bf16[144,2560]{1,0:T(8,128)(2,1)S(1)}, bf16[144,2560]{1,0:T(8,128)(2,1)S(1)}, u32[]{:S(2)}, u32[]{:S(2)}) collective-permute-start(bf16[144,2560]{1,0:T(8,128)(2,1)S(1)} %get-tuple-element.106), channel_id=1, source_target_pairs={{0,6},{2,4},{4,2},{6,0},{8,14},{10,12},{12,10},{14,8},{16,22},{18,... | collective-permute-start | bytes 2211848 | tf_op jit(solution)/shard_map/ppermute | solution.py:72
  88.7 4.3 %collective-permute-start.9 = (bf16[128,192]{1,0:T(8,128)(2,1)S(1)}, bf16[128,192]{1,0:T(8,128)(2,1)S(1)}, u32[]{:S(2)}, u32[]{:S(2)}) collective-permute-start(bf16[128,192]{1,0:T(8,128)(2,1)S(1)} %get-tuple-element.93), channel_id=1, source_target_pairs={{0,8},{2,10},{4,12},{6,14},{8,0},{10,2},{12,4},{14,6},{16,24},{18,... | collective-permute-start | bytes 147464 | tf_op jit(solution)/shard_map/ppermute | solution.py:72
  89.7 6.4 %collective-permute-start.10 = (bf16[128,192]{1,0:T(8,128)(2,1)S(1)}, bf16[128,192]{1,0:T(8,128)(2,1)S(1)}, u32[]{:S(2)}, u32[]{:S(2)}) collective-permute-start(bf16[128,192]{1,0:T(8,128)(2,1)S(1)} %get-tuple-element.94), channel_id=1, source_target_pairs={{0,16},{2,18},{4,20},{6,22},{8,24},{10,26},{12,28},{14,30},{16,0},... | collective-permute-start | bytes 147464 | tf_op jit(solution)/shard_map/ppermute | solution.py:72
  93.0 6.1 %collective-permute-start.11 = (bf16[128,192]{1,0:T(8,128)(2,1)S(1)}, bf16[128,192]{1,0:T(8,128)(2,1)S(1)}, u32[]{:S(2)}, u32[]{:S(2)}) collective-permute-start(bf16[128,192]{1,0:T(8,128)(2,1)S(1)} %get-tuple-element.95), channel_id=1, source_target_pairs={{0,24},{2,26},{4,28},{6,30},{8,16},{10,18},{12,20},{14,22},{16,8},... | collective-permute-start | bytes 147464 | tf_op jit(solution)/shard_map/ppermute | solution.py:72
  120.7 2.4 collective-permute-start.19
  123.8 39.5 %copy-start.2 = (bf16[128,768]{1,0:T(8,128)(2,1)S(1)}, bf16[128,768]{1,0:T(8,128)(2,1)}, u32[]{:S(2)}) copy-start(bf16[128,768]{1,0:T(8,128)(2,1)} %copy-done.1) | copy-start | bytes 589828
  123.8 11.2 %collective-permute-start.20 = (bf16[2,128,768]{2,1,0:T(8,128)(2,1)S(1)}, bf16[2,128,768]{2,1,0:T(8,128)(2,1)S(1)}, u32[]{:S(2)}, u32[]{:S(2)}) collective-permute-start(bf16[2,128,768]{2,1,0:T(8,128)(2,1)S(1)} %get-tuple-element.114), channel_id=1, source_target_pairs={{0,8},{2,10},{4,12},{6,14},{8,0},{10,2},{12,4},{14,6},{16,24},{18,... | collective-permute-start | bytes 1179656 | tf_op jit(solution)/shard_map/ppermute | solution.py:72
  125.3 11.9 %collective-permute-start.12 = (bf16[2,192,512]{2,1,0:T(8,128)(2,1)S(1)}, bf16[2,192,512]{2,1,0:T(8,128)(2,1)S(1)}, u32[]{:S(2)}, u32[]{:S(2)}) collective-permute-start(bf16[2,192,512]{2,1,0:T(8,128)(2,1)S(1)} %get-tuple-element.98), channel_id=1, source_target_pairs={{0,2},{2,0},{4,6},{6,4},{8,10},{10,8},{12,14},{14,12},{16,18},{18,... | collective-permute-start | bytes 1179656 | tf_op jit(solution)/shard_map/ppermute | solution.py:72
  125.9 26.3 %collective-permute-start.14 = (bf16[2,192,512]{2,1,0:T(8,128)(2,1)S(1)}, bf16[2,192,512]{2,1,0:T(8,128)(2,1)S(1)}, u32[]{:S(2)}, u32[]{:S(2)}) collective-permute-start(bf16[2,192,512]{2,1,0:T(8,128)(2,1)S(1)} %get-tuple-element.101), channel_id=1, source_target_pairs={{0,4},{2,6},{4,0},{6,2},{8,12},{10,14},{12,8},{14,10},{16,20},{18,... | collective-permute-start | bytes 1179656 | tf_op jit(solution)/shard_map/ppermute | solution.py:72
  135.1 8.1 %collective-permute-start.21 = (bf16[128,768]{1,0:T(8,128)(2,1)S(1)}, bf16[128,768]{1,0:T(8,128)(2,1)S(1)}, u32[]{:S(2)}, u32[]{:S(2)}) collective-permute-start(bf16[128,768]{1,0:T(8,128)(2,1)S(1)} %fusion.6), channel_id=1, source_target_pairs={{0,24},{2,26},{4,28},{6,30},{8,16},{10,18},{12,20},{14,22},{16,8},... | collective-permute-start | bytes 589832 | tf_op jit(solution)/shard_map/ppermute | solution.py:72
  137.3 19.2 %collective-permute-start.13 = (bf16[192,512]{1,0:T(8,128)(2,1)S(1)}, bf16[192,512]{1,0:T(8,128)(2,1)S(1)}, u32[]{:S(2)}, u32[]{:S(2)}) collective-permute-start(bf16[192,512]{1,0:T(8,128)(2,1)S(1)} %fusion.1), channel_id=1, source_target_pairs={{0,4},{2,6},{4,0},{6,2},{8,12},{10,14},{12,8},{14,10},{16,20},{18,... | collective-permute-start | bytes 589832 | tf_op jit(solution)/shard_map/ppermute | solution.py:72
  137.8 28.4 %collective-permute-start.39 = (bf16[128,1536]{1,0:T(8,128)(2,1)S(1)}, bf16[128,1536]{1,0:T(8,128)(2,1)S(1)}, u32[]{:S(2)}, u32[]{:S(2)}) collective-permute-start(bf16[128,1536]{1,0:T(8,128)(2,1)S(1)} %get-tuple-element.136), channel_id=1, source_target_pairs={{0,2},{2,0},{4,6},{6,4},{8,10},{10,8},{12,14},{14,12},{16,18},{18,... | collective-permute-start | bytes 1179656 | tf_op jit(solution)/shard_map/ppermute | solution.py:72
  139.4 26.7 %collective-permute-start.40 = (bf16[128,1536]{1,0:T(8,128)(2,1)S(1)}, bf16[128,1536]{1,0:T(8,128)(2,1)S(1)}, u32[]{:S(2)}, u32[]{:S(2)}) collective-permute-start(bf16[128,1536]{1,0:T(8,128)(2,1)S(1)} %get-tuple-element.137), channel_id=1, source_target_pairs={{0,4},{2,6},{4,0},{6,2},{8,12},{10,14},{12,8},{14,10},{16,20},{18,... | collective-permute-start | bytes 1179656 | tf_op jit(solution)/shard_map/ppermute | solution.py:72
  143.3 7.5 %collective-permute-start.29 = (bf16[120,768]{1,0:T(8,128)(2,1)S(1)}, bf16[120,768]{1,0:T(8,128)(2,1)S(1)}, u32[]{:S(2)}, u32[]{:S(2)}) collective-permute-start(bf16[120,768]{1,0:T(8,128)(2,1)S(1)} %slice.247), channel_id=1, source_target_pairs={{0,24},{2,26},{4,28},{6,30},{8,16},{10,18},{12,20},{14,22},{16,8},... | collective-permute-start | bytes 552968 | tf_op jit(solution)/shard_map/ppermute | solution.py:72
  150.8 15.4 %collective-permute-start.41 = (bf16[128,1536]{1,0:T(8,128)(2,1)S(1)}, bf16[128,1536]{1,0:T(8,128)(2,1)S(1)}, u32[]{:S(2)}, u32[]{:S(2)}) collective-permute-start(bf16[128,1536]{1,0:T(8,128)(2,1)S(1)} %get-tuple-element.138), channel_id=1, source_target_pairs={{0,6},{2,4},{4,2},{6,0},{8,14},{10,12},{12,10},{14,8},{16,22},{18,... | collective-permute-start | bytes 1179656 | tf_op jit(solution)/shard_map/ppermute | solution.py:72
  152.2 13.9 %collective-permute-start.30 = (bf16[2,120,768]{2,1,0:T(8,128)(2,1)S(1)}, bf16[2,120,768]{2,1,0:T(8,128)(2,1)S(1)}, u32[]{:S(2)}, u32[]{:S(2)}) collective-permute-start(bf16[2,120,768]{2,1,0:T(8,128)(2,1)S(1)} %pad_maximum_fusion.4), channel_id=1, source_target_pairs={{0,8},{2,10},{4,12},{6,14},{8,0},{10,2},{12,4},{14,6},{16,24},{18,... | collective-permute-start | bytes 1105928 | tf_op jit(solution)/shard_map/ppermute | solution.py:72
  156.5 6.8 %collective-permute-start.15 = (bf16[192,512]{1,0:T(8,128)(2,1)S(1)}, bf16[192,512]{1,0:T(8,128)(2,1)S(1)}, u32[]{:S(2)}, u32[]{:S(2)}) collective-permute-start(bf16[192,512]{1,0:T(8,128)(2,1)S(1)} %fusion), channel_id=1, source_target_pairs={{0,2},{2,0},{4,6},{6,4},{8,10},{10,8},{12,14},{14,12},{16,18},{18,... | collective-permute-start | bytes 589832 | tf_op jit(solution)/shard_map/ppermute | solution.py:72
  168.0 2.1 collective-permute-start.42
  168.1 8.7 %collective-permute-start.24 = (bf16[4,112,576]{2,1,0:T(8,128)(2,1)S(1)}, bf16[4,112,576]{2,1,0:T(8,128)(2,1)S(1)}, u32[]{:S(2)}, u32[]{:S(2)}) collective-permute-start(bf16[4,112,576]{2,1,0:T(8,128)(2,1)S(1)} %get-tuple-element.124), channel_id=1, source_target_pairs={{0,1},{1,0},{2,3},{3,2},{4,5},{5,4},{6,7},{7,6},{8,9},{9,8},{10,11... | collective-permute-start | bytes 1548296 | tf_op jit(solution)/shard_map/ppermute | solution.py:578
  170.7 13.3 %collective-permute-start.43 = (bf16[2,96,768]{2,1,0:T(8,128)(2,1)S(1)}, bf16[2,96,768]{2,1,0:T(8,128)(2,1)S(1)}, u32[]{:S(2)}, u32[]{:S(2)}) collective-permute-start(bf16[2,96,768]{2,1,0:T(8,128)(2,1)S(1)} %get-tuple-element.146), channel_id=1, source_target_pairs={{0,8},{2,10},{4,12},{6,14},{8,0},{10,2},{12,4},{14,6},{16,24},{18,... | collective-permute-start | bytes 884744 | tf_op jit(solution)/shard_map/ppermute | solution.py:72
  177.4 9.8 %collective-permute-start.25 = (bf16[2,112,576]{2,1,0:T(8,128)(2,1)S(1)}, bf16[2,112,576]{2,1,0:T(8,128)(2,1)S(1)}, u32[]{:S(2)}, u32[]{:S(2)}) collective-permute-start(bf16[2,112,576]{2,1,0:T(8,128)(2,1)S(1)} %get-tuple-element.126), channel_id=1, source_target_pairs={{0,2},{2,0},{4,6},{6,4},{8,10},{10,8},{12,14},{14,12},{16,18},{18,... | collective-permute-start | bytes 774152 | tf_op jit(solution)/shard_map/ppermute | solution.py:72
  178.1 24.0 %collective-permute-start.32 = (bf16[4,120,768]{2,1,0:T(8,128)(2,1)S(1)}, bf16[4,120,768]{2,1,0:T(8,128)(2,1)S(1)}, u32[]{:S(2)}, u32[]{:S(2)}) collective-permute-start(bf16[4,120,768]{2,1,0:T(8,128)(2,1)S(1)} %pad_maximum_fusion.refs_0_), channel_id=1, source_target_pairs={{0,4},{2,6},{4,0},{6,2},{8,12},{10,14},{12,8},{14,10},{16,20},{18,... | collective-permute-start | bytes 2211848 | tf_op jit(solution)/shard_map/ppermute | solution.py:72
  178.5 24.2 %collective-permute-start.31 = (bf16[4,120,768]{2,1,0:T(8,128)(2,1)S(1)}, bf16[4,120,768]{2,1,0:T(8,128)(2,1)S(1)}, u32[]{:S(2)}, u32[]{:S(2)}) collective-permute-start(bf16[4,120,768]{2,1,0:T(8,128)(2,1)S(1)} %pad_maximum_fusion.refs_0_), channel_id=1, source_target_pairs={{0,2},{2,0},{4,6},{6,4},{8,10},{10,8},{12,14},{14,12},{16,18},{18,... | collective-permute-start | bytes 2211848 | tf_op jit(solution)/shard_map/ppermute | solution.py:72
  184.1 7.4 %collective-permute-start.44 = (bf16[96,768]{1,0:T(8,128)(2,1)S(1)}, bf16[96,768]{1,0:T(8,128)(2,1)S(1)}, u32[]{:S(2)}, u32[]{:S(2)}) collective-permute-start(bf16[96,768]{1,0:T(8,128)(2,1)S(1)} %fusion.8), channel_id=1, source_target_pairs={{0,24},{2,26},{4,28},{6,30},{8,16},{10,18},{12,20},{14,22},{16,8},... | collective-permute-start | bytes 442376 | tf_op jit(solution)/shard_map/ppermute | solution.py:72
  187.3 11.9 %collective-permute-start.26 = (bf16[112,576]{1,0:T(8,128)(2,1)S(1)}, bf16[112,576]{1,0:T(8,128)(2,1)S(1)}, u32[]{:S(2)}, u32[]{:S(2)}) collective-permute-start(bf16[112,576]{1,0:T(8,128)(2,1)S(1)} %fusion.9), channel_id=1, source_target_pairs={{0,4},{2,6},{4,0},{6,2},{8,12},{10,14},{12,8},{14,10},{16,20},{18,... | collective-permute-start | bytes 387080 | tf_op jit(solution)/shard_map/ppermute | solution.py:72
  191.5 10.5 %collective-permute-start.45 = (bf16[96,768]{1,0:T(8,128)(2,1)S(1)}, bf16[96,768]{1,0:T(8,128)(2,1)S(1)}, u32[]{:S(2)}, u32[]{:S(2)}) collective-permute-start(bf16[96,768]{1,0:T(8,128)(2,1)S(1)} %fusion.4), channel_id=1, source_target_pairs={{0,24},{2,26},{4,28},{6,30},{8,16},{10,18},{12,20},{14,22},{16,8},... | collective-permute-start | bytes 442376 | tf_op jit(solution)/shard_map/ppermute | solution.py:72
  199.2 8.6 %collective-permute-start.27 = (bf16[112,576]{1,0:T(8,128)(2,1)S(1)}, bf16[112,576]{1,0:T(8,128)(2,1)S(1)}, u32[]{:S(2)}, u32[]{:S(2)}) collective-permute-start(bf16[112,576]{1,0:T(8,128)(2,1)S(1)} %fusion.5), channel_id=1, source_target_pairs={{0,24},{2,26},{4,28},{6,30},{8,16},{10,18},{12,20},{14,22},{16,8},... | collective-permute-start | bytes 387080 | tf_op jit(solution)/shard_map/ppermute | solution.py:72
  202.1 11.1 %collective-permute-start.46 = (bf16[2,96,768]{2,1,0:T(8,128)(2,1)S(1)}, bf16[2,96,768]{2,1,0:T(8,128)(2,1)S(1)}, u32[]{:S(2)}, u32[]{:S(2)}) collective-permute-start(bf16[2,96,768]{2,1,0:T(8,128)(2,1)S(1)} %pad_maximum_fusion.5), channel_id=1, source_target_pairs={{0,8},{2,10},{4,12},{6,14},{8,0},{10,2},{12,4},{14,6},{16,24},{18,... | collective-permute-start | bytes 884744 | tf_op jit(solution)/shard_map/ppermute | solution.py:72
  202.2 11.0 %collective-permute-start.34 = (bf16[2,120,768]{2,1,0:T(8,128)(2,1)S(1)}, bf16[2,120,768]{2,1,0:T(8,128)(2,1)S(1)}, u32[]{:S(2)}, u32[]{:S(2)}) collective-permute-start(bf16[2,120,768]{2,1,0:T(8,128)(2,1)S(1)} %slice.192), channel_id=1, source_target_pairs={{0,2},{2,0},{4,6},{6,4},{8,10},{10,8},{12,14},{14,12},{16,18},{18,... | collective-permute-start | bytes 1105928 | tf_op jit(solution)/shard_map/ppermute | solution.py:72
  202.8 10.4 %collective-permute-start.33 = (bf16[2,120,768]{2,1,0:T(8,128)(2,1)S(1)}, bf16[2,120,768]{2,1,0:T(8,128)(2,1)S(1)}, u32[]{:S(2)}, u32[]{:S(2)}) collective-permute-start(bf16[2,120,768]{2,1,0:T(8,128)(2,1)S(1)} %slice.191), channel_id=1, source_target_pairs={{0,4},{2,6},{4,0},{6,2},{8,12},{10,14},{12,8},{14,10},{16,20},{18,... | collective-permute-start | bytes 1105928 | tf_op jit(solution)/shard_map/ppermute | solution.py:72
  207.8 11.4 %collective-permute-start.28 = (bf16[2,112,576]{2,1,0:T(8,128)(2,1)S(1)}, bf16[2,112,576]{2,1,0:T(8,128)(2,1)S(1)}, u32[]{:S(2)}, u32[]{:S(2)}) collective-permute-start(bf16[2,112,576]{2,1,0:T(8,128)(2,1)S(1)} %pad_maximum_fusion.6), channel_id=1, source_target_pairs={{0,8},{2,10},{4,12},{6,14},{8,0},{10,2},{12,4},{14,6},{16,24},{18,... | collective-permute-start | bytes 774152 | tf_op jit(solution)/shard_map/ppermute | solution.py:72
  207.9 18.5 %collective-permute-start.22 = (bf16[2,128,768]{2,1,0:T(8,128)(2,1)S(1)}, bf16[2,128,768]{2,1,0:T(8,128)(2,1)S(1)}, u32[]{:S(2)}, u32[]{:S(2)}) collective-permute-start(bf16[2,128,768]{2,1,0:T(8,128)(2,1)S(1)} %get-tuple-element.122), channel_id=1, source_target_pairs={{0,8},{2,10},{4,12},{6,14},{8,0},{10,2},{12,4},{14,6},{16,24},{18,... | collective-permute-start | bytes 1179656 | tf_op jit(solution)/shard_map/ppermute | solution.py:72
  213.2 29.1 %collective-permute-start.48 = (bf16[4,96,768]{2,1,0:T(8,128)(2,1)S(1)}, bf16[4,96,768]{2,1,0:T(8,128)(2,1)S(1)}, u32[]{:S(2)}, u32[]{:S(2)}) collective-permute-start(bf16[4,96,768]{2,1,0:T(8,128)(2,1)S(1)} %pad_maximum_fusion.1.refs_0_), channel_id=1, source_target_pairs={{0,4},{2,6},{4,0},{6,2},{8,12},{10,14},{12,8},{14,10},{16,20},{18,... | collective-permute-start | bytes 1769480 | tf_op jit(solution)/shard_map/ppermute | solution.py:72
  213.7 30.0 %collective-permute-start.47 = (bf16[4,96,768]{2,1,0:T(8,128)(2,1)S(1)}, bf16[4,96,768]{2,1,0:T(8,128)(2,1)S(1)}, u32[]{:S(2)}, u32[]{:S(2)}) collective-permute-start(bf16[4,96,768]{2,1,0:T(8,128)(2,1)S(1)} %pad_maximum_fusion.1.refs_0_), channel_id=1, source_target_pairs={{0,2},{2,0},{4,6},{6,4},{8,10},{10,8},{12,14},{14,12},{16,18},{18,... | collective-permute-start | bytes 1769480 | tf_op jit(solution)/shard_map/ppermute | solution.py:72
  219.4 19.0 %collective-permute-start.36 = (bf16[4,112,576]{2,1,0:T(8,128)(2,1)S(1)}, bf16[4,112,576]{2,1,0:T(8,128)(2,1)S(1)}, u32[]{:S(2)}, u32[]{:S(2)}) collective-permute-start(bf16[4,112,576]{2,1,0:T(8,128)(2,1)S(1)} %pad_maximum_fusion.2.refs_0_), channel_id=1, source_target_pairs={{0,4},{2,6},{4,0},{6,2},{8,12},{10,14},{12,8},{14,10},{16,20},{18,... | collective-permute-start | bytes 1548296 | tf_op jit(solution)/shard_map/ppermute | solution.py:72
  219.9 20.0 %collective-permute-start.35 = (bf16[4,112,576]{2,1,0:T(8,128)(2,1)S(1)}, bf16[4,112,576]{2,1,0:T(8,128)(2,1)S(1)}, u32[]{:S(2)}, u32[]{:S(2)}) collective-permute-start(bf16[4,112,576]{2,1,0:T(8,128)(2,1)S(1)} %pad_maximum_fusion.2.refs_0_), channel_id=1, source_target_pairs={{0,2},{2,0},{4,6},{6,4},{8,10},{10,8},{12,14},{14,12},{16,18},{18,... | collective-permute-start | bytes 1548296 | tf_op jit(solution)/shard_map/ppermute | solution.py:72
  226.5 17.3 %collective-permute-start.23 = (bf16[128,768]{1,0:T(8,128)(2,1)S(1)}, bf16[128,768]{1,0:T(8,128)(2,1)S(1)}, u32[]{:S(2)}, u32[]{:S(2)}) collective-permute-start(bf16[128,768]{1,0:T(8,128)(2,1)S(1)} %fusion.7), channel_id=1, source_target_pairs={{0,24},{2,26},{4,28},{6,30},{8,16},{10,18},{12,20},{14,22},{16,8},... | collective-permute-start | bytes 589832 | tf_op jit(solution)/shard_map/ppermute | solution.py:72
  238.4 9.8 %collective-permute-start.38 = (bf16[2,112,576]{2,1,0:T(8,128)(2,1)S(1)}, bf16[2,112,576]{2,1,0:T(8,128)(2,1)S(1)}, u32[]{:S(2)}, u32[]{:S(2)}) collective-permute-start(bf16[2,112,576]{2,1,0:T(8,128)(2,1)S(1)} %slice.194), channel_id=1, source_target_pairs={{0,2},{2,0},{4,6},{6,4},{8,10},{10,8},{12,14},{14,12},{16,18},{18,... | collective-permute-start | bytes 774152 | tf_op jit(solution)/shard_map/ppermute | solution.py:72
  239.9 8.6 %collective-permute-start.37 = (bf16[2,112,576]{2,1,0:T(8,128)(2,1)S(1)}, bf16[2,112,576]{2,1,0:T(8,128)(2,1)S(1)}, u32[]{:S(2)}, u32[]{:S(2)}) collective-permute-start(bf16[2,112,576]{2,1,0:T(8,128)(2,1)S(1)} %slice.193), channel_id=1, source_target_pairs={{0,4},{2,6},{4,0},{6,2},{8,12},{10,14},{12,8},{14,10},{16,20},{18,... | collective-permute-start | bytes 774152 | tf_op jit(solution)/shard_map/ppermute | solution.py:72
  242.3 9.6 %collective-permute-start.50 = (bf16[2,96,768]{2,1,0:T(8,128)(2,1)S(1)}, bf16[2,96,768]{2,1,0:T(8,128)(2,1)S(1)}, u32[]{:S(2)}, u32[]{:S(2)}) collective-permute-start(bf16[2,96,768]{2,1,0:T(8,128)(2,1)S(1)} %slice.201), channel_id=1, source_target_pairs={{0,2},{2,0},{4,6},{6,4},{8,10},{10,8},{12,14},{14,12},{16,18},{18,... | collective-permute-start | bytes 884744 | tf_op jit(solution)/shard_map/ppermute | solution.py:72
  243.7 8.2 %collective-permute-start.49 = (bf16[2,96,768]{2,1,0:T(8,128)(2,1)S(1)}, bf16[2,96,768]{2,1,0:T(8,128)(2,1)S(1)}, u32[]{:S(2)}, u32[]{:S(2)}) collective-permute-start(bf16[2,96,768]{2,1,0:T(8,128)(2,1)S(1)} %slice.200), channel_id=1, source_target_pairs={{0,4},{2,6},{4,0},{6,2},{8,12},{10,14},{12,8},{14,10},{16,20},{18,... | collective-permute-start | bytes 884744 | tf_op jit(solution)/shard_map/ppermute | solution.py:72
  (8 other events, 26.9 us)
Sparse Core Ops, SparseCore 0:
  9.6 12.2 all-gather.5
  23.4 15.4 all-gather.7
  40.4 15.6 all-gather.9

commit v7 on v6

--- a/solution.py
+++ b/solution.py
@@ -207,12 +207,14 @@
 
 
 TALL, SHORT, EXTRA = 96, 24, 8
+PACKED = 32
 
 
 def dense_kernel(width, spot, c0, c1, c2, c3, x_ref, grad_ref, vectors, up_offset, out_hbm, up_hbm, down_hbm, *rest):
     layer_ref, one_grad_ref = rest[:2]
-    context_grads, up_parts, down_parts = rest[2:6], rest[6:10], rest[10:14]
-    out_w, up_w, down_w, slope, active_ref, inner_ref, sums_ref, sems = rest[14:]
+    branch_ref = rest[2]
+    context_grads, up_parts, down_parts = rest[3:7], rest[7:11], rest[11:15]
+    out_w, up_w, down_w, slope, active_ref, inner_ref, sums_ref, sems = rest[15:]
     copies = [
         pltpu.make_async_copy(source, target, sems.at[i])
         for i, (source, target) in enumerate(((out_hbm, out_w), (up_hbm, up_w), (down_hbm, down_w)))
@@ -235,18 +237,16 @@
     for ref in up_parts:
         ref[:, :width] = normed_low
     copies[1].wait()
-    copies[2].wait()
     step = 768
-    second = jnp.zeros((ROWS, width), F32) + down_offset
     for start in range(0, hidden, step):
         at = slice(start, start + step)
         inner = dot(normed_low, up_w[:, at]) + up_offset[:, at]
         share = 0.5 + 0.5 * lax.erf(inner * 0.7071067811865476)
         density = 0.3989422804014327 * jnp.exp(-0.5 * inner * inner)
         slope[:, at] = share + inner * density
-        active = (inner * share).astype(BF16)
-        active_ref[:, at] = active
-        second = second + dot(active, down_w[at, :])
+        active_ref[:, at] = (inner * share).astype(BF16)
+    copies[2].wait()
+    second = dot(active_ref[...], down_w[...]) + down_offset
     normal_two, scale_two = normalize(normed_low.astype(F32) + second)
     layer_ref[...] = (normal_two * gain_two + shift_two).astype(BF16)
     grad = grad_ref[...].astype(F32)
@@ -270,6 +270,7 @@
     one_grad = normalize_grad(normed_grad * gain_one, normal_one, scale_one)
     one_grad_ref[...] = one_grad
     branch_low = one_grad.astype(BF16)
+    branch_ref[...] = branch_low
     for i, ref in enumerate(context_grads):
         ref[...] = dot(branch_low, out_w[turned(i), :], TURNED).astype(BF16)
     out_bias_grad = column_sum(branch_low.astype(F32))
@@ -285,29 +286,16 @@
             up_parts[i][:, to] = inner_ref[:, at]
             down_parts[i][:ROWS, to] = active_ref[:, at]
         down_parts[i][:ROWS, :width] = second_low
-        down_parts[i][:ROWS, 2 * width : 3 * width] = branch_low
         down_parts[i][ROWS:, :width] = sums_ref[...].astype(BF16)
-    strip = width // 8
-    for i, c in enumerate(contexts):
-        for g in range(GROUPS):
-            @pl.when((group ^ i) == g)
-            def _():
-                for part in range(2):
-                    core, owner = divmod((g * WIDTH + part * strip) // strip, 4)
-                    for turn in range(4):
-                        @pl.when((quarter ^ turn) == owner)
-                        def _():
-                            to = 3 * width + core * strip
-                            down_parts[turn][:ROWS, to : to + strip] = c[:, part * strip : (part + 1) * strip]
 
 
 def dense(spot, contexts, inputs, grad, vectors, up_offset, out_matrix, up_matrix, down_matrix):
     width, hidden = up_matrix.shape
     outs = (
-        (shaped((ROWS, width)), shaped((ROWS, width), F32))
+        (shaped((ROWS, width)), shaped((ROWS, width), F32), shaped((ROWS, width)))
         + (shaped((ROWS, WIDTH)),) * GROUPS
         + (shaped((ROWS, width + hidden // 4)),) * 4
-        + (shaped((ROWS + 16, 3 * width + 256)),) * 4
+        + (shaped((ROWS + 16, width + hidden // 4)),) * 4
     )
     scratch = (
         pltpu.VMEM(out_matrix.shape, BF16),
@@ -323,7 +311,7 @@
     found = kernel_call(
         functools.partial(dense_kernel, width), "dense", outs, args, 22, 10, 1, (9, 10, 11), scratch
     )
-    return found[0], found[1], found[2:6], found[6:10], found[10:14]
+    return found[:3], found[3:7], found[7:11], found[11:15]
 
 
 def halves_of(spot, first, second):
@@ -349,16 +337,14 @@
     return kernel_call(up_grad_kernel, "up_grad", (out, out), (spot, *parts), 16, 4, 1, (), scratch)
 
 
-def down_grad_kernel(spot, p0, p1, p2, p3, other_ref, own_ref, turned, second, branch, sums):
+def down_grad_kernel(spot, p0, p1, p2, p3, other_ref, own_ref, turned, second, sums):
     parts = (p0, p1, p2, p3)
     width = second.shape[1]
-    tall, strip = GROUPS * TALL, GROUPS * SHORT
+    tall = GROUPS * TALL
     for i, part in enumerate(parts):
         rows = slice(i * ROWS, (i + 1) * ROWS)
-        turned[: 2 * tall, rows] = part[:ROWS, width : 2 * width].T
-        turned[2 * tall : 2 * tall + 256, rows] = part[:ROWS, 3 * width :].T
+        turned[:, rows] = part[:ROWS, width:].T
         second[rows, :] = part[:ROWS, :width]
-        branch[rows, :] = part[:ROWS, 2 * width : 3 * width]
     total = sum(part[ROWS:, :width].astype(F32) for part in parts)
     for core in range(2):
         start = core * (width // 2)
@@ -367,19 +353,15 @@
         )
     for ref, core in halves_of(spot, other_ref, own_ref):
         down = dot(turned[pl.ds(pl.multiple_of(core * tall, tall), tall), :], second[...])
-        out = dot(turned[pl.ds(pl.multiple_of(2 * tall + core * strip, 32), strip), :], branch[...])
         for g in range(GROUPS):
-            ref[g] = jnp.concatenate(
-                [down[g * TALL : (g + 1) * TALL], out[g * SHORT : (g + 1) * SHORT], sums[core]], axis=0
-            ).astype(BF16)
+            ref[g] = jnp.concatenate([down[g * TALL : (g + 1) * TALL], sums[core]], axis=0).astype(BF16)
 
 
 def down_grad_parts(spot, parts, width):
     tokens = 4 * ROWS
-    out = shaped((GROUPS, TALL + SHORT + EXTRA, width))
+    out = shaped((GROUPS, TALL + EXTRA, width))
     scratch = (
-        pltpu.VMEM((2 * GROUPS * TALL + 256, tokens), BF16),
-        pltpu.VMEM((tokens, width), BF16),
+        pltpu.VMEM((2 * GROUPS * TALL, tokens), BF16),
         pltpu.VMEM((tokens, width), BF16),
         pltpu.VMEM((2, EXTRA, width), F32),
     )
@@ -427,7 +409,9 @@
 def joined_grad_kernel(pieces, spot, query_grad, *rest):
     keys, values = rest[:pieces], rest[pieces : 2 * pieces]
     inputs = rest[2 * pieces : 2 * pieces + 4]
-    weight, other_ref, own_ref, kept_ref, sent_ref, joined, turned = rest[2 * pieces + 4 :]
+    contexts = rest[2 * pieces + 4 : 2 * pieces + 8]
+    branches = rest[2 * pieces + 8 : 2 * pieces + 12]
+    weight, other_ref, own_ref, kept_ref, sent_ref, joined, turned, context_turned, branch = rest[2 * pieces + 12 :]
 
     def total(parts):
         blocks = [p[0] if len(p.shape) == 3 else p[...] for p in parts]
@@ -439,52 +423,87 @@
     for i, ref in ((1, sent_ref.at[0]), (2, sent_ref.at[1]), (3, kept_ref.at[1]), (0, kept_ref.at[0])):
         ref[...] = dot(joined[i * ROWS : (i + 1) * ROWS, :], weight[...], TURNED).astype(BF16)
     for i, x in enumerate(inputs):
-        turned[:, i * ROWS : (i + 1) * ROWS] = x[...].T
+        at = slice(i * ROWS, (i + 1) * ROWS)
+        turned[:, at] = x[...].T
+        context_turned[:, at] = contexts[i][...].T
+        branch[at, :] = branches[i][...]
     sums = jnp.concatenate(
         [column_sum(joined[...].astype(F32)), jnp.zeros((BIAS_ROWS - 1, 3 * WIDTH), F32)], axis=0
     ).astype(BF16)
     half = turned.shape[0] // 2
     for ref, core in halves_of(spot, other_ref, own_ref):
         value = dot(turned[pl.ds(pl.multiple_of(core * half, half), half), :], joined[...]).astype(BF16)
+        strip = WIDTH // 2
+        out = dot(context_turned[pl.ds(pl.multiple_of(core * strip, 32), strip), :], branch[...])
         for quarter in range(4):
-            ref[quarter, : half // 4, :] = value[quarter * (half // 4) : (quarter + 1) * (half // 4)]
-            ref[quarter, half // 4 :, :] = sums
-
-
-def joined_grads(spot, query_grad, keys, values, inputs, weight):
+            ref[quarter, :TALL, :] = value[quarter * TALL : (quarter + 1) * TALL]
+            block = out[quarter * SHORT : (quarter + 1) * SHORT]
+            last = jnp.concatenate([block[k * 8 : k * 8 + 8, 3 * WIDTH :] for k in range(3)], axis=1)
+            packed = jnp.concatenate([block[:, : 3 * WIDTH], last], axis=0)
+            ref[quarter, TALL : TALL + PACKED, :] = packed.astype(BF16)
+            ref[quarter, TALL + PACKED :, :] = sums
+
+
+def joined_grads(spot, query_grad, keys, values, inputs, contexts, branches, weight):
     width = weight.shape[0]
-    part, pair = shaped((4, width // 8 + BIAS_ROWS, 3 * WIDTH)), shaped((2, ROWS, width))
-    scratch = (pltpu.VMEM((GROUPS * ROWS, 3 * WIDTH), BF16), pltpu.VMEM((width, GROUPS * ROWS), BF16))
-    args = (spot, query_grad, *keys, *values, *inputs, weight)
+    part, pair = shaped((4, TALL + PACKED + BIAS_ROWS, 3 * WIDTH)), shaped((2, ROWS, width))
+    tokens = GROUPS * ROWS
+    scratch = (
+        pltpu.VMEM((tokens, 3 * WIDTH), BF16),
+        pltpu.VMEM((width, tokens), BF16),
+        pltpu.VMEM((WIDTH, tokens), BF16),
+        pltpu.VMEM((tokens, width), BF16),
+    )
+    args = (spot, query_grad, *keys, *values, *inputs, *contexts, *branches, weight)
     kernel = functools.partial(joined_grad_kernel, len(keys))
     return kernel_call(kernel, "joined_grad", (part, part, pair, pair), args, 16, 6, 1, (), scratch)
 
 
 def place_down_kernel(spot, *refs):
-    down_ref, out_ref = refs[-2:]
-    for quarter, g, block in placed(spot, refs[:-2]):
-        block = block.astype(F32)
+    down_ref = refs[-1]
+    for quarter, g, block in placed(spot, refs[:-1]):
         place = quarter * GROUPS + g
-        down_ref[pl.ds(pl.multiple_of(place * TALL, 8), TALL), :] = block[:TALL]
-        out_ref[pl.ds(pl.multiple_of(place * SHORT, 8), SHORT), :] = block[TALL : TALL + SHORT]
+        down_ref[pl.ds(pl.multiple_of(place * TALL, 8), TALL), :] = block.astype(F32)
 
 
 def place_joined_kernel(spot, *refs):
-    weight_ref, bias_ref = refs[-2:]
+    weight_ref, bias_ref, kept_ref, sent_ref = refs[-4:]
     core = spot[2]
     width = weight_ref.shape[1] // 3
-    found = list(placed(spot, refs[:-2]))
+    found = list(placed(spot, refs[:-4]))
+    rows = TALL
     for i in range(4):
         quarter = found[i * GROUPS][0]
         blocks = [block.astype(F32) for _, _, block in found[i * GROUPS : (i + 1) * GROUPS]]
-        rows = blocks[0].shape[0] - BIAS_ROWS
         at = pl.ds(pl.multiple_of(quarter * rows, 16), rows)
         for part in range(3):
             value = jnp.concatenate([b[:, part * WIDTH : (part + 1) * WIDTH] for b in blocks], axis=1)
             weight_ref[at, part * width : (part + 1) * width] = value[:rows]
             if i == 0:
-                line = value[rows : rows + 1]
+                line = value[rows + PACKED : rows + PACKED + 1]
                 bias_ref[part : part + 1, :] = jnp.where(core == 0, line[:, : width // 2], line[:, width // 2 :])
+        for g, block in enumerate(blocks):
+            last = block[rows + SHORT : rows + PACKED]
+            last = jnp.concatenate([last[:, k * WIDTH : (k + 1) * WIDTH] for k in range(3)], axis=0)
+            strip = jnp.concatenate([block[rows : rows + SHORT], last], axis=1).astype(BF16)
+            target = g // 2
+
+            @pl.when(core == target)
+            def _():
+                kept_ref[g % 2, quarter] = strip
+
+            @pl.when(core != target)
+            def _():
+                sent_ref[g % 2, quarter] = strip
+
+
+def place_out_kernel(spot, kept, received, out_ref):
+    core = spot[2]
+    for g in range(2):
+        for ref, side in ((kept, core), (received, 1 - core)):
+            for quarter in range(4):
+                start = g * WIDTH + side * (WIDTH // 2) + quarter * SHORT
+                out_ref[pl.ds(pl.multiple_of(start, 8), SHORT), :] = ref[g, quarter].astype(F32)
 
 
 def body(
@@ -568,7 +587,7 @@
     context, log_total, context_lows = attend(query, key_values, bias, chunks)
     contexts = (context_lows[0], *(places.column_swap(context_lows[i], i) for i in turns))
 
-    layer_out, one_grad, context_grads, up_parts, down_parts = dense(
+    (layer_out, one_grad, branch_low), context_grads, up_parts, down_parts = dense(
         spot, contexts, inputs, cotangent[0], whole, up_offset, out_matrix, up_matrix, down_matrix
     )
     def after(value, *others):
@@ -597,59 +616,70 @@
         pair = jnp.stack([part, places.column_swap(part, 3)])
         return jnp.concatenate([pair, places.column_swap(pair, 1)])
 
-    def plane_gather(column):
+    def plane_gather(column, *others):
         first, second = places.four_swap(column, 1), places.four_swap(column, 2)
-        return column, first, second, places.four_swap(first[:2], 2), places.four_swap(second[2:], 1)
+        halves = (first[:2], second[2:])
+        if others:
+            halves = after(halves, *others)
+        return column, first, second, places.four_swap(halves[0], 2), places.four_swap(halves[1], 1)
 
     context_grads = (context_grads[0], *(places.column_swap(context_grads[i], i) for i in turns))
     down_parts = (down_parts[0], *(places.four_swap(down_parts[i], i) for i in turns))
+    branch_low = after(branch_low, context_grads)
+    far = places.column_swap(branch_low, 3)
+    branches = (branch_low, places.column_swap(branch_low, 1), places.column_swap(far, 1), far)
     query_grad, parts = attend_grad(query, context, context_grads, log_total, key_values, bias, chunks)
     if plane_size == 4:
         own_key, own_value, turned_key, turned_value, key_x, value_y = parts
-        key_x, value_y = places.swap(key_x, 1), places.swap(value_y, 2)
+        key_x, value_y = first_step = places.swap(key_x, 1), places.swap(value_y, 2)
         keys = (own_key, key_x, places.swap(add(turned_key, key_x[1]), 2))
         values = (own_value, value_y, places.swap(add(turned_value, value_y[1]), 1))
     else:
         blocks = jnp.stack(parts).reshape(2 * WIDTH, plane_size, column_rows)
         blocks = places.exchange(jnp.transpose(blocks, (1, 0, 2)), places.planes)
         blocks = jnp.sum(blocks.astype(F32), axis=0)
-        keys, values = (blocks[:WIDTH],), (blocks[WIDTH:],)
-    down_parts = after(down_parts, query_grad)
+        keys, values = first_step = (blocks[:WIDTH],), (blocks[WIDTH:],)
+    down_parts = after(down_parts, query_grad, branches)
     other, own = down_grad_parts(spot, down_parts, model_width)
-    down_part = rest_sum(column_total(*pair_sums(spot, own, to_other(other), "down_sum")))
-    keys, values = after((keys, values), down_part)
-    down_column = column_gather(down_part[: TALL + SHORT].astype(BF16))
-    other, own, kept, sent = joined_grads(spot, query_grad, keys, values, column_inputs, group_weight)
+    down_pieces = pair_sums(spot, own, to_other(other), "down_sum")
+    down_part = rest_sum(column_total(*down_pieces))
+    up_parts = after(up_parts, first_step)
+    up_parts = (up_parts[0], *(places.four_swap(up_parts[i], i) for i in turns))
+    keys, values = after((keys, values), down_part, up_parts)
+    down_column = column_gather(down_part[:TALL].astype(BF16))
+    other, own, kept, sent = joined_grads(
+        spot, query_grad, keys, values, column_inputs, context_lows, branches, group_weight
+    )
     input_grad = one_grad + column_total(kept, sent)
     joined_pieces = pair_sums(spot, own, to_other(other), "joined_sum", 1, (1, 3, 2, 0))
     joined_part = rest_sum(four_total(*joined_pieces)).astype(BF16)
-    up_parts = after(up_parts, down_parts)
-    up_parts = (up_parts[0], *(places.four_swap(up_parts[i], i) for i in turns))
-    up_parts = after(up_parts, kept, down_column)
+    up_parts = after(up_parts, kept)
     other, own = up_grad_parts(spot, up_parts, model_width)
     up_part = rest_sum(column_total(*pair_sums(spot, own, to_other(other), "up_sum"))).astype(BF16)
     down_all = plane_gather(down_column)
-    up_all = plane_gather(after(column_gather(up_part), down_all))
-    joined_all = plane_gather(after(column_gather(joined_part), down_all))
-    extra = down_part[TALL + SHORT :]
-    up_bias_grad = jnp.concatenate([extra[6, :half], extra[7, :half], extra[0, half:], extra[1, half:]])
-    down_grad, out_grad = kernel_call(
+    down_grad = kernel_call(
         place_down_kernel,
         "place_down",
-        (shaped((hidden_width // 2, model_width), F32), shaped((half, model_width), F32)),
+        shaped((hidden_width // 2, model_width), F32),
         (spot, *down_all),
         16,
         5,
         1,
     )
-    qkv_grad, bias_grad = kernel_call(
+    up_all = plane_gather(after(column_gather(up_part), down_all), down_grad)
+    joined_all = plane_gather(after(column_gather(joined_part), down_all), down_grad)
+    strips = shaped((2, 4, SHORT, model_width))
+    qkv_grad, bias_grad, out_kept, out_sent = kernel_call(
         place_joined_kernel,
         "place_joined",
-        (shaped((half, 3 * model_width), F32), shaped((8, half), F32)),
+        (shaped((half, 3 * model_width), F32), shaped((8, half), F32), strips, strips),
         (spot, *joined_all),
         16,
         5,
         1,
+    )
+    out_grad = kernel_call(
+        place_out_kernel, "place_out", shaped((half, model_width), F32), (spot, out_kept, to_other(out_sent)), 8, 2, 1
     )
     up_grad = kernel_call(
         place_up_kernel,
@@ -661,6 +691,8 @@
         1,
     )
 
+    extra = down_part[TALL:]
+    up_bias_grad = jnp.concatenate([extra[6, :half], extra[7, :half], extra[0, half:], extra[1, half:]])
     shape = (1, row_count, model_width)
     return (
         layer_out.reshape(shape),

time: 262 us -> 252 us (0.962)
  waiting for transfers between devices: 115 us -> 102 us
    ppermute x48 -> x51, waiting for transfers between devices: 109 us -> 100 us  [swap(): return lax.ppermute(block, 'seq', [(i, i ^ bits) for i in range(self.size)])]
    ppermute x3 -> x4, waiting for transfers between devices: 3.77 us -> 0.46 us  [to_other(): return lax.ppermute(block, 'shard', [(0, 1), (1, 0)])]
    pallas_call x13 -> x14, Pallas kernels: 48.3 us -> 50.4 us  [kernel_call(): pl.pallas_call(run if after else kernel, out_shape=outs, in_specs=spaces...]
    ppermute x48 -> x51, starting transfers between devices: 68.9 us -> 69.6 us  [swap(): return lax.ppermute(block, 'seq', [(i, i ^ bits) for i in range(self.size)])]
  transfers between devices with their start and end apart: 54 -> 58, of which waited for: 27 -> 27; matrix products, arithmetic and copies ran while one was open for 3% -> 3% of each run, Pallas kernels for 11% -> 13%
where the time goes in v7:
time: 252 us
  waiting for transfers between devices  102 us (40%)
  starting transfers between devices  70.2 us (28%)
  Pallas kernels  50.4 us (20%)
  between operations  14.4 us (6%)
  local copies, waits for them, and re-layouts  6.53 us (3%)
  blocking collectives  4.62 us (2%)
  other arithmetic  3.26 us (1%)
    ppermute x51, waiting for transfers between devices, swap(): return lax.ppermute(block, 'seq', [(i, i ^ bits) for i in range(self.size)])  100 us
    ppermute x51, starting transfers between devices, swap(): return lax.ppermute(block, 'seq', [(i, i ^ bits) for i in range(self.size)])  69.6 us
    pallas_call x14, Pallas kernels, kernel_call(): pl.pallas_call(run if after else kernel, out_shape=outs, in_specs=spaces...  50.4 us
  transfers between devices with their start and end apart: 58, of which 27 were waited for; matrix products, arithmetic and copies ran while one was open for 3% of the time, Pallas kernels for 13%

profile of v7, /device:TPU:0, one launch (start us, length us, event | category | flops | bytes accessed | tf_op | source)
XLA Modules:
  0.0 251.8 jit_solution(1236711425254878420)
XLA Ops:
  9.5 5.1 %collective-permute-start.2 = (bf16[128,768]{1,0:T(8,128)(2,1)S(1)}, bf16[128,768]{1,0:T(8,128)(2,1)S(1)}, u32[]{:S(2)}, u32[]{:S(2)}) collective-permute-start(bf16[128,768]{1,0:T(8,128)(2,1)S(1)} %bitcast.60), channel_id=1, source_target_pairs={{0,24},{2,26},{4,28},{6,30},{8,16},{10,18},{12,20},{14,22},{16,8},... | collective-permute-start | bytes 589832 | tf_op jit(solution)/shard_map/ppermute | solution.py:72
  15.5 1.8 all-gather.1
  17.6 1.5 constant_dynamic-slice_fusion.2
  19.3 2.8 %all_gather.18.weight.rest_18_ = bf16[768,576]{1,0:T(8,128)(2,1)S(1)} all-gather(bf16[384,576]{1,0:T(8,128)(2,1)S(1)} %pad_maximum_fusion.3), channel_id=1, replica_groups=mesh['seq'=16,'shard'=2] {'shard'}, dimensions={0}, use_global_device_ids=true | all-gather | bytes 1327104 | tf_op jit(solution)/shard_map/all_gather | solution.py:545
  22.1 9.2 %collective-permute-done.1.x2.rest_8_ = bf16[128,768]{1,0:T(8,128)(2,1)S(1)} collective-permute-done((bf16[128,768]{1,0:T(8,128)(2,1)S(1)}, bf16[128,768]{1,0:T(8,128)(2,1)S(1)}, u32[]{:S(2)}, u32[]{:S(2)}) %collective-permute-start.1) | collective-permute-done | bytes 196640 | tf_op jit(solution)/shard_map/ppermute | solution.py:72
  32.2 2.5 collective-permute-start.5
  37.3 8.0 %collective-permute-done.5.refs_4_.refs_10_ = bf16[512,384]{1,0:T(8,128)(2,1)S(1)} collective-permute-done((bf16[512,384]{1,0:T(8,128)(2,1)S(1)}, bf16[512,384]{1,0:T(8,128)(2,1)S(1)}, u32[]{:S(2)}, u32[]{:S(2)}) %collective-permute-start.5) | collective-permute-done | bytes 393248 | tf_op jit(solution)/shard_map/ppermute | solution.py:72
  45.3 6.5 %collective-permute-done.4.refs_3_.refs_9_ = bf16[512,384]{1,0:T(8,128)(2,1)S(1)} collective-permute-done((bf16[512,384]{1,0:T(8,128)(2,1)S(1)}, bf16[512,384]{1,0:T(8,128)(2,1)S(1)}, u32[]{:S(2)}, u32[]{:S(2)}) %collective-permute-start.4) | collective-permute-done | bytes 393248 | tf_op jit(solution)/shard_map/ppermute | solution.py:72
  51.9 9.1 %attend.1 = (f32[512,192]{1,0:T(8,128)S(1)}, f32[512,128]{1,0:T(8,128)S(1)}, bf16[128,192]{1,0:T(8,128)(2,1)S(1)}, bf16[128,192]{1,0:T(8,128)(2,1)}, bf16[128,192]{1,0:T(8,128)(2,1)}, /*index=5*/bf16[128,192]{1,0:T(8,128)(2,1)}) custom-call(bf16[512,192]{1,0:T(8,128)(2,1)S(1)} %get-tuple-element.88.refs_0_, ...), custom_call_target="tpu_custom_call" | custom-call | bytes 31500000 | tf_op jit(solution)/shard_map/attend/pallas_call | solution.py:39
  62.5 2.8 %collective-permute-start.7 = (bf16[128,192]{1,0:T(8,128)(2,1)}, bf16[128,192]{1,0:T(8,128)(2,1)}, u32[]{:S(2)}, u32[]{:S(2)}) collective-permute-start(bf16[128,192]{1,0:T(8,128)(2,1)} %get-tuple-element.92.rest_12_), channel_id=1, source_target_pairs={{0,16},{2,18},{4,20},{6,22},{8,24},{10,26},{12,28},{14,30},{16,0},... | collective-permute-start | bytes 147464 | tf_op jit(solution)/shard_map/ppermute | solution.py:72
  65.4 1.5 collective-permute-start.8
  67.8 3.0 %collective-permute-done.7.c2 = bf16[128,192]{1,0:T(8,128)(2,1)} collective-permute-done((bf16[128,192]{1,0:T(8,128)(2,1)}, bf16[128,192]{1,0:T(8,128)(2,1)}, u32[]{:S(2)}, u32[]{:S(2)}) %collective-permute-start.7) | collective-permute-done | bytes 49184 | tf_op jit(solution)/shard_map/ppermute | solution.py:72
  70.8 1.1 collective-permute-done.8.c3
  72.8 10.7 %dense.1 = (bf16[128,768]{1,0:T(8,128)(2,1)}, f32[128,768]{1,0:T(8,128)S(1)}, bf16[128,768]{1,0:T(8,128)(2,1)S(1)}, bf16[128,192]{1,0:T(8,128)(2,1)S(1)}, bf16[1...) custom-call(s32[3]{0:T(128)S(1)} %pad_add_fusion.spot, ...), custom_call_target="tpu_custom_call" | custom-call | bytes 35000000 | tf_op jit(solution)/shard_map/dense/pallas_call | solution.py:39
  83.5 1.0 collective-permute-start.9
  84.5 1.2 collective-permute-start.10
  85.8 2.2 collective-permute-start.11
  88.0 1.5 collective-permute-start.16
  90.1 1.4 collective-permute-start.18
  91.9 2.2 collective-permute-start.20
  94.1 6.3 %collective-permute-done.20.rest_17_ = bf16[128,768]{1,0:T(8,128)(2,1)S(1)} collective-permute-done((bf16[128,768]{1,0:T(8,128)(2,1)S(1)}, bf16[128,768]{1,0:T(8,128)(2,1)S(1)}, u32[]{:S(2)}, u32[]{:S(2)}) %collective-permute-start.20) | collective-permute-done | bytes 196640 | tf_op jit(solution)/shard_map/ppermute | solution.py:72
  101.1 8.0 %attend_grad.1 = (bf16[512,192]{1,0:T(8,128)(2,1)S(1)}, bf16[192,512]{1,0:T(8,128)(2,1)S(1)}, bf16[192,512]{1,0:T(8,128)(2,1)S(1)}, bf16[192,512]{1,0:T(8,128)(2...) custom-call(bf16[512,192]{1,0:T(8,128)(2,1)S(1)} %get-tuple-element.88.ref, ...), custom_call_target="tpu_custom_call" | custom-call | bytes 38500000 | tf_op jit(solution)/shard_map/attend_grad/pallas_call | solution.py:39
  109.2 1.5 down_grad.1
  110.8 1.5 collective-permute-start.12
  113.6 1.4 collective-permute-start.23
  115.0 7.4 %collective-permute-done.12.rest_1_ = bf16[2,192,512]{2,1,0:T(8,128)(2,1)S(1)} collective-permute-done((bf16[2,192,512]{2,1,0:T(8,128)(2,1)S(1)}, bf16[2,192,512]{2,1,0:T(8,128)(2,1)S(1)}, u32[]{:S(2)}, u32[]{:S(2)}) %collective-permute-start.12) | collective-permute-done | bytes 393248 | tf_op jit(solution)/shard_map/ppermute | solution.py:72
  122.4 1.5 collective-permute-start.13
  124.2 1.7 collective-permute-start.26
  125.9 1.5 collective-permute-start.27
  127.5 1.9 collective-permute-start.24
  129.4 5.3 %collective-permute-done.24 = bf16[104,768]{1,0:T(8,128)(2,1)S(1)} collective-permute-done((bf16[104,768]{1,0:T(8,128)(2,1)S(1)}, bf16[104,768]{1,0:T(8,128)(2,1)S(1)}, u32[]{:S(2)}, u32[]{:S(2)}) %collective-permute-start.24) | collective-permute-done | bytes 159776 | tf_op jit(solution)/shard_map/ppermute | solution.py:72
  135.0 12.0 %collective-permute-done.15.rest_5_ = bf16[192,512]{1,0:T(8,128)(2,1)S(1)} collective-permute-done((bf16[192,512]{1,0:T(8,128)(2,1)S(1)}, bf16[192,512]{1,0:T(8,128)(2,1)S(1)}, u32[]{:S(2)}, u32[]{:S(2)}) %collective-permute-start.15) | collective-permute-done | bytes 196640 | tf_op jit(solution)/shard_map/ppermute | solution.py:72
  147.1 3.7 %joined_grad.1 = (bf16[4,144,576]{2,1,0:T(8,128)(2,1)S(1)}, bf16[4,144,576]{2,1,0:T(8,128)(2,1)S(1)}, bf16[2,128,768]{2,1,0:T(8,128)(2,1)S(1)}, bf16[2,128,768]{2,1,0:T(8,128)(2,1)S(1)}) custom-call(s32[3]{0:T(128)S(1)} %pad_add_fusion.spot, bf16[512,192]{1,0:T(8,128)(2,1)S(1)} %get-tuple-element.102.query_grad, ...), custom_call_target="tpu_custom_call" | custom-call | bytes 21000000 | tf_op jit(solution)/shard_map/joined_grad/pallas_call | solution.py:39
  150.8 1.9 collective-permute-start.35
  152.7 1.5 up_grad.1
  155.9 3.1 %collective-permute-done.35 = bf16[96,768]{1,0:T(8,128)(2,1)S(1)} collective-permute-done((bf16[96,768]{1,0:T(8,128)(2,1)S(1)}, bf16[96,768]{1,0:T(8,128)(2,1)S(1)}, u32[]{:S(2)}, u32[]{:S(2)}) %collective-permute-start.35) | collective-permute-done | bytes 147488 | tf_op jit(solution)/shard_map/ppermute | solution.py:72
  159.1 2.7 %collective-permute-start.36 = (bf16[2,96,768]{2,1,0:T(8,128)(2,1)S(1)}, bf16[2,96,768]{2,1,0:T(8,128)(2,1)S(1)}, u32[]{:S(2)}, u32[]{:S(2)}) collective-permute-start(bf16[2,96,768]{2,1,0:T(8,128)(2,1)S(1)} %pad_maximum_fusion.5), channel_id=1, source_target_pairs={{0,8},{2,10},{4,12},{6,14},{8,0},{10,2},{12,4},{14,6},{16,24},{18,... | collective-permute-start | bytes 884744 | tf_op jit(solution)/shard_map/ppermute | solution.py:72
  161.8 4.4 %collective-permute-done.31 = bf16[2,144,576]{2,1,0:T(8,128)(2,1)S(1)} collective-permute-done((bf16[2,144,576]{2,1,0:T(8,128)(2,1)S(1)}, bf16[2,144,576]{2,1,0:T(8,128)(2,1)S(1)}, u32[]{:S(2)}, u32[]{:S(2)}) %collective-permute-start.31) | collective-permute-done | bytes 331808 | tf_op jit(solution)/shard_map/ppermute | solution.py:72
  169.4 1.4 collective-permute-start.37
  170.8 3.0 %collective-permute-done.32 = bf16[144,576]{1,0:T(8,128)(2,1)S(1)} collective-permute-done((bf16[144,576]{1,0:T(8,128)(2,1)S(1)}, bf16[144,576]{1,0:T(8,128)(2,1)S(1)}, u32[]{:S(2)}, u32[]{:S(2)}) %collective-permute-start.32) | collective-permute-done | bytes 165920 | tf_op jit(solution)/shard_map/ppermute | solution.py:72
  173.9 2.1 collective-permute-start.33
  176.0 2.0 collective-permute-start.48
  178.1 4.7 %collective-permute-done.33 = bf16[144,576]{1,0:T(8,128)(2,1)S(1)} collective-permute-done((bf16[144,576]{1,0:T(8,128)(2,1)S(1)}, bf16[144,576]{1,0:T(8,128)(2,1)S(1)}, u32[]{:S(2)}, u32[]{:S(2)}) %collective-permute-start.33) | collective-permute-done | bytes 165920 | tf_op jit(solution)/shard_map/ppermute | solution.py:72
  182.8 4.3 %collective-permute-start.34 = (bf16[2,144,576]{2,1,0:T(8,128)(2,1)S(1)}, bf16[2,144,576]{2,1,0:T(8,128)(2,1)S(1)}, u32[]{:S(2)}, u32[]{:S(2)}) collective-permute-start(bf16[2,144,576]{2,1,0:T(8,128)(2,1)S(1)} %pad_maximum_fusion.4), channel_id=1, source_target_pairs={{0,8},{2,10},{4,12},{6,14},{8,0},{10,2},{12,4},{14,6},{16,24},{18,... | collective-permute-start | bytes 995336 | tf_op jit(solution)/shard_map/ppermute | solution.py:72
  187.3 2.5 collective-permute-start.39
  189.8 1.9 collective-permute-start.49
  191.7 2.4 collective-permute-done.34
  194.3 2.4 collective-permute-done.39.refs_3_
  196.6 2.5 collective-permute-start.42
  199.5 2.0 collective-permute-start.28
  201.5 4.9 %collective-permute-done.50 = bf16[2,96,768]{2,1,0:T(8,128)(2,1)S(1)} collective-permute-done((bf16[2,96,768]{2,1,0:T(8,128)(2,1)S(1)}, bf16[2,96,768]{2,1,0:T(8,128)(2,1)S(1)}, u32[]{:S(2)}, u32[]{:S(2)}) %collective-permute-start.50) | collective-permute-done | bytes 294944 | tf_op jit(solution)/shard_map/ppermute | solution.py:72
  206.5 1.2 collective-permute-start.52
  207.7 1.4 collective-permute-start.51
  209.1 3.1 %place_down.1 = f32[1536,768]{1,0:T(8,128)} custom-call(s32[3]{0:T(128)S(1)} %pad_add_fusion.spot, bf16[4,96,768]{2,1,0:T(8,128)(2,1)S(1)} %pad_maximum_fusion.1.refs_0_, bf16[4,96,768]{2,1,0:T(8,128)(2,1)S(1)} %collective-permute-done.37.refs_1_, bf16[4,96,768]{2,1,0:T(8,128)(2,1)S(1)} %collective-permute-done.38.refs_2_, ...), custom_call_target="tpu_custom_call" | custom-call | bytes 17500000 | tf_op jit(solution)/shard_map/place_down/pallas_call | solution.py:39
  212.1 4.4 %collective-permute-done.42.refs_2_ = bf16[4,144,576]{2,1,0:T(8,128)(2,1)S(1)} collective-permute-done((bf16[4,144,576]{2,1,0:T(8,128)(2,1)S(1)}, bf16[4,144,576]{2,1,0:T(8,128)(2,1)S(1)}, u32[]{:S(2)}, u32[]{:S(2)}) %collective-permute-start.42) | collective-permute-done | bytes 663584 | tf_op jit(solution)/shard_map/ppermute | solution.py:72
  216.5 1.9 collective-permute-done.41.refs_1_
  219.7 3.1 %collective-permute-start.29 = (bf16[128,768]{1,0:T(8,128)(2,1)S(1)}, bf16[128,768]{1,0:T(8,128)(2,1)S(1)}, u32[]{:S(2)}, u32[]{:S(2)}) collective-permute-start(bf16[128,768]{1,0:T(8,128)(2,1)S(1)} %fusion.6), channel_id=1, source_target_pairs={{0,24},{2,26},{4,28},{6,30},{8,16},{10,18},{12,20},{14,22},{16,8},... | collective-permute-start | bytes 589832 | tf_op jit(solution)/shard_map/ppermute | solution.py:72
  223.4 5.8 %collective-permute-done.52.refs_2_ = bf16[4,96,768]{2,1,0:T(8,128)(2,1)S(1)} collective-permute-done((bf16[4,96,768]{2,1,0:T(8,128)(2,1)S(1)}, bf16[4,96,768]{2,1,0:T(8,128)(2,1)S(1)}, u32[]{:S(2)}, u32[]{:S(2)}) %collective-permute-start.52) | collective-permute-done | bytes 589856 | tf_op jit(solution)/shard_map/ppermute | solution.py:72
  229.2 1.0 collective-permute-done.51.refs_1_
  230.1 1.1 collective-permute-start.53
  232.6 1.3 collective-permute-done.43.refs_3_
  234.1 5.0 %place_joined.1 = (f32[384,2304]{1,0:T(8,128)}, f32[8,384]{1,0:T(8,128)S(1)}, bf16[2,4,24,768]{3,2,1,0:T(8,128)(2,1)S(1)}, bf16[2,4,24,768]{3,2,1,0:T(8,128)(2,1)S(1)}) custom-call(s32[3]{0:T(128)S(1)} %pad_add_fusion.spot, bf16[4,144,576]{2,1,0:T(8,128)(2,1)S(1)} %pad_maximum_fusion.refs_0_, bf16[4,144,576]{2,1,0:T(8,128)(2,1)S(1)} %collective-permute-done.41.refs_1_, ...), custom_call_target="tpu_custom_call" | custom-call | bytes 17500000 | tf_op jit(solution)/shard_map/place_joined/pallas_call | solution.py:39
  239.9 3.1 %place_up.1 = f32[384,3072]{1,0:T(8,128)} custom-call(s32[3]{0:T(128)S(1)} %pad_add_fusion.spot, bf16[4,96,768]{2,1,0:T(8,128)(2,1)S(1)} %pad_maximum_fusion.2.refs_0_, bf16[4,96,768]{2,1,0:T(8,128)(2,1)S(1)} %collective-permute-done.51.refs_1_, bf16[4,96,768]{2,1,0:T(8,128)(2,1)S(1)} %collective-permute-done.52.refs_2_, ...), custom_call_target="tpu_custom_call" | custom-call | bytes 14000000 | tf_op jit(solution)/shard_map/place_up/pallas_call | solution.py:39
  243.6 1.6 place_out.1
  (169 shorter events, 25.0 us)
Async XLA Ops:
  7.2 64.7 %all-gather.6.cloned.1.call-start = ((), (), s32[]{:S(2)}) async-start(), calls=%async_computation | async-start | bytes 1769472 | tf_op jit(solution)/shard_map/all_gather | solution.py:545
  8.0 7.4 %copy-start.16 = (bf16[384]{0:T(512)(128)(2,1)S(1)}, bf16[384]{0:T(512)(128)(2,1)}, u32[]{:S(2)}) copy-start(bf16[384]{0:T(512)(128)(2,1)} %param.31) | copy-start | bytes 2308
  8.0 7.4 %copy-start.8 = (bf16[1536]{0:T(1024)(128)(2,1)S(1)}, bf16[1536]{0:T(1024)(128)(2,1)}, u32[]{:S(2)}) copy-start(bf16[1536]{0:T(1024)(128)(2,1)} %param.27) | copy-start | bytes 9220
  8.0 63.8 %all-gather.8.cloned.1.call-start = ((), (), s32[]{:S(2)}) async-start(), calls=%async_computation.1 | async-start | bytes 7077888 | tf_op jit(solution)/shard_map/all_gather | solution.py:545
  8.8 63.1 %all-gather.10.cloned.1.call-start = ((), (), s32[]{:S(2)}) async-start(), calls=%async_computation.2 | async-start | bytes 7077888 | tf_op jit(solution)/shard_map/all_gather | solution.py:545
  9.5 12.6 %collective-permute-start.2 = (bf16[128,768]{1,0:T(8,128)(2,1)S(1)}, bf16[128,768]{1,0:T(8,128)(2,1)S(1)}, u32[]{:S(2)}, u32[]{:S(2)}) collective-permute-start(bf16[128,768]{1,0:T(8,128)(2,1)S(1)} %bitcast.60), channel_id=1, source_target_pairs={{0,24},{2,26},{4,28},{6,30},{8,16},{10,18},{12,20},{14,22},{16,8},... | collective-permute-start | bytes 589832 | tf_op jit(solution)/shard_map/ppermute | solution.py:72
  14.6 16.7 %collective-permute-start.1 = (bf16[128,768]{1,0:T(8,128)(2,1)S(1)}, bf16[128,768]{1,0:T(8,128)(2,1)S(1)}, u32[]{:S(2)}, u32[]{:S(2)}) collective-permute-start(bf16[128,768]{1,0:T(8,128)(2,1)S(1)} %bitcast.61), channel_id=1, source_target_pairs={{0,16},{2,18},{4,20},{6,22},{8,24},{10,26},{12,28},{14,30},{16,0},... | collective-permute-start | bytes 589832 | tf_op jit(solution)/shard_map/ppermute | solution.py:72
  14.6 16.7 %collective-permute-start = (bf16[128,768]{1,0:T(8,128)(2,1)S(1)}, bf16[128,768]{1,0:T(8,128)(2,1)S(1)}, u32[]{:S(2)}, u32[]{:S(2)}) collective-permute-start(bf16[128,768]{1,0:T(8,128)(2,1)S(1)} %bitcast.62), channel_id=1, source_target_pairs={{0,8},{2,10},{4,12},{6,14},{8,0},{10,2},{12,4},{14,6},{16,24},{18,... | collective-permute-start | bytes 589832 | tf_op jit(solution)/shard_map/ppermute | solution.py:72
  19.1 16.7 %copy-start.17 = (s32[2]{0:T(128)S(1)}, s32[2]{0:T(128)}, u32[]{:S(2)}) copy-start(s32[2]{0:T(128)} %param.18) | copy-start | bytes 28
  32.2 13.1 %collective-permute-start.5 = (bf16[512,384]{1,0:T(8,128)(2,1)S(1)}, bf16[512,384]{1,0:T(8,128)(2,1)S(1)}, u32[]{:S(2)}, u32[]{:S(2)}) collective-permute-start(bf16[512,384]{1,0:T(8,128)(2,1)S(1)} %get-tuple-element.89.refs_1_.refs_7_), channel_id=1, source_target_pairs={{0,6},{2,4},{4,2},{6,0},{8,14},{10,12},{12,10},{14,8},{16,22},{18,... | collective-permute-start | bytes 1179656 | tf_op jit(solution)/shard_map/ppermute | solution.py:72
  34.7 17.1 %collective-permute-start.4 = (bf16[512,384]{1,0:T(8,128)(2,1)S(1)}, bf16[512,384]{1,0:T(8,128)(2,1)S(1)}, u32[]{:S(2)}, u32[]{:S(2)}) collective-permute-start(bf16[512,384]{1,0:T(8,128)(2,1)S(1)} %get-tuple-element.89.refs_1_.refs_7_), channel_id=1, source_target_pairs={{0,4},{2,6},{4,0},{6,2},{8,12},{10,14},{12,8},{14,10},{16,20},{18,... | collective-permute-start | bytes 1179656 | tf_op jit(solution)/shard_map/ppermute | solution.py:72
  35.2 16.6 %collective-permute-start.3 = (bf16[512,384]{1,0:T(8,128)(2,1)S(1)}, bf16[512,384]{1,0:T(8,128)(2,1)S(1)}, u32[]{:S(2)}, u32[]{:S(2)}) collective-permute-start(bf16[512,384]{1,0:T(8,128)(2,1)S(1)} %get-tuple-element.89.refs_1_.refs_7_), channel_id=1, source_target_pairs={{0,2},{2,0},{4,6},{6,4},{8,10},{10,8},{12,14},{14,12},{16,18},{18,... | collective-permute-start | bytes 1179656 | tf_op jit(solution)/shard_map/ppermute | solution.py:72
  62.5 5.3 %collective-permute-start.6 = (bf16[128,192]{1,0:T(8,128)(2,1)}, bf16[128,192]{1,0:T(8,128)(2,1)}, u32[]{:S(2)}, u32[]{:S(2)}) collective-permute-start(bf16[128,192]{1,0:T(8,128)(2,1)} %get-tuple-element.91.rest_11_), channel_id=1, source_target_pairs={{0,8},{2,10},{4,12},{6,14},{8,0},{10,2},{12,4},{14,6},{16,24},{18,... | collective-permute-start | bytes 147464 | tf_op jit(solution)/shard_map/ppermute | solution.py:72
  62.5 8.2 %collective-permute-start.7 = (bf16[128,192]{1,0:T(8,128)(2,1)}, bf16[128,192]{1,0:T(8,128)(2,1)}, u32[]{:S(2)}, u32[]{:S(2)}) collective-permute-start(bf16[128,192]{1,0:T(8,128)(2,1)} %get-tuple-element.92.rest_12_), channel_id=1, source_target_pairs={{0,16},{2,18},{4,20},{6,22},{8,24},{10,26},{12,28},{14,30},{16,0},... | collective-permute-start | bytes 147464 | tf_op jit(solution)/shard_map/ppermute | solution.py:72
  65.4 6.5 %collective-permute-start.8 = (bf16[128,192]{1,0:T(8,128)(2,1)}, bf16[128,192]{1,0:T(8,128)(2,1)}, u32[]{:S(2)}, u32[]{:S(2)}) collective-permute-start(bf16[128,192]{1,0:T(8,128)(2,1)} %get-tuple-element.93.rest_13_), channel_id=1, source_target_pairs={{0,24},{2,26},{4,28},{6,30},{8,16},{10,18},{12,20},{14,22},{16,8},... | collective-permute-start | bytes 147464 | tf_op jit(solution)/shard_map/ppermute | solution.py:72
  72.8 28.3 %copy-start.4 = (f32[512,192]{1,0:T(8,128)S(1)}, f32[512,192]{1,0:T(8,128)}, u32[]{:S(2)}) copy-start(f32[512,192]{1,0:T(8,128)} %copy-done.3) | copy-start | bytes 1179652
  72.8 28.3 %copy-start.6 = (f32[512,128]{1,0:T(8,128)S(1)}, f32[512,128]{1,0:T(8,128)}, u32[]{:S(2)}) copy-start(f32[512,128]{1,0:T(8,128)} %copy-done.5) | copy-start | bytes 786436
  83.5 6.6 %collective-permute-start.9 = (bf16[128,192]{1,0:T(8,128)(2,1)S(1)}, bf16[128,192]{1,0:T(8,128)(2,1)S(1)}, u32[]{:S(2)}, u32[]{:S(2)}) collective-permute-start(bf16[128,192]{1,0:T(8,128)(2,1)S(1)} %get-tuple-element.99), channel_id=1, source_target_pairs={{0,8},{2,10},{4,12},{6,14},{8,0},{10,2},{12,4},{14,6},{16,24},{18,... | collective-permute-start | bytes 147464 | tf_op jit(solution)/shard_map/ppermute | solution.py:72
  84.5 6.9 %collective-permute-start.10 = (bf16[128,192]{1,0:T(8,128)(2,1)S(1)}, bf16[128,192]{1,0:T(8,128)(2,1)S(1)}, u32[]{:S(2)}, u32[]{:S(2)}) collective-permute-start(bf16[128,192]{1,0:T(8,128)(2,1)S(1)} %get-tuple-element.100), channel_id=1, source_target_pairs={{0,16},{2,18},{4,20},{6,22},{8,24},{10,26},{12,28},{14,30},{16,0},... | collective-permute-start | bytes 147464 | tf_op jit(solution)/shard_map/ppermute | solution.py:72
  85.8 6.2 %collective-permute-start.11 = (bf16[128,192]{1,0:T(8,128)(2,1)S(1)}, bf16[128,192]{1,0:T(8,128)(2,1)S(1)}, u32[]{:S(2)}, u32[]{:S(2)}) collective-permute-start(bf16[128,192]{1,0:T(8,128)(2,1)S(1)} %get-tuple-element.101), channel_id=1, source_target_pairs={{0,24},{2,26},{4,28},{6,30},{8,16},{10,18},{12,20},{14,22},{16,8},... | collective-permute-start | bytes 147464 | tf_op jit(solution)/shard_map/ppermute | solution.py:72
  88.0 21.2 %collective-permute-start.16 = (bf16[144,1536]{1,0:T(8,128)(2,1)S(1)}, bf16[144,1536]{1,0:T(8,128)(2,1)S(1)}, u32[]{:S(2)}, u32[]{:S(2)}) collective-permute-start(bf16[144,1536]{1,0:T(8,128)(2,1)S(1)} %get-tuple-element.110), channel_id=1, source_target_pairs={{0,2},{2,0},{4,6},{6,4},{8,10},{10,8},{12,14},{14,12},{16,18},{18,... | collective-permute-start | bytes 1327112 | tf_op jit(solution)/shard_map/ppermute | solution.py:72
  89.5 19.7 %collective-permute-start.17 = (bf16[144,1536]{1,0:T(8,128)(2,1)S(1)}, bf16[144,1536]{1,0:T(8,128)(2,1)S(1)}, u32[]{:S(2)}, u32[]{:S(2)}) collective-permute-start(bf16[144,1536]{1,0:T(8,128)(2,1)S(1)} %get-tuple-element.111), channel_id=1, source_target_pairs={{0,4},{2,6},{4,0},{6,2},{8,12},{10,14},{12,8},{14,10},{16,20},{18,... | collective-permute-start | bytes 1327112 | tf_op jit(solution)/shard_map/ppermute | solution.py:72
  90.1 19.1 %collective-permute-start.18 = (bf16[144,1536]{1,0:T(8,128)(2,1)S(1)}, bf16[144,1536]{1,0:T(8,128)(2,1)S(1)}, u32[]{:S(2)}, u32[]{:S(2)}) collective-permute-start(bf16[144,1536]{1,0:T(8,128)(2,1)S(1)} %get-tuple-element.112), channel_id=1, source_target_pairs={{0,6},{2,4},{4,2},{6,0},{8,14},{10,12},{12,10},{14,8},{16,22},{18,... | collective-permute-start | bytes 1327112 | tf_op jit(solution)/shard_map/ppermute | solution.py:72
  91.9 8.5 %collective-permute-start.20 = (bf16[128,768]{1,0:T(8,128)(2,1)S(1)}, bf16[128,768]{1,0:T(8,128)(2,1)S(1)}, u32[]{:S(2)}, u32[]{:S(2)}) collective-permute-start(bf16[128,768]{1,0:T(8,128)(2,1)S(1)} %get-tuple-element.114.rest_14_), channel_id=1, source_target_pairs={{0,24},{2,26},{4,28},{6,30},{8,16},{10,18},{12,20},{14,22},{16,8},... | collective-permute-start | bytes 589832 | tf_op jit(solution)/shard_map/ppermute | solution.py:72
  94.1 15.0 %collective-permute-start.19 = (bf16[128,768]{1,0:T(8,128)(2,1)S(1)}, bf16[128,768]{1,0:T(8,128)(2,1)S(1)}, u32[]{:S(2)}, u32[]{:S(2)}) collective-permute-start(bf16[128,768]{1,0:T(8,128)(2,1)S(1)} %get-tuple-element.114.rest_14_), channel_id=1, source_target_pairs={{0,8},{2,10},{4,12},{6,14},{8,0},{10,2},{12,4},{14,6},{16,24},{18,... | collective-permute-start | bytes 589832 | tf_op jit(solution)/shard_map/ppermute | solution.py:72
  100.4 8.7 %collective-permute-start.21 = (bf16[128,768]{1,0:T(8,128)(2,1)S(1)}, bf16[128,768]{1,0:T(8,128)(2,1)S(1)}, u32[]{:S(2)}, u32[]{:S(2)}) collective-permute-start(bf16[128,768]{1,0:T(8,128)(2,1)S(1)} %collective-permute-done.20.rest_17_), channel_id=1, source_target_pairs={{0,8},{2,10},{4,12},{6,14},{8,0},{10,2},{12,4},{14,6},{16,24},{18,... | collective-permute-start | bytes 589832 | tf_op jit(solution)/shard_map/ppermute | solution.py:72
  109.2 37.9 %copy-start.2 = (bf16[128,768]{1,0:T(8,128)(2,1)S(1)}, bf16[128,768]{1,0:T(8,128)(2,1)}, u32[]{:S(2)}) copy-start(bf16[128,768]{1,0:T(8,128)(2,1)} %copy-done.1) | copy-start | bytes 589828
  110.7 2.1 collective-permute-start.22
  110.8 11.5 %collective-permute-start.12 = (bf16[2,192,512]{2,1,0:T(8,128)(2,1)S(1)}, bf16[2,192,512]{2,1,0:T(8,128)(2,1)S(1)}, u32[]{:S(2)}, u32[]{:S(2)}) collective-permute-start(bf16[2,192,512]{2,1,0:T(8,128)(2,1)S(1)} %get-tuple-element.104), channel_id=1, source_target_pairs={{0,2},{2,0},{4,6},{6,4},{8,10},{10,8},{12,14},{14,12},{16,18},{18,... | collective-permute-start | bytes 1179656 | tf_op jit(solution)/shard_map/ppermute | solution.py:72
  112.3 11.6 %collective-permute-start.14 = (bf16[2,192,512]{2,1,0:T(8,128)(2,1)S(1)}, bf16[2,192,512]{2,1,0:T(8,128)(2,1)S(1)}, u32[]{:S(2)}, u32[]{:S(2)}) collective-permute-start(bf16[2,192,512]{2,1,0:T(8,128)(2,1)S(1)} %get-tuple-element.107), channel_id=1, source_target_pairs={{0,4},{2,6},{4,0},{6,2},{8,12},{10,14},{12,8},{14,10},{16,20},{18,... | collective-permute-start | bytes 1179656 | tf_op jit(solution)/shard_map/ppermute | solution.py:72
  113.6 13.9 %collective-permute-start.23 = (bf16[2,104,768]{2,1,0:T(8,128)(2,1)S(1)}, bf16[2,104,768]{2,1,0:T(8,128)(2,1)S(1)}, u32[]{:S(2)}, u32[]{:S(2)}) collective-permute-start(bf16[2,104,768]{2,1,0:T(8,128)(2,1)S(1)} %get-tuple-element.122), channel_id=1, source_target_pairs={{0,8},{2,10},{4,12},{6,14},{8,0},{10,2},{12,4},{14,6},{16,24},{18,... | collective-permute-start | bytes 958472 | tf_op jit(solution)/shard_map/ppermute | solution.py:72
  122.4 12.6 %collective-permute-start.13 = (bf16[192,512]{1,0:T(8,128)(2,1)S(1)}, bf16[192,512]{1,0:T(8,128)(2,1)S(1)}, u32[]{:S(2)}, u32[]{:S(2)}) collective-permute-start(bf16[192,512]{1,0:T(8,128)(2,1)S(1)} %fusion.1), channel_id=1, source_target_pairs={{0,4},{2,6},{4,0},{6,2},{8,12},{10,14},{12,8},{14,10},{16,20},{18,... | collective-permute-start | bytes 589832 | tf_op jit(solution)/shard_map/ppermute | solution.py:72
  123.9 23.1 %collective-permute-start.25 = (bf16[128,1536]{1,0:T(8,128)(2,1)S(1)}, bf16[128,1536]{1,0:T(8,128)(2,1)S(1)}, u32[]{:S(2)}, u32[]{:S(2)}) collective-permute-start(bf16[128,1536]{1,0:T(8,128)(2,1)S(1)} %get-tuple-element.128), channel_id=1, source_target_pairs={{0,2},{2,0},{4,6},{6,4},{8,10},{10,8},{12,14},{14,12},{16,18},{18,... | collective-permute-start | bytes 1179656 | tf_op jit(solution)/shard_map/ppermute | solution.py:72
  124.2 22.8 %collective-permute-start.26 = (bf16[128,1536]{1,0:T(8,128)(2,1)S(1)}, bf16[128,1536]{1,0:T(8,128)(2,1)S(1)}, u32[]{:S(2)}, u32[]{:S(2)}) collective-permute-start(bf16[128,1536]{1,0:T(8,128)(2,1)S(1)} %get-tuple-element.129), channel_id=1, source_target_pairs={{0,4},{2,6},{4,0},{6,2},{8,12},{10,14},{12,8},{14,10},{16,20},{18,... | collective-permute-start | bytes 1179656 | tf_op jit(solution)/shard_map/ppermute | solution.py:72
  125.9 21.1 %collective-permute-start.27 = (bf16[128,1536]{1,0:T(8,128)(2,1)S(1)}, bf16[128,1536]{1,0:T(8,128)(2,1)S(1)}, u32[]{:S(2)}, u32[]{:S(2)}) collective-permute-start(bf16[128,1536]{1,0:T(8,128)(2,1)S(1)} %get-tuple-element.130), channel_id=1, source_target_pairs={{0,6},{2,4},{4,2},{6,0},{8,14},{10,12},{12,10},{14,8},{16,22},{18,... | collective-permute-start | bytes 1179656 | tf_op jit(solution)/shard_map/ppermute | solution.py:72
  127.5 7.2 %collective-permute-start.24 = (bf16[104,768]{1,0:T(8,128)(2,1)S(1)}, bf16[104,768]{1,0:T(8,128)(2,1)S(1)}, u32[]{:S(2)}, u32[]{:S(2)}) collective-permute-start(bf16[104,768]{1,0:T(8,128)(2,1)S(1)} %fusion.8), channel_id=1, source_target_pairs={{0,24},{2,26},{4,28},{6,30},{8,16},{10,18},{12,20},{14,22},{16,8},... | collective-permute-start | bytes 479240 | tf_op jit(solution)/shard_map/ppermute | solution.py:72
  134.7 12.3 %collective-permute-start.15 = (bf16[192,512]{1,0:T(8,128)(2,1)S(1)}, bf16[192,512]{1,0:T(8,128)(2,1)S(1)}, u32[]{:S(2)}, u32[]{:S(2)}) collective-permute-start(bf16[192,512]{1,0:T(8,128)(2,1)S(1)} %fusion), channel_id=1, source_target_pairs={{0,2},{2,0},{4,6},{6,4},{8,10},{10,8},{12,14},{14,12},{16,18},{18,... | collective-permute-start | bytes 589832 | tf_op jit(solution)/shard_map/ppermute | solution.py:72
  150.7 3.8 %collective-permute-start.30 = (bf16[4,144,576]{2,1,0:T(8,128)(2,1)S(1)}, bf16[4,144,576]{2,1,0:T(8,128)(2,1)S(1)}, u32[]{:S(2)}, u32[]{:S(2)}) collective-permute-start(bf16[4,144,576]{2,1,0:T(8,128)(2,1)S(1)} %get-tuple-element.140), channel_id=1, source_target_pairs={{0,1},{1,0},{2,3},{3,2},{4,5},{5,4},{6,7},{7,6},{8,9},{9,8},{10,11... | collective-permute-start | bytes 1990664 | tf_op jit(solution)/shard_map/ppermute | solution.py:597
  150.8 8.2 %collective-permute-start.35 = (bf16[96,768]{1,0:T(8,128)(2,1)S(1)}, bf16[96,768]{1,0:T(8,128)(2,1)S(1)}, u32[]{:S(2)}, u32[]{:S(2)}) collective-permute-start(bf16[96,768]{1,0:T(8,128)(2,1)S(1)} %slice.247), channel_id=1, source_target_pairs={{0,24},{2,26},{4,28},{6,30},{8,16},{10,18},{12,20},{14,22},{16,8},... | collective-permute-start | bytes 442376 | tf_op jit(solution)/shard_map/ppermute | solution.py:72
  154.3 12.6 %collective-permute-start.46 = (bf16[4,96,768]{2,1,0:T(8,128)(2,1)S(1)}, bf16[4,96,768]{2,1,0:T(8,128)(2,1)S(1)}, u32[]{:S(2)}, u32[]{:S(2)}) collective-permute-start(bf16[4,96,768]{2,1,0:T(8,128)(2,1)S(1)} %get-tuple-element.155), channel_id=1, source_target_pairs={{0,1},{1,0},{2,3},{3,2},{4,5},{5,4},{6,7},{7,6},{8,9},{9,8},{10,11... | collective-permute-start | bytes 1769480 | tf_op jit(solution)/shard_map/ppermute | solution.py:597
  155.3 10.9 %collective-permute-start.31 = (bf16[2,144,576]{2,1,0:T(8,128)(2,1)S(1)}, bf16[2,144,576]{2,1,0:T(8,128)(2,1)S(1)}, u32[]{:S(2)}, u32[]{:S(2)}) collective-permute-start(bf16[2,144,576]{2,1,0:T(8,128)(2,1)S(1)} %get-tuple-element.142), channel_id=1, source_target_pairs={{0,2},{2,0},{4,6},{6,4},{8,10},{10,8},{12,14},{14,12},{16,18},{18,... | collective-permute-start | bytes 995336 | tf_op jit(solution)/shard_map/ppermute | solution.py:72
  159.1 9.6 %collective-permute-start.36 = (bf16[2,96,768]{2,1,0:T(8,128)(2,1)S(1)}, bf16[2,96,768]{2,1,0:T(8,128)(2,1)S(1)}, u32[]{:S(2)}, u32[]{:S(2)}) collective-permute-start(bf16[2,96,768]{2,1,0:T(8,128)(2,1)S(1)} %pad_maximum_fusion.5), channel_id=1, source_target_pairs={{0,8},{2,10},{4,12},{6,14},{8,0},{10,2},{12,4},{14,6},{16,24},{18,... | collective-permute-start | bytes 884744 | tf_op jit(solution)/shard_map/ppermute | solution.py:72
  166.2 7.6 %collective-permute-start.32 = (bf16[144,576]{1,0:T(8,128)(2,1)S(1)}, bf16[144,576]{1,0:T(8,128)(2,1)S(1)}, u32[]{:S(2)}, u32[]{:S(2)}) collective-permute-start(bf16[144,576]{1,0:T(8,128)(2,1)S(1)} %fusion.7), channel_id=1, source_target_pairs={{0,4},{2,6},{4,0},{6,2},{8,12},{10,14},{12,8},{14,10},{16,20},{18,... | collective-permute-start | bytes 497672 | tf_op jit(solution)/shard_map/ppermute | solution.py:72
  167.5 8.5 %collective-permute-start.47 = (bf16[2,96,768]{2,1,0:T(8,128)(2,1)S(1)}, bf16[2,96,768]{2,1,0:T(8,128)(2,1)S(1)}, u32[]{:S(2)}, u32[]{:S(2)}) collective-permute-start(bf16[2,96,768]{2,1,0:T(8,128)(2,1)S(1)} %get-tuple-element.157), channel_id=1, source_target_pairs={{0,8},{2,10},{4,12},{6,14},{8,0},{10,2},{12,4},{14,6},{16,24},{18,... | collective-permute-start | bytes 884744 | tf_op jit(solution)/shard_map/ppermute | solution.py:72
  168.7 18.3 %collective-permute-start.38 = (bf16[4,96,768]{2,1,0:T(8,128)(2,1)S(1)}, bf16[4,96,768]{2,1,0:T(8,128)(2,1)S(1)}, u32[]{:S(2)}, u32[]{:S(2)}) collective-permute-start(bf16[4,96,768]{2,1,0:T(8,128)(2,1)S(1)} %pad_maximum_fusion.1.refs_0_), channel_id=1, source_target_pairs={{0,4},{2,6},{4,0},{6,2},{8,12},{10,14},{12,8},{14,10},{16,20},{18,... | collective-permute-start | bytes 1769480 | tf_op jit(solution)/shard_map/ppermute | solution.py:72
  169.4 17.8 %collective-permute-start.37 = (bf16[4,96,768]{2,1,0:T(8,128)(2,1)S(1)}, bf16[4,96,768]{2,1,0:T(8,128)(2,1)S(1)}, u32[]{:S(2)}, u32[]{:S(2)}) collective-permute-start(bf16[4,96,768]{2,1,0:T(8,128)(2,1)S(1)} %pad_maximum_fusion.1.refs_0_), channel_id=1, source_target_pairs={{0,2},{2,0},{4,6},{6,4},{8,10},{10,8},{12,14},{14,12},{16,18},{18,... | collective-permute-start | bytes 1769480 | tf_op jit(solution)/shard_map/ppermute | solution.py:72
  173.9 8.8 %collective-permute-start.33 = (bf16[144,576]{1,0:T(8,128)(2,1)S(1)}, bf16[144,576]{1,0:T(8,128)(2,1)S(1)}, u32[]{:S(2)}, u32[]{:S(2)}) collective-permute-start(bf16[144,576]{1,0:T(8,128)(2,1)S(1)} %fusion.4), channel_id=1, source_target_pairs={{0,24},{2,26},{4,28},{6,30},{8,16},{10,18},{12,20},{14,22},{16,8},... | collective-permute-start | bytes 497672 | tf_op jit(solution)/shard_map/ppermute | solution.py:72
  176.0 13.7 %collective-permute-start.48 = (bf16[96,768]{1,0:T(8,128)(2,1)S(1)}, bf16[96,768]{1,0:T(8,128)(2,1)S(1)}, u32[]{:S(2)}, u32[]{:S(2)}) collective-permute-start(bf16[96,768]{1,0:T(8,128)(2,1)S(1)} %fusion.9), channel_id=1, source_target_pairs={{0,24},{2,26},{4,28},{6,30},{8,16},{10,18},{12,20},{14,22},{16,8},... | collective-permute-start | bytes 442376 | tf_op jit(solution)/shard_map/ppermute | solution.py:72
  182.8 11.3 %collective-permute-start.34 = (bf16[2,144,576]{2,1,0:T(8,128)(2,1)S(1)}, bf16[2,144,576]{2,1,0:T(8,128)(2,1)S(1)}, u32[]{:S(2)}, u32[]{:S(2)}) collective-permute-start(bf16[2,144,576]{2,1,0:T(8,128)(2,1)S(1)} %pad_maximum_fusion.4), channel_id=1, source_target_pairs={{0,8},{2,10},{4,12},{6,14},{8,0},{10,2},{12,4},{14,6},{16,24},{18,... | collective-permute-start | bytes 995336 | tf_op jit(solution)/shard_map/ppermute | solution.py:72
  187.1 7.2 %collective-permute-start.40 = (bf16[2,96,768]{2,1,0:T(8,128)(2,1)S(1)}, bf16[2,96,768]{2,1,0:T(8,128)(2,1)S(1)}, u32[]{:S(2)}, u32[]{:S(2)}) collective-permute-start(bf16[2,96,768]{2,1,0:T(8,128)(2,1)S(1)} %slice.192), channel_id=1, source_target_pairs={{0,2},{2,0},{4,6},{6,4},{8,10},{10,8},{12,14},{14,12},{16,18},{18,... | collective-permute-start | bytes 884744 | tf_op jit(solution)/shard_map/ppermute | solution.py:72
  187.3 9.3 %collective-permute-start.39 = (bf16[2,96,768]{2,1,0:T(8,128)(2,1)S(1)}, bf16[2,96,768]{2,1,0:T(8,128)(2,1)S(1)}, u32[]{:S(2)}, u32[]{:S(2)}) collective-permute-start(bf16[2,96,768]{2,1,0:T(8,128)(2,1)S(1)} %slice.191), channel_id=1, source_target_pairs={{0,4},{2,6},{4,0},{6,2},{8,12},{10,14},{12,8},{14,10},{16,20},{18,... | collective-permute-start | bytes 884744 | tf_op jit(solution)/shard_map/ppermute | solution.py:72
  189.8 9.5 %collective-permute-start.49 = (bf16[96,768]{1,0:T(8,128)(2,1)S(1)}, bf16[96,768]{1,0:T(8,128)(2,1)S(1)}, u32[]{:S(2)}, u32[]{:S(2)}) collective-permute-start(bf16[96,768]{1,0:T(8,128)(2,1)S(1)} %fusion.5), channel_id=1, source_target_pairs={{0,24},{2,26},{4,28},{6,30},{8,16},{10,18},{12,20},{14,22},{16,8},... | collective-permute-start | bytes 442376 | tf_op jit(solution)/shard_map/ppermute | solution.py:72
  196.6 19.9 %collective-permute-start.42 = (bf16[4,144,576]{2,1,0:T(8,128)(2,1)S(1)}, bf16[4,144,576]{2,1,0:T(8,128)(2,1)S(1)}, u32[]{:S(2)}, u32[]{:S(2)}) collective-permute-start(bf16[4,144,576]{2,1,0:T(8,128)(2,1)S(1)} %pad_maximum_fusion.refs_0_), channel_id=1, source_target_pairs={{0,4},{2,6},{4,0},{6,2},{8,12},{10,14},{12,8},{14,10},{16,20},{18,... | collective-permute-start | bytes 1990664 | tf_op jit(solution)/shard_map/ppermute | solution.py:72
  199.1 19.4 %collective-permute-start.41 = (bf16[4,144,576]{2,1,0:T(8,128)(2,1)S(1)}, bf16[4,144,576]{2,1,0:T(8,128)(2,1)S(1)}, u32[]{:S(2)}, u32[]{:S(2)}) collective-permute-start(bf16[4,144,576]{2,1,0:T(8,128)(2,1)S(1)} %pad_maximum_fusion.refs_0_), channel_id=1, source_target_pairs={{0,2},{2,0},{4,6},{6,4},{8,10},{10,8},{12,14},{14,12},{16,18},{18,... | collective-permute-start | bytes 1990664 | tf_op jit(solution)/shard_map/ppermute | solution.py:72
  199.4 7.0 %collective-permute-start.50 = (bf16[2,96,768]{2,1,0:T(8,128)(2,1)S(1)}, bf16[2,96,768]{2,1,0:T(8,128)(2,1)S(1)}, u32[]{:S(2)}, u32[]{:S(2)}) collective-permute-start(bf16[2,96,768]{2,1,0:T(8,128)(2,1)S(1)} %pad_maximum_fusion.6), channel_id=1, source_target_pairs={{0,8},{2,10},{4,12},{6,14},{8,0},{10,2},{12,4},{14,6},{16,24},{18,... | collective-permute-start | bytes 884744 | tf_op jit(solution)/shard_map/ppermute | solution.py:72
  199.5 20.1 %collective-permute-start.28 = (bf16[2,128,768]{2,1,0:T(8,128)(2,1)S(1)}, bf16[2,128,768]{2,1,0:T(8,128)(2,1)S(1)}, u32[]{:S(2)}, u32[]{:S(2)}) collective-permute-start(bf16[2,128,768]{2,1,0:T(8,128)(2,1)S(1)} %get-tuple-element.138), channel_id=1, source_target_pairs={{0,8},{2,10},{4,12},{6,14},{8,0},{10,2},{12,4},{14,6},{16,24},{18,... | collective-permute-start | bytes 1179656 | tf_op jit(solution)/shard_map/ppermute | solution.py:72
  206.5 22.6 %collective-permute-start.52 = (bf16[4,96,768]{2,1,0:T(8,128)(2,1)S(1)}, bf16[4,96,768]{2,1,0:T(8,128)(2,1)S(1)}, u32[]{:S(2)}, u32[]{:S(2)}) collective-permute-start(bf16[4,96,768]{2,1,0:T(8,128)(2,1)S(1)} %pad_maximum_fusion.2.refs_0_), channel_id=1, source_target_pairs={{0,4},{2,6},{4,0},{6,2},{8,12},{10,14},{12,8},{14,10},{16,20},{18,... | collective-permute-start | bytes 1769480 | tf_op jit(solution)/shard_map/ppermute | solution.py:72
  207.7 22.4 %collective-permute-start.51 = (bf16[4,96,768]{2,1,0:T(8,128)(2,1)S(1)}, bf16[4,96,768]{2,1,0:T(8,128)(2,1)S(1)}, u32[]{:S(2)}, u32[]{:S(2)}) collective-permute-start(bf16[4,96,768]{2,1,0:T(8,128)(2,1)S(1)} %pad_maximum_fusion.2.refs_0_), channel_id=1, source_target_pairs={{0,2},{2,0},{4,6},{6,4},{8,10},{10,8},{12,14},{14,12},{16,18},{18,... | collective-permute-start | bytes 1769480 | tf_op jit(solution)/shard_map/ppermute | solution.py:72
  218.5 15.5 %collective-permute-start.43 = (bf16[2,144,576]{2,1,0:T(8,128)(2,1)S(1)}, bf16[2,144,576]{2,1,0:T(8,128)(2,1)S(1)}, u32[]{:S(2)}, u32[]{:S(2)}) collective-permute-start(bf16[2,144,576]{2,1,0:T(8,128)(2,1)S(1)} %slice.193), channel_id=1, source_target_pairs={{0,4},{2,6},{4,0},{6,2},{8,12},{10,14},{12,8},{14,10},{16,20},{18,... | collective-permute-start | bytes 995336 | tf_op jit(solution)/shard_map/ppermute | solution.py:72
  218.7 15.4 %collective-permute-start.44 = (bf16[2,144,576]{2,1,0:T(8,128)(2,1)S(1)}, bf16[2,144,576]{2,1,0:T(8,128)(2,1)S(1)}, u32[]{:S(2)}, u32[]{:S(2)}) collective-permute-start(bf16[2,144,576]{2,1,0:T(8,128)(2,1)S(1)} %slice.194), channel_id=1, source_target_pairs={{0,2},{2,0},{4,6},{6,4},{8,10},{10,8},{12,14},{14,12},{16,18},{18,... | collective-permute-start | bytes 995336 | tf_op jit(solution)/shard_map/ppermute | solution.py:72
  219.7 19.4 %collective-permute-start.29 = (bf16[128,768]{1,0:T(8,128)(2,1)S(1)}, bf16[128,768]{1,0:T(8,128)(2,1)S(1)}, u32[]{:S(2)}, u32[]{:S(2)}) collective-permute-start(bf16[128,768]{1,0:T(8,128)(2,1)S(1)} %fusion.6), channel_id=1, source_target_pairs={{0,24},{2,26},{4,28},{6,30},{8,16},{10,18},{12,20},{14,22},{16,8},... | collective-permute-start | bytes 589832 | tf_op jit(solution)/shard_map/ppermute | solution.py:72
  230.1 9.8 %collective-permute-start.53 = (bf16[2,96,768]{2,1,0:T(8,128)(2,1)S(1)}, bf16[2,96,768]{2,1,0:T(8,128)(2,1)S(1)}, u32[]{:S(2)}, u32[]{:S(2)}) collective-permute-start(bf16[2,96,768]{2,1,0:T(8,128)(2,1)S(1)} %slice.200), channel_id=1, source_target_pairs={{0,4},{2,6},{4,0},{6,2},{8,12},{10,14},{12,8},{14,10},{16,20},{18,... | collective-permute-start | bytes 884744 | tf_op jit(solution)/shard_map/ppermute | solution.py:72
  231.3 8.6 %collective-permute-start.54 = (bf16[2,96,768]{2,1,0:T(8,128)(2,1)S(1)}, bf16[2,96,768]{2,1,0:T(8,128)(2,1)S(1)}, u32[]{:S(2)}, u32[]{:S(2)}) collective-permute-start(bf16[2,96,768]{2,1,0:T(8,128)(2,1)S(1)} %slice.201), channel_id=1, source_target_pairs={{0,2},{2,0},{4,6},{6,4},{8,10},{10,8},{12,14},{14,12},{16,18},{18,... | collective-permute-start | bytes 884744 | tf_op jit(solution)/shard_map/ppermute | solution.py:72
  239.1 4.5 %collective-permute-start.45 = (bf16[2,4,24,768]{3,2,1,0:T(8,128)(2,1)S(1)}, bf16[2,4,24,768]{3,2,1,0:T(8,128)(2,1)S(1)}, u32[]{:S(2)}, u32[]{:S(2)}) collective-permute-start(bf16[2,4,24,768]{3,2,1,0:T(8,128)(2,1)S(1)} %get-tuple-element.149), channel_id=1, source_target_pairs={{0,1},{1,0},{2,3},{3,2},{4,5},{5,4},{6,7},{7,6},{8,9},{9,8},{10,11... | collective-permute-start | bytes 884744 | tf_op jit(solution)/shard_map/ppermute | solution.py:597
  (12 other events, 56.4 us)
Sparse Core Ops, SparseCore 0:
  9.6 12.2 all-gather.5
  23.4 15.4 all-gather.7
  40.4 15.6 all-gather.9

commit v8 on v7

--- a/solution.py
+++ b/solution.py
@@ -625,9 +625,6 @@
 
     context_grads = (context_grads[0], *(places.column_swap(context_grads[i], i) for i in turns))
     down_parts = (down_parts[0], *(places.four_swap(down_parts[i], i) for i in turns))
-    branch_low = after(branch_low, context_grads)
-    far = places.column_swap(branch_low, 3)
-    branches = (branch_low, places.column_swap(branch_low, 1), places.column_swap(far, 1), far)
     query_grad, parts = attend_grad(query, context, context_grads, log_total, key_values, bias, chunks)
     if plane_size == 4:
         own_key, own_value, turned_key, turned_value, key_x, value_y = parts
@@ -639,11 +636,14 @@
         blocks = places.exchange(jnp.transpose(blocks, (1, 0, 2)), places.planes)
         blocks = jnp.sum(blocks.astype(F32), axis=0)
         keys, values = first_step = (blocks[:WIDTH],), (blocks[WIDTH:],)
-    down_parts = after(down_parts, query_grad, branches)
+    branch_low = after(branch_low, first_step)
+    far = places.column_swap(branch_low, 3)
+    branches = (branch_low, places.column_swap(branch_low, 1), places.column_swap(far, 1), far)
+    down_parts = after(down_parts, query_grad)
     other, own = down_grad_parts(spot, down_parts, model_width)
     down_pieces = pair_sums(spot, own, to_other(other), "down_sum")
     down_part = rest_sum(column_total(*down_pieces))
-    up_parts = after(up_parts, first_step)
+    up_parts = after(up_parts, query_grad)
     up_parts = (up_parts[0], *(places.four_swap(up_parts[i], i) for i in turns))
     keys, values = after((keys, values), down_part, up_parts)
     down_column = column_gather(down_part[:TALL].astype(BF16))

time: 252 us -> 249 us (0.988)
  starting transfers between devices: 70.2 us -> 66.7 us
    ppermute x51, starting transfers between devices: 69.6 us -> 66.2 us  [swap(): return lax.ppermute(block, 'seq', [(i, i ^ bits) for i in range(self.size)])]
  transfers between devices with their start and end apart: 58 -> 58, of which waited for: 27 -> 31; matrix products, arithmetic and copies ran while one was open for 3% -> 3% of each run, Pallas kernels for 13% -> 13%
where the time goes in v8:
time: 249 us; the launch traced here: 248 us
  waiting for transfers between devices  103 us (41%)
  starting transfers between devices  66.7 us (27%)
  Pallas kernels  50.4 us (20%)
  between operations  14.4 us (6%)
  local copies, waits for them, and re-layouts  6.53 us (3%)
  blocking collectives  4.62 us (2%)
  other arithmetic  3.27 us (1%)
    ppermute x51, waiting for transfers between devices, swap(): return lax.ppermute(block, 'seq', [(i, i ^ bits) for i in range(self.size)])  100 us
    ppermute x51, starting transfers between devices, swap(): return lax.ppermute(block, 'seq', [(i, i ^ bits) for i in range(self.size)])  66.2 us
    pallas_call x14, Pallas kernels, kernel_call(): pl.pallas_call(run if after else kernel, out_shape=outs, in_specs=spaces...  50.4 us
  transfers between devices with their start and end apart: 58, of which 31 were waited for; matrix products, arithmetic and copies ran while one was open for 3% of the time, Pallas kernels for 13%

profile of v8, /device:TPU:0, one launch (start us, length us, event | category | flops | bytes accessed | tf_op | source)
XLA Modules:
  0.0 248.4 jit_solution(539590958652295678)
XLA Ops:
  9.5 5.1 %collective-permute-start.2 = (bf16[128,768]{1,0:T(8,128)(2,1)S(1)}, bf16[128,768]{1,0:T(8,128)(2,1)S(1)}, u32[]{:S(2)}, u32[]{:S(2)}) collective-permute-start(bf16[128,768]{1,0:T(8,128)(2,1)S(1)} %bitcast.60), channel_id=1, source_target_pairs={{0,24},{2,26},{4,28},{6,30},{8,16},{10,18},{12,20},{14,22},{16,8},... | collective-permute-start | bytes 589832 | tf_op jit(solution)/shard_map/ppermute | solution.py:72
  15.5 1.8 all-gather.1
  17.6 1.5 constant_dynamic-slice_fusion.2
  19.3 2.8 %all_gather.18.weight.rest_18_ = bf16[768,576]{1,0:T(8,128)(2,1)S(1)} all-gather(bf16[384,576]{1,0:T(8,128)(2,1)S(1)} %pad_maximum_fusion.3), channel_id=1, replica_groups=mesh['seq'=16,'shard'=2] {'shard'}, dimensions={0}, use_global_device_ids=true | all-gather | bytes 1327104 | tf_op jit(solution)/shard_map/all_gather | solution.py:545
  22.1 9.2 %collective-permute-done.1.x2.rest_8_ = bf16[128,768]{1,0:T(8,128)(2,1)S(1)} collective-permute-done((bf16[128,768]{1,0:T(8,128)(2,1)S(1)}, bf16[128,768]{1,0:T(8,128)(2,1)S(1)}, u32[]{:S(2)}, u32[]{:S(2)}) %collective-permute-start.1) | collective-permute-done | bytes 196640 | tf_op jit(solution)/shard_map/ppermute | solution.py:72
  32.2 2.5 %collective-permute-start.5 = (bf16[512,384]{1,0:T(8,128)(2,1)S(1)}, bf16[512,384]{1,0:T(8,128)(2,1)S(1)}, u32[]{:S(2)}, u32[]{:S(2)}) collective-permute-start(bf16[512,384]{1,0:T(8,128)(2,1)S(1)} %get-tuple-element.89.refs_1_.refs_7_), channel_id=1, source_target_pairs={{0,6},{2,4},{4,2},{6,0},{8,14},{10,12},{12,10},{14,8},{16,22},{18,... | collective-permute-start | bytes 1179656 | tf_op jit(solution)/shard_map/ppermute | solution.py:72
  37.3 8.0 %collective-permute-done.5.refs_4_.refs_10_ = bf16[512,384]{1,0:T(8,128)(2,1)S(1)} collective-permute-done((bf16[512,384]{1,0:T(8,128)(2,1)S(1)}, bf16[512,384]{1,0:T(8,128)(2,1)S(1)}, u32[]{:S(2)}, u32[]{:S(2)}) %collective-permute-start.5) | collective-permute-done | bytes 393248 | tf_op jit(solution)/shard_map/ppermute | solution.py:72
  45.3 6.5 %collective-permute-done.4.refs_3_.refs_9_ = bf16[512,384]{1,0:T(8,128)(2,1)S(1)} collective-permute-done((bf16[512,384]{1,0:T(8,128)(2,1)S(1)}, bf16[512,384]{1,0:T(8,128)(2,1)S(1)}, u32[]{:S(2)}, u32[]{:S(2)}) %collective-permute-start.4) | collective-permute-done | bytes 393248 | tf_op jit(solution)/shard_map/ppermute | solution.py:72
  51.9 9.1 %attend.1 = (f32[512,192]{1,0:T(8,128)S(1)}, f32[512,128]{1,0:T(8,128)S(1)}, bf16[128,192]{1,0:T(8,128)(2,1)S(1)}, bf16[128,192]{1,0:T(8,128)(2,1)}, bf16[128,192]{1,0:T(8,128)(2,1)}, /*index=5*/bf16[128,192]{1,0:T(8,128)(2,1)}) custom-call(bf16[512,192]{1,0:T(8,128)(2,1)S(1)} %get-tuple-element.88.refs_0_, ...), custom_call_target="tpu_custom_call" | custom-call | bytes 31500000 | tf_op jit(solution)/shard_map/attend/pallas_call | solution.py:39
  62.5 2.8 %collective-permute-start.7 = (bf16[128,192]{1,0:T(8,128)(2,1)}, bf16[128,192]{1,0:T(8,128)(2,1)}, u32[]{:S(2)}, u32[]{:S(2)}) collective-permute-start(bf16[128,192]{1,0:T(8,128)(2,1)} %get-tuple-element.92.rest_12_), channel_id=1, source_target_pairs={{0,16},{2,18},{4,20},{6,22},{8,24},{10,26},{12,28},{14,30},{16,0},... | collective-permute-start | bytes 147464 | tf_op jit(solution)/shard_map/ppermute | solution.py:72
  65.4 1.5 collective-permute-start.8
  67.8 2.9 %collective-permute-done.7.c2 = bf16[128,192]{1,0:T(8,128)(2,1)} collective-permute-done((bf16[128,192]{1,0:T(8,128)(2,1)}, bf16[128,192]{1,0:T(8,128)(2,1)}, u32[]{:S(2)}, u32[]{:S(2)}) %collective-permute-start.7) | collective-permute-done | bytes 49184 | tf_op jit(solution)/shard_map/ppermute | solution.py:72
  70.8 1.1 collective-permute-done.8.c3
  72.8 10.7 %dense.1 = (bf16[128,768]{1,0:T(8,128)(2,1)}, f32[128,768]{1,0:T(8,128)S(1)}, bf16[128,768]{1,0:T(8,128)(2,1)S(1)}, bf16[128,192]{1,0:T(8,128)(2,1)S(1)}, bf16[1...) custom-call(s32[3]{0:T(128)S(1)} %pad_add_fusion.spot, ...), custom_call_target="tpu_custom_call" | custom-call | bytes 35000000 | tf_op jit(solution)/shard_map/dense/pallas_call | solution.py:39
  83.5 1.6 collective-permute-start.16
  85.7 1.4 collective-permute-start.18
  88.0 1.3 collective-permute-start.10
  89.3 2.1 collective-permute-done.9.refs_4_
  91.3 1.6 collective-permute-start.11
  93.0 1.4 collective-permute-done.10.refs_5_
  94.4 3.0 %collective-permute-done.11.refs_6_ = bf16[128,192]{1,0:T(8,128)(2,1)S(1)} collective-permute-done((bf16[128,192]{1,0:T(8,128)(2,1)S(1)}, bf16[128,192]{1,0:T(8,128)(2,1)S(1)}, u32[]{:S(2)}, u32[]{:S(2)}) %collective-permute-start.11) | collective-permute-done | bytes 49184 | tf_op jit(solution)/shard_map/ppermute | solution.py:72
  97.4 8.0 %attend_grad.1 = (bf16[512,192]{1,0:T(8,128)(2,1)S(1)}, bf16[192,512]{1,0:T(8,128)(2,1)S(1)}, bf16[192,512]{1,0:T(8,128)(2,1)S(1)}, bf16[192,512]{1,0:T(8,128)(2...) custom-call(bf16[512,192]{1,0:T(8,128)(2,1)S(1)} %get-tuple-element.88.ref, ...), custom_call_target="tpu_custom_call" | custom-call | bytes 38500000 | tf_op jit(solution)/shard_map/attend_grad/pallas_call | solution.py:39
  105.5 1.5 down_grad.1
  107.1 1.6 collective-permute-start.12
  111.5 1.1 collective-permute-start.23
  112.6 6.5 %collective-permute-done.12.rest_1_ = bf16[2,192,512]{2,1,0:T(8,128)(2,1)S(1)} collective-permute-done((bf16[2,192,512]{2,1,0:T(8,128)(2,1)S(1)}, bf16[2,192,512]{2,1,0:T(8,128)(2,1)S(1)}, u32[]{:S(2)}, u32[]{:S(2)}) %collective-permute-start.12) | collective-permute-done | bytes 393248 | tf_op jit(solution)/shard_map/ppermute | solution.py:72
  119.1 1.5 collective-permute-start.24
  120.6 1.6 collective-permute-start.26
  122.4 2.2 collective-permute-start.21
  124.7 2.8 %collective-permute-done.22.p1 = bf16[128,1536]{1,0:T(8,128)(2,1)S(1)} collective-permute-done((bf16[128,1536]{1,0:T(8,128)(2,1)S(1)}, bf16[128,1536]{1,0:T(8,128)(2,1)S(1)}, u32[]{:S(2)}, u32[]{:S(2)}) %collective-permute-start.22) | collective-permute-done | bytes 393248 | tf_op jit(solution)/shard_map/ppermute | solution.py:72
  128.1 8.8 %collective-permute-done.23.p2 = bf16[128,1536]{1,0:T(8,128)(2,1)S(1)} collective-permute-done((bf16[128,1536]{1,0:T(8,128)(2,1)S(1)}, bf16[128,1536]{1,0:T(8,128)(2,1)S(1)}, u32[]{:S(2)}, u32[]{:S(2)}) %collective-permute-start.23) | collective-permute-done | bytes 393248 | tf_op jit(solution)/shard_map/ppermute | solution.py:72
  138.5 4.1 %collective-permute-done.13.rest_2_ = bf16[192,512]{1,0:T(8,128)(2,1)S(1)} collective-permute-done((bf16[192,512]{1,0:T(8,128)(2,1)S(1)}, bf16[192,512]{1,0:T(8,128)(2,1)S(1)}, u32[]{:S(2)}, u32[]{:S(2)}) %collective-permute-start.13) | collective-permute-done | bytes 196640 | tf_op jit(solution)/shard_map/ppermute | solution.py:72
  144.1 3.7 %joined_grad.1 = (bf16[4,144,576]{2,1,0:T(8,128)(2,1)S(1)}, bf16[4,144,576]{2,1,0:T(8,128)(2,1)S(1)}, bf16[2,128,768]{2,1,0:T(8,128)(2,1)S(1)}, bf16[2,128,768]{2,1,0:T(8,128)(2,1)S(1)}) custom-call(s32[3]{0:T(128)S(1)} %pad_add_fusion.spot, bf16[512,192]{1,0:T(8,128)(2,1)S(1)} %get-tuple-element.102.query_grad, ...), custom_call_target="tpu_custom_call" | custom-call | bytes 21000000 | tf_op jit(solution)/shard_map/joined_grad/pallas_call | solution.py:39
  147.9 2.0 collective-permute-start.35
  149.9 1.5 up_grad.1
  153.3 2.8 %collective-permute-done.35 = bf16[96,768]{1,0:T(8,128)(2,1)S(1)} collective-permute-done((bf16[96,768]{1,0:T(8,128)(2,1)S(1)}, bf16[96,768]{1,0:T(8,128)(2,1)S(1)}, u32[]{:S(2)}, u32[]{:S(2)}) %collective-permute-start.35) | collective-permute-done | bytes 147488 | tf_op jit(solution)/shard_map/ppermute | solution.py:72
  156.1 1.3 collective-permute-start.36
  157.5 5.9 %collective-permute-done.31 = bf16[2,144,576]{2,1,0:T(8,128)(2,1)S(1)} collective-permute-done((bf16[2,144,576]{2,1,0:T(8,128)(2,1)S(1)}, bf16[2,144,576]{2,1,0:T(8,128)(2,1)S(1)}, u32[]{:S(2)}, u32[]{:S(2)}) %collective-permute-start.31) | collective-permute-done | bytes 331808 | tf_op jit(solution)/shard_map/ppermute | solution.py:72
  164.8 1.6 collective-permute-start.38
  166.4 1.0 collective-permute-start.37
  167.4 3.6 %collective-permute-done.32 = bf16[144,576]{1,0:T(8,128)(2,1)S(1)} collective-permute-done((bf16[144,576]{1,0:T(8,128)(2,1)S(1)}, bf16[144,576]{1,0:T(8,128)(2,1)S(1)}, u32[]{:S(2)}, u32[]{:S(2)}) %collective-permute-start.32) | collective-permute-done | bytes 165920 | tf_op jit(solution)/shard_map/ppermute | solution.py:72
  171.1 1.9 collective-permute-start.33
  173.1 4.2 %collective-permute-start.48 = (bf16[96,768]{1,0:T(8,128)(2,1)S(1)}, bf16[96,768]{1,0:T(8,128)(2,1)S(1)}, u32[]{:S(2)}, u32[]{:S(2)}) collective-permute-start(bf16[96,768]{1,0:T(8,128)(2,1)S(1)} %fusion.9), channel_id=1, source_target_pairs={{0,24},{2,26},{4,28},{6,30},{8,16},{10,18},{12,20},{14,22},{16,8},... | collective-permute-start | bytes 442376 | tf_op jit(solution)/shard_map/ppermute | solution.py:72
  177.2 3.2 %collective-permute-done.33 = bf16[144,576]{1,0:T(8,128)(2,1)S(1)} collective-permute-done((bf16[144,576]{1,0:T(8,128)(2,1)S(1)}, bf16[144,576]{1,0:T(8,128)(2,1)S(1)}, u32[]{:S(2)}, u32[]{:S(2)}) %collective-permute-start.33) | collective-permute-done | bytes 165920 | tf_op jit(solution)/shard_map/ppermute | solution.py:72
  180.5 1.6 collective-permute-start.34
  182.1 1.4 collective-permute-start.40
  184.4 2.7 %collective-permute-start.49 = (bf16[96,768]{1,0:T(8,128)(2,1)S(1)}, bf16[96,768]{1,0:T(8,128)(2,1)S(1)}, u32[]{:S(2)}, u32[]{:S(2)}) collective-permute-start(bf16[96,768]{1,0:T(8,128)(2,1)S(1)} %fusion.5), channel_id=1, source_target_pairs={{0,24},{2,26},{4,28},{6,30},{8,16},{10,18},{12,20},{14,22},{16,8},... | collective-permute-start | bytes 442376 | tf_op jit(solution)/shard_map/ppermute | solution.py:72
  187.1 3.2 %collective-permute-done.34 = bf16[2,144,576]{2,1,0:T(8,128)(2,1)S(1)} collective-permute-done((bf16[2,144,576]{2,1,0:T(8,128)(2,1)S(1)}, bf16[2,144,576]{2,1,0:T(8,128)(2,1)S(1)}, u32[]{:S(2)}, u32[]{:S(2)}) %collective-permute-start.34) | collective-permute-done | bytes 331808 | tf_op jit(solution)/shard_map/ppermute | solution.py:72
  191.6 1.2 collective-permute-start.41
  192.8 1.5 collective-permute-done.49
  194.4 2.0 collective-permute-start.28
  196.5 7.9 %collective-permute-done.50 = bf16[2,96,768]{2,1,0:T(8,128)(2,1)S(1)} collective-permute-done((bf16[2,96,768]{2,1,0:T(8,128)(2,1)S(1)}, bf16[2,96,768]{2,1,0:T(8,128)(2,1)S(1)}, u32[]{:S(2)}, u32[]{:S(2)}) %collective-permute-start.50) | collective-permute-done | bytes 294944 | tf_op jit(solution)/shard_map/ppermute | solution.py:72
  205.2 3.1 %place_down.1 = f32[1536,768]{1,0:T(8,128)} custom-call(s32[3]{0:T(128)S(1)} %pad_add_fusion.spot, bf16[4,96,768]{2,1,0:T(8,128)(2,1)S(1)} %pad_maximum_fusion.1.refs_0_, bf16[4,96,768]{2,1,0:T(8,128)(2,1)S(1)} %collective-permute-done.37.refs_1_, bf16[4,96,768]{2,1,0:T(8,128)(2,1)S(1)} %collective-permute-done.38.refs_2_, ...), custom_call_target="tpu_custom_call" | custom-call | bytes 17500000 | tf_op jit(solution)/shard_map/place_down/pallas_call | solution.py:39
  208.3 1.9 collective-permute-done.42.refs_2_
  211.1 1.2 collective-permute-start.43
  212.3 1.3 collective-permute-start.44
  213.6 3.2 %collective-permute-start.29 = (bf16[128,768]{1,0:T(8,128)(2,1)S(1)}, bf16[128,768]{1,0:T(8,128)(2,1)S(1)}, u32[]{:S(2)}, u32[]{:S(2)}) collective-permute-start(bf16[128,768]{1,0:T(8,128)(2,1)S(1)} %fusion.6), channel_id=1, source_target_pairs={{0,24},{2,26},{4,28},{6,30},{8,16},{10,18},{12,20},{14,22},{16,8},... | collective-permute-start | bytes 589832 | tf_op jit(solution)/shard_map/ppermute | solution.py:72
  217.5 5.3 %collective-permute-done.52.refs_2_ = bf16[4,96,768]{2,1,0:T(8,128)(2,1)S(1)} collective-permute-done((bf16[4,96,768]{2,1,0:T(8,128)(2,1)S(1)}, bf16[4,96,768]{2,1,0:T(8,128)(2,1)S(1)}, u32[]{:S(2)}, u32[]{:S(2)}) %collective-permute-start.52) | collective-permute-done | bytes 589856 | tf_op jit(solution)/shard_map/ppermute | solution.py:72
  223.7 1.2 collective-permute-start.53
  224.9 1.3 collective-permute-start.54
  226.8 3.1 %collective-permute-done.43.refs_3_ = bf16[2,144,576]{2,1,0:T(8,128)(2,1)S(1)} collective-permute-done((bf16[2,144,576]{2,1,0:T(8,128)(2,1)S(1)}, bf16[2,144,576]{2,1,0:T(8,128)(2,1)S(1)}, u32[]{:S(2)}, u32[]{:S(2)}) %collective-permute-start.43) | collective-permute-done | bytes 331808 | tf_op jit(solution)/shard_map/ppermute | solution.py:72
  230.7 5.0 %place_joined.1 = (f32[384,2304]{1,0:T(8,128)}, f32[8,384]{1,0:T(8,128)S(1)}, bf16[2,4,24,768]{3,2,1,0:T(8,128)(2,1)S(1)}, bf16[2,4,24,768]{3,2,1,0:T(8,128)(2,1)S(1)}) custom-call(s32[3]{0:T(128)S(1)} %pad_add_fusion.spot, bf16[4,144,576]{2,1,0:T(8,128)(2,1)S(1)} %pad_maximum_fusion.refs_0_, bf16[4,144,576]{2,1,0:T(8,128)(2,1)S(1)} %collective-permute-done.41.refs_1_, ...), custom_call_target="tpu_custom_call" | custom-call | bytes 17500000 | tf_op jit(solution)/shard_map/place_joined/pallas_call | solution.py:39
  236.5 3.1 %place_up.1 = f32[384,3072]{1,0:T(8,128)} custom-call(s32[3]{0:T(128)S(1)} %pad_add_fusion.spot, bf16[4,96,768]{2,1,0:T(8,128)(2,1)S(1)} %pad_maximum_fusion.2.refs_0_, bf16[4,96,768]{2,1,0:T(8,128)(2,1)S(1)} %collective-permute-done.51.refs_1_, bf16[4,96,768]{2,1,0:T(8,128)(2,1)S(1)} %collective-permute-done.52.refs_2_, ...), custom_call_target="tpu_custom_call" | custom-call | bytes 14000000 | tf_op jit(solution)/shard_map/place_up/pallas_call | solution.py:39
  240.2 1.6 place_out.1
  (169 shorter events, 30.8 us)
Async XLA Ops:
  7.2 64.7 %all-gather.6.cloned.1.call-start = ((), (), s32[]{:S(2)}) async-start(), calls=%async_computation | async-start | bytes 1769472 | tf_op jit(solution)/shard_map/all_gather | solution.py:545
  8.0 7.4 %copy-start.16 = (bf16[384]{0:T(512)(128)(2,1)S(1)}, bf16[384]{0:T(512)(128)(2,1)}, u32[]{:S(2)}) copy-start(bf16[384]{0:T(512)(128)(2,1)} %param.31) | copy-start | bytes 2308
  8.0 7.4 %copy-start.8 = (bf16[1536]{0:T(1024)(128)(2,1)S(1)}, bf16[1536]{0:T(1024)(128)(2,1)}, u32[]{:S(2)}) copy-start(bf16[1536]{0:T(1024)(128)(2,1)} %param.27) | copy-start | bytes 9220
  8.0 63.9 %all-gather.8.cloned.1.call-start = ((), (), s32[]{:S(2)}) async-start(), calls=%async_computation.1 | async-start | bytes 7077888 | tf_op jit(solution)/shard_map/all_gather | solution.py:545
  8.8 63.1 %all-gather.10.cloned.1.call-start = ((), (), s32[]{:S(2)}) async-start(), calls=%async_computation.2 | async-start | bytes 7077888 | tf_op jit(solution)/shard_map/all_gather | solution.py:545
  9.5 12.6 %collective-permute-start.2 = (bf16[128,768]{1,0:T(8,128)(2,1)S(1)}, bf16[128,768]{1,0:T(8,128)(2,1)S(1)}, u32[]{:S(2)}, u32[]{:S(2)}) collective-permute-start(bf16[128,768]{1,0:T(8,128)(2,1)S(1)} %bitcast.60), channel_id=1, source_target_pairs={{0,24},{2,26},{4,28},{6,30},{8,16},{10,18},{12,20},{14,22},{16,8},... | collective-permute-start | bytes 589832 | tf_op jit(solution)/shard_map/ppermute | solution.py:72
  14.6 16.7 %collective-permute-start.1 = (bf16[128,768]{1,0:T(8,128)(2,1)S(1)}, bf16[128,768]{1,0:T(8,128)(2,1)S(1)}, u32[]{:S(2)}, u32[]{:S(2)}) collective-permute-start(bf16[128,768]{1,0:T(8,128)(2,1)S(1)} %bitcast.61), channel_id=1, source_target_pairs={{0,16},{2,18},{4,20},{6,22},{8,24},{10,26},{12,28},{14,30},{16,0},... | collective-permute-start | bytes 589832 | tf_op jit(solution)/shard_map/ppermute | solution.py:72
  14.6 16.7 %collective-permute-start = (bf16[128,768]{1,0:T(8,128)(2,1)S(1)}, bf16[128,768]{1,0:T(8,128)(2,1)S(1)}, u32[]{:S(2)}, u32[]{:S(2)}) collective-permute-start(bf16[128,768]{1,0:T(8,128)(2,1)S(1)} %bitcast.62), channel_id=1, source_target_pairs={{0,8},{2,10},{4,12},{6,14},{8,0},{10,2},{12,4},{14,6},{16,24},{18,... | collective-permute-start | bytes 589832 | tf_op jit(solution)/shard_map/ppermute | solution.py:72
  19.1 16.7 %copy-start.17 = (s32[2]{0:T(128)S(1)}, s32[2]{0:T(128)}, u32[]{:S(2)}) copy-start(s32[2]{0:T(128)} %param.18) | copy-start | bytes 28
  32.2 13.1 %collective-permute-start.5 = (bf16[512,384]{1,0:T(8,128)(2,1)S(1)}, bf16[512,384]{1,0:T(8,128)(2,1)S(1)}, u32[]{:S(2)}, u32[]{:S(2)}) collective-permute-start(bf16[512,384]{1,0:T(8,128)(2,1)S(1)} %get-tuple-element.89.refs_1_.refs_7_), channel_id=1, source_target_pairs={{0,6},{2,4},{4,2},{6,0},{8,14},{10,12},{12,10},{14,8},{16,22},{18,... | collective-permute-start | bytes 1179656 | tf_op jit(solution)/shard_map/ppermute | solution.py:72
  34.7 17.1 %collective-permute-start.4 = (bf16[512,384]{1,0:T(8,128)(2,1)S(1)}, bf16[512,384]{1,0:T(8,128)(2,1)S(1)}, u32[]{:S(2)}, u32[]{:S(2)}) collective-permute-start(bf16[512,384]{1,0:T(8,128)(2,1)S(1)} %get-tuple-element.89.refs_1_.refs_7_), channel_id=1, source_target_pairs={{0,4},{2,6},{4,0},{6,2},{8,12},{10,14},{12,8},{14,10},{16,20},{18,... | collective-permute-start | bytes 1179656 | tf_op jit(solution)/shard_map/ppermute | solution.py:72
  35.2 16.6 %collective-permute-start.3 = (bf16[512,384]{1,0:T(8,128)(2,1)S(1)}, bf16[512,384]{1,0:T(8,128)(2,1)S(1)}, u32[]{:S(2)}, u32[]{:S(2)}) collective-permute-start(bf16[512,384]{1,0:T(8,128)(2,1)S(1)} %get-tuple-element.89.refs_1_.refs_7_), channel_id=1, source_target_pairs={{0,2},{2,0},{4,6},{6,4},{8,10},{10,8},{12,14},{14,12},{16,18},{18,... | collective-permute-start | bytes 1179656 | tf_op jit(solution)/shard_map/ppermute | solution.py:72
  62.5 5.3 %collective-permute-start.6 = (bf16[128,192]{1,0:T(8,128)(2,1)}, bf16[128,192]{1,0:T(8,128)(2,1)}, u32[]{:S(2)}, u32[]{:S(2)}) collective-permute-start(bf16[128,192]{1,0:T(8,128)(2,1)} %get-tuple-element.91.rest_11_), channel_id=1, source_target_pairs={{0,8},{2,10},{4,12},{6,14},{8,0},{10,2},{12,4},{14,6},{16,24},{18,... | collective-permute-start | bytes 147464 | tf_op jit(solution)/shard_map/ppermute | solution.py:72
  62.5 8.2 %collective-permute-start.7 = (bf16[128,192]{1,0:T(8,128)(2,1)}, bf16[128,192]{1,0:T(8,128)(2,1)}, u32[]{:S(2)}, u32[]{:S(2)}) collective-permute-start(bf16[128,192]{1,0:T(8,128)(2,1)} %get-tuple-element.92.rest_12_), channel_id=1, source_target_pairs={{0,16},{2,18},{4,20},{6,22},{8,24},{10,26},{12,28},{14,30},{16,0},... | collective-permute-start | bytes 147464 | tf_op jit(solution)/shard_map/ppermute | solution.py:72
  65.4 6.5 %collective-permute-start.8 = (bf16[128,192]{1,0:T(8,128)(2,1)}, bf16[128,192]{1,0:T(8,128)(2,1)}, u32[]{:S(2)}, u32[]{:S(2)}) collective-permute-start(bf16[128,192]{1,0:T(8,128)(2,1)} %get-tuple-element.93.rest_13_), channel_id=1, source_target_pairs={{0,24},{2,26},{4,28},{6,30},{8,16},{10,18},{12,20},{14,22},{16,8},... | collective-permute-start | bytes 147464 | tf_op jit(solution)/shard_map/ppermute | solution.py:72
  72.8 24.6 %copy-start.4 = (f32[512,192]{1,0:T(8,128)S(1)}, f32[512,192]{1,0:T(8,128)}, u32[]{:S(2)}) copy-start(f32[512,192]{1,0:T(8,128)} %copy-done.3) | copy-start | bytes 1179652
  72.8 24.6 %copy-start.6 = (f32[512,128]{1,0:T(8,128)S(1)}, f32[512,128]{1,0:T(8,128)}, u32[]{:S(2)}) copy-start(f32[512,128]{1,0:T(8,128)} %copy-done.5) | copy-start | bytes 786436
  83.5 21.9 %collective-permute-start.16 = (bf16[144,1536]{1,0:T(8,128)(2,1)S(1)}, bf16[144,1536]{1,0:T(8,128)(2,1)S(1)}, u32[]{:S(2)}, u32[]{:S(2)}) collective-permute-start(bf16[144,1536]{1,0:T(8,128)(2,1)S(1)} %get-tuple-element.110), channel_id=1, source_target_pairs={{0,2},{2,0},{4,6},{6,4},{8,10},{10,8},{12,14},{14,12},{16,18},{18,... | collective-permute-start | bytes 1327112 | tf_op jit(solution)/shard_map/ppermute | solution.py:72
  85.1 20.4 %collective-permute-start.17 = (bf16[144,1536]{1,0:T(8,128)(2,1)S(1)}, bf16[144,1536]{1,0:T(8,128)(2,1)S(1)}, u32[]{:S(2)}, u32[]{:S(2)}) collective-permute-start(bf16[144,1536]{1,0:T(8,128)(2,1)S(1)} %get-tuple-element.111), channel_id=1, source_target_pairs={{0,4},{2,6},{4,0},{6,2},{8,12},{10,14},{12,8},{14,10},{16,20},{18,... | collective-permute-start | bytes 1327112 | tf_op jit(solution)/shard_map/ppermute | solution.py:72
  85.7 19.8 %collective-permute-start.18 = (bf16[144,1536]{1,0:T(8,128)(2,1)S(1)}, bf16[144,1536]{1,0:T(8,128)(2,1)S(1)}, u32[]{:S(2)}, u32[]{:S(2)}) collective-permute-start(bf16[144,1536]{1,0:T(8,128)(2,1)S(1)} %get-tuple-element.112), channel_id=1, source_target_pairs={{0,6},{2,4},{4,2},{6,0},{8,14},{10,12},{12,10},{14,8},{16,22},{18,... | collective-permute-start | bytes 1327112 | tf_op jit(solution)/shard_map/ppermute | solution.py:72
  87.1 4.3 %collective-permute-start.9 = (bf16[128,192]{1,0:T(8,128)(2,1)S(1)}, bf16[128,192]{1,0:T(8,128)(2,1)S(1)}, u32[]{:S(2)}, u32[]{:S(2)}) collective-permute-start(bf16[128,192]{1,0:T(8,128)(2,1)S(1)} %get-tuple-element.99), channel_id=1, source_target_pairs={{0,8},{2,10},{4,12},{6,14},{8,0},{10,2},{12,4},{14,6},{16,24},{18,... | collective-permute-start | bytes 147464 | tf_op jit(solution)/shard_map/ppermute | solution.py:72
  88.0 6.4 %collective-permute-start.10 = (bf16[128,192]{1,0:T(8,128)(2,1)S(1)}, bf16[128,192]{1,0:T(8,128)(2,1)S(1)}, u32[]{:S(2)}, u32[]{:S(2)}) collective-permute-start(bf16[128,192]{1,0:T(8,128)(2,1)S(1)} %get-tuple-element.100), channel_id=1, source_target_pairs={{0,16},{2,18},{4,20},{6,22},{8,24},{10,26},{12,28},{14,30},{16,0},... | collective-permute-start | bytes 147464 | tf_op jit(solution)/shard_map/ppermute | solution.py:72
  91.3 6.1 %collective-permute-start.11 = (bf16[128,192]{1,0:T(8,128)(2,1)S(1)}, bf16[128,192]{1,0:T(8,128)(2,1)S(1)}, u32[]{:S(2)}, u32[]{:S(2)}) collective-permute-start(bf16[128,192]{1,0:T(8,128)(2,1)S(1)} %get-tuple-element.101), channel_id=1, source_target_pairs={{0,24},{2,26},{4,28},{6,30},{8,16},{10,18},{12,20},{14,22},{16,8},... | collective-permute-start | bytes 147464 | tf_op jit(solution)/shard_map/ppermute | solution.py:72
  105.5 38.6 %copy-start.2 = (bf16[128,768]{1,0:T(8,128)(2,1)S(1)}, bf16[128,768]{1,0:T(8,128)(2,1)}, u32[]{:S(2)}) copy-start(bf16[128,768]{1,0:T(8,128)(2,1)} %copy-done.1) | copy-start | bytes 589828
  107.0 2.2 collective-permute-start.19
  107.1 12.0 %collective-permute-start.12 = (bf16[2,192,512]{2,1,0:T(8,128)(2,1)S(1)}, bf16[2,192,512]{2,1,0:T(8,128)(2,1)S(1)}, u32[]{:S(2)}, u32[]{:S(2)}) collective-permute-start(bf16[2,192,512]{2,1,0:T(8,128)(2,1)S(1)} %get-tuple-element.104), channel_id=1, source_target_pairs={{0,2},{2,0},{4,6},{6,4},{8,10},{10,8},{12,14},{14,12},{16,18},{18,... | collective-permute-start | bytes 1179656 | tf_op jit(solution)/shard_map/ppermute | solution.py:72
  108.7 12.0 %collective-permute-start.14 = (bf16[2,192,512]{2,1,0:T(8,128)(2,1)S(1)}, bf16[2,192,512]{2,1,0:T(8,128)(2,1)S(1)}, u32[]{:S(2)}, u32[]{:S(2)}) collective-permute-start(bf16[2,192,512]{2,1,0:T(8,128)(2,1)S(1)} %get-tuple-element.107), channel_id=1, source_target_pairs={{0,4},{2,6},{4,0},{6,2},{8,12},{10,14},{12,8},{14,10},{16,20},{18,... | collective-permute-start | bytes 1179656 | tf_op jit(solution)/shard_map/ppermute | solution.py:72
  110.0 12.4 %collective-permute-start.20 = (bf16[2,104,768]{2,1,0:T(8,128)(2,1)S(1)}, bf16[2,104,768]{2,1,0:T(8,128)(2,1)S(1)}, u32[]{:S(2)}, u32[]{:S(2)}) collective-permute-start(bf16[2,104,768]{2,1,0:T(8,128)(2,1)S(1)} %get-tuple-element.120), channel_id=1, source_target_pairs={{0,8},{2,10},{4,12},{6,14},{8,0},{10,2},{12,4},{14,6},{16,24},{18,... | collective-permute-start | bytes 958472 | tf_op jit(solution)/shard_map/ppermute | solution.py:72
  110.6 17.0 %collective-permute-start.22 = (bf16[128,1536]{1,0:T(8,128)(2,1)S(1)}, bf16[128,1536]{1,0:T(8,128)(2,1)S(1)}, u32[]{:S(2)}, u32[]{:S(2)}) collective-permute-start(bf16[128,1536]{1,0:T(8,128)(2,1)S(1)} %get-tuple-element.126), channel_id=1, source_target_pairs={{0,2},{2,0},{4,6},{6,4},{8,10},{10,8},{12,14},{14,12},{16,18},{18,... | collective-permute-start | bytes 1179656 | tf_op jit(solution)/shard_map/ppermute | solution.py:72
  111.5 25.4 %collective-permute-start.23 = (bf16[128,1536]{1,0:T(8,128)(2,1)S(1)}, bf16[128,1536]{1,0:T(8,128)(2,1)S(1)}, u32[]{:S(2)}, u32[]{:S(2)}) collective-permute-start(bf16[128,1536]{1,0:T(8,128)(2,1)S(1)} %get-tuple-element.127), channel_id=1, source_target_pairs={{0,4},{2,6},{4,0},{6,2},{8,12},{10,14},{12,8},{14,10},{16,20},{18,... | collective-permute-start | bytes 1179656 | tf_op jit(solution)/shard_map/ppermute | solution.py:72
  119.1 19.4 %collective-permute-start.24 = (bf16[128,1536]{1,0:T(8,128)(2,1)S(1)}, bf16[128,1536]{1,0:T(8,128)(2,1)S(1)}, u32[]{:S(2)}, u32[]{:S(2)}) collective-permute-start(bf16[128,1536]{1,0:T(8,128)(2,1)S(1)} %get-tuple-element.128), channel_id=1, source_target_pairs={{0,6},{2,4},{4,2},{6,0},{8,14},{10,12},{12,10},{14,8},{16,22},{18,... | collective-permute-start | bytes 1179656 | tf_op jit(solution)/shard_map/ppermute | solution.py:72
  120.6 16.9 %collective-permute-start.26 = (bf16[128,768]{1,0:T(8,128)(2,1)S(1)}, bf16[128,768]{1,0:T(8,128)(2,1)S(1)}, u32[]{:S(2)}, u32[]{:S(2)}) collective-permute-start(bf16[128,768]{1,0:T(8,128)(2,1)S(1)} %get-tuple-element.136.rest_14_), channel_id=1, source_target_pairs={{0,24},{2,26},{4,28},{6,30},{8,16},{10,18},{12,20},{14,22},{16,8},... | collective-permute-start | bytes 589832 | tf_op jit(solution)/shard_map/ppermute | solution.py:72
  122.4 16.1 %collective-permute-start.21 = (bf16[104,768]{1,0:T(8,128)(2,1)S(1)}, bf16[104,768]{1,0:T(8,128)(2,1)S(1)}, u32[]{:S(2)}, u32[]{:S(2)}) collective-permute-start(bf16[104,768]{1,0:T(8,128)(2,1)S(1)} %fusion.8), channel_id=1, source_target_pairs={{0,24},{2,26},{4,28},{6,30},{8,16},{10,18},{12,20},{14,22},{16,8},... | collective-permute-start | bytes 479240 | tf_op jit(solution)/shard_map/ppermute | solution.py:72
  127.5 15.7 %collective-permute-start.25 = (bf16[128,768]{1,0:T(8,128)(2,1)S(1)}, bf16[128,768]{1,0:T(8,128)(2,1)S(1)}, u32[]{:S(2)}, u32[]{:S(2)}) collective-permute-start(bf16[128,768]{1,0:T(8,128)(2,1)S(1)} %get-tuple-element.136.rest_14_), channel_id=1, source_target_pairs={{0,8},{2,10},{4,12},{6,14},{8,0},{10,2},{12,4},{14,6},{16,24},{18,... | collective-permute-start | bytes 589832 | tf_op jit(solution)/shard_map/ppermute | solution.py:72
  136.9 5.7 %collective-permute-start.13 = (bf16[192,512]{1,0:T(8,128)(2,1)S(1)}, bf16[192,512]{1,0:T(8,128)(2,1)S(1)}, u32[]{:S(2)}, u32[]{:S(2)}) collective-permute-start(bf16[192,512]{1,0:T(8,128)(2,1)S(1)} %fusion.1), channel_id=1, source_target_pairs={{0,4},{2,6},{4,0},{6,2},{8,12},{10,14},{12,8},{14,10},{16,20},{18,... | collective-permute-start | bytes 589832 | tf_op jit(solution)/shard_map/ppermute | solution.py:72
  137.5 5.7 %collective-permute-start.15 = (bf16[192,512]{1,0:T(8,128)(2,1)S(1)}, bf16[192,512]{1,0:T(8,128)(2,1)S(1)}, u32[]{:S(2)}, u32[]{:S(2)}) collective-permute-start(bf16[192,512]{1,0:T(8,128)(2,1)S(1)} %fusion), channel_id=1, source_target_pairs={{0,2},{2,0},{4,6},{6,4},{8,10},{10,8},{12,14},{14,12},{16,18},{18,... | collective-permute-start | bytes 589832 | tf_op jit(solution)/shard_map/ppermute | solution.py:72
  138.4 5.7 %collective-permute-start.27 = (bf16[128,768]{1,0:T(8,128)(2,1)S(1)}, bf16[128,768]{1,0:T(8,128)(2,1)S(1)}, u32[]{:S(2)}, u32[]{:S(2)}) collective-permute-start(bf16[128,768]{1,0:T(8,128)(2,1)S(1)} %collective-permute-done.26.rest_17_), channel_id=1, source_target_pairs={{0,8},{2,10},{4,12},{6,14},{8,0},{10,2},{12,4},{14,6},{16,24},{18,... | collective-permute-start | bytes 589832 | tf_op jit(solution)/shard_map/ppermute | solution.py:72
  147.8 3.9 %collective-permute-start.30 = (bf16[4,144,576]{2,1,0:T(8,128)(2,1)S(1)}, bf16[4,144,576]{2,1,0:T(8,128)(2,1)S(1)}, u32[]{:S(2)}, u32[]{:S(2)}) collective-permute-start(bf16[4,144,576]{2,1,0:T(8,128)(2,1)S(1)} %get-tuple-element.140), channel_id=1, source_target_pairs={{0,1},{1,0},{2,3},{3,2},{4,5},{5,4},{6,7},{7,6},{8,9},{9,8},{10,11... | collective-permute-start | bytes 1990664 | tf_op jit(solution)/shard_map/ppermute | solution.py:597
  147.9 8.2 %collective-permute-start.35 = (bf16[96,768]{1,0:T(8,128)(2,1)S(1)}, bf16[96,768]{1,0:T(8,128)(2,1)S(1)}, u32[]{:S(2)}, u32[]{:S(2)}) collective-permute-start(bf16[96,768]{1,0:T(8,128)(2,1)S(1)} %slice.247), channel_id=1, source_target_pairs={{0,24},{2,26},{4,28},{6,30},{8,16},{10,18},{12,20},{14,22},{16,8},... | collective-permute-start | bytes 442376 | tf_op jit(solution)/shard_map/ppermute | solution.py:72
  151.4 12.3 %collective-permute-start.46 = (bf16[4,96,768]{2,1,0:T(8,128)(2,1)S(1)}, bf16[4,96,768]{2,1,0:T(8,128)(2,1)S(1)}, u32[]{:S(2)}, u32[]{:S(2)}) collective-permute-start(bf16[4,96,768]{2,1,0:T(8,128)(2,1)S(1)} %get-tuple-element.155), channel_id=1, source_target_pairs={{0,1},{1,0},{2,3},{3,2},{4,5},{5,4},{6,7},{7,6},{8,9},{9,8},{10,11... | collective-permute-start | bytes 1769480 | tf_op jit(solution)/shard_map/ppermute | solution.py:597
  152.5 10.9 %collective-permute-start.31 = (bf16[2,144,576]{2,1,0:T(8,128)(2,1)S(1)}, bf16[2,144,576]{2,1,0:T(8,128)(2,1)S(1)}, u32[]{:S(2)}, u32[]{:S(2)}) collective-permute-start(bf16[2,144,576]{2,1,0:T(8,128)(2,1)S(1)} %get-tuple-element.142), channel_id=1, source_target_pairs={{0,2},{2,0},{4,6},{6,4},{8,10},{10,8},{12,14},{14,12},{16,18},{18,... | collective-permute-start | bytes 995336 | tf_op jit(solution)/shard_map/ppermute | solution.py:72
  156.1 8.6 %collective-permute-start.36 = (bf16[2,96,768]{2,1,0:T(8,128)(2,1)S(1)}, bf16[2,96,768]{2,1,0:T(8,128)(2,1)S(1)}, u32[]{:S(2)}, u32[]{:S(2)}) collective-permute-start(bf16[2,96,768]{2,1,0:T(8,128)(2,1)S(1)} %pad_maximum_fusion.5), channel_id=1, source_target_pairs={{0,8},{2,10},{4,12},{6,14},{8,0},{10,2},{12,4},{14,6},{16,24},{18,... | collective-permute-start | bytes 884744 | tf_op jit(solution)/shard_map/ppermute | solution.py:72
  163.4 7.6 %collective-permute-start.32 = (bf16[144,576]{1,0:T(8,128)(2,1)S(1)}, bf16[144,576]{1,0:T(8,128)(2,1)S(1)}, u32[]{:S(2)}, u32[]{:S(2)}) collective-permute-start(bf16[144,576]{1,0:T(8,128)(2,1)S(1)} %fusion.7), channel_id=1, source_target_pairs={{0,4},{2,6},{4,0},{6,2},{8,12},{10,14},{12,8},{14,10},{16,20},{18,... | collective-permute-start | bytes 497672 | tf_op jit(solution)/shard_map/ppermute | solution.py:72
  164.4 8.6 %collective-permute-start.47 = (bf16[2,96,768]{2,1,0:T(8,128)(2,1)S(1)}, bf16[2,96,768]{2,1,0:T(8,128)(2,1)S(1)}, u32[]{:S(2)}, u32[]{:S(2)}) collective-permute-start(bf16[2,96,768]{2,1,0:T(8,128)(2,1)S(1)} %get-tuple-element.157), channel_id=1, source_target_pairs={{0,8},{2,10},{4,12},{6,14},{8,0},{10,2},{12,4},{14,6},{16,24},{18,... | collective-permute-start | bytes 884744 | tf_op jit(solution)/shard_map/ppermute | solution.py:72
  164.8 17.3 %collective-permute-start.38 = (bf16[4,96,768]{2,1,0:T(8,128)(2,1)S(1)}, bf16[4,96,768]{2,1,0:T(8,128)(2,1)S(1)}, u32[]{:S(2)}, u32[]{:S(2)}) collective-permute-start(bf16[4,96,768]{2,1,0:T(8,128)(2,1)S(1)} %pad_maximum_fusion.1.refs_0_), channel_id=1, source_target_pairs={{0,4},{2,6},{4,0},{6,2},{8,12},{10,14},{12,8},{14,10},{16,20},{18,... | collective-permute-start | bytes 1769480 | tf_op jit(solution)/shard_map/ppermute | solution.py:72
  166.4 17.2 %collective-permute-start.37 = (bf16[4,96,768]{2,1,0:T(8,128)(2,1)S(1)}, bf16[4,96,768]{2,1,0:T(8,128)(2,1)S(1)}, u32[]{:S(2)}, u32[]{:S(2)}) collective-permute-start(bf16[4,96,768]{2,1,0:T(8,128)(2,1)S(1)} %pad_maximum_fusion.1.refs_0_), channel_id=1, source_target_pairs={{0,2},{2,0},{4,6},{6,4},{8,10},{10,8},{12,14},{14,12},{16,18},{18,... | collective-permute-start | bytes 1769480 | tf_op jit(solution)/shard_map/ppermute | solution.py:72
  171.1 9.3 %collective-permute-start.33 = (bf16[144,576]{1,0:T(8,128)(2,1)S(1)}, bf16[144,576]{1,0:T(8,128)(2,1)S(1)}, u32[]{:S(2)}, u32[]{:S(2)}) collective-permute-start(bf16[144,576]{1,0:T(8,128)(2,1)S(1)} %fusion.4), channel_id=1, source_target_pairs={{0,24},{2,26},{4,28},{6,30},{8,16},{10,18},{12,20},{14,22},{16,8},... | collective-permute-start | bytes 497672 | tf_op jit(solution)/shard_map/ppermute | solution.py:72
  173.1 11.2 %collective-permute-start.48 = (bf16[96,768]{1,0:T(8,128)(2,1)S(1)}, bf16[96,768]{1,0:T(8,128)(2,1)S(1)}, u32[]{:S(2)}, u32[]{:S(2)}) collective-permute-start(bf16[96,768]{1,0:T(8,128)(2,1)S(1)} %fusion.9), channel_id=1, source_target_pairs={{0,24},{2,26},{4,28},{6,30},{8,16},{10,18},{12,20},{14,22},{16,8},... | collective-permute-start | bytes 442376 | tf_op jit(solution)/shard_map/ppermute | solution.py:72
  180.5 9.8 %collective-permute-start.34 = (bf16[2,144,576]{2,1,0:T(8,128)(2,1)S(1)}, bf16[2,144,576]{2,1,0:T(8,128)(2,1)S(1)}, u32[]{:S(2)}, u32[]{:S(2)}) collective-permute-start(bf16[2,144,576]{2,1,0:T(8,128)(2,1)S(1)} %pad_maximum_fusion.4), channel_id=1, source_target_pairs={{0,8},{2,10},{4,12},{6,14},{8,0},{10,2},{12,4},{14,6},{16,24},{18,... | collective-permute-start | bytes 995336 | tf_op jit(solution)/shard_map/ppermute | solution.py:72
  182.1 8.3 %collective-permute-start.40 = (bf16[2,96,768]{2,1,0:T(8,128)(2,1)S(1)}, bf16[2,96,768]{2,1,0:T(8,128)(2,1)S(1)}, u32[]{:S(2)}, u32[]{:S(2)}) collective-permute-start(bf16[2,96,768]{2,1,0:T(8,128)(2,1)S(1)} %slice.192), channel_id=1, source_target_pairs={{0,2},{2,0},{4,6},{6,4},{8,10},{10,8},{12,14},{14,12},{16,18},{18,... | collective-permute-start | bytes 884744 | tf_op jit(solution)/shard_map/ppermute | solution.py:72
  183.6 7.2 %collective-permute-start.39 = (bf16[2,96,768]{2,1,0:T(8,128)(2,1)S(1)}, bf16[2,96,768]{2,1,0:T(8,128)(2,1)S(1)}, u32[]{:S(2)}, u32[]{:S(2)}) collective-permute-start(bf16[2,96,768]{2,1,0:T(8,128)(2,1)S(1)} %slice.191), channel_id=1, source_target_pairs={{0,4},{2,6},{4,0},{6,2},{8,12},{10,14},{12,8},{14,10},{16,20},{18,... | collective-permute-start | bytes 884744 | tf_op jit(solution)/shard_map/ppermute | solution.py:72
  184.4 10.0 %collective-permute-start.49 = (bf16[96,768]{1,0:T(8,128)(2,1)S(1)}, bf16[96,768]{1,0:T(8,128)(2,1)S(1)}, u32[]{:S(2)}, u32[]{:S(2)}) collective-permute-start(bf16[96,768]{1,0:T(8,128)(2,1)S(1)} %fusion.5), channel_id=1, source_target_pairs={{0,24},{2,26},{4,28},{6,30},{8,16},{10,18},{12,20},{14,22},{16,8},... | collective-permute-start | bytes 442376 | tf_op jit(solution)/shard_map/ppermute | solution.py:72
  190.7 19.4 %collective-permute-start.42 = (bf16[4,144,576]{2,1,0:T(8,128)(2,1)S(1)}, bf16[4,144,576]{2,1,0:T(8,128)(2,1)S(1)}, u32[]{:S(2)}, u32[]{:S(2)}) collective-permute-start(bf16[4,144,576]{2,1,0:T(8,128)(2,1)S(1)} %pad_maximum_fusion.refs_0_), channel_id=1, source_target_pairs={{0,4},{2,6},{4,0},{6,2},{8,12},{10,14},{12,8},{14,10},{16,20},{18,... | collective-permute-start | bytes 1990664 | tf_op jit(solution)/shard_map/ppermute | solution.py:72
  191.6 19.4 %collective-permute-start.41 = (bf16[4,144,576]{2,1,0:T(8,128)(2,1)S(1)}, bf16[4,144,576]{2,1,0:T(8,128)(2,1)S(1)}, u32[]{:S(2)}, u32[]{:S(2)}) collective-permute-start(bf16[4,144,576]{2,1,0:T(8,128)(2,1)S(1)} %pad_maximum_fusion.refs_0_), channel_id=1, source_target_pairs={{0,2},{2,0},{4,6},{6,4},{8,10},{10,8},{12,14},{14,12},{16,18},{18,... | collective-permute-start | bytes 1990664 | tf_op jit(solution)/shard_map/ppermute | solution.py:72
  194.4 10.0 %collective-permute-start.50 = (bf16[2,96,768]{2,1,0:T(8,128)(2,1)S(1)}, bf16[2,96,768]{2,1,0:T(8,128)(2,1)S(1)}, u32[]{:S(2)}, u32[]{:S(2)}) collective-permute-start(bf16[2,96,768]{2,1,0:T(8,128)(2,1)S(1)} %pad_maximum_fusion.6), channel_id=1, source_target_pairs={{0,8},{2,10},{4,12},{6,14},{8,0},{10,2},{12,4},{14,6},{16,24},{18,... | collective-permute-start | bytes 884744 | tf_op jit(solution)/shard_map/ppermute | solution.py:72
  194.4 19.1 %collective-permute-start.28 = (bf16[2,128,768]{2,1,0:T(8,128)(2,1)S(1)}, bf16[2,128,768]{2,1,0:T(8,128)(2,1)S(1)}, u32[]{:S(2)}, u32[]{:S(2)}) collective-permute-start(bf16[2,128,768]{2,1,0:T(8,128)(2,1)S(1)} %get-tuple-element.138), channel_id=1, source_target_pairs={{0,8},{2,10},{4,12},{6,14},{8,0},{10,2},{12,4},{14,6},{16,24},{18,... | collective-permute-start | bytes 1179656 | tf_op jit(solution)/shard_map/ppermute | solution.py:72
  204.4 18.4 %collective-permute-start.52 = (bf16[4,96,768]{2,1,0:T(8,128)(2,1)S(1)}, bf16[4,96,768]{2,1,0:T(8,128)(2,1)S(1)}, u32[]{:S(2)}, u32[]{:S(2)}) collective-permute-start(bf16[4,96,768]{2,1,0:T(8,128)(2,1)S(1)} %pad_maximum_fusion.2.refs_0_), channel_id=1, source_target_pairs={{0,4},{2,6},{4,0},{6,2},{8,12},{10,14},{12,8},{14,10},{16,20},{18,... | collective-permute-start | bytes 1769480 | tf_op jit(solution)/shard_map/ppermute | solution.py:72
  205.2 18.5 %collective-permute-start.51 = (bf16[4,96,768]{2,1,0:T(8,128)(2,1)S(1)}, bf16[4,96,768]{2,1,0:T(8,128)(2,1)S(1)}, u32[]{:S(2)}, u32[]{:S(2)}) collective-permute-start(bf16[4,96,768]{2,1,0:T(8,128)(2,1)S(1)} %pad_maximum_fusion.2.refs_0_), channel_id=1, source_target_pairs={{0,2},{2,0},{4,6},{6,4},{8,10},{10,8},{12,14},{14,12},{16,18},{18,... | collective-permute-start | bytes 1769480 | tf_op jit(solution)/shard_map/ppermute | solution.py:72
  211.1 18.8 %collective-permute-start.43 = (bf16[2,144,576]{2,1,0:T(8,128)(2,1)S(1)}, bf16[2,144,576]{2,1,0:T(8,128)(2,1)S(1)}, u32[]{:S(2)}, u32[]{:S(2)}) collective-permute-start(bf16[2,144,576]{2,1,0:T(8,128)(2,1)S(1)} %slice.193), channel_id=1, source_target_pairs={{0,4},{2,6},{4,0},{6,2},{8,12},{10,14},{12,8},{14,10},{16,20},{18,... | collective-permute-start | bytes 995336 | tf_op jit(solution)/shard_map/ppermute | solution.py:72
  212.3 18.4 %collective-permute-start.44 = (bf16[2,144,576]{2,1,0:T(8,128)(2,1)S(1)}, bf16[2,144,576]{2,1,0:T(8,128)(2,1)S(1)}, u32[]{:S(2)}, u32[]{:S(2)}) collective-permute-start(bf16[2,144,576]{2,1,0:T(8,128)(2,1)S(1)} %slice.194), channel_id=1, source_target_pairs={{0,2},{2,0},{4,6},{6,4},{8,10},{10,8},{12,14},{14,12},{16,18},{18,... | collective-permute-start | bytes 995336 | tf_op jit(solution)/shard_map/ppermute | solution.py:72
  213.6 22.1 %collective-permute-start.29 = (bf16[128,768]{1,0:T(8,128)(2,1)S(1)}, bf16[128,768]{1,0:T(8,128)(2,1)S(1)}, u32[]{:S(2)}, u32[]{:S(2)}) collective-permute-start(bf16[128,768]{1,0:T(8,128)(2,1)S(1)} %fusion.6), channel_id=1, source_target_pairs={{0,24},{2,26},{4,28},{6,30},{8,16},{10,18},{12,20},{14,22},{16,8},... | collective-permute-start | bytes 589832 | tf_op jit(solution)/shard_map/ppermute | solution.py:72
  223.7 12.8 %collective-permute-start.53 = (bf16[2,96,768]{2,1,0:T(8,128)(2,1)S(1)}, bf16[2,96,768]{2,1,0:T(8,128)(2,1)S(1)}, u32[]{:S(2)}, u32[]{:S(2)}) collective-permute-start(bf16[2,96,768]{2,1,0:T(8,128)(2,1)S(1)} %slice.200), channel_id=1, source_target_pairs={{0,4},{2,6},{4,0},{6,2},{8,12},{10,14},{12,8},{14,10},{16,20},{18,... | collective-permute-start | bytes 884744 | tf_op jit(solution)/shard_map/ppermute | solution.py:72
  224.9 11.6 %collective-permute-start.54 = (bf16[2,96,768]{2,1,0:T(8,128)(2,1)S(1)}, bf16[2,96,768]{2,1,0:T(8,128)(2,1)S(1)}, u32[]{:S(2)}, u32[]{:S(2)}) collective-permute-start(bf16[2,96,768]{2,1,0:T(8,128)(2,1)S(1)} %slice.201), channel_id=1, source_target_pairs={{0,2},{2,0},{4,6},{6,4},{8,10},{10,8},{12,14},{14,12},{16,18},{18,... | collective-permute-start | bytes 884744 | tf_op jit(solution)/shard_map/ppermute | solution.py:72
  235.7 4.5 %collective-permute-start.45 = (bf16[2,4,24,768]{3,2,1,0:T(8,128)(2,1)S(1)}, bf16[2,4,24,768]{3,2,1,0:T(8,128)(2,1)S(1)}, u32[]{:S(2)}, u32[]{:S(2)}) collective-permute-start(bf16[2,4,24,768]{3,2,1,0:T(8,128)(2,1)S(1)} %get-tuple-element.149), channel_id=1, source_target_pairs={{0,1},{1,0},{2,3},{3,2},{4,5},{5,4},{6,7},{7,6},{8,9},{9,8},{10,11... | collective-permute-start | bytes 884744 | tf_op jit(solution)/shard_map/ppermute | solution.py:597
  (12 other events, 56.4 us)
Sparse Core Ops, SparseCore 0:
  9.6 12.2 all-gather.5
  23.4 15.4 all-gather.7
  40.4 15.6 all-gather.9

commit v9 on v8

--- a/solution.py
+++ b/solution.py
@@ -89,6 +89,9 @@
         key_value_ref[at, :] = joined[:, WIDTH:]
 
 
+SPAN = 512
+
+
 def attend_kernel(pieces, chunks, *refs):
     q_ref = refs[0]
     key_value_refs, bias_refs = refs[1 : 1 + pieces], refs[1 + pieces : 1 + 2 * pieces]
@@ -96,8 +99,8 @@
     low_refs = refs[3 + 2 * pieces :]
     rows = q_ref.shape[0]
     chunk = key_value_refs[0].shape[0] // chunks
-    for block in range(rows // ROWS):
-        at = slice(block * ROWS, (block + 1) * ROWS)
+    for block in range(rows // SPAN):
+        at = slice(block * SPAN, (block + 1) * SPAN)
         for head in range(GROUP_HEADS):
             columns = slice(head * HEAD_DIM, (head + 1) * HEAD_DIM)
             value_columns = slice(WIDTH + head * HEAD_DIM, WIDTH + (head + 1) * HEAD_DIM)
@@ -118,14 +121,16 @@
                 return raised, total, mix
 
             state = (
-                jnp.full((ROWS, 1), MASKED, F32),
-                jnp.zeros((ROWS, 1), F32),
-                jnp.zeros((ROWS, HEAD_DIM), F32),
+                jnp.full((SPAN, 1), MASKED, F32),
+                jnp.zeros((SPAN, 1), F32),
+                jnp.zeros((SPAN, HEAD_DIM), F32),
             )
             highest, total, mix = step(0, state) if chunks == 1 else lax.fori_loop(0, chunks, step, state)
             context = mix / total
             context_ref[at, columns] = context
-            low_refs[block][:, columns] = context.astype(BF16)
+            for part in range(SPAN // ROWS):
+                low = context[part * ROWS : (part + 1) * ROWS].astype(BF16)
+                low_refs[block * (SPAN // ROWS) + part][:, columns] = low
             log_ref[at, head : head + 1] = highest + jnp.log(total)
 
 

time: 249 us -> 246 us (0.988)
  waiting for transfers between devices: 103 us -> 111 us
  starting transfers between devices: 66.7 us -> 59.3 us
  Pallas kernels: 50.4 us -> 46.7 us
    ppermute x51, waiting for transfers between devices: 100 us -> 109 us  [swap(): return lax.ppermute(block, 'seq', [(i, i ^ bits) for i in range(self.size)])]
    ppermute x51, starting transfers between devices: 66.2 us -> 58.8 us  [swap(): return lax.ppermute(block, 'seq', [(i, i ^ bits) for i in range(self.size)])]
    pallas_call x14, Pallas kernels: 50.4 us -> 46.7 us  [kernel_call(): pl.pallas_call(run if after else kernel, out_shape=outs, in_specs=spaces...]
  transfers between devices with their start and end apart: 58 -> 58, of which waited for: 31 -> 28; matrix products, arithmetic and copies ran while one was open for 3% -> 3% of each run, Pallas kernels for 13% -> 12%
where the time goes in v9:
time: 246 us
  waiting for transfers between devices  111 us (45%)
  starting transfers between devices  59.3 us (24%)
  Pallas kernels  46.7 us (19%)
  between operations  14.4 us (6%)
  local copies, waits for them, and re-layouts  6.53 us (3%)
  blocking collectives  4.62 us (2%)
  other arithmetic  3.27 us (1%)
    ppermute x51, waiting for transfers between devices, swap(): return lax.ppermute(block, 'seq', [(i, i ^ bits) for i in range(self.size)])  109 us
    ppermute x51, starting transfers between devices, swap(): return lax.ppermute(block, 'seq', [(i, i ^ bits) for i in range(self.size)])  58.8 us
    pallas_call x14, Pallas kernels, kernel_call(): pl.pallas_call(run if after else kernel, out_shape=outs, in_specs=spaces...  46.7 us
  transfers between devices with their start and end apart: 58, of which 28 were waited for; matrix products, arithmetic and copies ran while one was open for 3% of the time, Pallas kernels for 12%

profile of v9, /device:TPU:0, one launch (start us, length us, event | category | flops | bytes accessed | tf_op | source)
XLA Modules:
  0.0 245.9 jit_solution(799169614831264637)
XLA Ops:
  9.5 5.1 %collective-permute-start.2 = (bf16[128,768]{1,0:T(8,128)(2,1)S(1)}, bf16[128,768]{1,0:T(8,128)(2,1)S(1)}, u32[]{:S(2)}, u32[]{:S(2)}) collective-permute-start(bf16[128,768]{1,0:T(8,128)(2,1)S(1)} %bitcast.60), channel_id=1, source_target_pairs={{0,24},{2,26},{4,28},{6,30},{8,16},{10,18},{12,20},{14,22},{16,8},... | collective-permute-start | bytes 589832 | tf_op jit(solution)/shard_map/ppermute | solution.py:72
  15.5 1.8 all-gather.1
  17.6 1.5 constant_dynamic-slice_fusion.2
  19.3 2.8 %all_gather.18.weight.rest_18_ = bf16[768,576]{1,0:T(8,128)(2,1)S(1)} all-gather(bf16[384,576]{1,0:T(8,128)(2,1)S(1)} %pad_maximum_fusion.3), channel_id=1, replica_groups=mesh['seq'=16,'shard'=2] {'shard'}, dimensions={0}, use_global_device_ids=true | all-gather | bytes 1327104 | tf_op jit(solution)/shard_map/all_gather | solution.py:550
  22.1 9.2 %collective-permute-done.1.x2.rest_8_ = bf16[128,768]{1,0:T(8,128)(2,1)S(1)} collective-permute-done((bf16[128,768]{1,0:T(8,128)(2,1)S(1)}, bf16[128,768]{1,0:T(8,128)(2,1)S(1)}, u32[]{:S(2)}, u32[]{:S(2)}) %collective-permute-start.1) | collective-permute-done | bytes 196640 | tf_op jit(solution)/shard_map/ppermute | solution.py:72
  32.2 2.5 %collective-permute-start.5 = (bf16[512,384]{1,0:T(8,128)(2,1)S(1)}, bf16[512,384]{1,0:T(8,128)(2,1)S(1)}, u32[]{:S(2)}, u32[]{:S(2)}) collective-permute-start(bf16[512,384]{1,0:T(8,128)(2,1)S(1)} %get-tuple-element.89.refs_1_.refs_7_), channel_id=1, source_target_pairs={{0,6},{2,4},{4,2},{6,0},{8,14},{10,12},{12,10},{14,8},{16,22},{18,... | collective-permute-start | bytes 1179656 | tf_op jit(solution)/shard_map/ppermute | solution.py:72
  37.3 8.0 %collective-permute-done.5.refs_4_.refs_10_ = bf16[512,384]{1,0:T(8,128)(2,1)S(1)} collective-permute-done((bf16[512,384]{1,0:T(8,128)(2,1)S(1)}, bf16[512,384]{1,0:T(8,128)(2,1)S(1)}, u32[]{:S(2)}, u32[]{:S(2)}) %collective-permute-start.5) | collective-permute-done | bytes 393248 | tf_op jit(solution)/shard_map/ppermute | solution.py:72
  45.3 6.5 %collective-permute-done.4.refs_3_.refs_9_ = bf16[512,384]{1,0:T(8,128)(2,1)S(1)} collective-permute-done((bf16[512,384]{1,0:T(8,128)(2,1)S(1)}, bf16[512,384]{1,0:T(8,128)(2,1)S(1)}, u32[]{:S(2)}, u32[]{:S(2)}) %collective-permute-start.4) | collective-permute-done | bytes 393248 | tf_op jit(solution)/shard_map/ppermute | solution.py:72
  51.9 5.5 %attend.1 = (f32[512,192]{1,0:T(8,128)S(1)}, f32[512,128]{1,0:T(8,128)S(1)}, bf16[128,192]{1,0:T(8,128)(2,1)S(1)}, bf16[128,192]{1,0:T(8,128)(2,1)}, bf16[128,192]{1,0:T(8,128)(2,1)}, /*index=5*/bf16[128,192]{1,0:T(8,128)(2,1)}) custom-call(bf16[512,192]{1,0:T(8,128)(2,1)S(1)} %get-tuple-element.88.refs_0_, ...), custom_call_target="tpu_custom_call" | custom-call | bytes 31500000 | tf_op jit(solution)/shard_map/attend/pallas_call | solution.py:39
  58.9 2.9 %collective-permute-start.7 = (bf16[128,192]{1,0:T(8,128)(2,1)}, bf16[128,192]{1,0:T(8,128)(2,1)}, u32[]{:S(2)}, u32[]{:S(2)}) collective-permute-start(bf16[128,192]{1,0:T(8,128)(2,1)} %get-tuple-element.92.rest_12_), channel_id=1, source_target_pairs={{0,16},{2,18},{4,20},{6,22},{8,24},{10,26},{12,28},{14,30},{16,0},... | collective-permute-start | bytes 147464 | tf_op jit(solution)/shard_map/ppermute | solution.py:72
  61.8 1.5 collective-permute-start.8
  64.2 2.9 %collective-permute-done.7.c2 = bf16[128,192]{1,0:T(8,128)(2,1)} collective-permute-done((bf16[128,192]{1,0:T(8,128)(2,1)}, bf16[128,192]{1,0:T(8,128)(2,1)}, u32[]{:S(2)}, u32[]{:S(2)}) %collective-permute-start.7) | collective-permute-done | bytes 49184 | tf_op jit(solution)/shard_map/ppermute | solution.py:72
  67.1 1.1 collective-permute-done.8.c3
  68.2 0.9 copy-done.7
  69.2 10.5 %dense.1 = (bf16[128,768]{1,0:T(8,128)(2,1)}, f32[128,768]{1,0:T(8,128)S(1)}, bf16[128,768]{1,0:T(8,128)(2,1)S(1)}, bf16[128,192]{1,0:T(8,128)(2,1)S(1)}, bf16[1...) custom-call(s32[3]{0:T(128)S(1)} %pad_add_fusion.spot, ...), custom_call_target="tpu_custom_call" | custom-call | bytes 35000000 | tf_op jit(solution)/shard_map/dense/pallas_call | solution.py:39
  79.7 1.6 collective-permute-start.16
  81.9 1.4 collective-permute-start.18
  83.3 0.9 collective-permute-start.9
  84.2 1.3 collective-permute-start.10
  85.5 2.1 collective-permute-done.9.refs_4_
  87.5 1.7 collective-permute-start.11
  89.3 1.3 collective-permute-done.10.refs_5_
  90.6 3.0 %collective-permute-done.11.refs_6_ = bf16[128,192]{1,0:T(8,128)(2,1)S(1)} collective-permute-done((bf16[128,192]{1,0:T(8,128)(2,1)S(1)}, bf16[128,192]{1,0:T(8,128)(2,1)S(1)}, u32[]{:S(2)}, u32[]{:S(2)}) %collective-permute-start.11) | collective-permute-done | bytes 49184 | tf_op jit(solution)/shard_map/ppermute | solution.py:72
  93.6 8.2 %attend_grad.1 = (bf16[512,192]{1,0:T(8,128)(2,1)S(1)}, bf16[192,512]{1,0:T(8,128)(2,1)S(1)}, bf16[192,512]{1,0:T(8,128)(2,1)S(1)}, bf16[192,512]{1,0:T(8,128)(2...) custom-call(bf16[512,192]{1,0:T(8,128)(2,1)S(1)} %get-tuple-element.88.ref, ...), custom_call_target="tpu_custom_call" | custom-call | bytes 38500000 | tf_op jit(solution)/shard_map/attend_grad/pallas_call | solution.py:39
  101.8 1.5 down_grad.1
  103.5 1.6 collective-permute-start.12
  106.7 1.1 collective-permute-start.22
  108.7 6.7 %collective-permute-done.12.rest_1_ = bf16[2,192,512]{2,1,0:T(8,128)(2,1)S(1)} collective-permute-done((bf16[2,192,512]{2,1,0:T(8,128)(2,1)S(1)}, bf16[2,192,512]{2,1,0:T(8,128)(2,1)S(1)}, u32[]{:S(2)}, u32[]{:S(2)}) %collective-permute-start.12) | collective-permute-done | bytes 393248 | tf_op jit(solution)/shard_map/ppermute | solution.py:72
  115.4 1.5 collective-permute-start.24
  117.0 1.7 collective-permute-start.26
  118.8 2.2 collective-permute-start.21
  121.1 2.8 %collective-permute-done.22.p1 = bf16[128,1536]{1,0:T(8,128)(2,1)S(1)} collective-permute-done((bf16[128,1536]{1,0:T(8,128)(2,1)S(1)}, bf16[128,1536]{1,0:T(8,128)(2,1)S(1)}, u32[]{:S(2)}, u32[]{:S(2)}) %collective-permute-start.22) | collective-permute-done | bytes 393248 | tf_op jit(solution)/shard_map/ppermute | solution.py:72
  124.3 9.0 %collective-permute-done.23.p2 = bf16[128,1536]{1,0:T(8,128)(2,1)S(1)} collective-permute-done((bf16[128,1536]{1,0:T(8,128)(2,1)S(1)}, bf16[128,1536]{1,0:T(8,128)(2,1)S(1)}, u32[]{:S(2)}, u32[]{:S(2)}) %collective-permute-start.23) | collective-permute-done | bytes 393248 | tf_op jit(solution)/shard_map/ppermute | solution.py:72
  134.8 4.1 %collective-permute-done.13.rest_2_ = bf16[192,512]{1,0:T(8,128)(2,1)S(1)} collective-permute-done((bf16[192,512]{1,0:T(8,128)(2,1)S(1)}, bf16[192,512]{1,0:T(8,128)(2,1)S(1)}, u32[]{:S(2)}, u32[]{:S(2)}) %collective-permute-start.13) | collective-permute-done | bytes 196640 | tf_op jit(solution)/shard_map/ppermute | solution.py:72
  140.4 3.5 %joined_grad.1 = (bf16[4,144,576]{2,1,0:T(8,128)(2,1)S(1)}, bf16[4,144,576]{2,1,0:T(8,128)(2,1)S(1)}, bf16[2,128,768]{2,1,0:T(8,128)(2,1)S(1)}, bf16[2,128,768]{2,1,0:T(8,128)(2,1)S(1)}) custom-call(s32[3]{0:T(128)S(1)} %pad_add_fusion.spot, bf16[512,192]{1,0:T(8,128)(2,1)S(1)} %get-tuple-element.102.query_grad, ...), custom_call_target="tpu_custom_call" | custom-call | bytes 21000000 | tf_op jit(solution)/shard_map/joined_grad/pallas_call | solution.py:39
  144.0 2.8 %collective-permute-start.35 = (bf16[96,768]{1,0:T(8,128)(2,1)S(1)}, bf16[96,768]{1,0:T(8,128)(2,1)S(1)}, u32[]{:S(2)}, u32[]{:S(2)}) collective-permute-start(bf16[96,768]{1,0:T(8,128)(2,1)S(1)} %slice.247), channel_id=1, source_target_pairs={{0,24},{2,26},{4,28},{6,30},{8,16},{10,18},{12,20},{14,22},{16,8},... | collective-permute-start | bytes 442376 | tf_op jit(solution)/shard_map/ppermute | solution.py:72
  146.8 1.5 up_grad.1
  148.7 0.9 joined_sum.1
  149.8 2.5 collective-permute-done.35
  152.2 1.5 collective-permute-start.36
  153.7 6.8 %collective-permute-done.31 = bf16[2,144,576]{2,1,0:T(8,128)(2,1)S(1)} collective-permute-done((bf16[2,144,576]{2,1,0:T(8,128)(2,1)S(1)}, bf16[2,144,576]{2,1,0:T(8,128)(2,1)S(1)}, u32[]{:S(2)}, u32[]{:S(2)}) %collective-permute-start.31) | collective-permute-done | bytes 331808 | tf_op jit(solution)/shard_map/ppermute | solution.py:72
  161.5 2.1 collective-permute-start.38
  163.8 4.3 %collective-permute-done.32 = bf16[144,576]{1,0:T(8,128)(2,1)S(1)} collective-permute-done((bf16[144,576]{1,0:T(8,128)(2,1)S(1)}, bf16[144,576]{1,0:T(8,128)(2,1)S(1)}, u32[]{:S(2)}, u32[]{:S(2)}) %collective-permute-start.32) | collective-permute-done | bytes 165920 | tf_op jit(solution)/shard_map/ppermute | solution.py:72
  168.2 1.1 collective-permute-start.33
  169.8 2.6 %collective-permute-start.48 = (bf16[96,768]{1,0:T(8,128)(2,1)S(1)}, bf16[96,768]{1,0:T(8,128)(2,1)S(1)}, u32[]{:S(2)}, u32[]{:S(2)}) collective-permute-start(bf16[96,768]{1,0:T(8,128)(2,1)S(1)} %fusion.9), channel_id=1, source_target_pairs={{0,24},{2,26},{4,28},{6,30},{8,16},{10,18},{12,20},{14,22},{16,8},... | collective-permute-start | bytes 442376 | tf_op jit(solution)/shard_map/ppermute | solution.py:72
  172.4 5.2 %collective-permute-done.33 = bf16[144,576]{1,0:T(8,128)(2,1)S(1)} collective-permute-done((bf16[144,576]{1,0:T(8,128)(2,1)S(1)}, bf16[144,576]{1,0:T(8,128)(2,1)S(1)}, u32[]{:S(2)}, u32[]{:S(2)}) %collective-permute-start.33) | collective-permute-done | bytes 165920 | tf_op jit(solution)/shard_map/ppermute | solution.py:72
  177.7 1.1 collective-permute-start.34
  179.3 2.6 %collective-permute-start.40 = (bf16[2,96,768]{2,1,0:T(8,128)(2,1)S(1)}, bf16[2,96,768]{2,1,0:T(8,128)(2,1)S(1)}, u32[]{:S(2)}, u32[]{:S(2)}) collective-permute-start(bf16[2,96,768]{2,1,0:T(8,128)(2,1)S(1)} %slice.192), channel_id=1, source_target_pairs={{0,2},{2,0},{4,6},{6,4},{8,10},{10,8},{12,14},{14,12},{16,18},{18,... | collective-permute-start | bytes 884744 | tf_op jit(solution)/shard_map/ppermute | solution.py:72
  182.1 1.4 collective-permute-start.49
  183.4 4.1 %collective-permute-done.34 = bf16[2,144,576]{2,1,0:T(8,128)(2,1)S(1)} collective-permute-done((bf16[2,144,576]{2,1,0:T(8,128)(2,1)S(1)}, bf16[2,144,576]{2,1,0:T(8,128)(2,1)S(1)}, u32[]{:S(2)}, u32[]{:S(2)}) %collective-permute-start.34) | collective-permute-done | bytes 331808 | tf_op jit(solution)/shard_map/ppermute | solution.py:72
  187.7 2.6 %collective-permute-done.39.refs_3_ = bf16[2,96,768]{2,1,0:T(8,128)(2,1)S(1)} collective-permute-done((bf16[2,96,768]{2,1,0:T(8,128)(2,1)S(1)}, bf16[2,96,768]{2,1,0:T(8,128)(2,1)S(1)}, u32[]{:S(2)}, u32[]{:S(2)}) %collective-permute-start.39) | collective-permute-done | bytes 294944 | tf_op jit(solution)/shard_map/ppermute | solution.py:72
  190.5 1.9 collective-permute-start.28
  192.4 7.3 %collective-permute-done.50 = bf16[2,96,768]{2,1,0:T(8,128)(2,1)S(1)} collective-permute-done((bf16[2,96,768]{2,1,0:T(8,128)(2,1)S(1)}, bf16[2,96,768]{2,1,0:T(8,128)(2,1)S(1)}, u32[]{:S(2)}, u32[]{:S(2)}) %collective-permute-start.50) | collective-permute-done | bytes 294944 | tf_op jit(solution)/shard_map/ppermute | solution.py:72
  199.8 2.6 %collective-permute-start.52 = (bf16[4,96,768]{2,1,0:T(8,128)(2,1)S(1)}, bf16[4,96,768]{2,1,0:T(8,128)(2,1)S(1)}, u32[]{:S(2)}, u32[]{:S(2)}) collective-permute-start(bf16[4,96,768]{2,1,0:T(8,128)(2,1)S(1)} %pad_maximum_fusion.2.refs_0_), channel_id=1, source_target_pairs={{0,4},{2,6},{4,0},{6,2},{8,12},{10,14},{12,8},{14,10},{16,20},{18,... | collective-permute-start | bytes 1769480 | tf_op jit(solution)/shard_map/ppermute | solution.py:72
  202.4 3.1 %place_down.1 = f32[1536,768]{1,0:T(8,128)} custom-call(s32[3]{0:T(128)S(1)} %pad_add_fusion.spot, bf16[4,96,768]{2,1,0:T(8,128)(2,1)S(1)} %pad_maximum_fusion.1.refs_0_, bf16[4,96,768]{2,1,0:T(8,128)(2,1)S(1)} %collective-permute-done.37.refs_1_, bf16[4,96,768]{2,1,0:T(8,128)(2,1)S(1)} %collective-permute-done.38.refs_2_, ...), custom_call_target="tpu_custom_call" | custom-call | bytes 17500000 | tf_op jit(solution)/shard_map/place_down/pallas_call | solution.py:39
  205.4 4.3 %collective-permute-done.42.refs_2_ = bf16[4,144,576]{2,1,0:T(8,128)(2,1)S(1)} collective-permute-done((bf16[4,144,576]{2,1,0:T(8,128)(2,1)S(1)}, bf16[4,144,576]{2,1,0:T(8,128)(2,1)S(1)}, u32[]{:S(2)}, u32[]{:S(2)}) %collective-permute-start.42) | collective-permute-done | bytes 663584 | tf_op jit(solution)/shard_map/ppermute | solution.py:72
  209.8 1.5 collective-permute-start.43
  211.9 1.2 collective-permute-start.29
  213.7 8.7 %collective-permute-done.52.refs_2_ = bf16[4,96,768]{2,1,0:T(8,128)(2,1)S(1)} collective-permute-done((bf16[4,96,768]{2,1,0:T(8,128)(2,1)S(1)}, bf16[4,96,768]{2,1,0:T(8,128)(2,1)S(1)}, u32[]{:S(2)}, u32[]{:S(2)}) %collective-permute-start.52) | collective-permute-done | bytes 589856 | tf_op jit(solution)/shard_map/ppermute | solution.py:72
  222.4 1.5 collective-permute-start.53
  225.1 3.1 %collective-permute-done.43.refs_3_ = bf16[2,144,576]{2,1,0:T(8,128)(2,1)S(1)} collective-permute-done((bf16[2,144,576]{2,1,0:T(8,128)(2,1)S(1)}, bf16[2,144,576]{2,1,0:T(8,128)(2,1)S(1)}, u32[]{:S(2)}, u32[]{:S(2)}) %collective-permute-start.43) | collective-permute-done | bytes 331808 | tf_op jit(solution)/shard_map/ppermute | solution.py:72
  228.2 5.0 %place_joined.1 = (f32[384,2304]{1,0:T(8,128)}, f32[8,384]{1,0:T(8,128)S(1)}, bf16[2,4,24,768]{3,2,1,0:T(8,128)(2,1)S(1)}, bf16[2,4,24,768]{3,2,1,0:T(8,128)(2,1)S(1)}) custom-call(s32[3]{0:T(128)S(1)} %pad_add_fusion.spot, bf16[4,144,576]{2,1,0:T(8,128)(2,1)S(1)} %pad_maximum_fusion.refs_0_, bf16[4,144,576]{2,1,0:T(8,128)(2,1)S(1)} %collective-permute-done.41.refs_1_, ...), custom_call_target="tpu_custom_call" | custom-call | bytes 17500000 | tf_op jit(solution)/shard_map/place_joined/pallas_call | solution.py:39
  234.0 3.1 %place_up.1 = f32[384,3072]{1,0:T(8,128)} custom-call(s32[3]{0:T(128)S(1)} %pad_add_fusion.spot, bf16[4,96,768]{2,1,0:T(8,128)(2,1)S(1)} %pad_maximum_fusion.2.refs_0_, bf16[4,96,768]{2,1,0:T(8,128)(2,1)S(1)} %collective-permute-done.51.refs_1_, bf16[4,96,768]{2,1,0:T(8,128)(2,1)S(1)} %collective-permute-done.52.refs_2_, ...), custom_call_target="tpu_custom_call" | custom-call | bytes 14000000 | tf_op jit(solution)/shard_map/place_up/pallas_call | solution.py:39
  237.7 1.6 place_out.1
  (169 shorter events, 23.5 us)
Async XLA Ops:
  7.2 61.1 %all-gather.6.cloned.1.call-start = ((), (), s32[]{:S(2)}) async-start(), calls=%async_computation | async-start | bytes 1769472 | tf_op jit(solution)/shard_map/all_gather | solution.py:550
  8.0 7.4 %copy-start.16 = (bf16[384]{0:T(512)(128)(2,1)S(1)}, bf16[384]{0:T(512)(128)(2,1)}, u32[]{:S(2)}) copy-start(bf16[384]{0:T(512)(128)(2,1)} %param.31) | copy-start | bytes 2308
  8.0 7.4 %copy-start.8 = (bf16[1536]{0:T(1024)(128)(2,1)S(1)}, bf16[1536]{0:T(1024)(128)(2,1)}, u32[]{:S(2)}) copy-start(bf16[1536]{0:T(1024)(128)(2,1)} %param.27) | copy-start | bytes 9220
  8.0 60.2 %all-gather.8.cloned.1.call-start = ((), (), s32[]{:S(2)}) async-start(), calls=%async_computation.1 | async-start | bytes 7077888 | tf_op jit(solution)/shard_map/all_gather | solution.py:550
  8.8 59.5 %all-gather.10.cloned.1.call-start = ((), (), s32[]{:S(2)}) async-start(), calls=%async_computation.2 | async-start | bytes 7077888 | tf_op jit(solution)/shard_map/all_gather | solution.py:550
  9.5 12.6 %collective-permute-start.2 = (bf16[128,768]{1,0:T(8,128)(2,1)S(1)}, bf16[128,768]{1,0:T(8,128)(2,1)S(1)}, u32[]{:S(2)}, u32[]{:S(2)}) collective-permute-start(bf16[128,768]{1,0:T(8,128)(2,1)S(1)} %bitcast.60), channel_id=1, source_target_pairs={{0,24},{2,26},{4,28},{6,30},{8,16},{10,18},{12,20},{14,22},{16,8},... | collective-permute-start | bytes 589832 | tf_op jit(solution)/shard_map/ppermute | solution.py:72
  14.6 16.7 %collective-permute-start.1 = (bf16[128,768]{1,0:T(8,128)(2,1)S(1)}, bf16[128,768]{1,0:T(8,128)(2,1)S(1)}, u32[]{:S(2)}, u32[]{:S(2)}) collective-permute-start(bf16[128,768]{1,0:T(8,128)(2,1)S(1)} %bitcast.61), channel_id=1, source_target_pairs={{0,16},{2,18},{4,20},{6,22},{8,24},{10,26},{12,28},{14,30},{16,0},... | collective-permute-start | bytes 589832 | tf_op jit(solution)/shard_map/ppermute | solution.py:72
  14.6 16.7 %collective-permute-start = (bf16[128,768]{1,0:T(8,128)(2,1)S(1)}, bf16[128,768]{1,0:T(8,128)(2,1)S(1)}, u32[]{:S(2)}, u32[]{:S(2)}) collective-permute-start(bf16[128,768]{1,0:T(8,128)(2,1)S(1)} %bitcast.62), channel_id=1, source_target_pairs={{0,8},{2,10},{4,12},{6,14},{8,0},{10,2},{12,4},{14,6},{16,24},{18,... | collective-permute-start | bytes 589832 | tf_op jit(solution)/shard_map/ppermute | solution.py:72
  19.1 16.7 %copy-start.17 = (s32[2]{0:T(128)S(1)}, s32[2]{0:T(128)}, u32[]{:S(2)}) copy-start(s32[2]{0:T(128)} %param.18) | copy-start | bytes 28
  32.2 13.1 %collective-permute-start.5 = (bf16[512,384]{1,0:T(8,128)(2,1)S(1)}, bf16[512,384]{1,0:T(8,128)(2,1)S(1)}, u32[]{:S(2)}, u32[]{:S(2)}) collective-permute-start(bf16[512,384]{1,0:T(8,128)(2,1)S(1)} %get-tuple-element.89.refs_1_.refs_7_), channel_id=1, source_target_pairs={{0,6},{2,4},{4,2},{6,0},{8,14},{10,12},{12,10},{14,8},{16,22},{18,... | collective-permute-start | bytes 1179656 | tf_op jit(solution)/shard_map/ppermute | solution.py:72
  34.7 17.1 %collective-permute-start.4 = (bf16[512,384]{1,0:T(8,128)(2,1)S(1)}, bf16[512,384]{1,0:T(8,128)(2,1)S(1)}, u32[]{:S(2)}, u32[]{:S(2)}) collective-permute-start(bf16[512,384]{1,0:T(8,128)(2,1)S(1)} %get-tuple-element.89.refs_1_.refs_7_), channel_id=1, source_target_pairs={{0,4},{2,6},{4,0},{6,2},{8,12},{10,14},{12,8},{14,10},{16,20},{18,... | collective-permute-start | bytes 1179656 | tf_op jit(solution)/shard_map/ppermute | solution.py:72
  35.2 16.6 %collective-permute-start.3 = (bf16[512,384]{1,0:T(8,128)(2,1)S(1)}, bf16[512,384]{1,0:T(8,128)(2,1)S(1)}, u32[]{:S(2)}, u32[]{:S(2)}) collective-permute-start(bf16[512,384]{1,0:T(8,128)(2,1)S(1)} %get-tuple-element.89.refs_1_.refs_7_), channel_id=1, source_target_pairs={{0,2},{2,0},{4,6},{6,4},{8,10},{10,8},{12,14},{14,12},{16,18},{18,... | collective-permute-start | bytes 1179656 | tf_op jit(solution)/shard_map/ppermute | solution.py:72
  58.9 5.3 %collective-permute-start.6 = (bf16[128,192]{1,0:T(8,128)(2,1)}, bf16[128,192]{1,0:T(8,128)(2,1)}, u32[]{:S(2)}, u32[]{:S(2)}) collective-permute-start(bf16[128,192]{1,0:T(8,128)(2,1)} %get-tuple-element.91.rest_11_), channel_id=1, source_target_pairs={{0,8},{2,10},{4,12},{6,14},{8,0},{10,2},{12,4},{14,6},{16,24},{18,... | collective-permute-start | bytes 147464 | tf_op jit(solution)/shard_map/ppermute | solution.py:72
  58.9 8.2 %collective-permute-start.7 = (bf16[128,192]{1,0:T(8,128)(2,1)}, bf16[128,192]{1,0:T(8,128)(2,1)}, u32[]{:S(2)}, u32[]{:S(2)}) collective-permute-start(bf16[128,192]{1,0:T(8,128)(2,1)} %get-tuple-element.92.rest_12_), channel_id=1, source_target_pairs={{0,16},{2,18},{4,20},{6,22},{8,24},{10,26},{12,28},{14,30},{16,0},... | collective-permute-start | bytes 147464 | tf_op jit(solution)/shard_map/ppermute | solution.py:72
  61.8 6.5 %collective-permute-start.8 = (bf16[128,192]{1,0:T(8,128)(2,1)}, bf16[128,192]{1,0:T(8,128)(2,1)}, u32[]{:S(2)}, u32[]{:S(2)}) collective-permute-start(bf16[128,192]{1,0:T(8,128)(2,1)} %get-tuple-element.93.rest_13_), channel_id=1, source_target_pairs={{0,24},{2,26},{4,28},{6,30},{8,16},{10,18},{12,20},{14,22},{16,8},... | collective-permute-start | bytes 147464 | tf_op jit(solution)/shard_map/ppermute | solution.py:72
  69.2 24.4 %copy-start.4 = (f32[512,192]{1,0:T(8,128)S(1)}, f32[512,192]{1,0:T(8,128)}, u32[]{:S(2)}) copy-start(f32[512,192]{1,0:T(8,128)} %copy-done.3) | copy-start | bytes 1179652
  69.2 24.4 %copy-start.6 = (f32[512,128]{1,0:T(8,128)S(1)}, f32[512,128]{1,0:T(8,128)}, u32[]{:S(2)}) copy-start(f32[512,128]{1,0:T(8,128)} %copy-done.5) | copy-start | bytes 786436
  79.7 22.1 %collective-permute-start.16 = (bf16[144,1536]{1,0:T(8,128)(2,1)S(1)}, bf16[144,1536]{1,0:T(8,128)(2,1)S(1)}, u32[]{:S(2)}, u32[]{:S(2)}) collective-permute-start(bf16[144,1536]{1,0:T(8,128)(2,1)S(1)} %get-tuple-element.110), channel_id=1, source_target_pairs={{0,2},{2,0},{4,6},{6,4},{8,10},{10,8},{12,14},{14,12},{16,18},{18,... | collective-permute-start | bytes 1327112 | tf_op jit(solution)/shard_map/ppermute | solution.py:72
  81.3 20.5 %collective-permute-start.17 = (bf16[144,1536]{1,0:T(8,128)(2,1)S(1)}, bf16[144,1536]{1,0:T(8,128)(2,1)S(1)}, u32[]{:S(2)}, u32[]{:S(2)}) collective-permute-start(bf16[144,1536]{1,0:T(8,128)(2,1)S(1)} %get-tuple-element.111), channel_id=1, source_target_pairs={{0,4},{2,6},{4,0},{6,2},{8,12},{10,14},{12,8},{14,10},{16,20},{18,... | collective-permute-start | bytes 1327112 | tf_op jit(solution)/shard_map/ppermute | solution.py:72
  81.9 19.9 %collective-permute-start.18 = (bf16[144,1536]{1,0:T(8,128)(2,1)S(1)}, bf16[144,1536]{1,0:T(8,128)(2,1)S(1)}, u32[]{:S(2)}, u32[]{:S(2)}) collective-permute-start(bf16[144,1536]{1,0:T(8,128)(2,1)S(1)} %get-tuple-element.112), channel_id=1, source_target_pairs={{0,6},{2,4},{4,2},{6,0},{8,14},{10,12},{12,10},{14,8},{16,22},{18,... | collective-permute-start | bytes 1327112 | tf_op jit(solution)/shard_map/ppermute | solution.py:72
  83.3 4.3 %collective-permute-start.9 = (bf16[128,192]{1,0:T(8,128)(2,1)S(1)}, bf16[128,192]{1,0:T(8,128)(2,1)S(1)}, u32[]{:S(2)}, u32[]{:S(2)}) collective-permute-start(bf16[128,192]{1,0:T(8,128)(2,1)S(1)} %get-tuple-element.99), channel_id=1, source_target_pairs={{0,8},{2,10},{4,12},{6,14},{8,0},{10,2},{12,4},{14,6},{16,24},{18,... | collective-permute-start | bytes 147464 | tf_op jit(solution)/shard_map/ppermute | solution.py:72
  84.2 6.4 %collective-permute-start.10 = (bf16[128,192]{1,0:T(8,128)(2,1)S(1)}, bf16[128,192]{1,0:T(8,128)(2,1)S(1)}, u32[]{:S(2)}, u32[]{:S(2)}) collective-permute-start(bf16[128,192]{1,0:T(8,128)(2,1)S(1)} %get-tuple-element.100), channel_id=1, source_target_pairs={{0,16},{2,18},{4,20},{6,22},{8,24},{10,26},{12,28},{14,30},{16,0},... | collective-permute-start | bytes 147464 | tf_op jit(solution)/shard_map/ppermute | solution.py:72
  87.5 6.1 %collective-permute-start.11 = (bf16[128,192]{1,0:T(8,128)(2,1)S(1)}, bf16[128,192]{1,0:T(8,128)(2,1)S(1)}, u32[]{:S(2)}, u32[]{:S(2)}) collective-permute-start(bf16[128,192]{1,0:T(8,128)(2,1)S(1)} %get-tuple-element.101), channel_id=1, source_target_pairs={{0,24},{2,26},{4,28},{6,30},{8,16},{10,18},{12,20},{14,22},{16,8},... | collective-permute-start | bytes 147464 | tf_op jit(solution)/shard_map/ppermute | solution.py:72
  101.8 38.6 %copy-start.2 = (bf16[128,768]{1,0:T(8,128)(2,1)S(1)}, bf16[128,768]{1,0:T(8,128)(2,1)}, u32[]{:S(2)}) copy-start(bf16[128,768]{1,0:T(8,128)(2,1)} %copy-done.1) | copy-start | bytes 589828
  103.4 2.3 collective-permute-start.19
  103.5 12.0 %collective-permute-start.12 = (bf16[2,192,512]{2,1,0:T(8,128)(2,1)S(1)}, bf16[2,192,512]{2,1,0:T(8,128)(2,1)S(1)}, u32[]{:S(2)}, u32[]{:S(2)}) collective-permute-start(bf16[2,192,512]{2,1,0:T(8,128)(2,1)S(1)} %get-tuple-element.104), channel_id=1, source_target_pairs={{0,2},{2,0},{4,6},{6,4},{8,10},{10,8},{12,14},{14,12},{16,18},{18,... | collective-permute-start | bytes 1179656 | tf_op jit(solution)/shard_map/ppermute | solution.py:72
  105.0 12.0 %collective-permute-start.14 = (bf16[2,192,512]{2,1,0:T(8,128)(2,1)S(1)}, bf16[2,192,512]{2,1,0:T(8,128)(2,1)S(1)}, u32[]{:S(2)}, u32[]{:S(2)}) collective-permute-start(bf16[2,192,512]{2,1,0:T(8,128)(2,1)S(1)} %get-tuple-element.107), channel_id=1, source_target_pairs={{0,4},{2,6},{4,0},{6,2},{8,12},{10,14},{12,8},{14,10},{16,20},{18,... | collective-permute-start | bytes 1179656 | tf_op jit(solution)/shard_map/ppermute | solution.py:72
  106.3 12.4 %collective-permute-start.20 = (bf16[2,104,768]{2,1,0:T(8,128)(2,1)S(1)}, bf16[2,104,768]{2,1,0:T(8,128)(2,1)S(1)}, u32[]{:S(2)}, u32[]{:S(2)}) collective-permute-start(bf16[2,104,768]{2,1,0:T(8,128)(2,1)S(1)} %get-tuple-element.120), channel_id=1, source_target_pairs={{0,8},{2,10},{4,12},{6,14},{8,0},{10,2},{12,4},{14,6},{16,24},{18,... | collective-permute-start | bytes 958472 | tf_op jit(solution)/shard_map/ppermute | solution.py:72
  106.7 17.1 %collective-permute-start.22 = (bf16[128,1536]{1,0:T(8,128)(2,1)S(1)}, bf16[128,1536]{1,0:T(8,128)(2,1)S(1)}, u32[]{:S(2)}, u32[]{:S(2)}) collective-permute-start(bf16[128,1536]{1,0:T(8,128)(2,1)S(1)} %get-tuple-element.126), channel_id=1, source_target_pairs={{0,2},{2,0},{4,6},{6,4},{8,10},{10,8},{12,14},{14,12},{16,18},{18,... | collective-permute-start | bytes 1179656 | tf_op jit(solution)/shard_map/ppermute | solution.py:72
  107.9 25.4 %collective-permute-start.23 = (bf16[128,1536]{1,0:T(8,128)(2,1)S(1)}, bf16[128,1536]{1,0:T(8,128)(2,1)S(1)}, u32[]{:S(2)}, u32[]{:S(2)}) collective-permute-start(bf16[128,1536]{1,0:T(8,128)(2,1)S(1)} %get-tuple-element.127), channel_id=1, source_target_pairs={{0,4},{2,6},{4,0},{6,2},{8,12},{10,14},{12,8},{14,10},{16,20},{18,... | collective-permute-start | bytes 1179656 | tf_op jit(solution)/shard_map/ppermute | solution.py:72
  115.4 19.4 %collective-permute-start.24 = (bf16[128,1536]{1,0:T(8,128)(2,1)S(1)}, bf16[128,1536]{1,0:T(8,128)(2,1)S(1)}, u32[]{:S(2)}, u32[]{:S(2)}) collective-permute-start(bf16[128,1536]{1,0:T(8,128)(2,1)S(1)} %get-tuple-element.128), channel_id=1, source_target_pairs={{0,6},{2,4},{4,2},{6,0},{8,14},{10,12},{12,10},{14,8},{16,22},{18,... | collective-permute-start | bytes 1179656 | tf_op jit(solution)/shard_map/ppermute | solution.py:72
  117.0 16.9 %collective-permute-start.26 = (bf16[128,768]{1,0:T(8,128)(2,1)S(1)}, bf16[128,768]{1,0:T(8,128)(2,1)S(1)}, u32[]{:S(2)}, u32[]{:S(2)}) collective-permute-start(bf16[128,768]{1,0:T(8,128)(2,1)S(1)} %get-tuple-element.136.rest_14_), channel_id=1, source_target_pairs={{0,24},{2,26},{4,28},{6,30},{8,16},{10,18},{12,20},{14,22},{16,8},... | collective-permute-start | bytes 589832 | tf_op jit(solution)/shard_map/ppermute | solution.py:72
  118.8 15.9 %collective-permute-start.21 = (bf16[104,768]{1,0:T(8,128)(2,1)S(1)}, bf16[104,768]{1,0:T(8,128)(2,1)S(1)}, u32[]{:S(2)}, u32[]{:S(2)}) collective-permute-start(bf16[104,768]{1,0:T(8,128)(2,1)S(1)} %fusion.8), channel_id=1, source_target_pairs={{0,24},{2,26},{4,28},{6,30},{8,16},{10,18},{12,20},{14,22},{16,8},... | collective-permute-start | bytes 479240 | tf_op jit(solution)/shard_map/ppermute | solution.py:72
  123.9 15.7 %collective-permute-start.25 = (bf16[128,768]{1,0:T(8,128)(2,1)S(1)}, bf16[128,768]{1,0:T(8,128)(2,1)S(1)}, u32[]{:S(2)}, u32[]{:S(2)}) collective-permute-start(bf16[128,768]{1,0:T(8,128)(2,1)S(1)} %get-tuple-element.136.rest_14_), channel_id=1, source_target_pairs={{0,8},{2,10},{4,12},{6,14},{8,0},{10,2},{12,4},{14,6},{16,24},{18,... | collective-permute-start | bytes 589832 | tf_op jit(solution)/shard_map/ppermute | solution.py:72
  133.3 5.7 %collective-permute-start.13 = (bf16[192,512]{1,0:T(8,128)(2,1)S(1)}, bf16[192,512]{1,0:T(8,128)(2,1)S(1)}, u32[]{:S(2)}, u32[]{:S(2)}) collective-permute-start(bf16[192,512]{1,0:T(8,128)(2,1)S(1)} %fusion.1), channel_id=1, source_target_pairs={{0,4},{2,6},{4,0},{6,2},{8,12},{10,14},{12,8},{14,10},{16,20},{18,... | collective-permute-start | bytes 589832 | tf_op jit(solution)/shard_map/ppermute | solution.py:72
  133.9 5.7 %collective-permute-start.15 = (bf16[192,512]{1,0:T(8,128)(2,1)S(1)}, bf16[192,512]{1,0:T(8,128)(2,1)S(1)}, u32[]{:S(2)}, u32[]{:S(2)}) collective-permute-start(bf16[192,512]{1,0:T(8,128)(2,1)S(1)} %fusion), channel_id=1, source_target_pairs={{0,2},{2,0},{4,6},{6,4},{8,10},{10,8},{12,14},{14,12},{16,18},{18,... | collective-permute-start | bytes 589832 | tf_op jit(solution)/shard_map/ppermute | solution.py:72
  134.8 5.7 %collective-permute-start.27 = (bf16[128,768]{1,0:T(8,128)(2,1)S(1)}, bf16[128,768]{1,0:T(8,128)(2,1)S(1)}, u32[]{:S(2)}, u32[]{:S(2)}) collective-permute-start(bf16[128,768]{1,0:T(8,128)(2,1)S(1)} %collective-permute-done.26.rest_17_), channel_id=1, source_target_pairs={{0,8},{2,10},{4,12},{6,14},{8,0},{10,2},{12,4},{14,6},{16,24},{18,... | collective-permute-start | bytes 589832 | tf_op jit(solution)/shard_map/ppermute | solution.py:72
  143.9 4.8 %collective-permute-start.30 = (bf16[4,144,576]{2,1,0:T(8,128)(2,1)S(1)}, bf16[4,144,576]{2,1,0:T(8,128)(2,1)S(1)}, u32[]{:S(2)}, u32[]{:S(2)}) collective-permute-start(bf16[4,144,576]{2,1,0:T(8,128)(2,1)S(1)} %get-tuple-element.140), channel_id=1, source_target_pairs={{0,1},{1,0},{2,3},{3,2},{4,5},{5,4},{6,7},{7,6},{8,9},{9,8},{10,11... | collective-permute-start | bytes 1990664 | tf_op jit(solution)/shard_map/ppermute | solution.py:602
  144.0 8.2 %collective-permute-start.35 = (bf16[96,768]{1,0:T(8,128)(2,1)S(1)}, bf16[96,768]{1,0:T(8,128)(2,1)S(1)}, u32[]{:S(2)}, u32[]{:S(2)}) collective-permute-start(bf16[96,768]{1,0:T(8,128)(2,1)S(1)} %slice.247), channel_id=1, source_target_pairs={{0,24},{2,26},{4,28},{6,30},{8,16},{10,18},{12,20},{14,22},{16,8},... | collective-permute-start | bytes 442376 | tf_op jit(solution)/shard_map/ppermute | solution.py:72
  148.4 12.2 %collective-permute-start.46 = (bf16[4,96,768]{2,1,0:T(8,128)(2,1)S(1)}, bf16[4,96,768]{2,1,0:T(8,128)(2,1)S(1)}, u32[]{:S(2)}, u32[]{:S(2)}) collective-permute-start(bf16[4,96,768]{2,1,0:T(8,128)(2,1)S(1)} %get-tuple-element.155), channel_id=1, source_target_pairs={{0,1},{1,0},{2,3},{3,2},{4,5},{5,4},{6,7},{7,6},{8,9},{9,8},{10,11... | collective-permute-start | bytes 1769480 | tf_op jit(solution)/shard_map/ppermute | solution.py:602
  149.6 10.9 %collective-permute-start.31 = (bf16[2,144,576]{2,1,0:T(8,128)(2,1)S(1)}, bf16[2,144,576]{2,1,0:T(8,128)(2,1)S(1)}, u32[]{:S(2)}, u32[]{:S(2)}) collective-permute-start(bf16[2,144,576]{2,1,0:T(8,128)(2,1)S(1)} %get-tuple-element.142), channel_id=1, source_target_pairs={{0,2},{2,0},{4,6},{6,4},{8,10},{10,8},{12,14},{14,12},{16,18},{18,... | collective-permute-start | bytes 995336 | tf_op jit(solution)/shard_map/ppermute | solution.py:72
  152.2 9.1 %collective-permute-start.36 = (bf16[2,96,768]{2,1,0:T(8,128)(2,1)S(1)}, bf16[2,96,768]{2,1,0:T(8,128)(2,1)S(1)}, u32[]{:S(2)}, u32[]{:S(2)}) collective-permute-start(bf16[2,96,768]{2,1,0:T(8,128)(2,1)S(1)} %pad_maximum_fusion.5), channel_id=1, source_target_pairs={{0,8},{2,10},{4,12},{6,14},{8,0},{10,2},{12,4},{14,6},{16,24},{18,... | collective-permute-start | bytes 884744 | tf_op jit(solution)/shard_map/ppermute | solution.py:72
  160.5 7.6 %collective-permute-start.32 = (bf16[144,576]{1,0:T(8,128)(2,1)S(1)}, bf16[144,576]{1,0:T(8,128)(2,1)S(1)}, u32[]{:S(2)}, u32[]{:S(2)}) collective-permute-start(bf16[144,576]{1,0:T(8,128)(2,1)S(1)} %fusion.7), channel_id=1, source_target_pairs={{0,4},{2,6},{4,0},{6,2},{8,12},{10,14},{12,8},{14,10},{16,20},{18,... | collective-permute-start | bytes 497672 | tf_op jit(solution)/shard_map/ppermute | solution.py:72
  161.3 8.5 %collective-permute-start.47 = (bf16[2,96,768]{2,1,0:T(8,128)(2,1)S(1)}, bf16[2,96,768]{2,1,0:T(8,128)(2,1)S(1)}, u32[]{:S(2)}, u32[]{:S(2)}) collective-permute-start(bf16[2,96,768]{2,1,0:T(8,128)(2,1)S(1)} %get-tuple-element.157), channel_id=1, source_target_pairs={{0,8},{2,10},{4,12},{6,14},{8,0},{10,2},{12,4},{14,6},{16,24},{18,... | collective-permute-start | bytes 884744 | tf_op jit(solution)/shard_map/ppermute | solution.py:72
  161.5 17.8 %collective-permute-start.38 = (bf16[4,96,768]{2,1,0:T(8,128)(2,1)S(1)}, bf16[4,96,768]{2,1,0:T(8,128)(2,1)S(1)}, u32[]{:S(2)}, u32[]{:S(2)}) collective-permute-start(bf16[4,96,768]{2,1,0:T(8,128)(2,1)S(1)} %pad_maximum_fusion.1.refs_0_), channel_id=1, source_target_pairs={{0,4},{2,6},{4,0},{6,2},{8,12},{10,14},{12,8},{14,10},{16,20},{18,... | collective-permute-start | bytes 1769480 | tf_op jit(solution)/shard_map/ppermute | solution.py:72
  163.5 18.3 %collective-permute-start.37 = (bf16[4,96,768]{2,1,0:T(8,128)(2,1)S(1)}, bf16[4,96,768]{2,1,0:T(8,128)(2,1)S(1)}, u32[]{:S(2)}, u32[]{:S(2)}) collective-permute-start(bf16[4,96,768]{2,1,0:T(8,128)(2,1)S(1)} %pad_maximum_fusion.1.refs_0_), channel_id=1, source_target_pairs={{0,2},{2,0},{4,6},{6,4},{8,10},{10,8},{12,14},{14,12},{16,18},{18,... | collective-permute-start | bytes 1769480 | tf_op jit(solution)/shard_map/ppermute | solution.py:72
  168.2 9.4 %collective-permute-start.33 = (bf16[144,576]{1,0:T(8,128)(2,1)S(1)}, bf16[144,576]{1,0:T(8,128)(2,1)S(1)}, u32[]{:S(2)}, u32[]{:S(2)}) collective-permute-start(bf16[144,576]{1,0:T(8,128)(2,1)S(1)} %fusion.4), channel_id=1, source_target_pairs={{0,24},{2,26},{4,28},{6,30},{8,16},{10,18},{12,20},{14,22},{16,8},... | collective-permute-start | bytes 497672 | tf_op jit(solution)/shard_map/ppermute | solution.py:72
  169.8 12.2 %collective-permute-start.48 = (bf16[96,768]{1,0:T(8,128)(2,1)S(1)}, bf16[96,768]{1,0:T(8,128)(2,1)S(1)}, u32[]{:S(2)}, u32[]{:S(2)}) collective-permute-start(bf16[96,768]{1,0:T(8,128)(2,1)S(1)} %fusion.9), channel_id=1, source_target_pairs={{0,24},{2,26},{4,28},{6,30},{8,16},{10,18},{12,20},{14,22},{16,8},... | collective-permute-start | bytes 442376 | tf_op jit(solution)/shard_map/ppermute | solution.py:72
  177.7 9.9 %collective-permute-start.34 = (bf16[2,144,576]{2,1,0:T(8,128)(2,1)S(1)}, bf16[2,144,576]{2,1,0:T(8,128)(2,1)S(1)}, u32[]{:S(2)}, u32[]{:S(2)}) collective-permute-start(bf16[2,144,576]{2,1,0:T(8,128)(2,1)S(1)} %pad_maximum_fusion.4), channel_id=1, source_target_pairs={{0,8},{2,10},{4,12},{6,14},{8,0},{10,2},{12,4},{14,6},{16,24},{18,... | collective-permute-start | bytes 995336 | tf_op jit(solution)/shard_map/ppermute | solution.py:72
  179.3 8.4 %collective-permute-start.40 = (bf16[2,96,768]{2,1,0:T(8,128)(2,1)S(1)}, bf16[2,96,768]{2,1,0:T(8,128)(2,1)S(1)}, u32[]{:S(2)}, u32[]{:S(2)}) collective-permute-start(bf16[2,96,768]{2,1,0:T(8,128)(2,1)S(1)} %slice.192), channel_id=1, source_target_pairs={{0,2},{2,0},{4,6},{6,4},{8,10},{10,8},{12,14},{14,12},{16,18},{18,... | collective-permute-start | bytes 884744 | tf_op jit(solution)/shard_map/ppermute | solution.py:72
  181.9 8.4 %collective-permute-start.39 = (bf16[2,96,768]{2,1,0:T(8,128)(2,1)S(1)}, bf16[2,96,768]{2,1,0:T(8,128)(2,1)S(1)}, u32[]{:S(2)}, u32[]{:S(2)}) collective-permute-start(bf16[2,96,768]{2,1,0:T(8,128)(2,1)S(1)} %slice.191), channel_id=1, source_target_pairs={{0,4},{2,6},{4,0},{6,2},{8,12},{10,14},{12,8},{14,10},{16,20},{18,... | collective-permute-start | bytes 884744 | tf_op jit(solution)/shard_map/ppermute | solution.py:72
  182.1 8.3 %collective-permute-start.49 = (bf16[96,768]{1,0:T(8,128)(2,1)S(1)}, bf16[96,768]{1,0:T(8,128)(2,1)S(1)}, u32[]{:S(2)}, u32[]{:S(2)}) collective-permute-start(bf16[96,768]{1,0:T(8,128)(2,1)S(1)} %fusion.5), channel_id=1, source_target_pairs={{0,24},{2,26},{4,28},{6,30},{8,16},{10,18},{12,20},{14,22},{16,8},... | collective-permute-start | bytes 442376 | tf_op jit(solution)/shard_map/ppermute | solution.py:72
  190.3 19.4 %collective-permute-start.42 = (bf16[4,144,576]{2,1,0:T(8,128)(2,1)S(1)}, bf16[4,144,576]{2,1,0:T(8,128)(2,1)S(1)}, u32[]{:S(2)}, u32[]{:S(2)}) collective-permute-start(bf16[4,144,576]{2,1,0:T(8,128)(2,1)S(1)} %pad_maximum_fusion.refs_0_), channel_id=1, source_target_pairs={{0,4},{2,6},{4,0},{6,2},{8,12},{10,14},{12,8},{14,10},{16,20},{18,... | collective-permute-start | bytes 1990664 | tf_op jit(solution)/shard_map/ppermute | solution.py:72
  190.3 19.5 %collective-permute-start.41 = (bf16[4,144,576]{2,1,0:T(8,128)(2,1)S(1)}, bf16[4,144,576]{2,1,0:T(8,128)(2,1)S(1)}, u32[]{:S(2)}, u32[]{:S(2)}) collective-permute-start(bf16[4,144,576]{2,1,0:T(8,128)(2,1)S(1)} %pad_maximum_fusion.refs_0_), channel_id=1, source_target_pairs={{0,2},{2,0},{4,6},{6,4},{8,10},{10,8},{12,14},{14,12},{16,18},{18,... | collective-permute-start | bytes 1990664 | tf_op jit(solution)/shard_map/ppermute | solution.py:72
  190.4 9.4 %collective-permute-start.50 = (bf16[2,96,768]{2,1,0:T(8,128)(2,1)S(1)}, bf16[2,96,768]{2,1,0:T(8,128)(2,1)S(1)}, u32[]{:S(2)}, u32[]{:S(2)}) collective-permute-start(bf16[2,96,768]{2,1,0:T(8,128)(2,1)S(1)} %pad_maximum_fusion.6), channel_id=1, source_target_pairs={{0,8},{2,10},{4,12},{6,14},{8,0},{10,2},{12,4},{14,6},{16,24},{18,... | collective-permute-start | bytes 884744 | tf_op jit(solution)/shard_map/ppermute | solution.py:72
  190.5 21.4 %collective-permute-start.28 = (bf16[2,128,768]{2,1,0:T(8,128)(2,1)S(1)}, bf16[2,128,768]{2,1,0:T(8,128)(2,1)S(1)}, u32[]{:S(2)}, u32[]{:S(2)}) collective-permute-start(bf16[2,128,768]{2,1,0:T(8,128)(2,1)S(1)} %get-tuple-element.138), channel_id=1, source_target_pairs={{0,8},{2,10},{4,12},{6,14},{8,0},{10,2},{12,4},{14,6},{16,24},{18,... | collective-permute-start | bytes 1179656 | tf_op jit(solution)/shard_map/ppermute | solution.py:72
  199.8 22.6 %collective-permute-start.52 = (bf16[4,96,768]{2,1,0:T(8,128)(2,1)S(1)}, bf16[4,96,768]{2,1,0:T(8,128)(2,1)S(1)}, u32[]{:S(2)}, u32[]{:S(2)}) collective-permute-start(bf16[4,96,768]{2,1,0:T(8,128)(2,1)S(1)} %pad_maximum_fusion.2.refs_0_), channel_id=1, source_target_pairs={{0,4},{2,6},{4,0},{6,2},{8,12},{10,14},{12,8},{14,10},{16,20},{18,... | collective-permute-start | bytes 1769480 | tf_op jit(solution)/shard_map/ppermute | solution.py:72
  202.4 20.0 %collective-permute-start.51 = (bf16[4,96,768]{2,1,0:T(8,128)(2,1)S(1)}, bf16[4,96,768]{2,1,0:T(8,128)(2,1)S(1)}, u32[]{:S(2)}, u32[]{:S(2)}) collective-permute-start(bf16[4,96,768]{2,1,0:T(8,128)(2,1)S(1)} %pad_maximum_fusion.2.refs_0_), channel_id=1, source_target_pairs={{0,2},{2,0},{4,6},{6,4},{8,10},{10,8},{12,14},{14,12},{16,18},{18,... | collective-permute-start | bytes 1769480 | tf_op jit(solution)/shard_map/ppermute | solution.py:72
  209.8 18.4 %collective-permute-start.43 = (bf16[2,144,576]{2,1,0:T(8,128)(2,1)S(1)}, bf16[2,144,576]{2,1,0:T(8,128)(2,1)S(1)}, u32[]{:S(2)}, u32[]{:S(2)}) collective-permute-start(bf16[2,144,576]{2,1,0:T(8,128)(2,1)S(1)} %slice.193), channel_id=1, source_target_pairs={{0,4},{2,6},{4,0},{6,2},{8,12},{10,14},{12,8},{14,10},{16,20},{18,... | collective-permute-start | bytes 995336 | tf_op jit(solution)/shard_map/ppermute | solution.py:72
  211.4 16.8 %collective-permute-start.44 = (bf16[2,144,576]{2,1,0:T(8,128)(2,1)S(1)}, bf16[2,144,576]{2,1,0:T(8,128)(2,1)S(1)}, u32[]{:S(2)}, u32[]{:S(2)}) collective-permute-start(bf16[2,144,576]{2,1,0:T(8,128)(2,1)S(1)} %slice.194), channel_id=1, source_target_pairs={{0,2},{2,0},{4,6},{6,4},{8,10},{10,8},{12,14},{14,12},{16,18},{18,... | collective-permute-start | bytes 995336 | tf_op jit(solution)/shard_map/ppermute | solution.py:72
  211.9 21.3 %collective-permute-start.29 = (bf16[128,768]{1,0:T(8,128)(2,1)S(1)}, bf16[128,768]{1,0:T(8,128)(2,1)S(1)}, u32[]{:S(2)}, u32[]{:S(2)}) collective-permute-start(bf16[128,768]{1,0:T(8,128)(2,1)S(1)} %fusion.6), channel_id=1, source_target_pairs={{0,24},{2,26},{4,28},{6,30},{8,16},{10,18},{12,20},{14,22},{16,8},... | collective-permute-start | bytes 589832 | tf_op jit(solution)/shard_map/ppermute | solution.py:72
  222.4 11.6 %collective-permute-start.53 = (bf16[2,96,768]{2,1,0:T(8,128)(2,1)S(1)}, bf16[2,96,768]{2,1,0:T(8,128)(2,1)S(1)}, u32[]{:S(2)}, u32[]{:S(2)}) collective-permute-start(bf16[2,96,768]{2,1,0:T(8,128)(2,1)S(1)} %slice.200), channel_id=1, source_target_pairs={{0,4},{2,6},{4,0},{6,2},{8,12},{10,14},{12,8},{14,10},{16,20},{18,... | collective-permute-start | bytes 884744 | tf_op jit(solution)/shard_map/ppermute | solution.py:72
  224.0 10.1 %collective-permute-start.54 = (bf16[2,96,768]{2,1,0:T(8,128)(2,1)S(1)}, bf16[2,96,768]{2,1,0:T(8,128)(2,1)S(1)}, u32[]{:S(2)}, u32[]{:S(2)}) collective-permute-start(bf16[2,96,768]{2,1,0:T(8,128)(2,1)S(1)} %slice.201), channel_id=1, source_target_pairs={{0,2},{2,0},{4,6},{6,4},{8,10},{10,8},{12,14},{14,12},{16,18},{18,... | collective-permute-start | bytes 884744 | tf_op jit(solution)/shard_map/ppermute | solution.py:72
  233.2 4.5 %collective-permute-start.45 = (bf16[2,4,24,768]{3,2,1,0:T(8,128)(2,1)S(1)}, bf16[2,4,24,768]{3,2,1,0:T(8,128)(2,1)S(1)}, u32[]{:S(2)}, u32[]{:S(2)}) collective-permute-start(bf16[2,4,24,768]{3,2,1,0:T(8,128)(2,1)S(1)} %get-tuple-element.149), channel_id=1, source_target_pairs={{0,1},{1,0},{2,3},{3,2},{4,5},{5,4},{6,7},{7,6},{8,9},{9,8},{10,11... | collective-permute-start | bytes 884744 | tf_op jit(solution)/shard_map/ppermute | solution.py:602
  (12 other events, 56.4 us)
Sparse Core Ops, SparseCore 0:
  9.6 12.2 all-gather.5
  23.4 15.4 all-gather.7
  40.4 15.5 all-gather.9

commit v10 on v9

--- a/solution.py
+++ b/solution.py
@@ -593,7 +593,7 @@
     contexts = (context_lows[0], *(places.column_swap(context_lows[i], i) for i in turns))
 
     (layer_out, one_grad, branch_low), context_grads, up_parts, down_parts = dense(
-        spot, contexts, inputs, cotangent[0], whole, up_offset, out_matrix, up_matrix, down_matrix
+        spot, contexts, inputs, in_hbm(cotangent[0]), whole, up_offset, out_matrix, up_matrix, down_matrix
     )
     def after(value, *others):
         return lax.optimization_barrier((value, *others))[0]

time: 246 us -> 245 us (level)
  no operation moved by 1% of the time
where the time goes in v10:
time: 245 us
  waiting for transfers between devices  111 us (45%)
  starting transfers between devices  59 us (24%)
  Pallas kernels  46.9 us (19%)
  between operations  14.4 us (6%)
  local copies, waits for them, and re-layouts  5.61 us (2%)
  blocking collectives  4.62 us (2%)
  other arithmetic  3.27 us (1%)
    ppermute x51, waiting for transfers between devices, swap(): return lax.ppermute(block, 'seq', [(i, i ^ bits) for i in range(self.size)])  109 us
    ppermute x51, starting transfers between devices, swap(): return lax.ppermute(block, 'seq', [(i, i ^ bits) for i in range(self.size)])  58.5 us
    pallas_call x14, Pallas kernels, kernel_call(): pl.pallas_call(run if after else kernel, out_shape=outs, in_specs=spaces...  46.9 us
  transfers between devices with their start and end apart: 58, of which 28 were waited for; matrix products, arithmetic and copies ran while one was open for 3% of the time, Pallas kernels for 12%

profile of v10, /device:TPU:0, one launch (start us, length us, event | category | flops | bytes accessed | tf_op | source)
XLA Modules:
  0.0 245.1 jit_solution(14283683569294633643)
XLA Ops:
  9.5 5.1 %collective-permute-start.2 = (bf16[128,768]{1,0:T(8,128)(2,1)S(1)}, bf16[128,768]{1,0:T(8,128)(2,1)S(1)}, u32[]{:S(2)}, u32[]{:S(2)}) collective-permute-start(bf16[128,768]{1,0:T(8,128)(2,1)S(1)} %bitcast.60), channel_id=1, source_target_pairs={{0,24},{2,26},{4,28},{6,30},{8,16},{10,18},{12,20},{14,22},{16,8},... | collective-permute-start | bytes 589832 | tf_op jit(solution)/shard_map/ppermute | solution.py:72
  15.5 1.8 all-gather.1
  17.6 1.5 constant_dynamic-slice_fusion.2
  19.3 2.8 %all_gather.18.weight.rest_18_ = bf16[768,576]{1,0:T(8,128)(2,1)S(1)} all-gather(bf16[384,576]{1,0:T(8,128)(2,1)S(1)} %pad_maximum_fusion.3), channel_id=1, replica_groups=mesh['seq'=16,'shard'=2] {'shard'}, dimensions={0}, use_global_device_ids=true | all-gather | bytes 1327104 | tf_op jit(solution)/shard_map/all_gather | solution.py:550
  22.1 9.2 %collective-permute-done.1.x2.rest_8_ = bf16[128,768]{1,0:T(8,128)(2,1)S(1)} collective-permute-done((bf16[128,768]{1,0:T(8,128)(2,1)S(1)}, bf16[128,768]{1,0:T(8,128)(2,1)S(1)}, u32[]{:S(2)}, u32[]{:S(2)}) %collective-permute-start.1) | collective-permute-done | bytes 196640 | tf_op jit(solution)/shard_map/ppermute | solution.py:72
  32.2 2.5 %collective-permute-start.5 = (bf16[512,384]{1,0:T(8,128)(2,1)S(1)}, bf16[512,384]{1,0:T(8,128)(2,1)S(1)}, u32[]{:S(2)}, u32[]{:S(2)}) collective-permute-start(bf16[512,384]{1,0:T(8,128)(2,1)S(1)} %get-tuple-element.89.refs_1_.refs_7_), channel_id=1, source_target_pairs={{0,6},{2,4},{4,2},{6,0},{8,14},{10,12},{12,10},{14,8},{16,22},{18,... | collective-permute-start | bytes 1179656 | tf_op jit(solution)/shard_map/ppermute | solution.py:72
  37.3 8.0 %collective-permute-done.5.refs_4_.refs_10_ = bf16[512,384]{1,0:T(8,128)(2,1)S(1)} collective-permute-done((bf16[512,384]{1,0:T(8,128)(2,1)S(1)}, bf16[512,384]{1,0:T(8,128)(2,1)S(1)}, u32[]{:S(2)}, u32[]{:S(2)}) %collective-permute-start.5) | collective-permute-done | bytes 393248 | tf_op jit(solution)/shard_map/ppermute | solution.py:72
  45.3 6.5 %collective-permute-done.4.refs_3_.refs_9_ = bf16[512,384]{1,0:T(8,128)(2,1)S(1)} collective-permute-done((bf16[512,384]{1,0:T(8,128)(2,1)S(1)}, bf16[512,384]{1,0:T(8,128)(2,1)S(1)}, u32[]{:S(2)}, u32[]{:S(2)}) %collective-permute-start.4) | collective-permute-done | bytes 393248 | tf_op jit(solution)/shard_map/ppermute | solution.py:72
  51.9 5.5 %attend.1 = (f32[512,192]{1,0:T(8,128)S(1)}, f32[512,128]{1,0:T(8,128)S(1)}, bf16[128,192]{1,0:T(8,128)(2,1)S(1)}, bf16[128,192]{1,0:T(8,128)(2,1)}, bf16[128,192]{1,0:T(8,128)(2,1)}, /*index=5*/bf16[128,192]{1,0:T(8,128)(2,1)}) custom-call(bf16[512,192]{1,0:T(8,128)(2,1)S(1)} %get-tuple-element.88.refs_0_, ...), custom_call_target="tpu_custom_call" | custom-call | bytes 31500000 | tf_op jit(solution)/shard_map/attend/pallas_call | solution.py:39
  58.9 2.9 %collective-permute-start.7 = (bf16[128,192]{1,0:T(8,128)(2,1)}, bf16[128,192]{1,0:T(8,128)(2,1)}, u32[]{:S(2)}, u32[]{:S(2)}) collective-permute-start(bf16[128,192]{1,0:T(8,128)(2,1)} %get-tuple-element.92.rest_12_), channel_id=1, source_target_pairs={{0,16},{2,18},{4,20},{6,22},{8,24},{10,26},{12,28},{14,30},{16,0},... | collective-permute-start | bytes 147464 | tf_op jit(solution)/shard_map/ppermute | solution.py:72
  61.8 1.5 collective-permute-start.8
  64.2 2.9 %collective-permute-done.7.c2 = bf16[128,192]{1,0:T(8,128)(2,1)} collective-permute-done((bf16[128,192]{1,0:T(8,128)(2,1)}, bf16[128,192]{1,0:T(8,128)(2,1)}, u32[]{:S(2)}, u32[]{:S(2)}) %collective-permute-start.7) | collective-permute-done | bytes 49184 | tf_op jit(solution)/shard_map/ppermute | solution.py:72
  67.1 1.1 collective-permute-done.8.c3
  68.3 10.7 %dense.1 = (bf16[128,768]{1,0:T(8,128)(2,1)}, f32[128,768]{1,0:T(8,128)S(1)}, bf16[128,768]{1,0:T(8,128)(2,1)S(1)}, bf16[128,192]{1,0:T(8,128)(2,1)S(1)}, bf16[1...) custom-call(s32[3]{0:T(128)S(1)} %pad_add_fusion.spot, ...), custom_call_target="tpu_custom_call" | custom-call | bytes 35000000 | tf_op jit(solution)/shard_map/dense/pallas_call | solution.py:39
  78.9 1.6 collective-permute-start.16
  81.1 1.4 collective-permute-start.18
  83.4 1.3 collective-permute-start.10
  84.7 2.1 collective-permute-done.9.refs_4_
  86.7 1.7 collective-permute-start.11
  88.5 1.3 collective-permute-done.10.refs_5_
  89.8 3.0 %collective-permute-done.11.refs_6_ = bf16[128,192]{1,0:T(8,128)(2,1)S(1)} collective-permute-done((bf16[128,192]{1,0:T(8,128)(2,1)S(1)}, bf16[128,192]{1,0:T(8,128)(2,1)S(1)}, u32[]{:S(2)}, u32[]{:S(2)}) %collective-permute-start.11) | collective-permute-done | bytes 49184 | tf_op jit(solution)/shard_map/ppermute | solution.py:72
  92.8 8.2 %attend_grad.1 = (bf16[512,192]{1,0:T(8,128)(2,1)S(1)}, bf16[192,512]{1,0:T(8,128)(2,1)S(1)}, bf16[192,512]{1,0:T(8,128)(2,1)S(1)}, bf16[192,512]{1,0:T(8,128)(2...) custom-call(bf16[512,192]{1,0:T(8,128)(2,1)S(1)} %get-tuple-element.88.ref, ...), custom_call_target="tpu_custom_call" | custom-call | bytes 38500000 | tf_op jit(solution)/shard_map/attend_grad/pallas_call | solution.py:39
  101.0 1.5 down_grad.1
  102.7 1.6 collective-permute-start.12
  106.0 1.1 collective-permute-start.22
  108.0 6.7 %collective-permute-done.12.rest_1_ = bf16[2,192,512]{2,1,0:T(8,128)(2,1)S(1)} collective-permute-done((bf16[2,192,512]{2,1,0:T(8,128)(2,1)S(1)}, bf16[2,192,512]{2,1,0:T(8,128)(2,1)S(1)}, u32[]{:S(2)}, u32[]{:S(2)}) %collective-permute-start.12) | collective-permute-done | bytes 393248 | tf_op jit(solution)/shard_map/ppermute | solution.py:72
  114.7 1.5 collective-permute-start.24
  116.2 1.7 collective-permute-start.26
  118.0 2.2 collective-permute-start.21
  120.3 2.8 %collective-permute-done.22.p1 = bf16[128,1536]{1,0:T(8,128)(2,1)S(1)} collective-permute-done((bf16[128,1536]{1,0:T(8,128)(2,1)S(1)}, bf16[128,1536]{1,0:T(8,128)(2,1)S(1)}, u32[]{:S(2)}, u32[]{:S(2)}) %collective-permute-start.22) | collective-permute-done | bytes 393248 | tf_op jit(solution)/shard_map/ppermute | solution.py:72
  123.5 9.0 %collective-permute-done.23.p2 = bf16[128,1536]{1,0:T(8,128)(2,1)S(1)} collective-permute-done((bf16[128,1536]{1,0:T(8,128)(2,1)S(1)}, bf16[128,1536]{1,0:T(8,128)(2,1)S(1)}, u32[]{:S(2)}, u32[]{:S(2)}) %collective-permute-start.23) | collective-permute-done | bytes 393248 | tf_op jit(solution)/shard_map/ppermute | solution.py:72
  133.1 0.9 collective-permute-start.15
  134.1 4.1 %collective-permute-done.13.rest_2_ = bf16[192,512]{1,0:T(8,128)(2,1)S(1)} collective-permute-done((bf16[192,512]{1,0:T(8,128)(2,1)S(1)}, bf16[192,512]{1,0:T(8,128)(2,1)S(1)}, u32[]{:S(2)}, u32[]{:S(2)}) %collective-permute-start.13) | collective-permute-done | bytes 196640 | tf_op jit(solution)/shard_map/ppermute | solution.py:72
  138.8 0.9 collective-permute-done.27.rest_16_
  139.7 3.5 %joined_grad.1 = (bf16[4,144,576]{2,1,0:T(8,128)(2,1)S(1)}, bf16[4,144,576]{2,1,0:T(8,128)(2,1)S(1)}, bf16[2,128,768]{2,1,0:T(8,128)(2,1)S(1)}, bf16[2,128,768]{2,1,0:T(8,128)(2,1)S(1)}) custom-call(s32[3]{0:T(128)S(1)} %pad_add_fusion.spot, bf16[512,192]{1,0:T(8,128)(2,1)S(1)} %get-tuple-element.102.query_grad, ...), custom_call_target="tpu_custom_call" | custom-call | bytes 21000000 | tf_op jit(solution)/shard_map/joined_grad/pallas_call | solution.py:39
  143.3 2.8 %collective-permute-start.35 = (bf16[96,768]{1,0:T(8,128)(2,1)S(1)}, bf16[96,768]{1,0:T(8,128)(2,1)S(1)}, u32[]{:S(2)}, u32[]{:S(2)}) collective-permute-start(bf16[96,768]{1,0:T(8,128)(2,1)S(1)} %slice.247), channel_id=1, source_target_pairs={{0,24},{2,26},{4,28},{6,30},{8,16},{10,18},{12,20},{14,22},{16,8},... | collective-permute-start | bytes 442376 | tf_op jit(solution)/shard_map/ppermute | solution.py:72
  146.0 1.5 up_grad.1
  147.9 0.9 joined_sum.1
  149.0 2.5 %collective-permute-done.35 = bf16[96,768]{1,0:T(8,128)(2,1)S(1)} collective-permute-done((bf16[96,768]{1,0:T(8,128)(2,1)S(1)}, bf16[96,768]{1,0:T(8,128)(2,1)S(1)}, u32[]{:S(2)}, u32[]{:S(2)}) %collective-permute-start.35) | collective-permute-done | bytes 147488 | tf_op jit(solution)/shard_map/ppermute | solution.py:72
  151.5 1.4 collective-permute-start.36
  152.9 6.8 %collective-permute-done.31 = bf16[2,144,576]{2,1,0:T(8,128)(2,1)S(1)} collective-permute-done((bf16[2,144,576]{2,1,0:T(8,128)(2,1)S(1)}, bf16[2,144,576]{2,1,0:T(8,128)(2,1)S(1)}, u32[]{:S(2)}, u32[]{:S(2)}) %collective-permute-start.31) | collective-permute-done | bytes 331808 | tf_op jit(solution)/shard_map/ppermute | solution.py:72
  160.7 2.1 collective-permute-start.38
  163.0 4.3 %collective-permute-done.32 = bf16[144,576]{1,0:T(8,128)(2,1)S(1)} collective-permute-done((bf16[144,576]{1,0:T(8,128)(2,1)S(1)}, bf16[144,576]{1,0:T(8,128)(2,1)S(1)}, u32[]{:S(2)}, u32[]{:S(2)}) %collective-permute-start.32) | collective-permute-done | bytes 165920 | tf_op jit(solution)/shard_map/ppermute | solution.py:72
  167.4 1.2 collective-permute-start.33
  169.0 2.5 %collective-permute-start.48 = (bf16[96,768]{1,0:T(8,128)(2,1)S(1)}, bf16[96,768]{1,0:T(8,128)(2,1)S(1)}, u32[]{:S(2)}, u32[]{:S(2)}) collective-permute-start(bf16[96,768]{1,0:T(8,128)(2,1)S(1)} %fusion.9), channel_id=1, source_target_pairs={{0,24},{2,26},{4,28},{6,30},{8,16},{10,18},{12,20},{14,22},{16,8},... | collective-permute-start | bytes 442376 | tf_op jit(solution)/shard_map/ppermute | solution.py:72
  171.5 5.3 %collective-permute-done.33 = bf16[144,576]{1,0:T(8,128)(2,1)S(1)} collective-permute-done((bf16[144,576]{1,0:T(8,128)(2,1)S(1)}, bf16[144,576]{1,0:T(8,128)(2,1)S(1)}, u32[]{:S(2)}, u32[]{:S(2)}) %collective-permute-start.33) | collective-permute-done | bytes 165920 | tf_op jit(solution)/shard_map/ppermute | solution.py:72
  176.9 1.1 collective-permute-start.34
  178.5 2.6 %collective-permute-start.40 = (bf16[2,96,768]{2,1,0:T(8,128)(2,1)S(1)}, bf16[2,96,768]{2,1,0:T(8,128)(2,1)S(1)}, u32[]{:S(2)}, u32[]{:S(2)}) collective-permute-start(bf16[2,96,768]{2,1,0:T(8,128)(2,1)S(1)} %slice.192), channel_id=1, source_target_pairs={{0,2},{2,0},{4,6},{6,4},{8,10},{10,8},{12,14},{14,12},{16,18},{18,... | collective-permute-start | bytes 884744 | tf_op jit(solution)/shard_map/ppermute | solution.py:72
  181.3 1.3 collective-permute-start.49
  182.6 4.2 %collective-permute-done.34 = bf16[2,144,576]{2,1,0:T(8,128)(2,1)S(1)} collective-permute-done((bf16[2,144,576]{2,1,0:T(8,128)(2,1)S(1)}, bf16[2,144,576]{2,1,0:T(8,128)(2,1)S(1)}, u32[]{:S(2)}, u32[]{:S(2)}) %collective-permute-start.34) | collective-permute-done | bytes 331808 | tf_op jit(solution)/shard_map/ppermute | solution.py:72
  186.9 2.7 %collective-permute-done.39.refs_3_ = bf16[2,96,768]{2,1,0:T(8,128)(2,1)S(1)} collective-permute-done((bf16[2,96,768]{2,1,0:T(8,128)(2,1)S(1)}, bf16[2,96,768]{2,1,0:T(8,128)(2,1)S(1)}, u32[]{:S(2)}, u32[]{:S(2)}) %collective-permute-start.39) | collective-permute-done | bytes 294944 | tf_op jit(solution)/shard_map/ppermute | solution.py:72
  189.7 2.0 collective-permute-start.28
  191.7 7.2 %collective-permute-done.50 = bf16[2,96,768]{2,1,0:T(8,128)(2,1)S(1)} collective-permute-done((bf16[2,96,768]{2,1,0:T(8,128)(2,1)S(1)}, bf16[2,96,768]{2,1,0:T(8,128)(2,1)S(1)}, u32[]{:S(2)}, u32[]{:S(2)}) %collective-permute-start.50) | collective-permute-done | bytes 294944 | tf_op jit(solution)/shard_map/ppermute | solution.py:72
  199.0 2.6 %collective-permute-start.52 = (bf16[4,96,768]{2,1,0:T(8,128)(2,1)S(1)}, bf16[4,96,768]{2,1,0:T(8,128)(2,1)S(1)}, u32[]{:S(2)}, u32[]{:S(2)}) collective-permute-start(bf16[4,96,768]{2,1,0:T(8,128)(2,1)S(1)} %pad_maximum_fusion.2.refs_0_), channel_id=1, source_target_pairs={{0,4},{2,6},{4,0},{6,2},{8,12},{10,14},{12,8},{14,10},{16,20},{18,... | collective-permute-start | bytes 1769480 | tf_op jit(solution)/shard_map/ppermute | solution.py:72
  201.6 3.1 %place_down.1 = f32[1536,768]{1,0:T(8,128)} custom-call(s32[3]{0:T(128)S(1)} %pad_add_fusion.spot, bf16[4,96,768]{2,1,0:T(8,128)(2,1)S(1)} %pad_maximum_fusion.1.refs_0_, bf16[4,96,768]{2,1,0:T(8,128)(2,1)S(1)} %collective-permute-done.37.refs_1_, bf16[4,96,768]{2,1,0:T(8,128)(2,1)S(1)} %collective-permute-done.38.refs_2_, ...), custom_call_target="tpu_custom_call" | custom-call | bytes 17500000 | tf_op jit(solution)/shard_map/place_down/pallas_call | solution.py:39
  204.6 4.4 %collective-permute-done.42.refs_2_ = bf16[4,144,576]{2,1,0:T(8,128)(2,1)S(1)} collective-permute-done((bf16[4,144,576]{2,1,0:T(8,128)(2,1)S(1)}, bf16[4,144,576]{2,1,0:T(8,128)(2,1)S(1)}, u32[]{:S(2)}, u32[]{:S(2)}) %collective-permute-start.42) | collective-permute-done | bytes 663584 | tf_op jit(solution)/shard_map/ppermute | solution.py:72
  209.1 1.5 collective-permute-start.43
  211.2 1.1 collective-permute-start.29
  212.8 8.8 %collective-permute-done.52.refs_2_ = bf16[4,96,768]{2,1,0:T(8,128)(2,1)S(1)} collective-permute-done((bf16[4,96,768]{2,1,0:T(8,128)(2,1)S(1)}, bf16[4,96,768]{2,1,0:T(8,128)(2,1)S(1)}, u32[]{:S(2)}, u32[]{:S(2)}) %collective-permute-start.52) | collective-permute-done | bytes 589856 | tf_op jit(solution)/shard_map/ppermute | solution.py:72
  221.7 1.5 collective-permute-start.53
  224.3 3.1 %collective-permute-done.43.refs_3_ = bf16[2,144,576]{2,1,0:T(8,128)(2,1)S(1)} collective-permute-done((bf16[2,144,576]{2,1,0:T(8,128)(2,1)S(1)}, bf16[2,144,576]{2,1,0:T(8,128)(2,1)S(1)}, u32[]{:S(2)}, u32[]{:S(2)}) %collective-permute-start.43) | collective-permute-done | bytes 331808 | tf_op jit(solution)/shard_map/ppermute | solution.py:72
  227.4 5.0 %place_joined.1 = (f32[384,2304]{1,0:T(8,128)}, f32[8,384]{1,0:T(8,128)S(1)}, bf16[2,4,24,768]{3,2,1,0:T(8,128)(2,1)S(1)}, bf16[2,4,24,768]{3,2,1,0:T(8,128)(2,1)S(1)}) custom-call(s32[3]{0:T(128)S(1)} %pad_add_fusion.spot, bf16[4,144,576]{2,1,0:T(8,128)(2,1)S(1)} %pad_maximum_fusion.refs_0_, bf16[4,144,576]{2,1,0:T(8,128)(2,1)S(1)} %collective-permute-done.41.refs_1_, ...), custom_call_target="tpu_custom_call" | custom-call | bytes 17500000 | tf_op jit(solution)/shard_map/place_joined/pallas_call | solution.py:39
  233.2 3.1 %place_up.1 = f32[384,3072]{1,0:T(8,128)} custom-call(s32[3]{0:T(128)S(1)} %pad_add_fusion.spot, bf16[4,96,768]{2,1,0:T(8,128)(2,1)S(1)} %pad_maximum_fusion.2.refs_0_, bf16[4,96,768]{2,1,0:T(8,128)(2,1)S(1)} %collective-permute-done.51.refs_1_, bf16[4,96,768]{2,1,0:T(8,128)(2,1)S(1)} %collective-permute-done.52.refs_2_, ...), custom_call_target="tpu_custom_call" | custom-call | bytes 14000000 | tf_op jit(solution)/shard_map/place_up/pallas_call | solution.py:39
  236.9 1.6 place_out.1
  (167 shorter events, 22.5 us)
Async XLA Ops:
  7.2 61.1 %all-gather.6.cloned.1.call-start = ((), (), s32[]{:S(2)}) async-start(), calls=%async_computation | async-start | bytes 1769472 | tf_op jit(solution)/shard_map/all_gather | solution.py:550
  8.0 7.4 %copy-start.15 = (bf16[384]{0:T(512)(128)(2,1)S(1)}, bf16[384]{0:T(512)(128)(2,1)}, u32[]{:S(2)}) copy-start(bf16[384]{0:T(512)(128)(2,1)} %param.31) | copy-start | bytes 2308
  8.0 7.4 %copy-start.7 = (bf16[1536]{0:T(1024)(128)(2,1)S(1)}, bf16[1536]{0:T(1024)(128)(2,1)}, u32[]{:S(2)}) copy-start(bf16[1536]{0:T(1024)(128)(2,1)} %param.27) | copy-start | bytes 9220
  8.0 60.2 %all-gather.8.cloned.1.call-start = ((), (), s32[]{:S(2)}) async-start(), calls=%async_computation.1 | async-start | bytes 7077888 | tf_op jit(solution)/shard_map/all_gather | solution.py:550
  8.8 59.5 %all-gather.10.cloned.1.call-start = ((), (), s32[]{:S(2)}) async-start(), calls=%async_computation.2 | async-start | bytes 7077888 | tf_op jit(solution)/shard_map/all_gather | solution.py:550
  9.5 12.6 %collective-permute-start.2 = (bf16[128,768]{1,0:T(8,128)(2,1)S(1)}, bf16[128,768]{1,0:T(8,128)(2,1)S(1)}, u32[]{:S(2)}, u32[]{:S(2)}) collective-permute-start(bf16[128,768]{1,0:T(8,128)(2,1)S(1)} %bitcast.60), channel_id=1, source_target_pairs={{0,24},{2,26},{4,28},{6,30},{8,16},{10,18},{12,20},{14,22},{16,8},... | collective-permute-start | bytes 589832 | tf_op jit(solution)/shard_map/ppermute | solution.py:72
  14.6 16.7 %collective-permute-start.1 = (bf16[128,768]{1,0:T(8,128)(2,1)S(1)}, bf16[128,768]{1,0:T(8,128)(2,1)S(1)}, u32[]{:S(2)}, u32[]{:S(2)}) collective-permute-start(bf16[128,768]{1,0:T(8,128)(2,1)S(1)} %bitcast.61), channel_id=1, source_target_pairs={{0,16},{2,18},{4,20},{6,22},{8,24},{10,26},{12,28},{14,30},{16,0},... | collective-permute-start | bytes 589832 | tf_op jit(solution)/shard_map/ppermute | solution.py:72
  14.6 16.7 %collective-permute-start = (bf16[128,768]{1,0:T(8,128)(2,1)S(1)}, bf16[128,768]{1,0:T(8,128)(2,1)S(1)}, u32[]{:S(2)}, u32[]{:S(2)}) collective-permute-start(bf16[128,768]{1,0:T(8,128)(2,1)S(1)} %bitcast.62), channel_id=1, source_target_pairs={{0,8},{2,10},{4,12},{6,14},{8,0},{10,2},{12,4},{14,6},{16,24},{18,... | collective-permute-start | bytes 589832 | tf_op jit(solution)/shard_map/ppermute | solution.py:72
  19.1 16.7 %copy-start.16 = (s32[2]{0:T(128)S(1)}, s32[2]{0:T(128)}, u32[]{:S(2)}) copy-start(s32[2]{0:T(128)} %param.18) | copy-start | bytes 28
  32.2 13.1 %collective-permute-start.5 = (bf16[512,384]{1,0:T(8,128)(2,1)S(1)}, bf16[512,384]{1,0:T(8,128)(2,1)S(1)}, u32[]{:S(2)}, u32[]{:S(2)}) collective-permute-start(bf16[512,384]{1,0:T(8,128)(2,1)S(1)} %get-tuple-element.89.refs_1_.refs_7_), channel_id=1, source_target_pairs={{0,6},{2,4},{4,2},{6,0},{8,14},{10,12},{12,10},{14,8},{16,22},{18,... | collective-permute-start | bytes 1179656 | tf_op jit(solution)/shard_map/ppermute | solution.py:72
  34.7 17.1 %collective-permute-start.4 = (bf16[512,384]{1,0:T(8,128)(2,1)S(1)}, bf16[512,384]{1,0:T(8,128)(2,1)S(1)}, u32[]{:S(2)}, u32[]{:S(2)}) collective-permute-start(bf16[512,384]{1,0:T(8,128)(2,1)S(1)} %get-tuple-element.89.refs_1_.refs_7_), channel_id=1, source_target_pairs={{0,4},{2,6},{4,0},{6,2},{8,12},{10,14},{12,8},{14,10},{16,20},{18,... | collective-permute-start | bytes 1179656 | tf_op jit(solution)/shard_map/ppermute | solution.py:72
  35.2 16.6 %collective-permute-start.3 = (bf16[512,384]{1,0:T(8,128)(2,1)S(1)}, bf16[512,384]{1,0:T(8,128)(2,1)S(1)}, u32[]{:S(2)}, u32[]{:S(2)}) collective-permute-start(bf16[512,384]{1,0:T(8,128)(2,1)S(1)} %get-tuple-element.89.refs_1_.refs_7_), channel_id=1, source_target_pairs={{0,2},{2,0},{4,6},{6,4},{8,10},{10,8},{12,14},{14,12},{16,18},{18,... | collective-permute-start | bytes 1179656 | tf_op jit(solution)/shard_map/ppermute | solution.py:72
  58.9 5.3 %collective-permute-start.6 = (bf16[128,192]{1,0:T(8,128)(2,1)}, bf16[128,192]{1,0:T(8,128)(2,1)}, u32[]{:S(2)}, u32[]{:S(2)}) collective-permute-start(bf16[128,192]{1,0:T(8,128)(2,1)} %get-tuple-element.91.rest_11_), channel_id=1, source_target_pairs={{0,8},{2,10},{4,12},{6,14},{8,0},{10,2},{12,4},{14,6},{16,24},{18,... | collective-permute-start | bytes 147464 | tf_op jit(solution)/shard_map/ppermute | solution.py:72
  58.9 8.2 %collective-permute-start.7 = (bf16[128,192]{1,0:T(8,128)(2,1)}, bf16[128,192]{1,0:T(8,128)(2,1)}, u32[]{:S(2)}, u32[]{:S(2)}) collective-permute-start(bf16[128,192]{1,0:T(8,128)(2,1)} %get-tuple-element.92.rest_12_), channel_id=1, source_target_pairs={{0,16},{2,18},{4,20},{6,22},{8,24},{10,26},{12,28},{14,30},{16,0},... | collective-permute-start | bytes 147464 | tf_op jit(solution)/shard_map/ppermute | solution.py:72
  61.8 6.5 %collective-permute-start.8 = (bf16[128,192]{1,0:T(8,128)(2,1)}, bf16[128,192]{1,0:T(8,128)(2,1)}, u32[]{:S(2)}, u32[]{:S(2)}) collective-permute-start(bf16[128,192]{1,0:T(8,128)(2,1)} %get-tuple-element.93.rest_13_), channel_id=1, source_target_pairs={{0,24},{2,26},{4,28},{6,30},{8,16},{10,18},{12,20},{14,22},{16,8},... | collective-permute-start | bytes 147464 | tf_op jit(solution)/shard_map/ppermute | solution.py:72
  68.2 24.6 %copy-start.4 = (f32[512,192]{1,0:T(8,128)S(1)}, f32[512,192]{1,0:T(8,128)}, u32[]{:S(2)}) copy-start(f32[512,192]{1,0:T(8,128)} %copy-done.3) | copy-start | bytes 1179652
  68.2 24.6 %copy-start.6 = (f32[512,128]{1,0:T(8,128)S(1)}, f32[512,128]{1,0:T(8,128)}, u32[]{:S(2)}) copy-start(f32[512,128]{1,0:T(8,128)} %copy-done.5) | copy-start | bytes 786436
  78.9 22.1 %collective-permute-start.16 = (bf16[144,1536]{1,0:T(8,128)(2,1)S(1)}, bf16[144,1536]{1,0:T(8,128)(2,1)S(1)}, u32[]{:S(2)}, u32[]{:S(2)}) collective-permute-start(bf16[144,1536]{1,0:T(8,128)(2,1)S(1)} %get-tuple-element.110), channel_id=1, source_target_pairs={{0,2},{2,0},{4,6},{6,4},{8,10},{10,8},{12,14},{14,12},{16,18},{18,... | collective-permute-start | bytes 1327112 | tf_op jit(solution)/shard_map/ppermute | solution.py:72
  80.5 20.5 %collective-permute-start.17 = (bf16[144,1536]{1,0:T(8,128)(2,1)S(1)}, bf16[144,1536]{1,0:T(8,128)(2,1)S(1)}, u32[]{:S(2)}, u32[]{:S(2)}) collective-permute-start(bf16[144,1536]{1,0:T(8,128)(2,1)S(1)} %get-tuple-element.111), channel_id=1, source_target_pairs={{0,4},{2,6},{4,0},{6,2},{8,12},{10,14},{12,8},{14,10},{16,20},{18,... | collective-permute-start | bytes 1327112 | tf_op jit(solution)/shard_map/ppermute | solution.py:72
  81.1 19.9 %collective-permute-start.18 = (bf16[144,1536]{1,0:T(8,128)(2,1)S(1)}, bf16[144,1536]{1,0:T(8,128)(2,1)S(1)}, u32[]{:S(2)}, u32[]{:S(2)}) collective-permute-start(bf16[144,1536]{1,0:T(8,128)(2,1)S(1)} %get-tuple-element.112), channel_id=1, source_target_pairs={{0,6},{2,4},{4,2},{6,0},{8,14},{10,12},{12,10},{14,8},{16,22},{18,... | collective-permute-start | bytes 1327112 | tf_op jit(solution)/shard_map/ppermute | solution.py:72
  82.5 4.3 %collective-permute-start.9 = (bf16[128,192]{1,0:T(8,128)(2,1)S(1)}, bf16[128,192]{1,0:T(8,128)(2,1)S(1)}, u32[]{:S(2)}, u32[]{:S(2)}) collective-permute-start(bf16[128,192]{1,0:T(8,128)(2,1)S(1)} %get-tuple-element.99), channel_id=1, source_target_pairs={{0,8},{2,10},{4,12},{6,14},{8,0},{10,2},{12,4},{14,6},{16,24},{18,... | collective-permute-start | bytes 147464 | tf_op jit(solution)/shard_map/ppermute | solution.py:72
  83.4 6.4 %collective-permute-start.10 = (bf16[128,192]{1,0:T(8,128)(2,1)S(1)}, bf16[128,192]{1,0:T(8,128)(2,1)S(1)}, u32[]{:S(2)}, u32[]{:S(2)}) collective-permute-start(bf16[128,192]{1,0:T(8,128)(2,1)S(1)} %get-tuple-element.100), channel_id=1, source_target_pairs={{0,16},{2,18},{4,20},{6,22},{8,24},{10,26},{12,28},{14,30},{16,0},... | collective-permute-start | bytes 147464 | tf_op jit(solution)/shard_map/ppermute | solution.py:72
  86.7 6.1 %collective-permute-start.11 = (bf16[128,192]{1,0:T(8,128)(2,1)S(1)}, bf16[128,192]{1,0:T(8,128)(2,1)S(1)}, u32[]{:S(2)}, u32[]{:S(2)}) collective-permute-start(bf16[128,192]{1,0:T(8,128)(2,1)S(1)} %get-tuple-element.101), channel_id=1, source_target_pairs={{0,24},{2,26},{4,28},{6,30},{8,16},{10,18},{12,20},{14,22},{16,8},... | collective-permute-start | bytes 147464 | tf_op jit(solution)/shard_map/ppermute | solution.py:72
  101.0 38.7 %copy-start.2 = (bf16[128,768]{1,0:T(8,128)(2,1)S(1)}, bf16[128,768]{1,0:T(8,128)(2,1)}, u32[]{:S(2)}) copy-start(bf16[128,768]{1,0:T(8,128)(2,1)} %copy-done.1) | copy-start | bytes 589828
  102.6 2.3 collective-permute-start.19
  102.7 12.0 %collective-permute-start.12 = (bf16[2,192,512]{2,1,0:T(8,128)(2,1)S(1)}, bf16[2,192,512]{2,1,0:T(8,128)(2,1)S(1)}, u32[]{:S(2)}, u32[]{:S(2)}) collective-permute-start(bf16[2,192,512]{2,1,0:T(8,128)(2,1)S(1)} %get-tuple-element.104), channel_id=1, source_target_pairs={{0,2},{2,0},{4,6},{6,4},{8,10},{10,8},{12,14},{14,12},{16,18},{18,... | collective-permute-start | bytes 1179656 | tf_op jit(solution)/shard_map/ppermute | solution.py:72
  104.2 12.0 %collective-permute-start.14 = (bf16[2,192,512]{2,1,0:T(8,128)(2,1)S(1)}, bf16[2,192,512]{2,1,0:T(8,128)(2,1)S(1)}, u32[]{:S(2)}, u32[]{:S(2)}) collective-permute-start(bf16[2,192,512]{2,1,0:T(8,128)(2,1)S(1)} %get-tuple-element.107), channel_id=1, source_target_pairs={{0,4},{2,6},{4,0},{6,2},{8,12},{10,14},{12,8},{14,10},{16,20},{18,... | collective-permute-start | bytes 1179656 | tf_op jit(solution)/shard_map/ppermute | solution.py:72
  105.5 12.4 %collective-permute-start.20 = (bf16[2,104,768]{2,1,0:T(8,128)(2,1)S(1)}, bf16[2,104,768]{2,1,0:T(8,128)(2,1)S(1)}, u32[]{:S(2)}, u32[]{:S(2)}) collective-permute-start(bf16[2,104,768]{2,1,0:T(8,128)(2,1)S(1)} %get-tuple-element.120), channel_id=1, source_target_pairs={{0,8},{2,10},{4,12},{6,14},{8,0},{10,2},{12,4},{14,6},{16,24},{18,... | collective-permute-start | bytes 958472 | tf_op jit(solution)/shard_map/ppermute | solution.py:72
  106.0 17.1 %collective-permute-start.22 = (bf16[128,1536]{1,0:T(8,128)(2,1)S(1)}, bf16[128,1536]{1,0:T(8,128)(2,1)S(1)}, u32[]{:S(2)}, u32[]{:S(2)}) collective-permute-start(bf16[128,1536]{1,0:T(8,128)(2,1)S(1)} %get-tuple-element.126), channel_id=1, source_target_pairs={{0,2},{2,0},{4,6},{6,4},{8,10},{10,8},{12,14},{14,12},{16,18},{18,... | collective-permute-start | bytes 1179656 | tf_op jit(solution)/shard_map/ppermute | solution.py:72
  107.1 25.4 %collective-permute-start.23 = (bf16[128,1536]{1,0:T(8,128)(2,1)S(1)}, bf16[128,1536]{1,0:T(8,128)(2,1)S(1)}, u32[]{:S(2)}, u32[]{:S(2)}) collective-permute-start(bf16[128,1536]{1,0:T(8,128)(2,1)S(1)} %get-tuple-element.127), channel_id=1, source_target_pairs={{0,4},{2,6},{4,0},{6,2},{8,12},{10,14},{12,8},{14,10},{16,20},{18,... | collective-permute-start | bytes 1179656 | tf_op jit(solution)/shard_map/ppermute | solution.py:72
  114.7 19.4 %collective-permute-start.24 = (bf16[128,1536]{1,0:T(8,128)(2,1)S(1)}, bf16[128,1536]{1,0:T(8,128)(2,1)S(1)}, u32[]{:S(2)}, u32[]{:S(2)}) collective-permute-start(bf16[128,1536]{1,0:T(8,128)(2,1)S(1)} %get-tuple-element.128), channel_id=1, source_target_pairs={{0,6},{2,4},{4,2},{6,0},{8,14},{10,12},{12,10},{14,8},{16,22},{18,... | collective-permute-start | bytes 1179656 | tf_op jit(solution)/shard_map/ppermute | solution.py:72
  116.2 16.9 %collective-permute-start.26 = (bf16[128,768]{1,0:T(8,128)(2,1)S(1)}, bf16[128,768]{1,0:T(8,128)(2,1)S(1)}, u32[]{:S(2)}, u32[]{:S(2)}) collective-permute-start(bf16[128,768]{1,0:T(8,128)(2,1)S(1)} %get-tuple-element.136.rest_14_), channel_id=1, source_target_pairs={{0,24},{2,26},{4,28},{6,30},{8,16},{10,18},{12,20},{14,22},{16,8},... | collective-permute-start | bytes 589832 | tf_op jit(solution)/shard_map/ppermute | solution.py:72
  118.0 16.0 %collective-permute-start.21 = (bf16[104,768]{1,0:T(8,128)(2,1)S(1)}, bf16[104,768]{1,0:T(8,128)(2,1)S(1)}, u32[]{:S(2)}, u32[]{:S(2)}) collective-permute-start(bf16[104,768]{1,0:T(8,128)(2,1)S(1)} %fusion.8), channel_id=1, source_target_pairs={{0,24},{2,26},{4,28},{6,30},{8,16},{10,18},{12,20},{14,22},{16,8},... | collective-permute-start | bytes 479240 | tf_op jit(solution)/shard_map/ppermute | solution.py:72
  123.1 15.7 %collective-permute-start.25 = (bf16[128,768]{1,0:T(8,128)(2,1)S(1)}, bf16[128,768]{1,0:T(8,128)(2,1)S(1)}, u32[]{:S(2)}, u32[]{:S(2)}) collective-permute-start(bf16[128,768]{1,0:T(8,128)(2,1)S(1)} %get-tuple-element.136.rest_14_), channel_id=1, source_target_pairs={{0,8},{2,10},{4,12},{6,14},{8,0},{10,2},{12,4},{14,6},{16,24},{18,... | collective-permute-start | bytes 589832 | tf_op jit(solution)/shard_map/ppermute | solution.py:72
  132.5 5.7 %collective-permute-start.13 = (bf16[192,512]{1,0:T(8,128)(2,1)S(1)}, bf16[192,512]{1,0:T(8,128)(2,1)S(1)}, u32[]{:S(2)}, u32[]{:S(2)}) collective-permute-start(bf16[192,512]{1,0:T(8,128)(2,1)S(1)} %fusion.1), channel_id=1, source_target_pairs={{0,4},{2,6},{4,0},{6,2},{8,12},{10,14},{12,8},{14,10},{16,20},{18,... | collective-permute-start | bytes 589832 | tf_op jit(solution)/shard_map/ppermute | solution.py:72
  133.1 5.7 %collective-permute-start.15 = (bf16[192,512]{1,0:T(8,128)(2,1)S(1)}, bf16[192,512]{1,0:T(8,128)(2,1)S(1)}, u32[]{:S(2)}, u32[]{:S(2)}) collective-permute-start(bf16[192,512]{1,0:T(8,128)(2,1)S(1)} %fusion), channel_id=1, source_target_pairs={{0,2},{2,0},{4,6},{6,4},{8,10},{10,8},{12,14},{14,12},{16,18},{18,... | collective-permute-start | bytes 589832 | tf_op jit(solution)/shard_map/ppermute | solution.py:72
  134.0 5.7 %collective-permute-start.27 = (bf16[128,768]{1,0:T(8,128)(2,1)S(1)}, bf16[128,768]{1,0:T(8,128)(2,1)S(1)}, u32[]{:S(2)}, u32[]{:S(2)}) collective-permute-start(bf16[128,768]{1,0:T(8,128)(2,1)S(1)} %collective-permute-done.26.rest_17_), channel_id=1, source_target_pairs={{0,8},{2,10},{4,12},{6,14},{8,0},{10,2},{12,4},{14,6},{16,24},{18,... | collective-permute-start | bytes 589832 | tf_op jit(solution)/shard_map/ppermute | solution.py:72
  143.2 4.7 %collective-permute-start.30 = (bf16[4,144,576]{2,1,0:T(8,128)(2,1)S(1)}, bf16[4,144,576]{2,1,0:T(8,128)(2,1)S(1)}, u32[]{:S(2)}, u32[]{:S(2)}) collective-permute-start(bf16[4,144,576]{2,1,0:T(8,128)(2,1)S(1)} %get-tuple-element.140), channel_id=1, source_target_pairs={{0,1},{1,0},{2,3},{3,2},{4,5},{5,4},{6,7},{7,6},{8,9},{9,8},{10,11... | collective-permute-start | bytes 1990664 | tf_op jit(solution)/shard_map/ppermute | solution.py:602
  143.3 8.2 %collective-permute-start.35 = (bf16[96,768]{1,0:T(8,128)(2,1)S(1)}, bf16[96,768]{1,0:T(8,128)(2,1)S(1)}, u32[]{:S(2)}, u32[]{:S(2)}) collective-permute-start(bf16[96,768]{1,0:T(8,128)(2,1)S(1)} %slice.247), channel_id=1, source_target_pairs={{0,24},{2,26},{4,28},{6,30},{8,16},{10,18},{12,20},{14,22},{16,8},... | collective-permute-start | bytes 442376 | tf_op jit(solution)/shard_map/ppermute | solution.py:72
  147.6 12.2 %collective-permute-start.46 = (bf16[4,96,768]{2,1,0:T(8,128)(2,1)S(1)}, bf16[4,96,768]{2,1,0:T(8,128)(2,1)S(1)}, u32[]{:S(2)}, u32[]{:S(2)}) collective-permute-start(bf16[4,96,768]{2,1,0:T(8,128)(2,1)S(1)} %get-tuple-element.155), channel_id=1, source_target_pairs={{0,1},{1,0},{2,3},{3,2},{4,5},{5,4},{6,7},{7,6},{8,9},{9,8},{10,11... | collective-permute-start | bytes 1769480 | tf_op jit(solution)/shard_map/ppermute | solution.py:602
  148.8 10.9 %collective-permute-start.31 = (bf16[2,144,576]{2,1,0:T(8,128)(2,1)S(1)}, bf16[2,144,576]{2,1,0:T(8,128)(2,1)S(1)}, u32[]{:S(2)}, u32[]{:S(2)}) collective-permute-start(bf16[2,144,576]{2,1,0:T(8,128)(2,1)S(1)} %get-tuple-element.142), channel_id=1, source_target_pairs={{0,2},{2,0},{4,6},{6,4},{8,10},{10,8},{12,14},{14,12},{16,18},{18,... | collective-permute-start | bytes 995336 | tf_op jit(solution)/shard_map/ppermute | solution.py:72
  151.5 9.1 %collective-permute-start.36 = (bf16[2,96,768]{2,1,0:T(8,128)(2,1)S(1)}, bf16[2,96,768]{2,1,0:T(8,128)(2,1)S(1)}, u32[]{:S(2)}, u32[]{:S(2)}) collective-permute-start(bf16[2,96,768]{2,1,0:T(8,128)(2,1)S(1)} %pad_maximum_fusion.5), channel_id=1, source_target_pairs={{0,8},{2,10},{4,12},{6,14},{8,0},{10,2},{12,4},{14,6},{16,24},{18,... | collective-permute-start | bytes 884744 | tf_op jit(solution)/shard_map/ppermute | solution.py:72
  159.7 7.6 %collective-permute-start.32 = (bf16[144,576]{1,0:T(8,128)(2,1)S(1)}, bf16[144,576]{1,0:T(8,128)(2,1)S(1)}, u32[]{:S(2)}, u32[]{:S(2)}) collective-permute-start(bf16[144,576]{1,0:T(8,128)(2,1)S(1)} %fusion.7), channel_id=1, source_target_pairs={{0,4},{2,6},{4,0},{6,2},{8,12},{10,14},{12,8},{14,10},{16,20},{18,... | collective-permute-start | bytes 497672 | tf_op jit(solution)/shard_map/ppermute | solution.py:72
  160.5 8.5 %collective-permute-start.47 = (bf16[2,96,768]{2,1,0:T(8,128)(2,1)S(1)}, bf16[2,96,768]{2,1,0:T(8,128)(2,1)S(1)}, u32[]{:S(2)}, u32[]{:S(2)}) collective-permute-start(bf16[2,96,768]{2,1,0:T(8,128)(2,1)S(1)} %get-tuple-element.157), channel_id=1, source_target_pairs={{0,8},{2,10},{4,12},{6,14},{8,0},{10,2},{12,4},{14,6},{16,24},{18,... | collective-permute-start | bytes 884744 | tf_op jit(solution)/shard_map/ppermute | solution.py:72
  160.7 17.8 %collective-permute-start.38 = (bf16[4,96,768]{2,1,0:T(8,128)(2,1)S(1)}, bf16[4,96,768]{2,1,0:T(8,128)(2,1)S(1)}, u32[]{:S(2)}, u32[]{:S(2)}) collective-permute-start(bf16[4,96,768]{2,1,0:T(8,128)(2,1)S(1)} %pad_maximum_fusion.1.refs_0_), channel_id=1, source_target_pairs={{0,4},{2,6},{4,0},{6,2},{8,12},{10,14},{12,8},{14,10},{16,20},{18,... | collective-permute-start | bytes 1769480 | tf_op jit(solution)/shard_map/ppermute | solution.py:72
  162.7 18.4 %collective-permute-start.37 = (bf16[4,96,768]{2,1,0:T(8,128)(2,1)S(1)}, bf16[4,96,768]{2,1,0:T(8,128)(2,1)S(1)}, u32[]{:S(2)}, u32[]{:S(2)}) collective-permute-start(bf16[4,96,768]{2,1,0:T(8,128)(2,1)S(1)} %pad_maximum_fusion.1.refs_0_), channel_id=1, source_target_pairs={{0,2},{2,0},{4,6},{6,4},{8,10},{10,8},{12,14},{14,12},{16,18},{18,... | collective-permute-start | bytes 1769480 | tf_op jit(solution)/shard_map/ppermute | solution.py:72
  167.4 9.4 %collective-permute-start.33 = (bf16[144,576]{1,0:T(8,128)(2,1)S(1)}, bf16[144,576]{1,0:T(8,128)(2,1)S(1)}, u32[]{:S(2)}, u32[]{:S(2)}) collective-permute-start(bf16[144,576]{1,0:T(8,128)(2,1)S(1)} %fusion.4), channel_id=1, source_target_pairs={{0,24},{2,26},{4,28},{6,30},{8,16},{10,18},{12,20},{14,22},{16,8},... | collective-permute-start | bytes 497672 | tf_op jit(solution)/shard_map/ppermute | solution.py:72
  169.0 12.2 %collective-permute-start.48 = (bf16[96,768]{1,0:T(8,128)(2,1)S(1)}, bf16[96,768]{1,0:T(8,128)(2,1)S(1)}, u32[]{:S(2)}, u32[]{:S(2)}) collective-permute-start(bf16[96,768]{1,0:T(8,128)(2,1)S(1)} %fusion.9), channel_id=1, source_target_pairs={{0,24},{2,26},{4,28},{6,30},{8,16},{10,18},{12,20},{14,22},{16,8},... | collective-permute-start | bytes 442376 | tf_op jit(solution)/shard_map/ppermute | solution.py:72
  176.9 9.9 %collective-permute-start.34 = (bf16[2,144,576]{2,1,0:T(8,128)(2,1)S(1)}, bf16[2,144,576]{2,1,0:T(8,128)(2,1)S(1)}, u32[]{:S(2)}, u32[]{:S(2)}) collective-permute-start(bf16[2,144,576]{2,1,0:T(8,128)(2,1)S(1)} %pad_maximum_fusion.4), channel_id=1, source_target_pairs={{0,8},{2,10},{4,12},{6,14},{8,0},{10,2},{12,4},{14,6},{16,24},{18,... | collective-permute-start | bytes 995336 | tf_op jit(solution)/shard_map/ppermute | solution.py:72
  178.5 8.4 %collective-permute-start.40 = (bf16[2,96,768]{2,1,0:T(8,128)(2,1)S(1)}, bf16[2,96,768]{2,1,0:T(8,128)(2,1)S(1)}, u32[]{:S(2)}, u32[]{:S(2)}) collective-permute-start(bf16[2,96,768]{2,1,0:T(8,128)(2,1)S(1)} %slice.192), channel_id=1, source_target_pairs={{0,2},{2,0},{4,6},{6,4},{8,10},{10,8},{12,14},{14,12},{16,18},{18,... | collective-permute-start | bytes 884744 | tf_op jit(solution)/shard_map/ppermute | solution.py:72
  181.1 8.4 %collective-permute-start.39 = (bf16[2,96,768]{2,1,0:T(8,128)(2,1)S(1)}, bf16[2,96,768]{2,1,0:T(8,128)(2,1)S(1)}, u32[]{:S(2)}, u32[]{:S(2)}) collective-permute-start(bf16[2,96,768]{2,1,0:T(8,128)(2,1)S(1)} %slice.191), channel_id=1, source_target_pairs={{0,4},{2,6},{4,0},{6,2},{8,12},{10,14},{12,8},{14,10},{16,20},{18,... | collective-permute-start | bytes 884744 | tf_op jit(solution)/shard_map/ppermute | solution.py:72
  181.3 8.3 %collective-permute-start.49 = (bf16[96,768]{1,0:T(8,128)(2,1)S(1)}, bf16[96,768]{1,0:T(8,128)(2,1)S(1)}, u32[]{:S(2)}, u32[]{:S(2)}) collective-permute-start(bf16[96,768]{1,0:T(8,128)(2,1)S(1)} %fusion.5), channel_id=1, source_target_pairs={{0,24},{2,26},{4,28},{6,30},{8,16},{10,18},{12,20},{14,22},{16,8},... | collective-permute-start | bytes 442376 | tf_op jit(solution)/shard_map/ppermute | solution.py:72
  189.5 19.4 %collective-permute-start.42 = (bf16[4,144,576]{2,1,0:T(8,128)(2,1)S(1)}, bf16[4,144,576]{2,1,0:T(8,128)(2,1)S(1)}, u32[]{:S(2)}, u32[]{:S(2)}) collective-permute-start(bf16[4,144,576]{2,1,0:T(8,128)(2,1)S(1)} %pad_maximum_fusion.refs_0_), channel_id=1, source_target_pairs={{0,4},{2,6},{4,0},{6,2},{8,12},{10,14},{12,8},{14,10},{16,20},{18,... | collective-permute-start | bytes 1990664 | tf_op jit(solution)/shard_map/ppermute | solution.py:72
  189.5 19.5 %collective-permute-start.41 = (bf16[4,144,576]{2,1,0:T(8,128)(2,1)S(1)}, bf16[4,144,576]{2,1,0:T(8,128)(2,1)S(1)}, u32[]{:S(2)}, u32[]{:S(2)}) collective-permute-start(bf16[4,144,576]{2,1,0:T(8,128)(2,1)S(1)} %pad_maximum_fusion.refs_0_), channel_id=1, source_target_pairs={{0,2},{2,0},{4,6},{6,4},{8,10},{10,8},{12,14},{14,12},{16,18},{18,... | collective-permute-start | bytes 1990664 | tf_op jit(solution)/shard_map/ppermute | solution.py:72
  189.6 9.3 %collective-permute-start.50 = (bf16[2,96,768]{2,1,0:T(8,128)(2,1)S(1)}, bf16[2,96,768]{2,1,0:T(8,128)(2,1)S(1)}, u32[]{:S(2)}, u32[]{:S(2)}) collective-permute-start(bf16[2,96,768]{2,1,0:T(8,128)(2,1)S(1)} %pad_maximum_fusion.6), channel_id=1, source_target_pairs={{0,8},{2,10},{4,12},{6,14},{8,0},{10,2},{12,4},{14,6},{16,24},{18,... | collective-permute-start | bytes 884744 | tf_op jit(solution)/shard_map/ppermute | solution.py:72
  189.7 21.4 %collective-permute-start.28 = (bf16[2,128,768]{2,1,0:T(8,128)(2,1)S(1)}, bf16[2,128,768]{2,1,0:T(8,128)(2,1)S(1)}, u32[]{:S(2)}, u32[]{:S(2)}) collective-permute-start(bf16[2,128,768]{2,1,0:T(8,128)(2,1)S(1)} %get-tuple-element.138), channel_id=1, source_target_pairs={{0,8},{2,10},{4,12},{6,14},{8,0},{10,2},{12,4},{14,6},{16,24},{18,... | collective-permute-start | bytes 1179656 | tf_op jit(solution)/shard_map/ppermute | solution.py:72
  199.0 22.6 %collective-permute-start.52 = (bf16[4,96,768]{2,1,0:T(8,128)(2,1)S(1)}, bf16[4,96,768]{2,1,0:T(8,128)(2,1)S(1)}, u32[]{:S(2)}, u32[]{:S(2)}) collective-permute-start(bf16[4,96,768]{2,1,0:T(8,128)(2,1)S(1)} %pad_maximum_fusion.2.refs_0_), channel_id=1, source_target_pairs={{0,4},{2,6},{4,0},{6,2},{8,12},{10,14},{12,8},{14,10},{16,20},{18,... | collective-permute-start | bytes 1769480 | tf_op jit(solution)/shard_map/ppermute | solution.py:72
  201.5 20.1 %collective-permute-start.51 = (bf16[4,96,768]{2,1,0:T(8,128)(2,1)S(1)}, bf16[4,96,768]{2,1,0:T(8,128)(2,1)S(1)}, u32[]{:S(2)}, u32[]{:S(2)}) collective-permute-start(bf16[4,96,768]{2,1,0:T(8,128)(2,1)S(1)} %pad_maximum_fusion.2.refs_0_), channel_id=1, source_target_pairs={{0,2},{2,0},{4,6},{6,4},{8,10},{10,8},{12,14},{14,12},{16,18},{18,... | collective-permute-start | bytes 1769480 | tf_op jit(solution)/shard_map/ppermute | solution.py:72
  209.1 18.3 %collective-permute-start.43 = (bf16[2,144,576]{2,1,0:T(8,128)(2,1)S(1)}, bf16[2,144,576]{2,1,0:T(8,128)(2,1)S(1)}, u32[]{:S(2)}, u32[]{:S(2)}) collective-permute-start(bf16[2,144,576]{2,1,0:T(8,128)(2,1)S(1)} %slice.193), channel_id=1, source_target_pairs={{0,4},{2,6},{4,0},{6,2},{8,12},{10,14},{12,8},{14,10},{16,20},{18,... | collective-permute-start | bytes 995336 | tf_op jit(solution)/shard_map/ppermute | solution.py:72
  210.6 16.8 %collective-permute-start.44 = (bf16[2,144,576]{2,1,0:T(8,128)(2,1)S(1)}, bf16[2,144,576]{2,1,0:T(8,128)(2,1)S(1)}, u32[]{:S(2)}, u32[]{:S(2)}) collective-permute-start(bf16[2,144,576]{2,1,0:T(8,128)(2,1)S(1)} %slice.194), channel_id=1, source_target_pairs={{0,2},{2,0},{4,6},{6,4},{8,10},{10,8},{12,14},{14,12},{16,18},{18,... | collective-permute-start | bytes 995336 | tf_op jit(solution)/shard_map/ppermute | solution.py:72
  211.2 21.2 %collective-permute-start.29 = (bf16[128,768]{1,0:T(8,128)(2,1)S(1)}, bf16[128,768]{1,0:T(8,128)(2,1)S(1)}, u32[]{:S(2)}, u32[]{:S(2)}) collective-permute-start(bf16[128,768]{1,0:T(8,128)(2,1)S(1)} %fusion.6), channel_id=1, source_target_pairs={{0,24},{2,26},{4,28},{6,30},{8,16},{10,18},{12,20},{14,22},{16,8},... | collective-permute-start | bytes 589832 | tf_op jit(solution)/shard_map/ppermute | solution.py:72
  221.7 11.6 %collective-permute-start.53 = (bf16[2,96,768]{2,1,0:T(8,128)(2,1)S(1)}, bf16[2,96,768]{2,1,0:T(8,128)(2,1)S(1)}, u32[]{:S(2)}, u32[]{:S(2)}) collective-permute-start(bf16[2,96,768]{2,1,0:T(8,128)(2,1)S(1)} %slice.200), channel_id=1, source_target_pairs={{0,4},{2,6},{4,0},{6,2},{8,12},{10,14},{12,8},{14,10},{16,20},{18,... | collective-permute-start | bytes 884744 | tf_op jit(solution)/shard_map/ppermute | solution.py:72
  223.2 10.1 %collective-permute-start.54 = (bf16[2,96,768]{2,1,0:T(8,128)(2,1)S(1)}, bf16[2,96,768]{2,1,0:T(8,128)(2,1)S(1)}, u32[]{:S(2)}, u32[]{:S(2)}) collective-permute-start(bf16[2,96,768]{2,1,0:T(8,128)(2,1)S(1)} %slice.201), channel_id=1, source_target_pairs={{0,2},{2,0},{4,6},{6,4},{8,10},{10,8},{12,14},{14,12},{16,18},{18,... | collective-permute-start | bytes 884744 | tf_op jit(solution)/shard_map/ppermute | solution.py:72
  232.4 4.5 %collective-permute-start.45 = (bf16[2,4,24,768]{3,2,1,0:T(8,128)(2,1)S(1)}, bf16[2,4,24,768]{3,2,1,0:T(8,128)(2,1)S(1)}, u32[]{:S(2)}, u32[]{:S(2)}) collective-permute-start(bf16[2,4,24,768]{3,2,1,0:T(8,128)(2,1)S(1)} %get-tuple-element.149), channel_id=1, source_target_pairs={{0,1},{1,0},{2,3},{3,2},{4,5},{5,4},{6,7},{7,6},{8,9},{9,8},{10,11... | collective-permute-start | bytes 884744 | tf_op jit(solution)/shard_map/ppermute | solution.py:602
  (11 other events, 55.5 us)
Sparse Core Ops, SparseCore 0:
  9.6 12.2 all-gather.5
  23.4 15.4 all-gather.7
  40.4 15.5 all-gather.9

commit v11 on v10

--- a/solution.py
+++ b/solution.py
@@ -242,7 +242,7 @@
     for ref in up_parts:
         ref[:, :width] = normed_low
     copies[1].wait()
-    step = 768
+    step = 1536
     for start in range(0, hidden, step):
         at = slice(start, start + step)
         inner = dot(normed_low, up_w[:, at]) + up_offset[:, at]

time: 245 us -> 246 us (level)
  no operation moved by 1% of the time
where the time goes in v11:
time: 246 us; the launch traced here: 245 us
  waiting for transfers between devices  111 us (45%)
  starting transfers between devices  58.8 us (24%)
  Pallas kernels  47 us (19%)
  between operations  14.4 us (6%)
  local copies, waits for them, and re-layouts  5.61 us (2%)
  blocking collectives  4.62 us (2%)
  other arithmetic  3.27 us (1%)
    ppermute x51, waiting for transfers between devices, swap(): return lax.ppermute(block, 'seq', [(i, i ^ bits) for i in range(self.size)])  109 us
    ppermute x51, starting transfers between devices, swap(): return lax.ppermute(block, 'seq', [(i, i ^ bits) for i in range(self.size)])  58.3 us
    pallas_call x14, Pallas kernels, kernel_call(): pl.pallas_call(run if after else kernel, out_shape=outs, in_specs=spaces...  47 us
  transfers between devices with their start and end apart: 58, of which 28 were waited for; matrix products, arithmetic and copies ran while one was open for 3% of the time, Pallas kernels for 12%

profile of v11, /device:TPU:0, one launch (start us, length us, event | category | flops | bytes accessed | tf_op | source)
XLA Modules:
  0.0 245.2 jit_solution(5508577163431421026)
XLA Ops:
  9.5 5.1 %collective-permute-start.2 = (bf16[128,768]{1,0:T(8,128)(2,1)S(1)}, bf16[128,768]{1,0:T(8,128)(2,1)S(1)}, u32[]{:S(2)}, u32[]{:S(2)}) collective-permute-start(bf16[128,768]{1,0:T(8,128)(2,1)S(1)} %bitcast.60), channel_id=1, source_target_pairs={{0,24},{2,26},{4,28},{6,30},{8,16},{10,18},{12,20},{14,22},{16,8},... | collective-permute-start | bytes 589832 | tf_op jit(solution)/shard_map/ppermute | solution.py:72
  15.5 1.8 all-gather.1
  17.6 1.5 constant_dynamic-slice_fusion.2
  19.3 2.8 %all_gather.18.weight.rest_18_ = bf16[768,576]{1,0:T(8,128)(2,1)S(1)} all-gather(bf16[384,576]{1,0:T(8,128)(2,1)S(1)} %pad_maximum_fusion.3), channel_id=1, replica_groups=mesh['seq'=16,'shard'=2] {'shard'}, dimensions={0}, use_global_device_ids=true | all-gather | bytes 1327104 | tf_op jit(solution)/shard_map/all_gather | solution.py:550
  22.1 9.2 %collective-permute-done.1.x2.rest_8_ = bf16[128,768]{1,0:T(8,128)(2,1)S(1)} collective-permute-done((bf16[128,768]{1,0:T(8,128)(2,1)S(1)}, bf16[128,768]{1,0:T(8,128)(2,1)S(1)}, u32[]{:S(2)}, u32[]{:S(2)}) %collective-permute-start.1) | collective-permute-done | bytes 196640 | tf_op jit(solution)/shard_map/ppermute | solution.py:72
  31.3 0.9 project.1
  32.2 2.5 %collective-permute-start.5 = (bf16[512,384]{1,0:T(8,128)(2,1)S(1)}, bf16[512,384]{1,0:T(8,128)(2,1)S(1)}, u32[]{:S(2)}, u32[]{:S(2)}) collective-permute-start(bf16[512,384]{1,0:T(8,128)(2,1)S(1)} %get-tuple-element.89.refs_1_.refs_7_), channel_id=1, source_target_pairs={{0,6},{2,4},{4,2},{6,0},{8,14},{10,12},{12,10},{14,8},{16,22},{18,... | collective-permute-start | bytes 1179656 | tf_op jit(solution)/shard_map/ppermute | solution.py:72
  37.3 8.0 %collective-permute-done.5.refs_4_.refs_10_ = bf16[512,384]{1,0:T(8,128)(2,1)S(1)} collective-permute-done((bf16[512,384]{1,0:T(8,128)(2,1)S(1)}, bf16[512,384]{1,0:T(8,128)(2,1)S(1)}, u32[]{:S(2)}, u32[]{:S(2)}) %collective-permute-start.5) | collective-permute-done | bytes 393248 | tf_op jit(solution)/shard_map/ppermute | solution.py:72
  45.3 6.5 %collective-permute-done.4.refs_3_.refs_9_ = bf16[512,384]{1,0:T(8,128)(2,1)S(1)} collective-permute-done((bf16[512,384]{1,0:T(8,128)(2,1)S(1)}, bf16[512,384]{1,0:T(8,128)(2,1)S(1)}, u32[]{:S(2)}, u32[]{:S(2)}) %collective-permute-start.4) | collective-permute-done | bytes 393248 | tf_op jit(solution)/shard_map/ppermute | solution.py:72
  51.9 5.5 %attend.1 = (f32[512,192]{1,0:T(8,128)S(1)}, f32[512,128]{1,0:T(8,128)S(1)}, bf16[128,192]{1,0:T(8,128)(2,1)S(1)}, bf16[128,192]{1,0:T(8,128)(2,1)}, bf16[128,192]{1,0:T(8,128)(2,1)}, /*index=5*/bf16[128,192]{1,0:T(8,128)(2,1)}) custom-call(bf16[512,192]{1,0:T(8,128)(2,1)S(1)} %get-tuple-element.88.refs_0_, ...), custom_call_target="tpu_custom_call" | custom-call | bytes 31500000 | tf_op jit(solution)/shard_map/attend/pallas_call | solution.py:39
  58.9 2.9 %collective-permute-start.7 = (bf16[128,192]{1,0:T(8,128)(2,1)}, bf16[128,192]{1,0:T(8,128)(2,1)}, u32[]{:S(2)}, u32[]{:S(2)}) collective-permute-start(bf16[128,192]{1,0:T(8,128)(2,1)} %get-tuple-element.92.rest_12_), channel_id=1, source_target_pairs={{0,16},{2,18},{4,20},{6,22},{8,24},{10,26},{12,28},{14,30},{16,0},... | collective-permute-start | bytes 147464 | tf_op jit(solution)/shard_map/ppermute | solution.py:72
  61.8 1.5 collective-permute-start.8
  64.2 2.9 %collective-permute-done.7.c2 = bf16[128,192]{1,0:T(8,128)(2,1)} collective-permute-done((bf16[128,192]{1,0:T(8,128)(2,1)}, bf16[128,192]{1,0:T(8,128)(2,1)}, u32[]{:S(2)}, u32[]{:S(2)}) %collective-permute-start.7) | collective-permute-done | bytes 49184 | tf_op jit(solution)/shard_map/ppermute | solution.py:72
  67.1 1.1 collective-permute-done.8.c3
  68.3 10.8 %dense.1 = (bf16[128,768]{1,0:T(8,128)(2,1)}, f32[128,768]{1,0:T(8,128)S(1)}, bf16[128,768]{1,0:T(8,128)(2,1)S(1)}, bf16[128,192]{1,0:T(8,128)(2,1)S(1)}, bf16[1...) custom-call(s32[3]{0:T(128)S(1)} %pad_add_fusion.spot, ...), custom_call_target="tpu_custom_call" | custom-call | bytes 35000000 | tf_op jit(solution)/shard_map/dense/pallas_call | solution.py:39
  79.0 1.6 collective-permute-start.16
  81.2 1.4 collective-permute-start.18
  82.6 0.9 collective-permute-start.9
  83.5 1.3 collective-permute-start.10
  84.8 2.1 collective-permute-done.9.refs_4_
  86.8 1.7 collective-permute-start.11
  88.6 1.3 collective-permute-done.10.refs_5_
  89.9 3.0 %collective-permute-done.11.refs_6_ = bf16[128,192]{1,0:T(8,128)(2,1)S(1)} collective-permute-done((bf16[128,192]{1,0:T(8,128)(2,1)S(1)}, bf16[128,192]{1,0:T(8,128)(2,1)S(1)}, u32[]{:S(2)}, u32[]{:S(2)}) %collective-permute-start.11) | collective-permute-done | bytes 49184 | tf_op jit(solution)/shard_map/ppermute | solution.py:72
  92.9 8.2 %attend_grad.1 = (bf16[512,192]{1,0:T(8,128)(2,1)S(1)}, bf16[192,512]{1,0:T(8,128)(2,1)S(1)}, bf16[192,512]{1,0:T(8,128)(2,1)S(1)}, bf16[192,512]{1,0:T(8,128)(2...) custom-call(bf16[512,192]{1,0:T(8,128)(2,1)S(1)} %get-tuple-element.88.ref, ...), custom_call_target="tpu_custom_call" | custom-call | bytes 38500000 | tf_op jit(solution)/shard_map/attend_grad/pallas_call | solution.py:39
  101.2 1.5 down_grad.1
  102.8 1.6 collective-permute-start.12
  106.0 1.1 collective-permute-start.22
  108.0 6.7 %collective-permute-done.12.rest_1_ = bf16[2,192,512]{2,1,0:T(8,128)(2,1)S(1)} collective-permute-done((bf16[2,192,512]{2,1,0:T(8,128)(2,1)S(1)}, bf16[2,192,512]{2,1,0:T(8,128)(2,1)S(1)}, u32[]{:S(2)}, u32[]{:S(2)}) %collective-permute-start.12) | collective-permute-done | bytes 393248 | tf_op jit(solution)/shard_map/ppermute | solution.py:72
  114.8 1.5 collective-permute-start.24
  116.3 1.7 collective-permute-start.26
  118.1 2.2 collective-permute-start.21
  120.4 2.8 %collective-permute-done.22.p1 = bf16[128,1536]{1,0:T(8,128)(2,1)S(1)} collective-permute-done((bf16[128,1536]{1,0:T(8,128)(2,1)S(1)}, bf16[128,1536]{1,0:T(8,128)(2,1)S(1)}, u32[]{:S(2)}, u32[]{:S(2)}) %collective-permute-start.22) | collective-permute-done | bytes 393248 | tf_op jit(solution)/shard_map/ppermute | solution.py:72
  123.6 9.0 %collective-permute-done.23.p2 = bf16[128,1536]{1,0:T(8,128)(2,1)S(1)} collective-permute-done((bf16[128,1536]{1,0:T(8,128)(2,1)S(1)}, bf16[128,1536]{1,0:T(8,128)(2,1)S(1)}, u32[]{:S(2)}, u32[]{:S(2)}) %collective-permute-start.23) | collective-permute-done | bytes 393248 | tf_op jit(solution)/shard_map/ppermute | solution.py:72
  134.2 4.1 %collective-permute-done.13.rest_2_ = bf16[192,512]{1,0:T(8,128)(2,1)S(1)} collective-permute-done((bf16[192,512]{1,0:T(8,128)(2,1)S(1)}, bf16[192,512]{1,0:T(8,128)(2,1)S(1)}, u32[]{:S(2)}, u32[]{:S(2)}) %collective-permute-start.13) | collective-permute-done | bytes 196640 | tf_op jit(solution)/shard_map/ppermute | solution.py:72
  139.8 3.5 %joined_grad.1 = (bf16[4,144,576]{2,1,0:T(8,128)(2,1)S(1)}, bf16[4,144,576]{2,1,0:T(8,128)(2,1)S(1)}, bf16[2,128,768]{2,1,0:T(8,128)(2,1)S(1)}, bf16[2,128,768]{2,1,0:T(8,128)(2,1)S(1)}) custom-call(s32[3]{0:T(128)S(1)} %pad_add_fusion.spot, bf16[512,192]{1,0:T(8,128)(2,1)S(1)} %get-tuple-element.102.query_grad, ...), custom_call_target="tpu_custom_call" | custom-call | bytes 21000000 | tf_op jit(solution)/shard_map/joined_grad/pallas_call | solution.py:39
  143.3 2.8 %collective-permute-start.35 = (bf16[96,768]{1,0:T(8,128)(2,1)S(1)}, bf16[96,768]{1,0:T(8,128)(2,1)S(1)}, u32[]{:S(2)}, u32[]{:S(2)}) collective-permute-start(bf16[96,768]{1,0:T(8,128)(2,1)S(1)} %slice.247), channel_id=1, source_target_pairs={{0,24},{2,26},{4,28},{6,30},{8,16},{10,18},{12,20},{14,22},{16,8},... | collective-permute-start | bytes 442376 | tf_op jit(solution)/shard_map/ppermute | solution.py:72
  146.2 1.5 up_grad.1
  148.0 0.9 joined_sum.1
  149.1 2.5 %collective-permute-done.35 = bf16[96,768]{1,0:T(8,128)(2,1)S(1)} collective-permute-done((bf16[96,768]{1,0:T(8,128)(2,1)S(1)}, bf16[96,768]{1,0:T(8,128)(2,1)S(1)}, u32[]{:S(2)}, u32[]{:S(2)}) %collective-permute-start.35) | collective-permute-done | bytes 147488 | tf_op jit(solution)/shard_map/ppermute | solution.py:72
  151.6 1.4 collective-permute-start.36
  153.0 6.8 %collective-permute-done.31 = bf16[2,144,576]{2,1,0:T(8,128)(2,1)S(1)} collective-permute-done((bf16[2,144,576]{2,1,0:T(8,128)(2,1)S(1)}, bf16[2,144,576]{2,1,0:T(8,128)(2,1)S(1)}, u32[]{:S(2)}, u32[]{:S(2)}) %collective-permute-start.31) | collective-permute-done | bytes 331808 | tf_op jit(solution)/shard_map/ppermute | solution.py:72
  160.8 2.1 collective-permute-start.38
  163.1 4.3 %collective-permute-done.32 = bf16[144,576]{1,0:T(8,128)(2,1)S(1)} collective-permute-done((bf16[144,576]{1,0:T(8,128)(2,1)S(1)}, bf16[144,576]{1,0:T(8,128)(2,1)S(1)}, u32[]{:S(2)}, u32[]{:S(2)}) %collective-permute-start.32) | collective-permute-done | bytes 165920 | tf_op jit(solution)/shard_map/ppermute | solution.py:72
  167.6 1.1 collective-permute-start.33
  169.1 2.5 %collective-permute-start.48 = (bf16[96,768]{1,0:T(8,128)(2,1)S(1)}, bf16[96,768]{1,0:T(8,128)(2,1)S(1)}, u32[]{:S(2)}, u32[]{:S(2)}) collective-permute-start(bf16[96,768]{1,0:T(8,128)(2,1)S(1)} %fusion.9), channel_id=1, source_target_pairs={{0,24},{2,26},{4,28},{6,30},{8,16},{10,18},{12,20},{14,22},{16,8},... | collective-permute-start | bytes 442376 | tf_op jit(solution)/shard_map/ppermute | solution.py:72
  171.7 5.3 %collective-permute-done.33 = bf16[144,576]{1,0:T(8,128)(2,1)S(1)} collective-permute-done((bf16[144,576]{1,0:T(8,128)(2,1)S(1)}, bf16[144,576]{1,0:T(8,128)(2,1)S(1)}, u32[]{:S(2)}, u32[]{:S(2)}) %collective-permute-start.33) | collective-permute-done | bytes 165920 | tf_op jit(solution)/shard_map/ppermute | solution.py:72
  177.0 1.1 collective-permute-start.34
  178.6 2.6 %collective-permute-start.40 = (bf16[2,96,768]{2,1,0:T(8,128)(2,1)S(1)}, bf16[2,96,768]{2,1,0:T(8,128)(2,1)S(1)}, u32[]{:S(2)}, u32[]{:S(2)}) collective-permute-start(bf16[2,96,768]{2,1,0:T(8,128)(2,1)S(1)} %slice.192), channel_id=1, source_target_pairs={{0,2},{2,0},{4,6},{6,4},{8,10},{10,8},{12,14},{14,12},{16,18},{18,... | collective-permute-start | bytes 884744 | tf_op jit(solution)/shard_map/ppermute | solution.py:72
  181.4 1.3 collective-permute-start.49
  182.7 4.2 %collective-permute-done.34 = bf16[2,144,576]{2,1,0:T(8,128)(2,1)S(1)} collective-permute-done((bf16[2,144,576]{2,1,0:T(8,128)(2,1)S(1)}, bf16[2,144,576]{2,1,0:T(8,128)(2,1)S(1)}, u32[]{:S(2)}, u32[]{:S(2)}) %collective-permute-start.34) | collective-permute-done | bytes 331808 | tf_op jit(solution)/shard_map/ppermute | solution.py:72
  187.0 2.6 %collective-permute-done.39.refs_3_ = bf16[2,96,768]{2,1,0:T(8,128)(2,1)S(1)} collective-permute-done((bf16[2,96,768]{2,1,0:T(8,128)(2,1)S(1)}, bf16[2,96,768]{2,1,0:T(8,128)(2,1)S(1)}, u32[]{:S(2)}, u32[]{:S(2)}) %collective-permute-start.39) | collective-permute-done | bytes 294944 | tf_op jit(solution)/shard_map/ppermute | solution.py:72
  189.7 2.0 collective-permute-start.28
  191.8 7.4 %collective-permute-done.50 = bf16[2,96,768]{2,1,0:T(8,128)(2,1)S(1)} collective-permute-done((bf16[2,96,768]{2,1,0:T(8,128)(2,1)S(1)}, bf16[2,96,768]{2,1,0:T(8,128)(2,1)S(1)}, u32[]{:S(2)}, u32[]{:S(2)}) %collective-permute-start.50) | collective-permute-done | bytes 294944 | tf_op jit(solution)/shard_map/ppermute | solution.py:72
  199.2 2.4 collective-permute-start.52
  201.6 3.1 %place_down.1 = f32[1536,768]{1,0:T(8,128)} custom-call(s32[3]{0:T(128)S(1)} %pad_add_fusion.spot, bf16[4,96,768]{2,1,0:T(8,128)(2,1)S(1)} %pad_maximum_fusion.1.refs_0_, bf16[4,96,768]{2,1,0:T(8,128)(2,1)S(1)} %collective-permute-done.37.refs_1_, bf16[4,96,768]{2,1,0:T(8,128)(2,1)S(1)} %collective-permute-done.38.refs_2_, ...), custom_call_target="tpu_custom_call" | custom-call | bytes 17500000 | tf_op jit(solution)/shard_map/place_down/pallas_call | solution.py:39
  204.7 4.3 %collective-permute-done.42.refs_2_ = bf16[4,144,576]{2,1,0:T(8,128)(2,1)S(1)} collective-permute-done((bf16[4,144,576]{2,1,0:T(8,128)(2,1)S(1)}, bf16[4,144,576]{2,1,0:T(8,128)(2,1)S(1)}, u32[]{:S(2)}, u32[]{:S(2)}) %collective-permute-start.42) | collective-permute-done | bytes 663584 | tf_op jit(solution)/shard_map/ppermute | solution.py:72
  209.1 1.6 collective-permute-start.43
  211.2 1.0 collective-permute-start.29
  212.9 8.8 %collective-permute-done.52.refs_2_ = bf16[4,96,768]{2,1,0:T(8,128)(2,1)S(1)} collective-permute-done((bf16[4,96,768]{2,1,0:T(8,128)(2,1)S(1)}, bf16[4,96,768]{2,1,0:T(8,128)(2,1)S(1)}, u32[]{:S(2)}, u32[]{:S(2)}) %collective-permute-start.52) | collective-permute-done | bytes 589856 | tf_op jit(solution)/shard_map/ppermute | solution.py:72
  221.7 1.6 collective-permute-start.53
  224.4 3.1 %collective-permute-done.43.refs_3_ = bf16[2,144,576]{2,1,0:T(8,128)(2,1)S(1)} collective-permute-done((bf16[2,144,576]{2,1,0:T(8,128)(2,1)S(1)}, bf16[2,144,576]{2,1,0:T(8,128)(2,1)S(1)}, u32[]{:S(2)}, u32[]{:S(2)}) %collective-permute-start.43) | collective-permute-done | bytes 331808 | tf_op jit(solution)/shard_map/ppermute | solution.py:72
  227.5 5.0 %place_joined.1 = (f32[384,2304]{1,0:T(8,128)}, f32[8,384]{1,0:T(8,128)S(1)}, bf16[2,4,24,768]{3,2,1,0:T(8,128)(2,1)S(1)}, bf16[2,4,24,768]{3,2,1,0:T(8,128)(2,1)S(1)}) custom-call(s32[3]{0:T(128)S(1)} %pad_add_fusion.spot, bf16[4,144,576]{2,1,0:T(8,128)(2,1)S(1)} %pad_maximum_fusion.refs_0_, bf16[4,144,576]{2,1,0:T(8,128)(2,1)S(1)} %collective-permute-done.41.refs_1_, ...), custom_call_target="tpu_custom_call" | custom-call | bytes 17500000 | tf_op jit(solution)/shard_map/place_joined/pallas_call | solution.py:39
  233.3 3.1 %place_up.1 = f32[384,3072]{1,0:T(8,128)} custom-call(s32[3]{0:T(128)S(1)} %pad_add_fusion.spot, bf16[4,96,768]{2,1,0:T(8,128)(2,1)S(1)} %pad_maximum_fusion.2.refs_0_, bf16[4,96,768]{2,1,0:T(8,128)(2,1)S(1)} %collective-permute-done.51.refs_1_, bf16[4,96,768]{2,1,0:T(8,128)(2,1)S(1)} %collective-permute-done.52.refs_2_, ...), custom_call_target="tpu_custom_call" | custom-call | bytes 14000000 | tf_op jit(solution)/shard_map/place_up/pallas_call | solution.py:39
  237.0 1.6 place_out.1
  (167 shorter events, 22.2 us)
Async XLA Ops:
  7.2 61.1 %all-gather.6.cloned.1.call-start = ((), (), s32[]{:S(2)}) async-start(), calls=%async_computation | async-start | bytes 1769472 | tf_op jit(solution)/shard_map/all_gather | solution.py:550
  8.0 7.4 %copy-start.15 = (bf16[384]{0:T(512)(128)(2,1)S(1)}, bf16[384]{0:T(512)(128)(2,1)}, u32[]{:S(2)}) copy-start(bf16[384]{0:T(512)(128)(2,1)} %param.31) | copy-start | bytes 2308
  8.0 7.4 %copy-start.7 = (bf16[1536]{0:T(1024)(128)(2,1)S(1)}, bf16[1536]{0:T(1024)(128)(2,1)}, u32[]{:S(2)}) copy-start(bf16[1536]{0:T(1024)(128)(2,1)} %param.27) | copy-start | bytes 9220
  8.0 60.2 %all-gather.8.cloned.1.call-start = ((), (), s32[]{:S(2)}) async-start(), calls=%async_computation.1 | async-start | bytes 7077888 | tf_op jit(solution)/shard_map/all_gather | solution.py:550
  8.8 59.5 %all-gather.10.cloned.1.call-start = ((), (), s32[]{:S(2)}) async-start(), calls=%async_computation.2 | async-start | bytes 7077888 | tf_op jit(solution)/shard_map/all_gather | solution.py:550
  9.5 12.6 %collective-permute-start.2 = (bf16[128,768]{1,0:T(8,128)(2,1)S(1)}, bf16[128,768]{1,0:T(8,128)(2,1)S(1)}, u32[]{:S(2)}, u32[]{:S(2)}) collective-permute-start(bf16[128,768]{1,0:T(8,128)(2,1)S(1)} %bitcast.60), channel_id=1, source_target_pairs={{0,24},{2,26},{4,28},{6,30},{8,16},{10,18},{12,20},{14,22},{16,8},... | collective-permute-start | bytes 589832 | tf_op jit(solution)/shard_map/ppermute | solution.py:72
  14.6 16.7 %collective-permute-start.1 = (bf16[128,768]{1,0:T(8,128)(2,1)S(1)}, bf16[128,768]{1,0:T(8,128)(2,1)S(1)}, u32[]{:S(2)}, u32[]{:S(2)}) collective-permute-start(bf16[128,768]{1,0:T(8,128)(2,1)S(1)} %bitcast.61), channel_id=1, source_target_pairs={{0,16},{2,18},{4,20},{6,22},{8,24},{10,26},{12,28},{14,30},{16,0},... | collective-permute-start | bytes 589832 | tf_op jit(solution)/shard_map/ppermute | solution.py:72
  14.6 16.7 %collective-permute-start = (bf16[128,768]{1,0:T(8,128)(2,1)S(1)}, bf16[128,768]{1,0:T(8,128)(2,1)S(1)}, u32[]{:S(2)}, u32[]{:S(2)}) collective-permute-start(bf16[128,768]{1,0:T(8,128)(2,1)S(1)} %bitcast.62), channel_id=1, source_target_pairs={{0,8},{2,10},{4,12},{6,14},{8,0},{10,2},{12,4},{14,6},{16,24},{18,... | collective-permute-start | bytes 589832 | tf_op jit(solution)/shard_map/ppermute | solution.py:72
  19.1 16.7 %copy-start.16 = (s32[2]{0:T(128)S(1)}, s32[2]{0:T(128)}, u32[]{:S(2)}) copy-start(s32[2]{0:T(128)} %param.18) | copy-start | bytes 28
  32.2 13.1 %collective-permute-start.5 = (bf16[512,384]{1,0:T(8,128)(2,1)S(1)}, bf16[512,384]{1,0:T(8,128)(2,1)S(1)}, u32[]{:S(2)}, u32[]{:S(2)}) collective-permute-start(bf16[512,384]{1,0:T(8,128)(2,1)S(1)} %get-tuple-element.89.refs_1_.refs_7_), channel_id=1, source_target_pairs={{0,6},{2,4},{4,2},{6,0},{8,14},{10,12},{12,10},{14,8},{16,22},{18,... | collective-permute-start | bytes 1179656 | tf_op jit(solution)/shard_map/ppermute | solution.py:72
  34.7 17.1 %collective-permute-start.4 = (bf16[512,384]{1,0:T(8,128)(2,1)S(1)}, bf16[512,384]{1,0:T(8,128)(2,1)S(1)}, u32[]{:S(2)}, u32[]{:S(2)}) collective-permute-start(bf16[512,384]{1,0:T(8,128)(2,1)S(1)} %get-tuple-element.89.refs_1_.refs_7_), channel_id=1, source_target_pairs={{0,4},{2,6},{4,0},{6,2},{8,12},{10,14},{12,8},{14,10},{16,20},{18,... | collective-permute-start | bytes 1179656 | tf_op jit(solution)/shard_map/ppermute | solution.py:72
  35.2 16.6 %collective-permute-start.3 = (bf16[512,384]{1,0:T(8,128)(2,1)S(1)}, bf16[512,384]{1,0:T(8,128)(2,1)S(1)}, u32[]{:S(2)}, u32[]{:S(2)}) collective-permute-start(bf16[512,384]{1,0:T(8,128)(2,1)S(1)} %get-tuple-element.89.refs_1_.refs_7_), channel_id=1, source_target_pairs={{0,2},{2,0},{4,6},{6,4},{8,10},{10,8},{12,14},{14,12},{16,18},{18,... | collective-permute-start | bytes 1179656 | tf_op jit(solution)/shard_map/ppermute | solution.py:72
  58.9 5.3 %collective-permute-start.6 = (bf16[128,192]{1,0:T(8,128)(2,1)}, bf16[128,192]{1,0:T(8,128)(2,1)}, u32[]{:S(2)}, u32[]{:S(2)}) collective-permute-start(bf16[128,192]{1,0:T(8,128)(2,1)} %get-tuple-element.91.rest_11_), channel_id=1, source_target_pairs={{0,8},{2,10},{4,12},{6,14},{8,0},{10,2},{12,4},{14,6},{16,24},{18,... | collective-permute-start | bytes 147464 | tf_op jit(solution)/shard_map/ppermute | solution.py:72
  58.9 8.2 %collective-permute-start.7 = (bf16[128,192]{1,0:T(8,128)(2,1)}, bf16[128,192]{1,0:T(8,128)(2,1)}, u32[]{:S(2)}, u32[]{:S(2)}) collective-permute-start(bf16[128,192]{1,0:T(8,128)(2,1)} %get-tuple-element.92.rest_12_), channel_id=1, source_target_pairs={{0,16},{2,18},{4,20},{6,22},{8,24},{10,26},{12,28},{14,30},{16,0},... | collective-permute-start | bytes 147464 | tf_op jit(solution)/shard_map/ppermute | solution.py:72
  61.8 6.5 %collective-permute-start.8 = (bf16[128,192]{1,0:T(8,128)(2,1)}, bf16[128,192]{1,0:T(8,128)(2,1)}, u32[]{:S(2)}, u32[]{:S(2)}) collective-permute-start(bf16[128,192]{1,0:T(8,128)(2,1)} %get-tuple-element.93.rest_13_), channel_id=1, source_target_pairs={{0,24},{2,26},{4,28},{6,30},{8,16},{10,18},{12,20},{14,22},{16,8},... | collective-permute-start | bytes 147464 | tf_op jit(solution)/shard_map/ppermute | solution.py:72
  68.2 24.7 %copy-start.4 = (f32[512,192]{1,0:T(8,128)S(1)}, f32[512,192]{1,0:T(8,128)}, u32[]{:S(2)}) copy-start(f32[512,192]{1,0:T(8,128)} %copy-done.3) | copy-start | bytes 1179652
  68.2 24.7 %copy-start.6 = (f32[512,128]{1,0:T(8,128)S(1)}, f32[512,128]{1,0:T(8,128)}, u32[]{:S(2)}) copy-start(f32[512,128]{1,0:T(8,128)} %copy-done.5) | copy-start | bytes 786436
  79.0 22.1 %collective-permute-start.16 = (bf16[144,1536]{1,0:T(8,128)(2,1)S(1)}, bf16[144,1536]{1,0:T(8,128)(2,1)S(1)}, u32[]{:S(2)}, u32[]{:S(2)}) collective-permute-start(bf16[144,1536]{1,0:T(8,128)(2,1)S(1)} %get-tuple-element.110), channel_id=1, source_target_pairs={{0,2},{2,0},{4,6},{6,4},{8,10},{10,8},{12,14},{14,12},{16,18},{18,... | collective-permute-start | bytes 1327112 | tf_op jit(solution)/shard_map/ppermute | solution.py:72
  80.6 20.6 %collective-permute-start.17 = (bf16[144,1536]{1,0:T(8,128)(2,1)S(1)}, bf16[144,1536]{1,0:T(8,128)(2,1)S(1)}, u32[]{:S(2)}, u32[]{:S(2)}) collective-permute-start(bf16[144,1536]{1,0:T(8,128)(2,1)S(1)} %get-tuple-element.111), channel_id=1, source_target_pairs={{0,4},{2,6},{4,0},{6,2},{8,12},{10,14},{12,8},{14,10},{16,20},{18,... | collective-permute-start | bytes 1327112 | tf_op jit(solution)/shard_map/ppermute | solution.py:72
  81.2 20.0 %collective-permute-start.18 = (bf16[144,1536]{1,0:T(8,128)(2,1)S(1)}, bf16[144,1536]{1,0:T(8,128)(2,1)S(1)}, u32[]{:S(2)}, u32[]{:S(2)}) collective-permute-start(bf16[144,1536]{1,0:T(8,128)(2,1)S(1)} %get-tuple-element.112), channel_id=1, source_target_pairs={{0,6},{2,4},{4,2},{6,0},{8,14},{10,12},{12,10},{14,8},{16,22},{18,... | collective-permute-start | bytes 1327112 | tf_op jit(solution)/shard_map/ppermute | solution.py:72
  82.6 4.3 %collective-permute-start.9 = (bf16[128,192]{1,0:T(8,128)(2,1)S(1)}, bf16[128,192]{1,0:T(8,128)(2,1)S(1)}, u32[]{:S(2)}, u32[]{:S(2)}) collective-permute-start(bf16[128,192]{1,0:T(8,128)(2,1)S(1)} %get-tuple-element.99), channel_id=1, source_target_pairs={{0,8},{2,10},{4,12},{6,14},{8,0},{10,2},{12,4},{14,6},{16,24},{18,... | collective-permute-start | bytes 147464 | tf_op jit(solution)/shard_map/ppermute | solution.py:72
  83.5 6.4 %collective-permute-start.10 = (bf16[128,192]{1,0:T(8,128)(2,1)S(1)}, bf16[128,192]{1,0:T(8,128)(2,1)S(1)}, u32[]{:S(2)}, u32[]{:S(2)}) collective-permute-start(bf16[128,192]{1,0:T(8,128)(2,1)S(1)} %get-tuple-element.100), channel_id=1, source_target_pairs={{0,16},{2,18},{4,20},{6,22},{8,24},{10,26},{12,28},{14,30},{16,0},... | collective-permute-start | bytes 147464 | tf_op jit(solution)/shard_map/ppermute | solution.py:72
  86.8 6.1 %collective-permute-start.11 = (bf16[128,192]{1,0:T(8,128)(2,1)S(1)}, bf16[128,192]{1,0:T(8,128)(2,1)S(1)}, u32[]{:S(2)}, u32[]{:S(2)}) collective-permute-start(bf16[128,192]{1,0:T(8,128)(2,1)S(1)} %get-tuple-element.101), channel_id=1, source_target_pairs={{0,24},{2,26},{4,28},{6,30},{8,16},{10,18},{12,20},{14,22},{16,8},... | collective-permute-start | bytes 147464 | tf_op jit(solution)/shard_map/ppermute | solution.py:72
  101.2 38.6 %copy-start.2 = (bf16[128,768]{1,0:T(8,128)(2,1)S(1)}, bf16[128,768]{1,0:T(8,128)(2,1)}, u32[]{:S(2)}) copy-start(bf16[128,768]{1,0:T(8,128)(2,1)} %copy-done.1) | copy-start | bytes 589828
  102.7 2.3 collective-permute-start.19
  102.8 12.0 %collective-permute-start.12 = (bf16[2,192,512]{2,1,0:T(8,128)(2,1)S(1)}, bf16[2,192,512]{2,1,0:T(8,128)(2,1)S(1)}, u32[]{:S(2)}, u32[]{:S(2)}) collective-permute-start(bf16[2,192,512]{2,1,0:T(8,128)(2,1)S(1)} %get-tuple-element.104), channel_id=1, source_target_pairs={{0,2},{2,0},{4,6},{6,4},{8,10},{10,8},{12,14},{14,12},{16,18},{18,... | collective-permute-start | bytes 1179656 | tf_op jit(solution)/shard_map/ppermute | solution.py:72
  104.4 12.0 %collective-permute-start.14 = (bf16[2,192,512]{2,1,0:T(8,128)(2,1)S(1)}, bf16[2,192,512]{2,1,0:T(8,128)(2,1)S(1)}, u32[]{:S(2)}, u32[]{:S(2)}) collective-permute-start(bf16[2,192,512]{2,1,0:T(8,128)(2,1)S(1)} %get-tuple-element.107), channel_id=1, source_target_pairs={{0,4},{2,6},{4,0},{6,2},{8,12},{10,14},{12,8},{14,10},{16,20},{18,... | collective-permute-start | bytes 1179656 | tf_op jit(solution)/shard_map/ppermute | solution.py:72
  105.7 12.4 %collective-permute-start.20 = (bf16[2,104,768]{2,1,0:T(8,128)(2,1)S(1)}, bf16[2,104,768]{2,1,0:T(8,128)(2,1)S(1)}, u32[]{:S(2)}, u32[]{:S(2)}) collective-permute-start(bf16[2,104,768]{2,1,0:T(8,128)(2,1)S(1)} %get-tuple-element.120), channel_id=1, source_target_pairs={{0,8},{2,10},{4,12},{6,14},{8,0},{10,2},{12,4},{14,6},{16,24},{18,... | collective-permute-start | bytes 958472 | tf_op jit(solution)/shard_map/ppermute | solution.py:72
  106.0 17.2 %collective-permute-start.22 = (bf16[128,1536]{1,0:T(8,128)(2,1)S(1)}, bf16[128,1536]{1,0:T(8,128)(2,1)S(1)}, u32[]{:S(2)}, u32[]{:S(2)}) collective-permute-start(bf16[128,1536]{1,0:T(8,128)(2,1)S(1)} %get-tuple-element.126), channel_id=1, source_target_pairs={{0,2},{2,0},{4,6},{6,4},{8,10},{10,8},{12,14},{14,12},{16,18},{18,... | collective-permute-start | bytes 1179656 | tf_op jit(solution)/shard_map/ppermute | solution.py:72
  107.2 25.4 %collective-permute-start.23 = (bf16[128,1536]{1,0:T(8,128)(2,1)S(1)}, bf16[128,1536]{1,0:T(8,128)(2,1)S(1)}, u32[]{:S(2)}, u32[]{:S(2)}) collective-permute-start(bf16[128,1536]{1,0:T(8,128)(2,1)S(1)} %get-tuple-element.127), channel_id=1, source_target_pairs={{0,4},{2,6},{4,0},{6,2},{8,12},{10,14},{12,8},{14,10},{16,20},{18,... | collective-permute-start | bytes 1179656 | tf_op jit(solution)/shard_map/ppermute | solution.py:72
  114.8 19.4 %collective-permute-start.24 = (bf16[128,1536]{1,0:T(8,128)(2,1)S(1)}, bf16[128,1536]{1,0:T(8,128)(2,1)S(1)}, u32[]{:S(2)}, u32[]{:S(2)}) collective-permute-start(bf16[128,1536]{1,0:T(8,128)(2,1)S(1)} %get-tuple-element.128), channel_id=1, source_target_pairs={{0,6},{2,4},{4,2},{6,0},{8,14},{10,12},{12,10},{14,8},{16,22},{18,... | collective-permute-start | bytes 1179656 | tf_op jit(solution)/shard_map/ppermute | solution.py:72
  116.3 16.9 %collective-permute-start.26 = (bf16[128,768]{1,0:T(8,128)(2,1)S(1)}, bf16[128,768]{1,0:T(8,128)(2,1)S(1)}, u32[]{:S(2)}, u32[]{:S(2)}) collective-permute-start(bf16[128,768]{1,0:T(8,128)(2,1)S(1)} %get-tuple-element.136.rest_14_), channel_id=1, source_target_pairs={{0,24},{2,26},{4,28},{6,30},{8,16},{10,18},{12,20},{14,22},{16,8},... | collective-permute-start | bytes 589832 | tf_op jit(solution)/shard_map/ppermute | solution.py:72
  118.1 15.9 %collective-permute-start.21 = (bf16[104,768]{1,0:T(8,128)(2,1)S(1)}, bf16[104,768]{1,0:T(8,128)(2,1)S(1)}, u32[]{:S(2)}, u32[]{:S(2)}) collective-permute-start(bf16[104,768]{1,0:T(8,128)(2,1)S(1)} %fusion.8), channel_id=1, source_target_pairs={{0,24},{2,26},{4,28},{6,30},{8,16},{10,18},{12,20},{14,22},{16,8},... | collective-permute-start | bytes 479240 | tf_op jit(solution)/shard_map/ppermute | solution.py:72
  123.2 15.7 %collective-permute-start.25 = (bf16[128,768]{1,0:T(8,128)(2,1)S(1)}, bf16[128,768]{1,0:T(8,128)(2,1)S(1)}, u32[]{:S(2)}, u32[]{:S(2)}) collective-permute-start(bf16[128,768]{1,0:T(8,128)(2,1)S(1)} %get-tuple-element.136.rest_14_), channel_id=1, source_target_pairs={{0,8},{2,10},{4,12},{6,14},{8,0},{10,2},{12,4},{14,6},{16,24},{18,... | collective-permute-start | bytes 589832 | tf_op jit(solution)/shard_map/ppermute | solution.py:72
  132.6 5.7 %collective-permute-start.13 = (bf16[192,512]{1,0:T(8,128)(2,1)S(1)}, bf16[192,512]{1,0:T(8,128)(2,1)S(1)}, u32[]{:S(2)}, u32[]{:S(2)}) collective-permute-start(bf16[192,512]{1,0:T(8,128)(2,1)S(1)} %fusion.1), channel_id=1, source_target_pairs={{0,4},{2,6},{4,0},{6,2},{8,12},{10,14},{12,8},{14,10},{16,20},{18,... | collective-permute-start | bytes 589832 | tf_op jit(solution)/shard_map/ppermute | solution.py:72
  133.2 5.7 %collective-permute-start.15 = (bf16[192,512]{1,0:T(8,128)(2,1)S(1)}, bf16[192,512]{1,0:T(8,128)(2,1)S(1)}, u32[]{:S(2)}, u32[]{:S(2)}) collective-permute-start(bf16[192,512]{1,0:T(8,128)(2,1)S(1)} %fusion), channel_id=1, source_target_pairs={{0,2},{2,0},{4,6},{6,4},{8,10},{10,8},{12,14},{14,12},{16,18},{18,... | collective-permute-start | bytes 589832 | tf_op jit(solution)/shard_map/ppermute | solution.py:72
  134.1 5.7 %collective-permute-start.27 = (bf16[128,768]{1,0:T(8,128)(2,1)S(1)}, bf16[128,768]{1,0:T(8,128)(2,1)S(1)}, u32[]{:S(2)}, u32[]{:S(2)}) collective-permute-start(bf16[128,768]{1,0:T(8,128)(2,1)S(1)} %collective-permute-done.26.rest_17_), channel_id=1, source_target_pairs={{0,8},{2,10},{4,12},{6,14},{8,0},{10,2},{12,4},{14,6},{16,24},{18,... | collective-permute-start | bytes 589832 | tf_op jit(solution)/shard_map/ppermute | solution.py:72
  143.2 4.8 %collective-permute-start.30 = (bf16[4,144,576]{2,1,0:T(8,128)(2,1)S(1)}, bf16[4,144,576]{2,1,0:T(8,128)(2,1)S(1)}, u32[]{:S(2)}, u32[]{:S(2)}) collective-permute-start(bf16[4,144,576]{2,1,0:T(8,128)(2,1)S(1)} %get-tuple-element.140), channel_id=1, source_target_pairs={{0,1},{1,0},{2,3},{3,2},{4,5},{5,4},{6,7},{7,6},{8,9},{9,8},{10,11... | collective-permute-start | bytes 1990664 | tf_op jit(solution)/shard_map/ppermute | solution.py:602
  143.3 8.2 %collective-permute-start.35 = (bf16[96,768]{1,0:T(8,128)(2,1)S(1)}, bf16[96,768]{1,0:T(8,128)(2,1)S(1)}, u32[]{:S(2)}, u32[]{:S(2)}) collective-permute-start(bf16[96,768]{1,0:T(8,128)(2,1)S(1)} %slice.247), channel_id=1, source_target_pairs={{0,24},{2,26},{4,28},{6,30},{8,16},{10,18},{12,20},{14,22},{16,8},... | collective-permute-start | bytes 442376 | tf_op jit(solution)/shard_map/ppermute | solution.py:72
  147.7 12.2 %collective-permute-start.46 = (bf16[4,96,768]{2,1,0:T(8,128)(2,1)S(1)}, bf16[4,96,768]{2,1,0:T(8,128)(2,1)S(1)}, u32[]{:S(2)}, u32[]{:S(2)}) collective-permute-start(bf16[4,96,768]{2,1,0:T(8,128)(2,1)S(1)} %get-tuple-element.155), channel_id=1, source_target_pairs={{0,1},{1,0},{2,3},{3,2},{4,5},{5,4},{6,7},{7,6},{8,9},{9,8},{10,11... | collective-permute-start | bytes 1769480 | tf_op jit(solution)/shard_map/ppermute | solution.py:602
  148.9 10.9 %collective-permute-start.31 = (bf16[2,144,576]{2,1,0:T(8,128)(2,1)S(1)}, bf16[2,144,576]{2,1,0:T(8,128)(2,1)S(1)}, u32[]{:S(2)}, u32[]{:S(2)}) collective-permute-start(bf16[2,144,576]{2,1,0:T(8,128)(2,1)S(1)} %get-tuple-element.142), channel_id=1, source_target_pairs={{0,2},{2,0},{4,6},{6,4},{8,10},{10,8},{12,14},{14,12},{16,18},{18,... | collective-permute-start | bytes 995336 | tf_op jit(solution)/shard_map/ppermute | solution.py:72
  151.6 9.1 %collective-permute-start.36 = (bf16[2,96,768]{2,1,0:T(8,128)(2,1)S(1)}, bf16[2,96,768]{2,1,0:T(8,128)(2,1)S(1)}, u32[]{:S(2)}, u32[]{:S(2)}) collective-permute-start(bf16[2,96,768]{2,1,0:T(8,128)(2,1)S(1)} %pad_maximum_fusion.5), channel_id=1, source_target_pairs={{0,8},{2,10},{4,12},{6,14},{8,0},{10,2},{12,4},{14,6},{16,24},{18,... | collective-permute-start | bytes 884744 | tf_op jit(solution)/shard_map/ppermute | solution.py:72
  159.8 7.6 %collective-permute-start.32 = (bf16[144,576]{1,0:T(8,128)(2,1)S(1)}, bf16[144,576]{1,0:T(8,128)(2,1)S(1)}, u32[]{:S(2)}, u32[]{:S(2)}) collective-permute-start(bf16[144,576]{1,0:T(8,128)(2,1)S(1)} %fusion.7), channel_id=1, source_target_pairs={{0,4},{2,6},{4,0},{6,2},{8,12},{10,14},{12,8},{14,10},{16,20},{18,... | collective-permute-start | bytes 497672 | tf_op jit(solution)/shard_map/ppermute | solution.py:72
  160.6 8.5 %collective-permute-start.47 = (bf16[2,96,768]{2,1,0:T(8,128)(2,1)S(1)}, bf16[2,96,768]{2,1,0:T(8,128)(2,1)S(1)}, u32[]{:S(2)}, u32[]{:S(2)}) collective-permute-start(bf16[2,96,768]{2,1,0:T(8,128)(2,1)S(1)} %get-tuple-element.157), channel_id=1, source_target_pairs={{0,8},{2,10},{4,12},{6,14},{8,0},{10,2},{12,4},{14,6},{16,24},{18,... | collective-permute-start | bytes 884744 | tf_op jit(solution)/shard_map/ppermute | solution.py:72
  160.8 17.8 %collective-permute-start.38 = (bf16[4,96,768]{2,1,0:T(8,128)(2,1)S(1)}, bf16[4,96,768]{2,1,0:T(8,128)(2,1)S(1)}, u32[]{:S(2)}, u32[]{:S(2)}) collective-permute-start(bf16[4,96,768]{2,1,0:T(8,128)(2,1)S(1)} %pad_maximum_fusion.1.refs_0_), channel_id=1, source_target_pairs={{0,4},{2,6},{4,0},{6,2},{8,12},{10,14},{12,8},{14,10},{16,20},{18,... | collective-permute-start | bytes 1769480 | tf_op jit(solution)/shard_map/ppermute | solution.py:72
  162.8 18.3 %collective-permute-start.37 = (bf16[4,96,768]{2,1,0:T(8,128)(2,1)S(1)}, bf16[4,96,768]{2,1,0:T(8,128)(2,1)S(1)}, u32[]{:S(2)}, u32[]{:S(2)}) collective-permute-start(bf16[4,96,768]{2,1,0:T(8,128)(2,1)S(1)} %pad_maximum_fusion.1.refs_0_), channel_id=1, source_target_pairs={{0,2},{2,0},{4,6},{6,4},{8,10},{10,8},{12,14},{14,12},{16,18},{18,... | collective-permute-start | bytes 1769480 | tf_op jit(solution)/shard_map/ppermute | solution.py:72
  167.6 9.4 %collective-permute-start.33 = (bf16[144,576]{1,0:T(8,128)(2,1)S(1)}, bf16[144,576]{1,0:T(8,128)(2,1)S(1)}, u32[]{:S(2)}, u32[]{:S(2)}) collective-permute-start(bf16[144,576]{1,0:T(8,128)(2,1)S(1)} %fusion.4), channel_id=1, source_target_pairs={{0,24},{2,26},{4,28},{6,30},{8,16},{10,18},{12,20},{14,22},{16,8},... | collective-permute-start | bytes 497672 | tf_op jit(solution)/shard_map/ppermute | solution.py:72
  169.1 12.2 %collective-permute-start.48 = (bf16[96,768]{1,0:T(8,128)(2,1)S(1)}, bf16[96,768]{1,0:T(8,128)(2,1)S(1)}, u32[]{:S(2)}, u32[]{:S(2)}) collective-permute-start(bf16[96,768]{1,0:T(8,128)(2,1)S(1)} %fusion.9), channel_id=1, source_target_pairs={{0,24},{2,26},{4,28},{6,30},{8,16},{10,18},{12,20},{14,22},{16,8},... | collective-permute-start | bytes 442376 | tf_op jit(solution)/shard_map/ppermute | solution.py:72
  177.0 9.9 %collective-permute-start.34 = (bf16[2,144,576]{2,1,0:T(8,128)(2,1)S(1)}, bf16[2,144,576]{2,1,0:T(8,128)(2,1)S(1)}, u32[]{:S(2)}, u32[]{:S(2)}) collective-permute-start(bf16[2,144,576]{2,1,0:T(8,128)(2,1)S(1)} %pad_maximum_fusion.4), channel_id=1, source_target_pairs={{0,8},{2,10},{4,12},{6,14},{8,0},{10,2},{12,4},{14,6},{16,24},{18,... | collective-permute-start | bytes 995336 | tf_op jit(solution)/shard_map/ppermute | solution.py:72
  178.6 8.4 %collective-permute-start.40 = (bf16[2,96,768]{2,1,0:T(8,128)(2,1)S(1)}, bf16[2,96,768]{2,1,0:T(8,128)(2,1)S(1)}, u32[]{:S(2)}, u32[]{:S(2)}) collective-permute-start(bf16[2,96,768]{2,1,0:T(8,128)(2,1)S(1)} %slice.192), channel_id=1, source_target_pairs={{0,2},{2,0},{4,6},{6,4},{8,10},{10,8},{12,14},{14,12},{16,18},{18,... | collective-permute-start | bytes 884744 | tf_op jit(solution)/shard_map/ppermute | solution.py:72
  181.2 8.4 %collective-permute-start.39 = (bf16[2,96,768]{2,1,0:T(8,128)(2,1)S(1)}, bf16[2,96,768]{2,1,0:T(8,128)(2,1)S(1)}, u32[]{:S(2)}, u32[]{:S(2)}) collective-permute-start(bf16[2,96,768]{2,1,0:T(8,128)(2,1)S(1)} %slice.191), channel_id=1, source_target_pairs={{0,4},{2,6},{4,0},{6,2},{8,12},{10,14},{12,8},{14,10},{16,20},{18,... | collective-permute-start | bytes 884744 | tf_op jit(solution)/shard_map/ppermute | solution.py:72
  181.4 8.2 %collective-permute-start.49 = (bf16[96,768]{1,0:T(8,128)(2,1)S(1)}, bf16[96,768]{1,0:T(8,128)(2,1)S(1)}, u32[]{:S(2)}, u32[]{:S(2)}) collective-permute-start(bf16[96,768]{1,0:T(8,128)(2,1)S(1)} %fusion.5), channel_id=1, source_target_pairs={{0,24},{2,26},{4,28},{6,30},{8,16},{10,18},{12,20},{14,22},{16,8},... | collective-permute-start | bytes 442376 | tf_op jit(solution)/shard_map/ppermute | solution.py:72
  189.6 19.4 %collective-permute-start.42 = (bf16[4,144,576]{2,1,0:T(8,128)(2,1)S(1)}, bf16[4,144,576]{2,1,0:T(8,128)(2,1)S(1)}, u32[]{:S(2)}, u32[]{:S(2)}) collective-permute-start(bf16[4,144,576]{2,1,0:T(8,128)(2,1)S(1)} %pad_maximum_fusion.refs_0_), channel_id=1, source_target_pairs={{0,4},{2,6},{4,0},{6,2},{8,12},{10,14},{12,8},{14,10},{16,20},{18,... | collective-permute-start | bytes 1990664 | tf_op jit(solution)/shard_map/ppermute | solution.py:72
  189.6 19.5 %collective-permute-start.41 = (bf16[4,144,576]{2,1,0:T(8,128)(2,1)S(1)}, bf16[4,144,576]{2,1,0:T(8,128)(2,1)S(1)}, u32[]{:S(2)}, u32[]{:S(2)}) collective-permute-start(bf16[4,144,576]{2,1,0:T(8,128)(2,1)S(1)} %pad_maximum_fusion.refs_0_), channel_id=1, source_target_pairs={{0,2},{2,0},{4,6},{6,4},{8,10},{10,8},{12,14},{14,12},{16,18},{18,... | collective-permute-start | bytes 1990664 | tf_op jit(solution)/shard_map/ppermute | solution.py:72
  189.7 9.5 %collective-permute-start.50 = (bf16[2,96,768]{2,1,0:T(8,128)(2,1)S(1)}, bf16[2,96,768]{2,1,0:T(8,128)(2,1)S(1)}, u32[]{:S(2)}, u32[]{:S(2)}) collective-permute-start(bf16[2,96,768]{2,1,0:T(8,128)(2,1)S(1)} %pad_maximum_fusion.6), channel_id=1, source_target_pairs={{0,8},{2,10},{4,12},{6,14},{8,0},{10,2},{12,4},{14,6},{16,24},{18,... | collective-permute-start | bytes 884744 | tf_op jit(solution)/shard_map/ppermute | solution.py:72
  189.7 21.4 %collective-permute-start.28 = (bf16[2,128,768]{2,1,0:T(8,128)(2,1)S(1)}, bf16[2,128,768]{2,1,0:T(8,128)(2,1)S(1)}, u32[]{:S(2)}, u32[]{:S(2)}) collective-permute-start(bf16[2,128,768]{2,1,0:T(8,128)(2,1)S(1)} %get-tuple-element.138), channel_id=1, source_target_pairs={{0,8},{2,10},{4,12},{6,14},{8,0},{10,2},{12,4},{14,6},{16,24},{18,... | collective-permute-start | bytes 1179656 | tf_op jit(solution)/shard_map/ppermute | solution.py:72
  199.2 22.5 %collective-permute-start.52 = (bf16[4,96,768]{2,1,0:T(8,128)(2,1)S(1)}, bf16[4,96,768]{2,1,0:T(8,128)(2,1)S(1)}, u32[]{:S(2)}, u32[]{:S(2)}) collective-permute-start(bf16[4,96,768]{2,1,0:T(8,128)(2,1)S(1)} %pad_maximum_fusion.2.refs_0_), channel_id=1, source_target_pairs={{0,4},{2,6},{4,0},{6,2},{8,12},{10,14},{12,8},{14,10},{16,20},{18,... | collective-permute-start | bytes 1769480 | tf_op jit(solution)/shard_map/ppermute | solution.py:72
  201.6 20.1 %collective-permute-start.51 = (bf16[4,96,768]{2,1,0:T(8,128)(2,1)S(1)}, bf16[4,96,768]{2,1,0:T(8,128)(2,1)S(1)}, u32[]{:S(2)}, u32[]{:S(2)}) collective-permute-start(bf16[4,96,768]{2,1,0:T(8,128)(2,1)S(1)} %pad_maximum_fusion.2.refs_0_), channel_id=1, source_target_pairs={{0,2},{2,0},{4,6},{6,4},{8,10},{10,8},{12,14},{14,12},{16,18},{18,... | collective-permute-start | bytes 1769480 | tf_op jit(solution)/shard_map/ppermute | solution.py:72
  209.1 18.4 %collective-permute-start.43 = (bf16[2,144,576]{2,1,0:T(8,128)(2,1)S(1)}, bf16[2,144,576]{2,1,0:T(8,128)(2,1)S(1)}, u32[]{:S(2)}, u32[]{:S(2)}) collective-permute-start(bf16[2,144,576]{2,1,0:T(8,128)(2,1)S(1)} %slice.193), channel_id=1, source_target_pairs={{0,4},{2,6},{4,0},{6,2},{8,12},{10,14},{12,8},{14,10},{16,20},{18,... | collective-permute-start | bytes 995336 | tf_op jit(solution)/shard_map/ppermute | solution.py:72
  210.8 16.8 %collective-permute-start.44 = (bf16[2,144,576]{2,1,0:T(8,128)(2,1)S(1)}, bf16[2,144,576]{2,1,0:T(8,128)(2,1)S(1)}, u32[]{:S(2)}, u32[]{:S(2)}) collective-permute-start(bf16[2,144,576]{2,1,0:T(8,128)(2,1)S(1)} %slice.194), channel_id=1, source_target_pairs={{0,2},{2,0},{4,6},{6,4},{8,10},{10,8},{12,14},{14,12},{16,18},{18,... | collective-permute-start | bytes 995336 | tf_op jit(solution)/shard_map/ppermute | solution.py:72
  211.2 21.3 %collective-permute-start.29 = (bf16[128,768]{1,0:T(8,128)(2,1)S(1)}, bf16[128,768]{1,0:T(8,128)(2,1)S(1)}, u32[]{:S(2)}, u32[]{:S(2)}) collective-permute-start(bf16[128,768]{1,0:T(8,128)(2,1)S(1)} %fusion.6), channel_id=1, source_target_pairs={{0,24},{2,26},{4,28},{6,30},{8,16},{10,18},{12,20},{14,22},{16,8},... | collective-permute-start | bytes 589832 | tf_op jit(solution)/shard_map/ppermute | solution.py:72
  221.7 11.6 %collective-permute-start.53 = (bf16[2,96,768]{2,1,0:T(8,128)(2,1)S(1)}, bf16[2,96,768]{2,1,0:T(8,128)(2,1)S(1)}, u32[]{:S(2)}, u32[]{:S(2)}) collective-permute-start(bf16[2,96,768]{2,1,0:T(8,128)(2,1)S(1)} %slice.200), channel_id=1, source_target_pairs={{0,4},{2,6},{4,0},{6,2},{8,12},{10,14},{12,8},{14,10},{16,20},{18,... | collective-permute-start | bytes 884744 | tf_op jit(solution)/shard_map/ppermute | solution.py:72
  223.4 10.0 %collective-permute-start.54 = (bf16[2,96,768]{2,1,0:T(8,128)(2,1)S(1)}, bf16[2,96,768]{2,1,0:T(8,128)(2,1)S(1)}, u32[]{:S(2)}, u32[]{:S(2)}) collective-permute-start(bf16[2,96,768]{2,1,0:T(8,128)(2,1)S(1)} %slice.201), channel_id=1, source_target_pairs={{0,2},{2,0},{4,6},{6,4},{8,10},{10,8},{12,14},{14,12},{16,18},{18,... | collective-permute-start | bytes 884744 | tf_op jit(solution)/shard_map/ppermute | solution.py:72
  232.5 4.5 %collective-permute-start.45 = (bf16[2,4,24,768]{3,2,1,0:T(8,128)(2,1)S(1)}, bf16[2,4,24,768]{3,2,1,0:T(8,128)(2,1)S(1)}, u32[]{:S(2)}, u32[]{:S(2)}) collective-permute-start(bf16[2,4,24,768]{3,2,1,0:T(8,128)(2,1)S(1)} %get-tuple-element.149), channel_id=1, source_target_pairs={{0,1},{1,0},{2,3},{3,2},{4,5},{5,4},{6,7},{7,6},{8,9},{9,8},{10,11... | collective-permute-start | bytes 884744 | tf_op jit(solution)/shard_map/ppermute | solution.py:602
  (11 other events, 55.5 us)
Sparse Core Ops, SparseCore 0:
  9.6 12.2 all-gather.5
  23.4 15.4 all-gather.7
  40.4 15.5 all-gather.9
